TPU v7x, 256 devices: a whole 4x4x8 slice. The times are simulated.
256 devices in a mesh: row: 16 (over z_lo, x, core), col: 16 (over y, z_hi).
Axes of the slice: x: 4, y: 4, z: 8 (z_hi: 4, z_lo: 2; z = z_hi * 2 + z_lo), core: 2. Of those that a mesh axis runs over, the one named last changes fastest.
Arguments:
- pool: bfloat16 [16384, 1024], P(('row', 'col')), may hold values from -16 to 16
- targets: bfloat16 [16384, 1024], P(('row', 'col')), may hold values from -16 to 16
- counts: int32 [16384], P(('row', 'col')), may hold values from 0 to 7, as said below
Outputs:
- proof: float32 [16384], P(('row', 'col'))
- gradient: float32 [16384, 1024], P(('row', 'col'))
Inputs may be any that keep to these rules, and one draw needn't show every extreme that they name: `counts`: counts of selections; the last pool example has count 7.
All inputs are finite; a program needn't handle non-finite values.
Results may differ from a plain program's by a relative error of at most 0.0014.
Values may be sent and summed in bfloat16 or wider, within the bound.
No kernel may reach another device: no remote copies, remote signals or barrier semaphores. Data moves between devices by JAX's collectives and lax.ppermute only.
A program may use at most 64 MiB of HBM per device.

v0:
```python
import jax
import jax.numpy as jnp
from jax import lax
from jax.sharding import Mesh
from jax.sharding import PartitionSpec as P

ROW_COL = ("row_0", "row_1", "row_2", "col_0", "col_1")
ROW = ("row_0", "row_1", "row_2")
COL = ("col_0", "col_1")


def over_axes(x, axes):
    for axis in axes:
        x = lax.psum(x, axis)
    return x


def copy_for_each(x, axis):
    copies = jnp.broadcast_to(x, (lax.axis_size(axis), *x.shape))
    return lax.all_to_all(copies, axis, split_axis=0, concat_axis=0, tiled=True)


def laid_out(blocks, dim):
    blocks = jnp.moveaxis(blocks, 0, dim)
    lengths = blocks.shape
    return blocks.reshape(*lengths[:dim], lengths[dim] * lengths[dim + 1], *lengths[dim + 2 :])


def gathered_copies(x, axis, dim):
    blocks = copy_for_each(x, axis)
    return laid_out(blocks, dim)


def side_by_side(arrays, axis, dim, along):
    columns = [a.reshape(*a.shape[:along], -1) for a in arrays]
    both = jnp.concatenate(columns, axis=along)
    filled, at, gathered = (lax.psum_scatter(both, axis, scatter_dimension=dim, tiled=True), 0, [])
    for a, column in zip(arrays, columns):
        piece = filled[..., at : at + column.shape[along]]
        gathered.append(piece.reshape(*piece.shape[:along], *a.shape[along:]))
        at += column.shape[along]
    return tuple(gathered)


def kernel_tile(row_panel, row_norms, columns):
    col_float = columns.astype(jnp.float32)
    col_norms = jnp.sum(col_float * col_float, axis=1)
    inner = lax.dot_general(
        row_panel, columns, (((1,), (1,)), ((), ())), preferred_element_type=jnp.float32
    )
    squared = row_norms[:, None] + col_norms[None, :] - 2.0 * inner
    return jnp.exp(-squared * (0.5 / columns.shape[1]))


def make_update(row_panel, row_norms):

    def update(totals, pieces, offset):
        col_pool, col_counts, col_targets = pieces
        pool_kernel = (
            kernel_tile(row_panel, row_norms, col_pool) * col_counts.astype(jnp.float32)[None, :]
        )
        target_kernel = kernel_tile(row_panel, row_norms, col_targets)
        pool_mass = jnp.sum(pool_kernel, axis=1)
        target_mass = jnp.sum(target_kernel, axis=1)
        pool_pull = jnp.dot(
            pool_kernel.astype(jnp.bfloat16), col_pool, preferred_element_type=jnp.float32
        )
        target_pull = jnp.dot(
            target_kernel.astype(jnp.bfloat16), col_targets, preferred_element_type=jnp.float32
        )
        return (pool_mass, target_mass, pool_pull, target_pull)

    return update


def finish(row_panel, totals, weight_total, target_count):
    row_float = row_panel.astype(jnp.float32)
    pool_mass, target_mass, pool_pull, target_pull = totals
    proof = target_mass / target_count - pool_mass / weight_total
    gradient = (target_pull - target_mass[:, None] * row_float) / target_count - (
        pool_pull - pool_mass[:, None] * row_float
    ) / weight_total
    return (proof, gradient)


def on_device(pool, targets, counts):
    weight_total = over_axes(jnp.sum(counts.astype(jnp.float32)), ROW_COL)
    target_count = targets.shape[0] * lax.axis_size(ROW) * lax.axis_size(COL)
    row_panel = gathered_copies(pool, ROW, 0)
    row_float = row_panel.astype(jnp.float32)
    row_norms = jnp.sum(row_float * row_float, axis=1)
    panel_size = row_panel.shape[0]
    width = row_panel.shape[1]
    initial = (
        jnp.zeros((panel_size,), jnp.float32),
        jnp.zeros((panel_size,), jnp.float32),
        jnp.zeros((panel_size, width), jnp.float32),
        jnp.zeros((panel_size, width), jnp.float32),
    )
    update = make_update(row_panel, row_norms)
    totals = update(
        initial,
        (
            lax.all_gather(pool, COL, axis=0, tiled=True),
            lax.all_gather(counts, COL, axis=0, tiled=True),
            lax.all_gather(targets, COL, axis=0, tiled=True),
        ),
        jnp.int32(0),
    )
    proof, gradient = finish(row_panel, totals, weight_total, target_count)
    proof, gradient = side_by_side((proof, gradient), ROW, 0, 1)
    return (proof, gradient)


def solution(mesh):
    split = Mesh(mesh.devices.reshape(2, 4, 2, 4, 4), ("row_0", "row_1", "row_2", "col_0", "col_1"))
    in_specs = (P(ROW_COL, None), P(ROW_COL, None), P(ROW_COL))
    out_specs = (P(ROW_COL), P(ROW_COL, None))
    return jax.shard_map(
        on_device, mesh=split, in_specs=in_specs, out_specs=out_specs, check_vma=False
    )
```

profile of v0, /device:TPU:8, one launch (start us, length us, event | category | flops | bytes accessed | tf_op | source)
XLA Modules:
  0.0 236.9 jit_solution(2199442942115737959)
XLA Ops:
  7.2 0.7 all-gather.5.cloned.1.call-update
  7.9 2.5 %broadcast_in_dim.2 = bf16[16,64,1024]{2,1,0:T(8,128)(2,1)} broadcast(bf16[64,1024]{1,0:T(8,128)(2,1)} %param.3), dimensions={1,2} | broadcast | bytes 2228224 | tf_op jit(solution)/shard_map/broadcast_in_dim | solution.py:19
  10.4 5.8 %all-to-all-start = ((bf16[16,64,1024]{2,1,0:T(8,128)(2,1)}), bf16[16,64,1024]{2,1,0:T(8,128)(2,1)S(1)}, u32[]{:S(2)}, u32[]{:S(2)}) async-start(bf16[16,64,1024]{2,1,0:T(8,128)(2,1)} %broadcast_in_dim.2), calls=%async_computation | async-start | bytes 4194304 | tf_op jit(solution)/shard_map/all_to_all | solution.py:20
  16.2 0.0 all-gather.3.cloned.1.call-start
  16.3 0.7 all-gather.3.cloned.1.call-update
  17.0 0.0 reduce-scatter.4.cloned.1.call-start
  17.0 0.6 convert_reduce_fusion
  17.6 29.2 %psum.35 = f32[]{:T(128)} all-reduce(f32[]{:T(128)} %convert_reduce_fusion), channel_id=1, replica_groups=mesh['row_0'=2,'row_1'=4,'row_2'=2,'col_0'=4,'col_1'=4] {'row_0'}, use_global_device_ids=true, to_apply=%region_6.0 | all-reduce | flops 1 | bytes 8 | tf_op jit(solution)/shard_map/psum | solution.py:14
  46.9 12.6 %psum.36 = f32[]{:T(128)} all-reduce(f32[]{:T(128)} %psum.35), channel_id=1, replica_groups=mesh['row_0'=2,'row_1'=4,'row_2'=2,'col_0'=4,'col_1'=4] {'row_1'}, use_global_device_ids=true, to_apply=%region_7.0 | all-reduce | flops 1 | bytes 8 | tf_op jit(solution)/shard_map/psum | solution.py:14
  59.4 3.1 %psum.37 = f32[]{:T(128)} all-reduce(f32[]{:T(128)} %psum.36), channel_id=1, replica_groups=mesh['row_0'=2,'row_1'=4,'row_2'=2,'col_0'=4,'col_1'=4] {'row_2'}, use_global_device_ids=true, to_apply=%region_8.0 | all-reduce | flops 1 | bytes 8 | tf_op jit(solution)/shard_map/psum | solution.py:14
  62.5 9.3 %psum.38 = f32[]{:T(128)} all-reduce(f32[]{:T(128)} %psum.37), channel_id=1, replica_groups=mesh['row_0'=2,'row_1'=4,'row_2'=2,'col_0'=4,'col_1'=4] {'col_0'}, use_global_device_ids=true, to_apply=%region_9.0 | all-reduce | flops 1 | bytes 8 | tf_op jit(solution)/shard_map/psum | solution.py:14
  71.8 13.2 %psum.39 = f32[]{:T(128)} all-reduce(f32[]{:T(128)} %psum.38), channel_id=1, replica_groups=mesh['row_0'=2,'row_1'=4,'row_2'=2,'col_0'=4,'col_1'=4] {'col_1'}, use_global_device_ids=true, to_apply=%region_10.0 | all-reduce | flops 1 | bytes 8 | tf_op jit(solution)/shard_map/psum | solution.py:14
  85.1 0.6 dynamic-slice
  86.3 0.2 dynamic-update-slice
  86.6 15.5 %all-reduce = s32[1024]{0:T(1024)S(1)} all-reduce(s32[1024]{0:T(1024)S(1)} %dynamic-update-slice), channel_id=1, replica_groups=mesh['row_0'=2,'row_1'=4,'row_2'=2,'col_0'=4,'col_1'=4] {'col_0','col_1'}, use_global_device_ids=true, to_apply=%add | all-reduce | flops 1024 | bytes 8192
  102.1 2.6 %copy.9 = bf16[1024,1024]{0,1:T(8,128)(2,1)} copy(bf16[1024,1024]{1,0:T(8,128)(2,1)S(1)} %bitcast.11) | data formatting | bytes 4194304 | tf_op jit(solution)/shard_map/reshape | solution.py:26
  104.7 0.5 multiply_reduce_fusion.2
  105.2 0.1 add.16
  105.2 2.1 multiply_reduce_fusion
  107.3 5.9 %fusion.28 = f32[1024,1024]{0,1:T(8,128)} fusion(bf16[1024,1024]{1,0:T(8,128)(2,1)S(1)} %bitcast.12, bf16[1024,1024]{1,0:T(8,128)(2,1)} %all-gather.5.cloned.1.call-done), kind=kOutput, calls=%fused_computation.34 | convolution fusion | flops 2147483648 | bytes 8388608 | tf_op jit(solution)/shard_map/dot_general | solution.py:48
  113.2 20.5 %all-gather.3.cloned.1.call-done = bf16[1024,1024]{1,0:T(8,128)(2,1)} async-done(((bf16[64,1024]{1,0:T(8,128)(2,1)}), bf16[1024,1024]{1,0:T(8,128)(2,1)}) %all-gather.3.cloned.1.call-update) | async-done | bytes 2097168 | tf_op jit(solution)/shard_map/all_gather | solution.py:106
  133.7 2.1 multiply_reduce_fusion.1
  135.8 6.4 %fusion.6 = (f32[1024]{0:T(1024)S(1)}, f32[1024]{0:T(1024)S(1)}, f32[1024,1024]{0,1:T(8,128)S(1)}) fusion(f32[1024]{0:T(1024)S(1)} %multiply_reduce_fusion.1, f32[1024]{0:T(1024)S(1)} %add.16, f32[1024]{0:T(1024)S(1)} %convert_element_type.28, f32[1024,1024]{0,1:T(8,128)} %fusion.28, f32[1024]{0:T(1024)S(1)} %multiply_reduce_fusion, ...), kind=kOutput, calls=%fused_computation.14 | convolution fusion | flops 2161113088 | bytes 12607488 | tf_op jit(solution)/shard_map/dot_general | solution.py:48
  142.2 0.7 divide_subtract_fusion
  142.9 2.9 %fusion.9 = f32[1024,1024]{0,1:T(8,128)S(1)} fusion(bf16[1024,1024]{1,0:T(8,128)(2,1)S(1)} %copy-done, f32[1024,1024]{0,1:T(8,128)S(1)} %copy-done.5, f32[1024]{0:T(1024)S(1)} %convert_element_type.28, f32[1024]{0:T(1024)S(1)} %multiply_reduce_fusion, f32[1024]{0:T(1024)S(1)} %add.16), kind=kOutput, calls=%fused_computation.17 | convolution fusion | flops 2154823680 | bytes 10498048 | tf_op jit(solution)/shard_map/dot_general | solution.py:65
  145.8 4.4 %fusion.2 = f32[1024,1024]{0,1:T(8,128)S(1)} fusion(bf16[1024,1024]{0,1:T(8,128)(2,1)S(1)} %copy-done.2, f32[1024,1024]{0,1:T(8,128)S(1)} %fusion.9, f32[]{:T(128)} %psum.39, f32[1024]{0:T(1024)S(1)} %get-tuple-element.9, f32[1024]{0:T(1024)S(1)} %get-tuple-element.8, bf16[1024,1024]{1,0:T(8,128)(2,1)S(1)} %copy-done.1, ...), kind=kOutput, calls=%fused_computation.5 | convolution fusion | flops 2162163712 | bytes 16793604 | tf_op jit(solution)/shard_map/dot_general | solution.py:68
  150.2 2.5 %pad_maximum_fusion = f32[1024,1025]{0,1:T(8,128)} fusion(f32[1024,1024]{0,1:T(8,128)S(1)} %fusion.2, f32[1024,1]{0,1:T(1,128)S(1)} %bitcast.14), kind=kLoop, calls=%fused_computation.2 | loop fusion | flops 1049600 | bytes 8396800 | tf_op jit(solution)/shard_map/concatenate | solution.py:36
  152.8 5.6 %copy.11 = f32[1024,1025]{1,0:T(8,128)} copy(f32[1024,1025]{0,1:T(8,128)} %pad_maximum_fusion) | data formatting | bytes 8396800
  158.4 68.9 %reduce-scatter.4.cloned.1.call-done = f32[64,1025]{1,0:T(8,128)} async-done(((f32[1024,1025]{1,0:T(8,128)}), f32[64,1025]{1,0:T(8,128)}) %reduce-scatter.4.cloned.1.call-update) | async-done | bytes 262416
  227.3 0.8 slice.8
  228.0 0.6 copy.13
  228.6 1.8 slice.9
  (18 shorter events, 0.1 us)
Async XLA Ops:
  7.2 77.9 %copy-start.4 = (u32[256]{0:T(256)S(1)}, u32[256]{0:T(256)}, u32[]{:S(2)}) copy-start(u32[256]{0:T(256)} %constant.16) | copy-start | bytes 3076
  7.2 9.8 %copy-start.3 = (s32[64]{0:T(128)S(1)}, s32[64]{0:T(128)}, u32[]{:S(2)}) copy-start(s32[64]{0:T(128)} %param.5) | copy-start | bytes 772
  7.2 98.1 %all-gather.5.cloned.1.call-start = ((), (), s32[]{:S(2)}) async-start(), calls=%async_computation.3 | async-start | bytes 2228224 | tf_op jit(solution)/shard_map/all_gather | solution.py:104
  10.4 91.6 %all-to-all-start = ((bf16[16,64,1024]{2,1,0:T(8,128)(2,1)}), bf16[16,64,1024]{2,1,0:T(8,128)(2,1)S(1)}, u32[]{:S(2)}, u32[]{:S(2)}) async-start(bf16[16,64,1024]{2,1,0:T(8,128)(2,1)} %broadcast_in_dim.2), calls=%async_computation | async-start | bytes 4194304 | tf_op jit(solution)/shard_map/all_to_all | solution.py:20
  16.2 117.5 %all-gather.3.cloned.1.call-start = ((), (), s32[]{:S(2)}) async-start(), calls=%async_computation.2 | async-start | bytes 2228224 | tf_op jit(solution)/shard_map/all_gather | solution.py:106
  17.0 210.3 %reduce-scatter.4.cloned.1.call-start = ((), (), s32[]{:S(2)}) async-start(), calls=%async_computation.4 | async-start | bytes 5013504
  135.8 7.1 %copy-start = (bf16[1024,1024]{1,0:T(8,128)(2,1)S(1)}, bf16[1024,1024]{1,0:T(8,128)(2,1)}, u32[]{:S(2)}) copy-start(bf16[1024,1024]{1,0:T(8,128)(2,1)} %all-gather.5.cloned.1.call-done) | copy-start | bytes 6291460
  135.8 7.1 %copy-start.5 = (f32[1024,1024]{0,1:T(8,128)S(1)}, f32[1024,1024]{0,1:T(8,128)}, u32[]{:S(2)}) copy-start(f32[1024,1024]{0,1:T(8,128)} %fusion.28) | copy-start | bytes 12582916
  142.9 2.9 %copy-start.1 = (bf16[1024,1024]{1,0:T(8,128)(2,1)S(1)}, bf16[1024,1024]{1,0:T(8,128)(2,1)}, u32[]{:S(2)}) copy-start(bf16[1024,1024]{1,0:T(8,128)(2,1)} %all-gather.3.cloned.1.call-done) | copy-start | bytes 6291460
  142.9 2.9 %copy-start.2 = (bf16[1024,1024]{0,1:T(8,128)(2,1)S(1)}, bf16[1024,1024]{0,1:T(8,128)(2,1)}, u32[]{:S(2)}) copy-start(bf16[1024,1024]{0,1:T(8,128)(2,1)} %copy.9) | copy-start | bytes 6291460
Sparse Core Ops, SparseCore 0:
  10.5 63.3 all-gather.4
  76.2 57.4 all-gather.2
  158.5 68.7 reduce-scatter.3
where the time goes:
time: 237 us
  waiting for transfers between devices  90.8 us (38%)
  blocking collectives  83 us (35%)
  matrix products  19.6 us (8%)
  local copies, waits for them, and re-layouts  14.8 us (6%)
  between operations  14.5 us (6%)
  other arithmetic  8.4 us (4%)
  starting transfers between devices  5.88 us (2%)
    unnamed x4, waiting for transfers between devices  70.3 us
    psum x5, blocking collectives, over_axes(): x = lax.psum(x, axis)  67.4 us
    all_gather x1, waiting for transfers between devices, on_device(): lax.all_gather(targets, COL, axis=0, tiled=True)  20.5 us
    unnamed x1, blocking collectives  15.5 us
    dot_general x2, matrix products, kernel_tile(): lax.dot_general(row_panel, columns, (((1,), (1,)), ((), ())), preferred_e...  12.3 us
    unnamed x17, local copies, waits for them, and re-layouts  7.05 us
    all_to_all x1, starting transfers between devices, copy_for_each(): return lax.all_to_all(copies, axis, split_axis=0, concat_axis=0, tiled=True)  5.76 us
  transfers between devices with their start and end apart: 4, of which 2 were waited for; matrix products, arithmetic and copies ran while one was open for 6% of the time, Pallas kernels for 0%

commit v1 on v0

v1 whole, which is shorter than its diff:
```python
import functools

import jax
import jax.numpy as jnp
from jax import lax
from jax.experimental import pallas as pl
from jax.experimental.pallas import tpu as pltpu
from jax.sharding import Mesh
from jax.sharding import PartitionSpec as P

AXES = ("zl", "x", "c", "y", "zh")
RING = ("zl", "zh")
PLANE = ("x", "c", "y")
LANES = 128
META = 16
LEVELS = 32767.0
F32, BF16 = jnp.float32, jnp.bfloat16
VMEM = pltpu.CompilerParams(vmem_limit_bytes=56 * 1024 * 1024)


def shape(dims, dtype):
    return jax.ShapeDtypeStruct(dims, dtype)


def in_vmem(body, name, out_shape, flops=0, traffic=1 << 20, scratch=(), **more):
    spec = pl.BlockSpec(memory_space=pltpu.VMEM)

    def call(*args):
        return pl.pallas_call(
            body,
            out_shape=out_shape,
            in_specs=[spec] * len(args),
            out_specs=jax.tree.map(lambda _: spec, out_shape),
            scratch_shapes=scratch,
            compiler_params=VMEM,
            cost_estimate=pl.CostEstimate(flops=flops, bytes_accessed=traffic, transcendentals=0),
            name=name,
            **more,
        )(*args)

    return call


def lane_sums(x):
    total = x[:, :LANES]
    for at in range(LANES, x.shape[1], LANES):
        total = total + x[:, at : at + LANES]
    return total


def square_norms(block):
    wide = block.astype(F32)
    return jnp.sum(lane_sums(wide * wide), axis=1, keepdims=True)


def along_lanes(column):
    return jnp.transpose(jnp.broadcast_to(column, (column.shape[0], LANES)))[:1]


def halves(a, b):
    return jnp.concatenate([a, b], axis=1)


def pack_block(pool, targets, counts, block, copies):
    height = pool.shape[0]
    block[:height, :] = pool[...]
    block[height : 2 * height, :] = targets[...]
    norms = along_lanes(jnp.concatenate([square_norms(pool[...]), square_norms(targets[...])], axis=0))
    high = norms.astype(BF16).astype(F32)
    middle = (norms - high).astype(BF16).astype(F32)
    low = norms - high - middle
    weights = halves(counts[...].astype(F32), jnp.ones((1, height), F32))
    meta = jnp.concatenate([weights, high, middle, low, jnp.zeros((META - 4, LANES), F32)], axis=0)
    block[2 * height :, :] = jnp.concatenate(
        [meta, jnp.zeros((META, block.shape[1] - LANES), F32)], axis=1
    ).astype(BF16)
    for i in range(copies.shape[0]):
        copies[i] = pool[...]


def pack_line(*refs):
    blocks, (piece, chosen) = refs[:-2], refs[-2:]
    count, height = len(blocks), (blocks[0].shape[0] - META) // 2
    for j, block in enumerate(blocks):
        piece[j * height : (j + 1) * height, :] = block[:height, :]
        piece[(count + j) * height : (count + j + 1) * height, :] = block[height : 2 * height, :]
    metas = [block[2 * height :, :LANES].astype(F32) for block in blocks]
    lanes = [meta[:, half : half + height] for half in (0, height) for meta in metas]
    pairs = [halves(a, b) for a, b in zip(lanes[::2], lanes[1::2])]
    width = piece.shape[1] - LANES * len(pairs)
    piece[2 * count * height :, :] = jnp.concatenate(
        [*pairs, jnp.zeros((META, width), F32)], axis=1
    ).astype(BF16)
    total = jnp.zeros((), F32)
    for j in range(count):
        total += jnp.sum(lanes[j][:1])
    chosen[...] = jnp.full(chosen.shape, total, F32)


def kernels_into(panel, norms, pieces, weights, masses, rows):
    ring, height, width = panel.shape
    blocks = rows // height
    for half in range(2):
        for i, piece in enumerate(pieces):
            size = (piece.shape[0] - META) // 2
            at = half * size
            columns = piece[at : at + size, :]
            meta = piece[2 * size :, at : at + size].astype(F32)
            col_norms = meta[1:2] + meta[2:3] + meta[3:4]
            for r in range(ring // blocks):
                part = slice(r * rows, (r + 1) * rows)
                left = panel[r * blocks : (r + 1) * blocks].reshape(rows, width)
                inner = lax.dot_general(
                    left, columns, (((1,), (1,)), ((), ())), preferred_element_type=F32
                )
                squared = norms[part, :1] + col_norms - 2.0 * inner
                kernel = jnp.exp(-squared * (0.5 / width))
                if half == 0:
                    kernel = kernel * meta[:1]
                masses[half][part, :] += lane_sums(kernel)
                weights[half][part, i * size : (i + 1) * size] = kernel.astype(BF16)


def pulled(weights, pieces, half, part):
    size = (pieces[0].shape[0] - META) // 2
    total = None
    for i, piece in enumerate(pieces):
        one = jnp.dot(
            weights[half][part, i * size : (i + 1) * size],
            piece[half * size : (half + 1) * size, :],
            preferred_element_type=F32,
        )
        total = one if total is None else total + one
    return total


def own_columns(rows, lines, panel, *refs):
    pieces, (pp, tp, pm, tm, norms), weights = refs[:lines], refs[lines : lines + 5], refs[lines + 5 :]
    ring, height, _ = panel.shape
    for i in range(ring):
        part = slice(i * height, (i + 1) * height)
        norms[part, :] = jnp.broadcast_to(square_norms(panel[i]), (height, LANES))
    pm[...] = jnp.zeros_like(pm)
    tm[...] = jnp.zeros_like(tm)
    kernels_into(panel, norms, pieces, weights, (pm, tm), rows)
    for at in range(0, ring * height, rows):
        part = slice(at, at + rows)
        pp[part, :] = pulled(weights, pieces, 0, part)
        tp[part, :] = pulled(weights, pieces, 1, part)


def other_columns(rows, lines, target_count, panel, *refs):
    pieces, refs = refs[:lines], refs[lines:]
    pp, tp, pm_old, tm_old, norms, total, coded, pm, tm, *weights = refs
    ring, height, width = panel.shape
    pm[...] = pm_old[...]
    tm[...] = tm_old[...]
    kernels_into(panel, norms, pieces, weights, (pm, tm), rows)
    weight = total[:1, :1]
    for at in range(0, ring * height, rows):
        part = slice(at, at + rows)
        pool_pull = pp[part, :] + pulled(weights, pieces, 0, part)
        target_pull = tp[part, :] + pulled(weights, pieces, 1, part)
        pool_mass = jnp.sum(pm[part, :], axis=1, keepdims=True)
        target_mass = jnp.sum(tm[part, :], axis=1, keepdims=True)
        own = panel[at // height : (at + rows) // height].reshape(rows, width).astype(F32)
        proof = target_mass / target_count - pool_mass / weight
        term = (target_pull - target_mass * own) * (1.0 / target_count) - (
            pool_pull - pool_mass * own
        ) * (1.0 / weight)
        code = encode(term, proof)
        for i in range(rows // height):
            coded[at // height + i] = code[i * height : (i + 1) * height, :]


def step_scale(step):
    return jnp.exp2(step * (1.0 / 128.0))


def encode(term, proof):
    top = jnp.maximum(jnp.max(jnp.abs(term), axis=1, keepdims=True), 1e-30)
    step = jnp.ceil(jnp.log2(top) * 128.0)
    steps = jnp.round(term * (LEVELS / step_scale(step)))
    steps = jnp.clip(steps, -LEVELS, LEVELS)
    first = jnp.round(proof * 8192.0)
    rest = (proof * 8192.0 - first) * 32768.0
    second = jnp.round(rest)
    third = jnp.round((rest - second) * 32768.0)
    lane = lax.broadcasted_iota(jnp.int32, (term.shape[0], LANES), 1)
    notes = jnp.where(
        lane == 0, step, jnp.where(lane == 1, first, jnp.where(lane == 2, second, third))
    )
    return jnp.concatenate([steps, notes], axis=1).astype(jnp.int32).astype(jnp.int16)


def add_terms(coded, proof, gradient):
    width = gradient.shape[1]
    total, small = 0.0, 0.0
    for i in range(coded.shape[0]):
        code = coded[i].astype(jnp.int32).astype(F32)
        notes = code[:, width:]
        total += code[:, :width] * (step_scale(notes[:, :1]) * (1.0 / LEVELS))
        parts = notes[:, 1:2], notes[:, 2:3], notes[:, 3:4]
        small += (parts[0] + (parts[1] + parts[2] * (1.0 / 32768.0)) * (1.0 / 32768.0)) * (1.0 / 8192.0)
    gradient[...] = total
    proof[...] = along_lanes(small)


def place(z):
    return z % 2 * 4 + z // 2


def along_line(x, shift, phase):
    pairs = []
    for i in range(4):
        for j in range(4):
            for c in range(2):
                there = (shift(i), j) if (c + phase) % 2 == 0 else (i, shift(j))
                pairs.append(((i * 2 + c) * 4 + j, (there[0] * 2 + c) * 4 + there[1]))
    return lax.ppermute(x, PLANE, pairs)


def line(x, phase):
    return [x] + [along_line(x, lambda i, k=k: (i + k) % 4, phase) for k in (1, 3, 2)]


def other_core(x):
    return lax.ppermute(x, "c", [(0, 1), (1, 0)])


def on_device(pool, targets, counts):
    ring = lax.axis_size(RING)
    height, width = pool.shape
    rows = ring * height
    target_count = float(height * lax.axis_size(AXES))

    block, copies = in_vmem(
        pack_block,
        "pack_block",
        (shape((2 * height + META, width), BF16), shape((ring, height, width), BF16)),
    )(pool, targets, counts.reshape(1, height))
    blocks = line(block, 0)
    panel = lax.all_to_all(copies, RING, split_axis=0, concat_axis=0, tiled=True)
    piece, total = in_vmem(
        pack_line,
        "pack_line",
        (shape((2 * height * len(blocks) + META, width), BF16), shape((8, LANES), F32)),
    )(*blocks)
    pieces = line(piece, 1)
    others = [other_core(p) for p in pieces]

    for bit in (1, 2):
        total = total + along_line(total, lambda i: i ^ bit, 1)
    for bit in (1, 2, 4):
        total = total + lax.ppermute(total, RING, [(place(i), place(i ^ bit)) for i in range(ring)])
    total = total + other_core(total)

    columns = height * len(blocks) * len(pieces)
    flops = 8 * rows * columns * width
    weights = [pltpu.VMEM((rows, columns), BF16)] * 2
    state = in_vmem(
        functools.partial(own_columns, 256, len(pieces)),
        "own_columns",
        (shape((rows, width), F32),) * 2 + (shape((rows, LANES), F32),) * 3,
        flops=flops,
        scratch=weights,
    )(panel, *pieces)
    coded = in_vmem(
        functools.partial(other_columns, 256, len(pieces), target_count),
        "other_columns",
        shape((ring, height, width + LANES), jnp.int16),
        flops=flops,
        scratch=[pltpu.VMEM((rows, LANES), F32)] * 2 + weights,
    )(panel, *others, *state, total)
    coded = lax.all_to_all(coded, RING, split_axis=0, concat_axis=0, tiled=True)
    proof, gradient = in_vmem(
        add_terms, "add_terms", (shape((1, height), F32), shape((height, width), F32))
    )(coded)
    return proof.reshape(height), gradient


def solution(mesh):
    split = Mesh(mesh.devices.reshape(2, 4, 2, 4, 4), AXES)
    return jax.shard_map(
        on_device,
        mesh=split,
        in_specs=(P(AXES, None), P(AXES, None), P(AXES)),
        out_specs=(P(AXES), P(AXES, None)),
        check_vma=False,
    )
```

time: 237 us -> 140 us (0.59)
  waiting for transfers between devices: 90.8 us -> 29.7 us
  blocking collectives: 83 us -> 38.4 us
  starting transfers between devices: 5.88 us -> 38.9 us
  Pallas kernels: 0 us -> 27.4 us
  matrix products: 19.6 us -> 0 us
  between operations: 14.5 us -> 0.72 us
  local copies, waits for them, and re-layouts: 14.8 us -> 3.48 us
  other arithmetic: 8.4 us -> 1.29 us
    unnamed x4 -> x0, waiting for transfers between devices: 70.3 us -> none
    psum x5 -> x0, blocking collectives: 67.4 us -> none  [over_axes(): x = lax.psum(x, axis)]
    all_to_all x0 -> x1, blocking collectives: none -> 38.4 us  [on_device(): coded = lax.all_to_all(coded, RING, split_axis=0, concat_axis=0, tiled=True)]
    ppermute x0 -> x16, starting transfers between devices: none -> 30.5 us  [the longest x8 11.9 us: along_line(): return lax.ppermute(x, PLANE, pairs)]
    ppermute x0 -> x16, waiting for transfers between devices: none -> 29.7 us  [the longest x8 23.8 us: along_line(): return lax.ppermute(x, PLANE, pairs)]
    pallas_call x0 -> x5, Pallas kernels: none -> 27.4 us  [call(): pl.pallas_call(body, out_shape=out_shape, in_specs=[spec] * len(args), ou...]
    all_gather x2 -> x0, waiting for transfers between devices: 20.5 us -> none  [the longest x1 20.5 us: on_device(): lax.all_gather(targets, COL, axis=0, tiled=True)]
    dot_general x4 -> x0, matrix products: 19.6 us -> none  [the longest x2 12.3 us: kernel_tile(): lax.dot_general(row_panel, columns, (((1,), (1,)), ((), ())), preferred_e...]
  transfers between devices with their start and end apart: 4 -> 17, of which waited for: 2 -> 9; matrix products, arithmetic and copies ran while one was open for 6% -> 1% of each run, Pallas kernels for 0% -> 8%
where the time goes in v1:
time: 140 us
  starting transfers between devices  38.9 us (28%)
  blocking collectives  38.4 us (27%)
  waiting for transfers between devices  29.7 us (21%)
  Pallas kernels  27.4 us (20%)
  local copies, waits for them, and re-layouts  3.48 us (2%)
    all_to_all x1, blocking collectives, on_device(): coded = lax.all_to_all(coded, RING, split_axis=0, concat_axis=0, tiled=True)  38.4 us
    pallas_call x5, Pallas kernels, call(): pl.pallas_call(body, out_shape=out_shape, in_specs=[spec] * len(args), ou...  27.4 us
    ppermute x8, waiting for transfers between devices, along_line(): return lax.ppermute(x, PLANE, pairs)  23.8 us
    ppermute x8, starting transfers between devices, along_line(): return lax.ppermute(x, PLANE, pairs)  11.9 us
    ppermute x3, starting transfers between devices, on_device(): lax.ppermute(total, RING, [(place(i), place(i ^ bit)) for i in range(ring)])  10.9 us
    all_to_all x1, starting transfers between devices, on_device(): lax.all_to_all(copies, RING, split_axis=0, concat_axis=0, tiled=True)  8.47 us
    ppermute x5, starting transfers between devices, other_core(): return lax.ppermute(x, 'c', [(0, 1), (1, 0)])  7.66 us
    ppermute x3, waiting for transfers between devices, on_device(): lax.ppermute(total, RING, [(place(i), place(i ^ bit)) for i in range(ring)])  4.76 us
  transfers between devices with their start and end apart: 17, of which 9 were waited for; matrix products, arithmetic and copies ran while one was open for 1% of the time, Pallas kernels for 8%

profile of v1, /device:TPU:8, one launch (start us, length us, event | category | flops | bytes accessed | tf_op | source)
XLA Modules:
  0.0 139.9 jit_solution(14248097307904780560)
XLA Ops:
  0.6 2.2 %pack_block.1 = (bf16[144,1024]{1,0:T(8,128)(2,1)}, bf16[8,64,1024]{2,1,0:T(8,128)(2,1)}) custom-call(bf16[64,1024]{1,0:T(8,128)(2,1)} %pool.1, bf16[64,1024]{1,0:T(8,128)(2,1)} %targets.1, s32[1,64]{1,0:T(1,128)} %bitcast.2), custom_call_target="tpu_custom_call" | custom-call | bytes 1048576 | tf_op jit(solution)/shard_map/pack_block/pallas_call | solution.py:29
  2.8 1.5 %collective-permute-start = (bf16[144,1024]{1,0:T(8,128)(2,1)}, bf16[144,1024]{1,0:T(8,128)(2,1)S(1)}, u32[]{:S(2)}, u32[]{:S(2)}) collective-permute-start(bf16[144,1024]{1,0:T(8,128)(2,1)} %get-tuple-element.14.refs_0_), channel_id=1, source_target_pairs={{0,32},{16,20},{4,36},{20,24},{8,40},{24,28},{12,44},{28,16},{32,6... | collective-permute-start | bytes 884744 | tf_op jit(solution)/shard_map/ppermute | solution.py:220
  4.3 1.7 %collective-permute-start.1 = (bf16[144,1024]{1,0:T(8,128)(2,1)}, bf16[144,1024]{1,0:T(8,128)(2,1)S(1)}, u32[]{:S(2)}, u32[]{:S(2)}) collective-permute-start(bf16[144,1024]{1,0:T(8,128)(2,1)} %get-tuple-element.14.refs_0_), channel_id=1, source_target_pairs={{0,96},{16,28},{4,100},{20,16},{8,104},{24,20},{12,108},{28,24},{3... | collective-permute-start | bytes 884744 | tf_op jit(solution)/shard_map/ppermute | solution.py:220
  6.1 1.8 %collective-permute-start.2 = (bf16[144,1024]{1,0:T(8,128)(2,1)}, bf16[144,1024]{1,0:T(8,128)(2,1)S(1)}, u32[]{:S(2)}, u32[]{:S(2)}) collective-permute-start(bf16[144,1024]{1,0:T(8,128)(2,1)} %get-tuple-element.14.refs_0_), channel_id=1, source_target_pairs={{0,64},{16,24},{4,68},{20,28},{8,72},{24,16},{12,76},{28,20},{32,9... | collective-permute-start | bytes 884744 | tf_op jit(solution)/shard_map/ppermute | solution.py:220
  7.9 8.5 %all-to-all-start = ((bf16[8,64,1024]{2,1,0:T(8,128)(2,1)}), bf16[8,64,1024]{2,1,0:T(8,128)(2,1)S(1)}, u32[]{:S(2)}, u32[]{:S(2)}) async-start(bf16[8,64,1024]{2,1,0:T(8,128)(2,1)} %get-tuple-element.13), calls=%async_computation | async-start | bytes 2097152 | tf_op jit(solution)/shard_map/all_to_all | solution.py:243
  16.4 0.7 copy-done.1
  17.2 0.7 copy-done.3
  17.9 2.3 %pack_line.1 = (bf16[528,1024]{1,0:T(8,128)(2,1)}, f32[8,128]{1,0:T(8,128)}) custom-call(bf16[144,1024]{1,0:T(8,128)(2,1)} %get-tuple-element.14.refs_0_, bf16[144,1024]{1,0:T(8,128)(2,1)} %copy-done.1, bf16[144,1024]{1,0:T(8,128)(2,1)} %copy-done.2, bf16[144,1024]{1,0:T(8,128)(2,1)} %copy-done.3), custom_call_target="tpu_custom_call" | custom-call | bytes 1048576 | tf_op jit(solution)/shard_map/pack_line/pallas_call | solution.py:29
  20.2 1.6 %collective-permute-start.4 = (bf16[528,1024]{1,0:T(8,128)(2,1)}, bf16[528,1024]{1,0:T(8,128)(2,1)S(1)}, u32[]{:S(2)}, u32[]{:S(2)}) collective-permute-start(bf16[528,1024]{1,0:T(8,128)(2,1)} %get-tuple-element.15.refs_0_), channel_id=1, source_target_pairs={{0,4},{16,48},{4,8},{20,52},{8,12},{24,56},{12,0},{28,60},{32,36},... | collective-permute-start | bytes 3244040 | tf_op jit(solution)/shard_map/ppermute | solution.py:220
  22.3 2.3 %collective-permute-start.8 = (bf16[528,1024]{1,0:T(8,128)(2,1)}, bf16[528,1024]{1,0:T(8,128)(2,1)}, u32[]{:S(2)}, u32[]{:S(2)}) collective-permute-start(bf16[528,1024]{1,0:T(8,128)(2,1)} %get-tuple-element.15.refs_0_), channel_id=1, source_target_pairs={{0,8},{16,80},{4,12},{20,84},{8,0},{24,88},{12,4},{28,92},{32,40},... | collective-permute-start | bytes 3244040 | tf_op jit(solution)/shard_map/ppermute | solution.py:220
  24.6 11.0 %collective-permute-done.4.refs_1_ = bf16[528,1024]{1,0:T(8,128)(2,1)S(1)} collective-permute-done((bf16[528,1024]{1,0:T(8,128)(2,1)}, bf16[528,1024]{1,0:T(8,128)(2,1)S(1)}, u32[]{:S(2)}, u32[]{:S(2)}) %collective-permute-start.4) | collective-permute-done | bytes 1081376 | tf_op jit(solution)/shard_map/ppermute | solution.py:220
  35.6 1.7 %collective-permute-done.6.refs_2_ = bf16[528,1024]{1,0:T(8,128)(2,1)} collective-permute-done((bf16[528,1024]{1,0:T(8,128)(2,1)}, bf16[528,1024]{1,0:T(8,128)(2,1)}, u32[]{:S(2)}, u32[]{:S(2)}) %collective-permute-start.6) | collective-permute-done | bytes 1081376 | tf_op jit(solution)/shard_map/ppermute | solution.py:220
  37.3 7.6 %collective-permute-start.7 = (bf16[528,1024]{1,0:T(8,128)(2,1)}, bf16[528,1024]{1,0:T(8,128)(2,1)}, u32[]{:S(2)}, u32[]{:S(2)}) collective-permute-start(bf16[528,1024]{1,0:T(8,128)(2,1)} %collective-permute-done.6.refs_2_), channel_id=1, source_target_pairs={{0,16},{16,0},{1,17},{17,1},{2,18},{18,2},{3,19},{19,3},{4,20},{20... | collective-permute-start | bytes 3244040 | tf_op jit(solution)/shard_map/ppermute | solution.py:228
  44.9 4.7 %collective-permute-done.8.refs_3_ = bf16[528,1024]{1,0:T(8,128)(2,1)} collective-permute-done((bf16[528,1024]{1,0:T(8,128)(2,1)}, bf16[528,1024]{1,0:T(8,128)(2,1)}, u32[]{:S(2)}, u32[]{:S(2)}) %collective-permute-start.8) | collective-permute-done | bytes 1081376 | tf_op jit(solution)/shard_map/ppermute | solution.py:220
  49.6 0.6 collective-permute-start.10
  50.2 3.2 %collective-permute-done.10 = f32[8,128]{1,0:T(8,128)S(1)} collective-permute-done((f32[8,128]{1,0:T(8,128)}, f32[8,128]{1,0:T(8,128)S(1)}, u32[]{:S(2)}, u32[]{:S(2)}) %collective-permute-start.10) | collective-permute-done | bytes 4128 | tf_op jit(solution)/shard_map/ppermute | solution.py:220
  53.4 0.7 add.18
  54.1 1.9 %collective-permute-start.11 = (f32[8,128]{1,0:T(8,128)S(1)}, f32[8,128]{1,0:T(8,128)S(1)}, u32[]{:S(2)}, u32[]{:S(2)}) collective-permute-start(f32[8,128]{1,0:T(8,128)S(1)} %add.18), channel_id=1, source_target_pairs={{0,8},{16,80},{4,12},{20,84},{8,0},{24,88},{12,4},{28,92},{32,40},... | collective-permute-start | bytes 12296 | tf_op jit(solution)/shard_map/ppermute | solution.py:220
  56.0 3.2 %collective-permute-done.11 = f32[8,128]{1,0:T(8,128)S(1)} collective-permute-done((f32[8,128]{1,0:T(8,128)S(1)}, f32[8,128]{1,0:T(8,128)S(1)}, u32[]{:S(2)}, u32[]{:S(2)}) %collective-permute-start.11) | collective-permute-done | bytes 4128 | tf_op jit(solution)/shard_map/ppermute | solution.py:220
  59.2 2.0 %collective-permute-start.12 = (f32[8,128]{1,0:T(8,128)S(1)}, f32[8,128]{1,0:T(8,128)S(1)}, u32[]{:S(2)}, u32[]{:S(2)}) collective-permute-start(f32[8,128]{1,0:T(8,128)S(1)} %add.19), channel_id=1, source_target_pairs={{0,128},{128,0},{1,129},{129,1},{2,130},{130,2},{3,131},{131,3},{4... | collective-permute-start | bytes 12296 | tf_op jit(solution)/shard_map/ppermute | solution.py:255
  61.2 1.6 %collective-permute-done.12 = f32[8,128]{1,0:T(8,128)S(1)} collective-permute-done((f32[8,128]{1,0:T(8,128)S(1)}, f32[8,128]{1,0:T(8,128)S(1)}, u32[]{:S(2)}, u32[]{:S(2)}) %collective-permute-start.12) | collective-permute-done | bytes 4128 | tf_op jit(solution)/shard_map/ppermute | solution.py:255
  62.8 2.9 %collective-permute-start.13 = (f32[8,128]{1,0:T(8,128)S(1)}, f32[8,128]{1,0:T(8,128)S(1)}, u32[]{:S(2)}, u32[]{:S(2)}) collective-permute-start(f32[8,128]{1,0:T(8,128)S(1)} %add.20), channel_id=1, source_target_pairs={{0,1},{128,129},{1,0},{129,128},{2,3},{130,131},{3,2},{131,130},{4... | collective-permute-start | bytes 12296 | tf_op jit(solution)/shard_map/ppermute | solution.py:255
  65.7 1.6 %collective-permute-done.13 = f32[8,128]{1,0:T(8,128)S(1)} collective-permute-done((f32[8,128]{1,0:T(8,128)S(1)}, f32[8,128]{1,0:T(8,128)S(1)}, u32[]{:S(2)}, u32[]{:S(2)}) %collective-permute-start.13) | collective-permute-done | bytes 4128 | tf_op jit(solution)/shard_map/ppermute | solution.py:255
  67.3 5.9 %collective-permute-start.14 = (f32[8,128]{1,0:T(8,128)S(1)}, f32[8,128]{1,0:T(8,128)S(1)}, u32[]{:S(2)}, u32[]{:S(2)}) collective-permute-start(f32[8,128]{1,0:T(8,128)S(1)} %add.21), channel_id=1, source_target_pairs={{0,2},{128,130},{1,3},{129,131},{2,0},{130,128},{3,1},{131,129},{4... | collective-permute-start | bytes 12296 | tf_op jit(solution)/shard_map/ppermute | solution.py:255
  73.3 1.6 %collective-permute-done.14 = f32[8,128]{1,0:T(8,128)S(1)} collective-permute-done((f32[8,128]{1,0:T(8,128)S(1)}, f32[8,128]{1,0:T(8,128)S(1)}, u32[]{:S(2)}, u32[]{:S(2)}) %collective-permute-start.14) | collective-permute-done | bytes 4128 | tf_op jit(solution)/shard_map/ppermute | solution.py:255
  74.9 1.2 collective-permute-done.15
  76.6 1.0 copy-done
  77.7 9.3 %own_columns.1 = (f32[512,1024]{1,0:T(8,128)}, f32[512,1024]{1,0:T(8,128)}, f32[512,128]{1,0:T(8,128)}, f32[512,128]{1,0:T(8,128)}, f32[512,128]{1,0:T(8,128)}) custom-call(bf16[8,64,1024]{2,1,0:T(8,128)(2,1)} %copy-done, bf16[528,1024]{1,0:T(8,128)(2,1)} %get-tuple-element.15.refs_0_, bf16[528,1024]{1,0:T(8,128)(2,1)} %copy-done.5, ...), custom_call_target="tpu_custom_call" | custom-call | flops 4294967296 | bytes 1048576 | tf_op jit(solution)/shard_map/own_columns/pallas_call | solution.py:29
  86.9 0.9 copy-done.4
  87.9 11.0 %other_columns.1 = s16[8,64,1152]{2,1,0:T(8,128)(2,1)} custom-call(bf16[8,64,1024]{2,1,0:T(8,128)(2,1)} %copy-done, bf16[528,1024]{1,0:T(8,128)(2,1)} %copy-done.4, bf16[528,1024]{1,0:T(8,128)(2,1)} %collective-permute-done.5.refs_1_, bf16[528,1024]{1,0:T(8,128)(2,1)} %collective-permute-done.7.refs_2_, bf16[528,1024]{1,0:T(8,128)(2,1)} %collective-permute-done.9.refs_3_, ...), custom_call_target="tpu_custom_call" | custom-call | flops 4294967296 | bytes 1048576 | tf_op jit(solution)/shard_map/other_columns/pallas_call | solution.py:29
  98.9 38.4 %all_to_all.10.coded = s16[8,64,1152]{2,1,0:T(8,128)(2,1)} all-to-all(s16[8,64,1152]{2,1,0:T(8,128)(2,1)} %other_columns.1), channel_id=1, replica_groups=mesh['zl'=2,'x'=4,'c'=2,'y'=4,'zh'=4] {'zl','zh'}, dimensions={0} | all-to-all | bytes 2359296 | tf_op jit(solution)/shard_map/all_to_all | solution.py:275
  137.3 2.6 %add_terms.1 = (f32[1,64]{1,0:T(1,128)}, f32[64,1024]{1,0:T(8,128)}) custom-call(s16[8,64,1152]{2,1,0:T(8,128)(2,1)} %all_to_all.10.coded), custom_call_target="tpu_custom_call" | custom-call | bytes 1048576 | tf_op jit(solution)/shard_map/add_terms/pallas_call | solution.py:29
  (26 shorter events, 1.2 us)
Async XLA Ops:
  2.8 13.5 %collective-permute-start = (bf16[144,1024]{1,0:T(8,128)(2,1)}, bf16[144,1024]{1,0:T(8,128)(2,1)S(1)}, u32[]{:S(2)}, u32[]{:S(2)}) collective-permute-start(bf16[144,1024]{1,0:T(8,128)(2,1)} %get-tuple-element.14.refs_0_), channel_id=1, source_target_pairs={{0,32},{16,20},{4,36},{20,24},{8,40},{24,28},{12,44},{28,16},{32,6... | collective-permute-start | bytes 884744 | tf_op jit(solution)/shard_map/ppermute | solution.py:220
  4.3 12.0 %collective-permute-start.1 = (bf16[144,1024]{1,0:T(8,128)(2,1)}, bf16[144,1024]{1,0:T(8,128)(2,1)S(1)}, u32[]{:S(2)}, u32[]{:S(2)}) collective-permute-start(bf16[144,1024]{1,0:T(8,128)(2,1)} %get-tuple-element.14.refs_0_), channel_id=1, source_target_pairs={{0,96},{16,28},{4,100},{20,16},{8,104},{24,20},{12,108},{28,24},{3... | collective-permute-start | bytes 884744 | tf_op jit(solution)/shard_map/ppermute | solution.py:220
  6.1 10.3 %collective-permute-start.2 = (bf16[144,1024]{1,0:T(8,128)(2,1)}, bf16[144,1024]{1,0:T(8,128)(2,1)S(1)}, u32[]{:S(2)}, u32[]{:S(2)}) collective-permute-start(bf16[144,1024]{1,0:T(8,128)(2,1)} %get-tuple-element.14.refs_0_), channel_id=1, source_target_pairs={{0,64},{16,24},{4,68},{20,28},{8,72},{24,16},{12,76},{28,20},{32,9... | collective-permute-start | bytes 884744 | tf_op jit(solution)/shard_map/ppermute | solution.py:220
  7.9 68.8 %all-to-all-start = ((bf16[8,64,1024]{2,1,0:T(8,128)(2,1)}), bf16[8,64,1024]{2,1,0:T(8,128)(2,1)S(1)}, u32[]{:S(2)}, u32[]{:S(2)}) async-start(bf16[8,64,1024]{2,1,0:T(8,128)(2,1)} %get-tuple-element.13), calls=%async_computation | async-start | bytes 2097152 | tf_op jit(solution)/shard_map/all_to_all | solution.py:243
  16.3 0.7 copy-start.1
  16.4 0.8 copy-start.2
  17.2 0.7 copy-start.3
  20.2 15.4 %collective-permute-start.4 = (bf16[528,1024]{1,0:T(8,128)(2,1)}, bf16[528,1024]{1,0:T(8,128)(2,1)S(1)}, u32[]{:S(2)}, u32[]{:S(2)}) collective-permute-start(bf16[528,1024]{1,0:T(8,128)(2,1)} %get-tuple-element.15.refs_0_), channel_id=1, source_target_pairs={{0,4},{16,48},{4,8},{20,52},{8,12},{24,56},{12,0},{28,60},{32,36},... | collective-permute-start | bytes 3244040 | tf_op jit(solution)/shard_map/ppermute | solution.py:220
  21.8 15.5 %collective-permute-start.6 = (bf16[528,1024]{1,0:T(8,128)(2,1)}, bf16[528,1024]{1,0:T(8,128)(2,1)}, u32[]{:S(2)}, u32[]{:S(2)}) collective-permute-start(bf16[528,1024]{1,0:T(8,128)(2,1)} %get-tuple-element.15.refs_0_), channel_id=1, source_target_pairs={{0,12},{16,112},{4,0},{20,116},{8,4},{24,120},{12,8},{28,124},{32,... | collective-permute-start | bytes 3244040 | tf_op jit(solution)/shard_map/ppermute | solution.py:220
  22.3 27.3 %collective-permute-start.8 = (bf16[528,1024]{1,0:T(8,128)(2,1)}, bf16[528,1024]{1,0:T(8,128)(2,1)}, u32[]{:S(2)}, u32[]{:S(2)}) collective-permute-start(bf16[528,1024]{1,0:T(8,128)(2,1)} %get-tuple-element.15.refs_0_), channel_id=1, source_target_pairs={{0,8},{16,80},{4,12},{20,84},{8,0},{24,88},{12,4},{28,92},{32,40},... | collective-permute-start | bytes 3244040 | tf_op jit(solution)/shard_map/ppermute | solution.py:220
  24.6 62.3 %collective-permute-start.3 = (bf16[528,1024]{1,0:T(8,128)(2,1)}, bf16[528,1024]{1,0:T(8,128)(2,1)S(1)}, u32[]{:S(2)}, u32[]{:S(2)}) collective-permute-start(bf16[528,1024]{1,0:T(8,128)(2,1)} %get-tuple-element.15.refs_0_), channel_id=1, source_target_pairs={{0,16},{16,0},{1,17},{17,1},{2,18},{18,2},{3,19},{19,3},{4,20},{20... | collective-permute-start | bytes 3244040 | tf_op jit(solution)/shard_map/ppermute | solution.py:228
  35.6 41.0 %copy-start.5 = (bf16[528,1024]{1,0:T(8,128)(2,1)}, bf16[528,1024]{1,0:T(8,128)(2,1)S(1)}, u32[]{:S(2)}) copy-start(bf16[528,1024]{1,0:T(8,128)(2,1)S(1)} %collective-permute-done.4.refs_1_) | copy-start | bytes 3244036
  35.6 51.3 %collective-permute-start.5 = (bf16[528,1024]{1,0:T(8,128)(2,1)S(1)}, bf16[528,1024]{1,0:T(8,128)(2,1)}, u32[]{:S(2)}, u32[]{:S(2)}) collective-permute-start(bf16[528,1024]{1,0:T(8,128)(2,1)S(1)} %collective-permute-done.4.refs_1_), channel_id=1, source_target_pairs={{0,16},{16,0},{1,17},{17,1},{2,18},{18,2},{3,19},{19,3},{4,20},{20... | collective-permute-start | bytes 3244040 | tf_op jit(solution)/shard_map/ppermute | solution.py:228
  37.3 49.6 %collective-permute-start.7 = (bf16[528,1024]{1,0:T(8,128)(2,1)}, bf16[528,1024]{1,0:T(8,128)(2,1)}, u32[]{:S(2)}, u32[]{:S(2)}) collective-permute-start(bf16[528,1024]{1,0:T(8,128)(2,1)} %collective-permute-done.6.refs_2_), channel_id=1, source_target_pairs={{0,16},{16,0},{1,17},{17,1},{2,18},{18,2},{3,19},{19,3},{4,20},{20... | collective-permute-start | bytes 3244040 | tf_op jit(solution)/shard_map/ppermute | solution.py:228
  49.6 37.4 %collective-permute-start.9 = (bf16[528,1024]{1,0:T(8,128)(2,1)}, bf16[528,1024]{1,0:T(8,128)(2,1)}, u32[]{:S(2)}, u32[]{:S(2)}) collective-permute-start(bf16[528,1024]{1,0:T(8,128)(2,1)} %collective-permute-done.8.refs_3_), channel_id=1, source_target_pairs={{0,16},{16,0},{1,17},{17,1},{2,18},{18,2},{3,19},{19,3},{4,20},{20... | collective-permute-start | bytes 3244040 | tf_op jit(solution)/shard_map/ppermute | solution.py:228
  49.6 3.8 %collective-permute-start.10 = (f32[8,128]{1,0:T(8,128)}, f32[8,128]{1,0:T(8,128)S(1)}, u32[]{:S(2)}, u32[]{:S(2)}) collective-permute-start(f32[8,128]{1,0:T(8,128)} %get-tuple-element.21), channel_id=1, source_target_pairs={{0,4},{16,48},{4,0},{20,52},{8,12},{24,56},{12,8},{28,60},{32,36},... | collective-permute-start | bytes 12296 | tf_op jit(solution)/shard_map/ppermute | solution.py:220
  54.1 5.1 %collective-permute-start.11 = (f32[8,128]{1,0:T(8,128)S(1)}, f32[8,128]{1,0:T(8,128)S(1)}, u32[]{:S(2)}, u32[]{:S(2)}) collective-permute-start(f32[8,128]{1,0:T(8,128)S(1)} %add.18), channel_id=1, source_target_pairs={{0,8},{16,80},{4,12},{20,84},{8,0},{24,88},{12,4},{28,92},{32,40},... | collective-permute-start | bytes 12296 | tf_op jit(solution)/shard_map/ppermute | solution.py:220
  59.2 3.6 %collective-permute-start.12 = (f32[8,128]{1,0:T(8,128)S(1)}, f32[8,128]{1,0:T(8,128)S(1)}, u32[]{:S(2)}, u32[]{:S(2)}) collective-permute-start(f32[8,128]{1,0:T(8,128)S(1)} %add.19), channel_id=1, source_target_pairs={{0,128},{128,0},{1,129},{129,1},{2,130},{130,2},{3,131},{131,3},{4... | collective-permute-start | bytes 12296 | tf_op jit(solution)/shard_map/ppermute | solution.py:255
  62.8 4.5 %collective-permute-start.13 = (f32[8,128]{1,0:T(8,128)S(1)}, f32[8,128]{1,0:T(8,128)S(1)}, u32[]{:S(2)}, u32[]{:S(2)}) collective-permute-start(f32[8,128]{1,0:T(8,128)S(1)} %add.20), channel_id=1, source_target_pairs={{0,1},{128,129},{1,0},{129,128},{2,3},{130,131},{3,2},{131,130},{4... | collective-permute-start | bytes 12296 | tf_op jit(solution)/shard_map/ppermute | solution.py:255
  67.3 7.5 %collective-permute-start.14 = (f32[8,128]{1,0:T(8,128)S(1)}, f32[8,128]{1,0:T(8,128)S(1)}, u32[]{:S(2)}, u32[]{:S(2)}) collective-permute-start(f32[8,128]{1,0:T(8,128)S(1)} %add.21), channel_id=1, source_target_pairs={{0,2},{128,130},{1,3},{129,131},{2,0},{130,128},{3,1},{131,129},{4... | collective-permute-start | bytes 12296 | tf_op jit(solution)/shard_map/ppermute | solution.py:255
  74.9 1.2 collective-permute-start.15
  76.6 1.0 copy-start
  86.9 1.0 copy-start.4

commit v2 on v1

--- a/solution.py
+++ b/solution.py
@@ -15,14 +15,13 @@
 META = 16
 LEVELS = 32767.0
 F32, BF16 = jnp.float32, jnp.bfloat16
-VMEM = pltpu.CompilerParams(vmem_limit_bytes=56 * 1024 * 1024)
 
 
 def shape(dims, dtype):
     return jax.ShapeDtypeStruct(dims, dtype)
 
 
-def in_vmem(body, name, out_shape, flops=0, traffic=1 << 20, scratch=(), **more):
+def in_vmem(body, name, out_shape, flops=0, traffic=1 << 20, scratch=(), limit=16):
     spec = pl.BlockSpec(memory_space=pltpu.VMEM)
 
     def call(*args):
@@ -32,10 +31,9 @@
             in_specs=[spec] * len(args),
             out_specs=jax.tree.map(lambda _: spec, out_shape),
             scratch_shapes=scratch,
-            compiler_params=VMEM,
+            compiler_params=pltpu.CompilerParams(vmem_limit_bytes=limit << 20),
             cost_estimate=pl.CostEstimate(flops=flops, bytes_accessed=traffic, transcendentals=0),
             name=name,
-            **more,
         )(*args)
 
     return call
@@ -210,6 +208,18 @@
     return z % 2 * 4 + z // 2
 
 
+def handed_on(arrays, awaited):
+    spec = pl.BlockSpec(memory_space=pl.ANY)
+    return pl.pallas_call(
+        lambda *refs: None,
+        out_shape=[shape(a.shape, a.dtype) for a in arrays],
+        in_specs=[spec] * (len(arrays) + 1),
+        out_specs=[spec] * len(arrays),
+        input_output_aliases={i: i for i in range(len(arrays))},
+        name="handed_on",
+    )(*arrays, awaited)
+
+
 def along_line(x, shift, phase):
     pairs = []
     for i in range(4):
@@ -247,13 +257,13 @@
         (shape((2 * height * len(blocks) + META, width), BF16), shape((8, LANES), F32)),
     )(*blocks)
     pieces = line(piece, 1)
-    others = [other_core(p) for p in pieces]
-
     for bit in (1, 2):
         total = total + along_line(total, lambda i: i ^ bit, 1)
     for bit in (1, 2, 4):
         total = total + lax.ppermute(total, RING, [(place(i), place(i ^ bit)) for i in range(ring)])
     total = total + other_core(total)
+    pieces = [piece, *handed_on(pieces[1:], total)]
+    others = [other_core(p) for p in pieces]
 
     columns = height * len(blocks) * len(pieces)
     flops = 8 * rows * columns * width
@@ -264,6 +274,7 @@
         (shape((rows, width), F32),) * 2 + (shape((rows, LANES), F32),) * 3,
         flops=flops,
         scratch=weights,
+        limit=28,
     )(panel, *pieces)
     coded = in_vmem(
         functools.partial(other_columns, 256, len(pieces), target_count),
@@ -271,6 +282,7 @@
         shape((ring, height, width + LANES), jnp.int16),
         flops=flops,
         scratch=[pltpu.VMEM((rows, LANES), F32)] * 2 + weights,
+        limit=28,
     )(panel, *others, *state, total)
     coded = lax.all_to_all(coded, RING, split_axis=0, concat_axis=0, tiled=True)
     proof, gradient = in_vmem(

time: 140 us -> 131 us (0.936); the launches traced: 140 us -> 129 us
  Pallas kernels: 27.4 us -> 17.9 us
  starting transfers between devices: 38.9 us -> 33.4 us
  local copies, waits for them, and re-layouts: 3.48 us -> 8.53 us
    pallas_call x5, Pallas kernels: 27.4 us -> 17.9 us  [call(): pl.pallas_call(body, out_shape=out_shape, in_specs=[spec] * len(args), ou...]
    ppermute x5, starting transfers between devices: 7.66 us -> 1.19 us  [other_core(): return lax.ppermute(x, 'c', [(0, 1), (1, 0)])]
    unnamed x12 -> x20, local copies, waits for them, and re-layouts: 3.48 us -> 8.53 us
  transfers between devices with their start and end apart: 17 -> 17, of which waited for: 9 -> 6; matrix products, arithmetic and copies ran while one was open for 1% -> 0% of each run, Pallas kernels for 8% -> 6%
where the time goes in v2:
time: 131 us; the launch traced here: 129 us
  blocking collectives  37.9 us (29%)
  starting transfers between devices  33.4 us (25%)
  waiting for transfers between devices  29.7 us (23%)
  Pallas kernels  17.9 us (14%)
  local copies, waits for them, and re-layouts  8.53 us (7%)
    all_to_all x1, blocking collectives, on_device(): coded = lax.all_to_all(coded, RING, split_axis=0, concat_axis=0, tiled=True)  37.9 us
    ppermute x8, waiting for transfers between devices, along_line(): return lax.ppermute(x, PLANE, pairs)  24.2 us
    pallas_call x5, Pallas kernels, call(): pl.pallas_call(body, out_shape=out_shape, in_specs=[spec] * len(args), ou...  17.9 us
    ppermute x8, starting transfers between devices, along_line(): return lax.ppermute(x, PLANE, pairs)  13 us
    ppermute x3, starting transfers between devices, on_device(): lax.ppermute(total, RING, [(place(i), place(i ^ bit)) for i in range(ring)])  10.8 us
    unnamed x20, local copies, waits for them, and re-layouts  8.53 us
    all_to_all x1, starting transfers between devices, on_device(): lax.all_to_all(copies, RING, split_axis=0, concat_axis=0, tiled=True)  8.47 us
    ppermute x3, waiting for transfers between devices, on_device(): lax.ppermute(total, RING, [(place(i), place(i ^ bit)) for i in range(ring)])  4.81 us
  transfers between devices with their start and end apart: 17, of which 6 were waited for; matrix products, arithmetic and copies ran while one was open for 0% of the time, Pallas kernels for 6%

profile of v2, /device:TPU:8, one launch (start us, length us, event | category | flops | bytes accessed | tf_op | source)
XLA Modules:
  0.0 128.9 jit_solution(4406564894741689272)
XLA Ops:
  0.6 0.9 copy-done.6
  1.5 0.9 copy-done.7
  2.4 0.7 copy-done.9
  3.1 1.1 pack_block.1
  4.2 1.5 %collective-permute-start = (bf16[144,1024]{1,0:T(8,128)(2,1)S(1)}, bf16[144,1024]{1,0:T(8,128)(2,1)S(1)}, u32[]{:S(2)}, u32[]{:S(2)}) collective-permute-start(bf16[144,1024]{1,0:T(8,128)(2,1)S(1)} %get-tuple-element.17.refs_0_), channel_id=1, source_target_pairs={{0,32},{16,20},{4,36},{20,24},{8,40},{24,28},{12,44},{28,16},{32,6... | collective-permute-start | bytes 884744 | tf_op jit(solution)/shard_map/ppermute | solution.py:230
  5.7 1.7 %collective-permute-start.1 = (bf16[144,1024]{1,0:T(8,128)(2,1)S(1)}, bf16[144,1024]{1,0:T(8,128)(2,1)S(1)}, u32[]{:S(2)}, u32[]{:S(2)}) collective-permute-start(bf16[144,1024]{1,0:T(8,128)(2,1)S(1)} %get-tuple-element.17.refs_0_), channel_id=1, source_target_pairs={{0,96},{16,28},{4,100},{20,16},{8,104},{24,20},{12,108},{28,24},{3... | collective-permute-start | bytes 884744 | tf_op jit(solution)/shard_map/ppermute | solution.py:230
  7.4 1.8 %collective-permute-start.2 = (bf16[144,1024]{1,0:T(8,128)(2,1)S(1)}, bf16[144,1024]{1,0:T(8,128)(2,1)S(1)}, u32[]{:S(2)}, u32[]{:S(2)}) collective-permute-start(bf16[144,1024]{1,0:T(8,128)(2,1)S(1)} %get-tuple-element.17.refs_0_), channel_id=1, source_target_pairs={{0,64},{16,24},{4,68},{20,28},{8,72},{24,16},{12,76},{28,20},{32,9... | collective-permute-start | bytes 884744 | tf_op jit(solution)/shard_map/ppermute | solution.py:230
  9.3 8.5 %all-to-all-start = ((bf16[8,64,1024]{2,1,0:T(8,128)(2,1)}), bf16[8,64,1024]{2,1,0:T(8,128)(2,1)}, u32[]{:S(2)}, u32[]{:S(2)}) async-start(bf16[8,64,1024]{2,1,0:T(8,128)(2,1)} %get-tuple-element.16), calls=%async_computation | async-start | bytes 2097152 | tf_op jit(solution)/shard_map/all_to_all | solution.py:253
  17.8 1.1 pack_line.1
  18.8 1.6 %collective-permute-start.4 = (bf16[528,1024]{1,0:T(8,128)(2,1)}, bf16[528,1024]{1,0:T(8,128)(2,1)S(1)}, u32[]{:S(2)}, u32[]{:S(2)}) collective-permute-start(bf16[528,1024]{1,0:T(8,128)(2,1)} %get-tuple-element.18.refs_0_), channel_id=1, source_target_pairs={{0,4},{16,48},{4,8},{20,52},{8,12},{24,56},{12,0},{28,60},{32,36},... | collective-permute-start | bytes 3244040 | tf_op jit(solution)/shard_map/ppermute | solution.py:230
  20.8 2.3 %collective-permute-start.6 = (bf16[528,1024]{1,0:T(8,128)(2,1)}, bf16[528,1024]{1,0:T(8,128)(2,1)S(1)}, u32[]{:S(2)}, u32[]{:S(2)}) collective-permute-start(bf16[528,1024]{1,0:T(8,128)(2,1)} %get-tuple-element.18.refs_0_), channel_id=1, source_target_pairs={{0,8},{16,80},{4,12},{20,84},{8,0},{24,88},{12,4},{28,92},{32,40},... | collective-permute-start | bytes 3244040 | tf_op jit(solution)/shard_map/ppermute | solution.py:230
  23.1 1.3 %collective-permute-start.7 = (f32[8,128]{1,0:T(8,128)S(1)}, f32[8,128]{1,0:T(8,128)S(1)}, u32[]{:S(2)}, u32[]{:S(2)}) collective-permute-start(f32[8,128]{1,0:T(8,128)S(1)} %get-tuple-element.19), channel_id=1, source_target_pairs={{0,4},{16,48},{4,0},{20,52},{8,12},{24,56},{12,8},{28,60},{32,36},... | collective-permute-start | bytes 12296 | tf_op jit(solution)/shard_map/ppermute | solution.py:230
  24.5 21.4 %collective-permute-done.7 = f32[8,128]{1,0:T(8,128)S(1)} collective-permute-done((f32[8,128]{1,0:T(8,128)S(1)}, f32[8,128]{1,0:T(8,128)S(1)}, u32[]{:S(2)}, u32[]{:S(2)}) %collective-permute-start.7) | collective-permute-done | bytes 4128 | tf_op jit(solution)/shard_map/ppermute | solution.py:230
  45.9 2.2 %collective-permute-start.8 = (f32[8,128]{1,0:T(8,128)S(1)}, f32[8,128]{1,0:T(8,128)S(1)}, u32[]{:S(2)}, u32[]{:S(2)}) collective-permute-start(f32[8,128]{1,0:T(8,128)S(1)} %add.18), channel_id=1, source_target_pairs={{0,8},{16,80},{4,12},{20,84},{8,0},{24,88},{12,4},{28,92},{32,40},... | collective-permute-start | bytes 12296 | tf_op jit(solution)/shard_map/ppermute | solution.py:230
  48.1 2.9 %collective-permute-done.8 = f32[8,128]{1,0:T(8,128)S(1)} collective-permute-done((f32[8,128]{1,0:T(8,128)S(1)}, f32[8,128]{1,0:T(8,128)S(1)}, u32[]{:S(2)}, u32[]{:S(2)}) %collective-permute-start.8) | collective-permute-done | bytes 4128 | tf_op jit(solution)/shard_map/ppermute | solution.py:230
  51.0 2.0 %collective-permute-start.9 = (f32[8,128]{1,0:T(8,128)S(1)}, f32[8,128]{1,0:T(8,128)S(1)}, u32[]{:S(2)}, u32[]{:S(2)}) collective-permute-start(f32[8,128]{1,0:T(8,128)S(1)} %add.19), channel_id=1, source_target_pairs={{0,128},{128,0},{1,129},{129,1},{2,130},{130,2},{3,131},{131,3},{4... | collective-permute-start | bytes 12296 | tf_op jit(solution)/shard_map/ppermute | solution.py:263
  53.0 1.6 %collective-permute-done.9 = f32[8,128]{1,0:T(8,128)S(1)} collective-permute-done((f32[8,128]{1,0:T(8,128)S(1)}, f32[8,128]{1,0:T(8,128)S(1)}, u32[]{:S(2)}, u32[]{:S(2)}) %collective-permute-start.9) | collective-permute-done | bytes 4128 | tf_op jit(solution)/shard_map/ppermute | solution.py:263
  54.6 2.9 %collective-permute-start.10 = (f32[8,128]{1,0:T(8,128)S(1)}, f32[8,128]{1,0:T(8,128)S(1)}, u32[]{:S(2)}, u32[]{:S(2)}) collective-permute-start(f32[8,128]{1,0:T(8,128)S(1)} %add.20), channel_id=1, source_target_pairs={{0,1},{128,129},{1,0},{129,128},{2,3},{130,131},{3,2},{131,130},{4... | collective-permute-start | bytes 12296 | tf_op jit(solution)/shard_map/ppermute | solution.py:263
  57.5 1.6 %collective-permute-done.10 = f32[8,128]{1,0:T(8,128)S(1)} collective-permute-done((f32[8,128]{1,0:T(8,128)S(1)}, f32[8,128]{1,0:T(8,128)S(1)}, u32[]{:S(2)}, u32[]{:S(2)}) %collective-permute-start.10) | collective-permute-done | bytes 4128 | tf_op jit(solution)/shard_map/ppermute | solution.py:263
  59.1 5.9 %collective-permute-start.11 = (f32[8,128]{1,0:T(8,128)S(1)}, f32[8,128]{1,0:T(8,128)S(1)}, u32[]{:S(2)}, u32[]{:S(2)}) collective-permute-start(f32[8,128]{1,0:T(8,128)S(1)} %add.21), channel_id=1, source_target_pairs={{0,2},{128,130},{1,3},{129,131},{2,0},{130,128},{3,1},{131,129},{4... | collective-permute-start | bytes 12296 | tf_op jit(solution)/shard_map/ppermute | solution.py:263
  65.0 1.6 %collective-permute-done.11 = f32[8,128]{1,0:T(8,128)S(1)} collective-permute-done((f32[8,128]{1,0:T(8,128)S(1)}, f32[8,128]{1,0:T(8,128)S(1)}, u32[]{:S(2)}, u32[]{:S(2)}) %collective-permute-start.11) | collective-permute-done | bytes 4128 | tf_op jit(solution)/shard_map/ppermute | solution.py:263
  67.1 0.7 collective-permute-done.12
  67.8 0.6 add.23.refs_3_.refs_9_
  68.4 1.0 copy-done
  69.8 1.0 copy-done.4
  71.5 1.2 copy-done.1
  72.7 1.2 copy-done.3
  73.9 1.2 copy-done.5
  75.2 6.8 %own_columns.1 = (f32[512,1024]{1,0:T(8,128)S(1)}, f32[512,1024]{1,0:T(8,128)S(1)}, f32[512,128]{1,0:T(8,128)S(1)}, f32[512,128]{1,0:T(8,128)S(1)}, f32[512,128]{1,0:T(8,128)S(1)}) custom-call(bf16[8,64,1024]{2,1,0:T(8,128)(2,1)} %all-to-all-done.panel, bf16[528,1024]{1,0:T(8,128)(2,1)} %get-tuple-element.18.refs_0_, bf16[528,1024]{1,0:T(8,128)(2,1)S(1)} %copy-done.1, ...), custom_call_target="tpu_custom_call" | custom-call | flops 4294967296 | bytes 1048576 | tf_op jit(solution)/shard_map/own_columns/pallas_call | solution.py:28
  82.0 7.7 %other_columns.1 = s16[8,64,1152]{2,1,0:T(8,128)(2,1)S(1)} custom-call(bf16[8,64,1024]{2,1,0:T(8,128)(2,1)} %all-to-all-done.panel, bf16[528,1024]{1,0:T(8,128)(2,1)} %collective-permute-done.3.refs_0_, bf16[528,1024]{1,0:T(8,128)(2,1)S(1)} %collective-permute-done.13.refs_1_, bf16[528,1024]{1,0:T(8,128)(2,1)S(1)} %collective-permute-done.14.refs_2_, ...), custom_call_target="tpu_custom_call" | custom-call | flops 4294967296 | bytes 1048576 | tf_op jit(solution)/shard_map/other_columns/pallas_call | solution.py:28
  89.7 37.9 %all_to_all.10.coded = s16[8,64,1152]{2,1,0:T(8,128)(2,1)S(1)} all-to-all(s16[8,64,1152]{2,1,0:T(8,128)(2,1)S(1)} %other_columns.1), channel_id=1, replica_groups=mesh['zl'=2,'x'=4,'c'=2,'y'=4,'zh'=4] {'zl','zh'}, dimensions={0} | all-to-all | bytes 2359296 | tf_op jit(solution)/shard_map/all_to_all | solution.py:287
  127.6 1.3 %add_terms.1 = (f32[1,64]{1,0:T(1,128)}, f32[64,1024]{1,0:T(8,128)}) custom-call(s16[8,64,1152]{2,1,0:T(8,128)(2,1)S(1)} %all_to_all.10.coded), custom_call_target="tpu_custom_call" | custom-call | bytes 1048576 | tf_op jit(solution)/shard_map/add_terms/pallas_call | solution.py:28
  (35 shorter events, 2.1 us)
Async XLA Ops:
  0.6 0.9 copy-start.6
  1.5 0.9 copy-start.7
  2.4 0.7 copy-start.9
  4.2 13.5 %collective-permute-start = (bf16[144,1024]{1,0:T(8,128)(2,1)S(1)}, bf16[144,1024]{1,0:T(8,128)(2,1)S(1)}, u32[]{:S(2)}, u32[]{:S(2)}) collective-permute-start(bf16[144,1024]{1,0:T(8,128)(2,1)S(1)} %get-tuple-element.17.refs_0_), channel_id=1, source_target_pairs={{0,32},{16,20},{4,36},{20,24},{8,40},{24,28},{12,44},{28,16},{32,6... | collective-permute-start | bytes 884744 | tf_op jit(solution)/shard_map/ppermute | solution.py:230
  5.7 12.0 %collective-permute-start.1 = (bf16[144,1024]{1,0:T(8,128)(2,1)S(1)}, bf16[144,1024]{1,0:T(8,128)(2,1)S(1)}, u32[]{:S(2)}, u32[]{:S(2)}) collective-permute-start(bf16[144,1024]{1,0:T(8,128)(2,1)S(1)} %get-tuple-element.17.refs_0_), channel_id=1, source_target_pairs={{0,96},{16,28},{4,100},{20,16},{8,104},{24,20},{12,108},{28,24},{3... | collective-permute-start | bytes 884744 | tf_op jit(solution)/shard_map/ppermute | solution.py:230
  7.4 10.3 %collective-permute-start.2 = (bf16[144,1024]{1,0:T(8,128)(2,1)S(1)}, bf16[144,1024]{1,0:T(8,128)(2,1)S(1)}, u32[]{:S(2)}, u32[]{:S(2)}) collective-permute-start(bf16[144,1024]{1,0:T(8,128)(2,1)S(1)} %get-tuple-element.17.refs_0_), channel_id=1, source_target_pairs={{0,64},{16,24},{4,68},{20,28},{8,72},{24,16},{12,76},{28,20},{32,9... | collective-permute-start | bytes 884744 | tf_op jit(solution)/shard_map/ppermute | solution.py:230
  9.3 62.2 %all-to-all-start = ((bf16[8,64,1024]{2,1,0:T(8,128)(2,1)}), bf16[8,64,1024]{2,1,0:T(8,128)(2,1)}, u32[]{:S(2)}, u32[]{:S(2)}) async-start(bf16[8,64,1024]{2,1,0:T(8,128)(2,1)} %get-tuple-element.16), calls=%async_computation | async-start | bytes 2097152 | tf_op jit(solution)/shard_map/all_to_all | solution.py:253
  18.8 49.6 %collective-permute-start.4 = (bf16[528,1024]{1,0:T(8,128)(2,1)}, bf16[528,1024]{1,0:T(8,128)(2,1)S(1)}, u32[]{:S(2)}, u32[]{:S(2)}) collective-permute-start(bf16[528,1024]{1,0:T(8,128)(2,1)} %get-tuple-element.18.refs_0_), channel_id=1, source_target_pairs={{0,4},{16,48},{4,8},{20,52},{8,12},{24,56},{12,0},{28,60},{32,36},... | collective-permute-start | bytes 3244040 | tf_op jit(solution)/shard_map/ppermute | solution.py:230
  20.4 48.0 %collective-permute-start.5 = (bf16[528,1024]{1,0:T(8,128)(2,1)}, bf16[528,1024]{1,0:T(8,128)(2,1)S(1)}, u32[]{:S(2)}, u32[]{:S(2)}) collective-permute-start(bf16[528,1024]{1,0:T(8,128)(2,1)} %get-tuple-element.18.refs_0_), channel_id=1, source_target_pairs={{0,12},{16,112},{4,0},{20,116},{8,4},{24,120},{12,8},{28,124},{32,... | collective-permute-start | bytes 3244040 | tf_op jit(solution)/shard_map/ppermute | solution.py:230
  20.8 47.6 %collective-permute-start.6 = (bf16[528,1024]{1,0:T(8,128)(2,1)}, bf16[528,1024]{1,0:T(8,128)(2,1)S(1)}, u32[]{:S(2)}, u32[]{:S(2)}) collective-permute-start(bf16[528,1024]{1,0:T(8,128)(2,1)} %get-tuple-element.18.refs_0_), channel_id=1, source_target_pairs={{0,8},{16,80},{4,12},{20,84},{8,0},{24,88},{12,4},{28,92},{32,40},... | collective-permute-start | bytes 3244040 | tf_op jit(solution)/shard_map/ppermute | solution.py:230
  23.1 22.7 %collective-permute-start.7 = (f32[8,128]{1,0:T(8,128)S(1)}, f32[8,128]{1,0:T(8,128)S(1)}, u32[]{:S(2)}, u32[]{:S(2)}) collective-permute-start(f32[8,128]{1,0:T(8,128)S(1)} %get-tuple-element.19), channel_id=1, source_target_pairs={{0,4},{16,48},{4,0},{20,52},{8,12},{24,56},{12,8},{28,60},{32,36},... | collective-permute-start | bytes 12296 | tf_op jit(solution)/shard_map/ppermute | solution.py:230
  45.9 5.1 %collective-permute-start.8 = (f32[8,128]{1,0:T(8,128)S(1)}, f32[8,128]{1,0:T(8,128)S(1)}, u32[]{:S(2)}, u32[]{:S(2)}) collective-permute-start(f32[8,128]{1,0:T(8,128)S(1)} %add.18), channel_id=1, source_target_pairs={{0,8},{16,80},{4,12},{20,84},{8,0},{24,88},{12,4},{28,92},{32,40},... | collective-permute-start | bytes 12296 | tf_op jit(solution)/shard_map/ppermute | solution.py:230
  51.0 3.6 %collective-permute-start.9 = (f32[8,128]{1,0:T(8,128)S(1)}, f32[8,128]{1,0:T(8,128)S(1)}, u32[]{:S(2)}, u32[]{:S(2)}) collective-permute-start(f32[8,128]{1,0:T(8,128)S(1)} %add.19), channel_id=1, source_target_pairs={{0,128},{128,0},{1,129},{129,1},{2,130},{130,2},{3,131},{131,3},{4... | collective-permute-start | bytes 12296 | tf_op jit(solution)/shard_map/ppermute | solution.py:263
  54.6 4.5 %collective-permute-start.10 = (f32[8,128]{1,0:T(8,128)S(1)}, f32[8,128]{1,0:T(8,128)S(1)}, u32[]{:S(2)}, u32[]{:S(2)}) collective-permute-start(f32[8,128]{1,0:T(8,128)S(1)} %add.20), channel_id=1, source_target_pairs={{0,1},{128,129},{1,0},{129,128},{2,3},{130,131},{3,2},{131,130},{4... | collective-permute-start | bytes 12296 | tf_op jit(solution)/shard_map/ppermute | solution.py:263
  59.1 7.5 %collective-permute-start.11 = (f32[8,128]{1,0:T(8,128)S(1)}, f32[8,128]{1,0:T(8,128)S(1)}, u32[]{:S(2)}, u32[]{:S(2)}) collective-permute-start(f32[8,128]{1,0:T(8,128)S(1)} %add.21), channel_id=1, source_target_pairs={{0,2},{128,130},{1,3},{129,131},{2,0},{130,128},{3,1},{131,129},{4... | collective-permute-start | bytes 12296 | tf_op jit(solution)/shard_map/ppermute | solution.py:263
  66.6 1.2 collective-permute-start.12
  66.6 15.3 %collective-permute-start.3 = (bf16[528,1024]{1,0:T(8,128)(2,1)}, bf16[528,1024]{1,0:T(8,128)(2,1)}, u32[]{:S(2)}, u32[]{:S(2)}) collective-permute-start(bf16[528,1024]{1,0:T(8,128)(2,1)} %get-tuple-element.18.refs_0_), channel_id=1, source_target_pairs={{0,16},{16,0},{1,17},{17,1},{2,18},{18,2},{3,19},{19,3},{4,20},{20... | collective-permute-start | bytes 3244040 | tf_op jit(solution)/shard_map/ppermute | solution.py:238
  68.4 1.0 copy-start
  68.4 1.4 %copy-start.2 = (bf16[528,1024]{1,0:T(8,128)(2,1)}, bf16[528,1024]{1,0:T(8,128)(2,1)S(1)}, u32[]{:S(2)}) copy-start(bf16[528,1024]{1,0:T(8,128)(2,1)S(1)} %collective-permute-done.5.refs_1_) | copy-start | bytes 3244036
  69.8 1.0 copy-start.4
  70.8 11.2 %collective-permute-start.13 = (bf16[528,1024]{1,0:T(8,128)(2,1)}, bf16[528,1024]{1,0:T(8,128)(2,1)S(1)}, u32[]{:S(2)}, u32[]{:S(2)}) collective-permute-start(bf16[528,1024]{1,0:T(8,128)(2,1)} %get-tuple-element.20.refs_1_), channel_id=1, source_target_pairs={{0,16},{16,0},{1,17},{17,1},{2,18},{18,2},{3,19},{19,3},{4,20},{20... | collective-permute-start | bytes 3244040 | tf_op jit(solution)/shard_map/ppermute | solution.py:238
  71.0 11.0 %collective-permute-start.14 = (bf16[528,1024]{1,0:T(8,128)(2,1)}, bf16[528,1024]{1,0:T(8,128)(2,1)S(1)}, u32[]{:S(2)}, u32[]{:S(2)}) collective-permute-start(bf16[528,1024]{1,0:T(8,128)(2,1)} %get-tuple-element.21.refs_2_), channel_id=1, source_target_pairs={{0,16},{16,0},{1,17},{17,1},{2,18},{18,2},{3,19},{19,3},{4,20},{20... | collective-permute-start | bytes 3244040 | tf_op jit(solution)/shard_map/ppermute | solution.py:238
  71.3 10.7 %collective-permute-start.15 = (bf16[528,1024]{1,0:T(8,128)(2,1)}, bf16[528,1024]{1,0:T(8,128)(2,1)S(1)}, u32[]{:S(2)}, u32[]{:S(2)}) collective-permute-start(bf16[528,1024]{1,0:T(8,128)(2,1)} %get-tuple-element.22.refs_3_), channel_id=1, source_target_pairs={{0,16},{16,0},{1,17},{17,1},{2,18},{18,2},{3,19},{19,3},{4,20},{20... | collective-permute-start | bytes 3244040 | tf_op jit(solution)/shard_map/ppermute | solution.py:238
  71.5 1.2 copy-start.1
  72.7 1.2 copy-start.3
  73.9 1.2 copy-start.5
  75.2 6.8 %copy-start.8 = (f32[8,128]{1,0:T(8,128)S(1)}, f32[8,128]{1,0:T(8,128)}, u32[]{:S(2)}) copy-start(f32[8,128]{1,0:T(8,128)} %add.23.refs_3_.refs_9_) | copy-start | bytes 12292

commit v3 on v1

v3 whole, which is shorter than its diff:
```python
import functools

import jax
import jax.numpy as jnp
from jax import lax
from jax.experimental import pallas as pl
from jax.experimental.pallas import tpu as pltpu
from jax.sharding import Mesh
from jax.sharding import PartitionSpec as P

AXES = ("zl", "x", "c", "y", "zh")
RING = ("zl", "zh")
PLANE = ("x", "c", "y")
LANES = 128
META = 16
LEVELS = 32767.0
OFFSETS = (3, 1, 5, 7, 4, 2, 6, 0)
F32, BF16 = jnp.float32, jnp.bfloat16


def shape(dims, dtype):
    return jax.ShapeDtypeStruct(dims, dtype)


def in_vmem(body, name, out_shape, flops=0, traffic=1 << 20, scratch=(), limit=16, aliases=None):
    spec = pl.BlockSpec(memory_space=pltpu.VMEM)

    def call(*args):
        return pl.pallas_call(
            body,
            out_shape=out_shape,
            in_specs=[spec] * len(args),
            out_specs=jax.tree.map(lambda _: spec, out_shape),
            scratch_shapes=scratch,
            compiler_params=pltpu.CompilerParams(vmem_limit_bytes=limit << 20),
            cost_estimate=pl.CostEstimate(flops=flops, bytes_accessed=traffic, transcendentals=0),
            input_output_aliases=aliases or {},
            name=name,
        )(*args)

    return call


def lane_sums(x):
    total = x[:, :LANES]
    for at in range(LANES, x.shape[1], LANES):
        total = total + x[:, at : at + LANES]
    return total


def square_norms(block):
    wide = block.astype(F32)
    return jnp.sum(lane_sums(wide * wide), axis=1, keepdims=True)


def along_lanes(column):
    return jnp.transpose(jnp.broadcast_to(column, (column.shape[0], LANES)))[:1]


def halves(a, b):
    return jnp.concatenate([a, b], axis=1)


def pack_block(pool, targets, counts, block, copies):
    height = pool.shape[0]
    block[:height, :] = pool[...]
    block[height : 2 * height, :] = targets[...]
    norms = along_lanes(jnp.concatenate([square_norms(pool[...]), square_norms(targets[...])], axis=0))
    high = norms.astype(BF16).astype(F32)
    middle = (norms - high).astype(BF16).astype(F32)
    low = norms - high - middle
    weights = halves(counts[...].astype(F32), jnp.ones((1, height), F32))
    meta = jnp.concatenate([weights, high, middle, low, jnp.zeros((META - 4, LANES), F32)], axis=0)
    block[2 * height :, :] = jnp.concatenate(
        [meta, jnp.zeros((META, block.shape[1] - LANES), F32)], axis=1
    ).astype(BF16)
    for i in range(copies.shape[0]):
        copies[i] = pool[...]


def pack_line(*refs):
    blocks, piece = refs[:-1], refs[-1]
    count, height = len(blocks), (blocks[0].shape[0] - META) // 2
    for j, block in enumerate(blocks):
        piece[j * height : (j + 1) * height, :] = block[:height, :]
        piece[(count + j) * height : (count + j + 1) * height, :] = block[height : 2 * height, :]
    metas = [block[2 * height :, :LANES].astype(F32) for block in blocks]
    lanes = [meta[:, half : half + height] for half in (0, height) for meta in metas]
    pairs = [halves(a, b) for a, b in zip(lanes[::2], lanes[1::2])]
    width = piece.shape[1] - LANES * len(pairs)
    piece[2 * count * height :, :] = jnp.concatenate(
        [*pairs, jnp.zeros((META, width), F32)], axis=1
    ).astype(BF16)


def add_columns(panel, norms, pieces, pulls, masses, weights, rows, first):
    height, width = panel.shape
    size = (pieces[0].shape[0] - META) // 2
    for half in range(2):
        for i, piece in enumerate(pieces):
            columns = piece[half * size : (half + 1) * size, :]
            meta = piece[2 * size :, half * size : (half + 1) * size].astype(F32)
            col_norms = meta[1:2] + meta[2:3] + meta[3:4]
            for at in range(0, height, rows):
                part = slice(at, at + rows)
                inner = lax.dot_general(
                    panel[part, :], columns, (((1,), (1,)), ((), ())), preferred_element_type=F32
                )
                squared = norms[part, :1] + col_norms - 2.0 * inner
                kernel = jnp.exp(-squared * (0.5 / width))
                if half == 0:
                    kernel = kernel * meta[:1]
                if first and i == 0:
                    masses[half][part, :] = lane_sums(kernel)
                else:
                    masses[half][part, :] += lane_sums(kernel)
                weights[half][part, i * size : (i + 1) * size] = kernel.astype(BF16)
    for half in range(2):
        for at in range(0, height, rows):
            part = slice(at, at + rows)
            total = None if first else pulls[half][part, :]
            for i, piece in enumerate(pieces):
                one = jnp.dot(
                    weights[half][part, i * size : (i + 1) * size],
                    piece[half * size : (half + 1) * size, :],
                    preferred_element_type=F32,
                )
                total = one if total is None else total + one
            pulls[half][part, :] = total


def first_columns(rows, lines, panel, *refs):
    pieces, refs = refs[:lines], refs[lines:]
    ordered, norms, pp, tp, pm, tm, *weights = refs
    ring, height, _ = panel.shape
    z = 2 * lax.axis_index("zh") + lax.axis_index("zl")
    for i, offset in enumerate(OFFSETS):
        part = slice(i * height, (i + 1) * height)
        there = lax.rem(z + offset, ring)
        block = panel[lax.rem(there, 2) * 4 + lax.div(there, 2)]
        ordered[part, :] = block
        norms[part, :] = jnp.broadcast_to(square_norms(block), (height, LANES))
    add_columns(ordered, norms, pieces, (pp, tp), (pm, tm), weights, rows, True)


def more_columns(rows, lines, panel, norms, *refs):
    pieces, refs = refs[:lines], refs[lines + 4 :]
    pp, tp, pm, tm, *weights = refs
    add_columns(panel, norms, pieces, (pp, tp), (pm, tm), weights, rows, False)


def count_chosen(*refs):
    pieces, chosen = refs[:-1], refs[-1]
    size = (pieces[0].shape[0] - META) // 2
    total = jnp.zeros((1, size), F32)
    for piece in pieces:
        total = total + piece[2 * size :, :size].astype(F32)[:1]
    chosen[...] = jnp.full(chosen.shape, jnp.sum(total), F32)


def terms(target_count, panel, pp, tp, pm, tm, total, part):
    weight = total[:1, :1]
    pool_mass = jnp.sum(pm[part, :], axis=1, keepdims=True)
    target_mass = jnp.sum(tm[part, :], axis=1, keepdims=True)
    own = panel[part, :].astype(F32)
    proof = target_mass / target_count - pool_mass / weight
    gradient = (tp[part, :] - target_mass * own) * (1.0 / target_count) - (
        pp[part, :] - pool_mass * own
    ) * (1.0 / weight)
    return gradient, proof


def far_terms(target_count, height, *refs):
    inputs, (up, down, up_half, down_half) = refs[:6], refs[6:]
    for i in range(4):
        code = encode(*terms(target_count, *inputs, slice(i * height, (i + 1) * height)))
        (up, down)[i // 2][i % 2 * height : (i % 2 + 1) * height, :] = code
    code = encode(*terms(target_count, *inputs, slice(4 * height, 5 * height)))
    down_half[...] = code[: height // 2, :]
    up_half[...] = code[height // 2 :, :]


def near_terms(target_count, height, *refs):
    inputs, (gradient, proof) = refs[:6], refs[6:]
    for i in range(5, 8):
        part = slice((i - 5) * height, (i - 4) * height)
        gradient[part, :], small = terms(target_count, *inputs, slice(i * height, (i + 1) * height))
        proof[part, :] = jnp.broadcast_to(small, (height, LANES))


def pass_on(gradient, proof, from_below, from_above, half_below, half_above, up, down):
    width, height = gradient.shape[1], gradient.shape[0] // 3
    for i, near, half, out in ((0, from_below, half_below, up), (1, from_above, half_above, down)):
        part = slice(i * height, (i + 1) * height)
        near_gradient, near_proof = decode(near[:height, :], width)
        half_gradient, half_proof = decode(half[...], width)
        zeros = jnp.zeros((height // 2, width), F32), jnp.zeros((height // 2, 1), F32)
        both = [(half_gradient, zeros[0]), (half_proof, zeros[1])]
        if i == 0:
            both = [pair[::-1] for pair in both]
        half_gradient, half_proof = (jnp.concatenate(pair, axis=0) for pair in both)
        out[...] = encode(
            gradient[part, :] + near_gradient + half_gradient,
            proof[part, :1] + near_proof + half_proof,
        )


def add_up(gradient, proof, from_below, from_above, far_below, far_above, out_proof, out):
    width, height = gradient.shape[1], gradient.shape[0] // 3
    total, small = gradient[2 * height :, :], proof[2 * height :, :1]
    for coded in (from_below[height:, :], from_above[height:, :], far_below[...], far_above[...]):
        one, part = decode(coded, width)
        total, small = total + one, small + part
    out[...] = total
    out_proof[...] = along_lanes(small)


def step_scale(step):
    return jnp.exp2(step * (1.0 / 128.0))


def encode(term, proof):
    top = jnp.maximum(jnp.max(jnp.abs(term), axis=1, keepdims=True), 1e-30)
    step = jnp.ceil(jnp.log2(top) * 128.0)
    steps = jnp.round(term * (LEVELS / step_scale(step)))
    steps = jnp.clip(steps, -LEVELS, LEVELS)
    first = jnp.round(proof * 8192.0)
    rest = (proof * 8192.0 - first) * 32768.0
    second = jnp.round(rest)
    third = jnp.round((rest - second) * 32768.0)
    lane = lax.broadcasted_iota(jnp.int32, (term.shape[0], LANES), 1)
    notes = jnp.where(
        lane == 0, step, jnp.where(lane == 1, first, jnp.where(lane == 2, second, third))
    )
    return jnp.concatenate([steps, notes], axis=1).astype(jnp.int32).astype(jnp.int16)


def decode(coded, width):
    code = coded.astype(jnp.int32).astype(F32)
    notes = code[:, width:]
    first, second, third = notes[:, 1:2], notes[:, 2:3], notes[:, 3:4]
    proof = (first + (second + third * (1.0 / 32768.0)) * (1.0 / 32768.0)) * (1.0 / 8192.0)
    return code[:, :width] * (step_scale(notes[:, :1]) * (1.0 / LEVELS)), proof


def place(z):
    return z % 2 * 4 + z // 2


def up_the_ring(x, step):
    ring = lax.axis_size(RING)
    return lax.ppermute(x, RING, [(place(i), place((i + step) % ring)) for i in range(ring)])


def along_line(x, shift, phase):
    pairs = []
    for i in range(4):
        for j in range(4):
            for c in range(2):
                there = (shift(i), j) if (c + phase) % 2 == 0 else (i, shift(j))
                pairs.append(((i * 2 + c) * 4 + j, (there[0] * 2 + c) * 4 + there[1]))
    return lax.ppermute(x, PLANE, pairs)


def line(x, phase):
    return [x] + [along_line(x, lambda i, k=k: (i + k) % 4, phase) for k in (1, 3, 2)]


def other_core(x):
    return lax.ppermute(x, "c", [(0, 1), (1, 0)])


def on_device(pool, targets, counts):
    ring = lax.axis_size(RING)
    height, width = pool.shape
    rows = ring * height
    target_count = float(height * lax.axis_size(AXES))

    block, copies = in_vmem(
        pack_block,
        "pack_block",
        (shape((2 * height + META, width), BF16), shape((ring, height, width), BF16)),
        limit=56,
    )(pool, targets, counts.reshape(1, height))
    blocks = line(block, 0)
    panel = lax.all_to_all(copies, RING, split_axis=0, concat_axis=0, tiled=True)
    piece = in_vmem(
        pack_line, "pack_line", shape((2 * height * len(blocks) + META, width), BF16)
    )(*blocks)
    pieces = line(piece, 1)
    others = [other_core(p) for p in pieces]

    size = height * len(blocks)
    sums = (shape((rows, width), F32),) * 2 + (shape((rows, LANES), F32),) * 2

    def add(body, arrays, some, state, out_shape, aliases):
        return in_vmem(
            functools.partial(body, 256, len(some)),
            body.__name__,
            out_shape,
            flops=8 * rows * len(some) * size * width,
            scratch=[pltpu.VMEM((rows, len(some) * size), BF16)] * 2,
            limit=20,
            aliases=aliases,
        )(*arrays, *some, *state)

    def more(some, state):
        return add(more_columns, (panel, norms), some, state, sums, {2 + len(some) + i: i for i in range(4)})

    panel, norms, *state = add(
        first_columns,
        (panel,),
        (pieces[0], others[0]),
        (),
        (shape((rows, width), BF16), shape((rows, LANES), F32), *sums),
        {},
    )
    state = more(pieces[1:3], state)
    total = in_vmem(count_chosen, "count_chosen", shape((8, LANES), F32))(*pieces, *others)
    for bit in (1, 2, 4):
        total = total + lax.ppermute(total, RING, [(place(i), place(i ^ bit)) for i in range(ring)])
    for some in ((pieces[3], others[1]), others[2:3], others[3:]):
        state = more(some, state)

    inputs = panel, *state, total
    whole, half = (shape((n, width + LANES), jnp.int16) for n in (2 * height, height // 2))
    up, down, up_half, down_half = in_vmem(
        functools.partial(far_terms, target_count, height),
        "far_terms",
        (whole, whole, half, half),
    )(*inputs)
    from_above, from_below = up_the_ring(down, ring - 1), up_the_ring(up, 1)
    half_above, half_below = up_the_ring(down_half, ring - 2), up_the_ring(up_half, 2)
    near = in_vmem(
        functools.partial(near_terms, target_count, height),
        "near_terms",
        (shape((3 * height, width), F32), shape((3 * height, LANES), F32)),
    )(*inputs)
    up, down = in_vmem(pass_on, "pass_on", (shape((height, width + LANES), jnp.int16),) * 2)(
        *near, from_below, from_above, half_below, half_above
    )
    far_above, far_below = up_the_ring(down, ring - 2), up_the_ring(up, 2)
    proof, gradient = in_vmem(
        add_up, "add_up", (shape((1, height), F32), shape((height, width), F32))
    )(*near, from_below, from_above, far_below, far_above)
    return proof.reshape(height), gradient


def solution(mesh):
    split = Mesh(mesh.devices.reshape(2, 4, 2, 4, 4), AXES)
    return jax.shard_map(
        on_device,
        mesh=split,
        in_specs=(P(AXES, None), P(AXES, None), P(AXES)),
        out_specs=(P(AXES), P(AXES, None)),
        check_vma=False,
    )
```

time: 140 us -> 104 us (0.74)
  blocking collectives: 38.4 us -> 0 us
  waiting for transfers between devices: 29.7 us -> 37.5 us
  Pallas kernels: 27.4 us -> 23.1 us
    all_to_all x1 -> x0, blocking collectives: 38.4 us -> none  [on_device(): coded = lax.all_to_all(coded, RING, split_axis=0, concat_axis=0, tiled=True)]
    ppermute x0 -> x6, starting transfers between devices: none -> 12.1 us  [up_the_ring(): lax.ppermute(x, RING, [(place(i), place((i + step) % ring)) for i in rang...]
    ppermute x0 -> x6, waiting for transfers between devices: none -> 11 us  [up_the_ring(): lax.ppermute(x, RING, [(place(i), place((i + step) % ring)) for i in rang...]
    ppermute x5 -> x4, starting transfers between devices: 7.66 us -> 0.01 us  [other_core(): return lax.ppermute(x, 'c', [(0, 1), (1, 0)])]
    pallas_call x5 -> x12, Pallas kernels: 27.4 us -> 23.1 us  [call(): pl.pallas_call(body, out_shape=out_shape, in_specs=[spec] * len(args), ou...]
    ppermute x3, waiting for transfers between devices: 4.76 us -> 1.73 us  [on_device(): lax.ppermute(total, RING, [(place(i), place(i ^ bit)) for i in range(ring)])]
    ppermute x8 -> x6, starting transfers between devices: 11.9 us -> 9.45 us  [along_line(): return lax.ppermute(x, PLANE, pairs)]
    unnamed x12 -> x8, local copies, waits for them, and re-layouts: 3.48 us -> 2.26 us
  transfers between devices with their start and end apart: 17 -> 20, of which waited for: 9 -> 8; matrix products, arithmetic and copies ran while one was open for 1% -> 0% of each run, Pallas kernels for 8% -> 15%
where the time goes in v3:
time: 104 us; the launch traced here: 103 us
  starting transfers between devices  39.7 us (38%)
  waiting for transfers between devices  37.5 us (36%)
  Pallas kernels  23.1 us (22%)
  local copies, waits for them, and re-layouts  2.26 us (2%)
    ppermute x6, waiting for transfers between devices, along_line(): return lax.ppermute(x, PLANE, pairs)  24.8 us
    pallas_call x12, Pallas kernels, call(): pl.pallas_call(body, out_shape=out_shape, in_specs=[spec] * len(args), ou...  23.1 us
    ppermute x6, starting transfers between devices, up_the_ring(): lax.ppermute(x, RING, [(place(i), place((i + step) % ring)) for i in rang...  12.1 us
    ppermute x6, waiting for transfers between devices, up_the_ring(): lax.ppermute(x, RING, [(place(i), place((i + step) % ring)) for i in rang...  11 us
    ppermute x3, starting transfers between devices, on_device(): lax.ppermute(total, RING, [(place(i), place(i ^ bit)) for i in range(ring)])  9.68 us
    ppermute x6, starting transfers between devices, along_line(): return lax.ppermute(x, PLANE, pairs)  9.45 us
    all_to_all x1, starting transfers between devices, on_device(): lax.all_to_all(copies, RING, split_axis=0, concat_axis=0, tiled=True)  8.47 us
    unnamed x8, local copies, waits for them, and re-layouts  2.26 us
  transfers between devices with their start and end apart: 20, of which 8 were waited for; matrix products, arithmetic and copies ran while one was open for 0% of the time, Pallas kernels for 15%

profile of v3, /device:TPU:8, one launch (start us, length us, event | category | flops | bytes accessed | tf_op | source)
XLA Modules:
  0.0 103.4 jit_solution(12325124953465733109)
XLA Ops:
  0.6 2.2 %pack_block.1 = (bf16[144,1024]{1,0:T(8,128)(2,1)}, bf16[8,64,1024]{2,1,0:T(8,128)(2,1)}) custom-call(bf16[64,1024]{1,0:T(8,128)(2,1)} %pool.1, bf16[64,1024]{1,0:T(8,128)(2,1)} %targets.1, s32[1,64]{1,0:T(1,128)} %bitcast.2), custom_call_target="tpu_custom_call" | custom-call | bytes 1048576 | tf_op jit(solution)/shard_map/pack_block/pallas_call | solution.py:29
  2.8 3.0 %collective-permute-start.2 = (bf16[144,1024]{1,0:T(8,128)(2,1)}, bf16[144,1024]{1,0:T(8,128)(2,1)S(1)}, u32[]{:S(2)}, u32[]{:S(2)}) collective-permute-start(bf16[144,1024]{1,0:T(8,128)(2,1)} %get-tuple-element.37.refs_0_), channel_id=1, source_target_pairs={{0,64},{16,24},{4,68},{20,28},{8,72},{24,16},{12,76},{28,20},{32,9... | collective-permute-start | bytes 884744 | tf_op jit(solution)/shard_map/ppermute | solution.py:262
  5.8 1.1 %collective-permute-start.1 = (bf16[144,1024]{1,0:T(8,128)(2,1)}, bf16[144,1024]{1,0:T(8,128)(2,1)S(1)}, u32[]{:S(2)}, u32[]{:S(2)}) collective-permute-start(bf16[144,1024]{1,0:T(8,128)(2,1)} %get-tuple-element.37.refs_0_), channel_id=1, source_target_pairs={{0,96},{16,28},{4,100},{20,16},{8,104},{24,20},{12,108},{28,24},{3... | collective-permute-start | bytes 884744 | tf_op jit(solution)/shard_map/ppermute | solution.py:262
  7.0 0.9 collective-permute-start
  7.9 8.5 %all-to-all-start = ((bf16[8,64,1024]{2,1,0:T(8,128)(2,1)}), bf16[8,64,1024]{2,1,0:T(8,128)(2,1)}, u32[]{:S(2)}, u32[]{:S(2)}) async-start(bf16[8,64,1024]{2,1,0:T(8,128)(2,1)} %get-tuple-element.36), calls=%async_computation | async-start | bytes 2097152 | tf_op jit(solution)/shard_map/all_to_all | solution.py:286
  16.5 1.7 %collective-permute-start.8 = (bf16[528,1024]{1,0:T(8,128)(2,1)S(1)}, bf16[528,1024]{1,0:T(8,128)(2,1)}, u32[]{:S(2)}, u32[]{:S(2)}) collective-permute-start(bf16[528,1024]{1,0:T(8,128)(2,1)S(1)} %pack_line.1.refs_0_), channel_id=1, source_target_pairs={{0,4},{16,48},{4,8},{20,52},{8,12},{24,56},{12,0},{28,60},{32,36},... | collective-permute-start | bytes 3244040 | tf_op jit(solution)/shard_map/ppermute | solution.py:262
  18.6 2.3 %collective-permute-start.4 = (bf16[528,1024]{1,0:T(8,128)(2,1)S(1)}, bf16[528,1024]{1,0:T(8,128)(2,1)}, u32[]{:S(2)}, u32[]{:S(2)}) collective-permute-start(bf16[528,1024]{1,0:T(8,128)(2,1)S(1)} %pack_line.1.refs_0_), channel_id=1, source_target_pairs={{0,8},{16,80},{4,12},{20,84},{8,0},{24,88},{12,4},{28,92},{32,40},... | collective-permute-start | bytes 3244040 | tf_op jit(solution)/shard_map/ppermute | solution.py:262
  20.9 10.9 %collective-permute-done.8.refs_0_.refs_1_ = bf16[528,1024]{1,0:T(8,128)(2,1)} collective-permute-done((bf16[528,1024]{1,0:T(8,128)(2,1)S(1)}, bf16[528,1024]{1,0:T(8,128)(2,1)}, u32[]{:S(2)}, u32[]{:S(2)}) %collective-permute-start.8) | collective-permute-done | bytes 1081376 | tf_op jit(solution)/shard_map/ppermute | solution.py:262
  31.8 1.6 %collective-permute-done.6.refs_1_.refs_2_ = bf16[528,1024]{1,0:T(8,128)(2,1)} collective-permute-done((bf16[528,1024]{1,0:T(8,128)(2,1)S(1)}, bf16[528,1024]{1,0:T(8,128)(2,1)}, u32[]{:S(2)}, u32[]{:S(2)}) %collective-permute-start.6) | collective-permute-done | bytes 1081376 | tf_op jit(solution)/shard_map/ppermute | solution.py:262
  33.4 12.3 %collective-permute-done.4.refs_0_.refs_3_ = bf16[528,1024]{1,0:T(8,128)(2,1)} collective-permute-done((bf16[528,1024]{1,0:T(8,128)(2,1)S(1)}, bf16[528,1024]{1,0:T(8,128)(2,1)}, u32[]{:S(2)}, u32[]{:S(2)}) %collective-permute-start.4) | collective-permute-done | bytes 1081376 | tf_op jit(solution)/shard_map/ppermute | solution.py:262
  45.7 1.0 copy-done
  46.7 1.2 %copy-done.1 = bf16[528,1024]{1,0:T(8,128)(2,1)S(1)} copy-done((bf16[528,1024]{1,0:T(8,128)(2,1)S(1)}, bf16[528,1024]{1,0:T(8,128)(2,1)}, u32[]{:S(2)}) %copy-start.1) | copy-done | bytes 1081368
  47.9 3.9 %first_columns.1 = (bf16[512,1024]{1,0:T(8,128)(2,1)S(1)}, f32[512,128]{1,0:T(8,128)S(1)}, f32[512,1024]{1,0:T(8,128)S(1)}, f32[512,1024]{1,0:T(8,128)S(1)}, f32...) custom-call(bf16[8,64,1024]{2,1,0:T(8,128)(2,1)} %all-to-all-done.panel, bf16[528,1024]{1,0:T(8,128)(2,1)S(1)} %pack_line.1.refs_0_, ...), custom_call_target="tpu_custom_call" | custom-call | flops 2147483648 | bytes 1048576 | tf_op jit(solution)/shard_map/first_columns/pallas_call | solution.py:29
  51.9 4.3 %more_columns.4 = (f32[512,1024]{1,0:T(8,128)S(1)}, f32[512,1024]{1,0:T(8,128)S(1)}, f32[512,128]{1,0:T(8,128)S(1)}, f32[512,128]{1,0:T(8,128)S(1)}) custom-call(bf16[512,1024]{1,0:T(8,128)(2,1)S(1)} %get-tuple-element.38.panel.refs_0_, ...), custom_call_target="tpu_custom_call", output_to_operand_aliasing={{0}: (4, {}), {1}: (5, {}), {2}: (6, {}), {3}: (7, {})} | custom-call | flops 2147483648 | bytes 1048576 | tf_op jit(solution)/shard_map/more_columns/pallas_call | solution.py:29
  56.2 2.3 %count_chosen.1 = f32[8,128]{1,0:T(8,128)S(1)} custom-call(bf16[528,1024]{1,0:T(8,128)(2,1)S(1)} %pack_line.1.refs_0_, bf16[528,1024]{1,0:T(8,128)(2,1)} %collective-permute-done.8.refs_0_.refs_1_, bf16[528,1024]{1,0:T(8,128)(2,1)} %collective-permute-done.6.refs_1_.refs_2_, bf16[528,1024]{1,0:T(8,128)(2,1)} %collective-permute-done.4.refs_0_.refs_3_, ...), custom_call_target="tpu_custom_call" | custom-call | bytes 1048576 | tf_op jit(solution)/shard_map/count_chosen/pallas_call | solution.py:29
  58.6 2.3 %collective-permute-start.10 = (f32[8,128]{1,0:T(8,128)S(1)}, f32[8,128]{1,0:T(8,128)S(1)}, u32[]{:S(2)}, u32[]{:S(2)}) collective-permute-start(f32[8,128]{1,0:T(8,128)S(1)} %count_chosen.1), channel_id=1, source_target_pairs={{0,128},{128,0},{1,129},{129,1},{2,130},{130,2},{3,131},{131,3},{4... | collective-permute-start | bytes 12296 | tf_op jit(solution)/shard_map/ppermute | solution.py:321
  60.9 4.2 %more_columns.5 = (f32[512,1024]{1,0:T(8,128)S(1)}, f32[512,1024]{1,0:T(8,128)S(1)}, f32[512,128]{1,0:T(8,128)S(1)}, f32[512,128]{1,0:T(8,128)S(1)}) custom-call(bf16[512,1024]{1,0:T(8,128)(2,1)S(1)} %get-tuple-element.38.panel.refs_0_, ...), custom_call_target="tpu_custom_call", output_to_operand_aliasing={{0}: (4, {}), {1}: (5, {}), {2}: (6, {}), {3}: (7, {})} | custom-call | flops 2147483648 | bytes 1048576 | tf_op jit(solution)/shard_map/more_columns/pallas_call | solution.py:29
  65.1 2.5 %collective-permute-start.11 = (f32[8,128]{1,0:T(8,128)S(1)}, f32[8,128]{1,0:T(8,128)S(1)}, u32[]{:S(2)}, u32[]{:S(2)}) collective-permute-start(f32[8,128]{1,0:T(8,128)S(1)} %add.9), channel_id=1, source_target_pairs={{0,1},{128,129},{1,0},{129,128},{2,3},{130,131},{3,2},{131,130},{4... | collective-permute-start | bytes 12296 | tf_op jit(solution)/shard_map/ppermute | solution.py:321
  67.6 1.5 %more_columns.6 = (f32[512,1024]{1,0:T(8,128)S(1)}, f32[512,1024]{1,0:T(8,128)S(1)}, f32[512,128]{1,0:T(8,128)S(1)}, f32[512,128]{1,0:T(8,128)S(1)}) custom-call(bf16[512,1024]{1,0:T(8,128)(2,1)S(1)} %get-tuple-element.38.panel.refs_0_, ...), custom_call_target="tpu_custom_call", output_to_operand_aliasing={{0}: (3, {}), {1}: (4, {}), {2}: (5, {}), {3}: (6, {})} | custom-call | flops 1073741824 | bytes 1048576 | tf_op jit(solution)/shard_map/more_columns/pallas_call | solution.py:29
  69.1 0.7 collective-permute-done.11
  69.7 4.9 %collective-permute-start.12 = (f32[8,128]{1,0:T(8,128)S(1)}, f32[8,128]{1,0:T(8,128)S(1)}, u32[]{:S(2)}, u32[]{:S(2)}) collective-permute-start(f32[8,128]{1,0:T(8,128)S(1)} %add.10), channel_id=1, source_target_pairs={{0,2},{128,130},{1,3},{129,131},{2,0},{130,128},{3,1},{131,129},{4... | collective-permute-start | bytes 12296 | tf_op jit(solution)/shard_map/ppermute | solution.py:321
  74.7 1.5 %more_columns.7 = (f32[512,1024]{1,0:T(8,128)S(1)}, f32[512,1024]{1,0:T(8,128)S(1)}, f32[512,128]{1,0:T(8,128)S(1)}, f32[512,128]{1,0:T(8,128)S(1)}) custom-call(bf16[512,1024]{1,0:T(8,128)(2,1)S(1)} %get-tuple-element.38.panel.refs_0_, ...), custom_call_target="tpu_custom_call", output_to_operand_aliasing={{0}: (3, {}), {1}: (4, {}), {2}: (5, {}), {3}: (6, {})} | custom-call | flops 1073741824 | bytes 1048576 | tf_op jit(solution)/shard_map/more_columns/pallas_call | solution.py:29
  76.2 1.1 %collective-permute-done.12 = f32[8,128]{1,0:T(8,128)S(1)} collective-permute-done((f32[8,128]{1,0:T(8,128)S(1)}, f32[8,128]{1,0:T(8,128)S(1)}, u32[]{:S(2)}, u32[]{:S(2)}) %collective-permute-start.12) | collective-permute-done | bytes 4128 | tf_op jit(solution)/shard_map/ppermute | solution.py:321
  77.3 1.0 far_terms.1
  78.4 3.6 %collective-permute-start.14 = (s16[128,1152]{1,0:T(8,128)(2,1)S(1)}, s16[128,1152]{1,0:T(8,128)(2,1)S(1)}, u32[]{:S(2)}, u32[]{:S(2)}) collective-permute-start(s16[128,1152]{1,0:T(8,128)(2,1)S(1)} %get-tuple-element.63), channel_id=1, source_target_pairs={{0,131},{128,0},{1,128},{129,1},{2,129},{130,2},{3,130},{131,3},{4... | collective-permute-start | bytes 884744 | tf_op jit(solution)/shard_map/ppermute | solution.py:252
  82.0 0.7 collective-permute-start.15
  82.8 3.4 %collective-permute-start.16 = (s16[32,1152]{1,0:T(8,128)(2,1)S(1)}, s16[32,1152]{1,0:T(8,128)(2,1)S(1)}, u32[]{:S(2)}, u32[]{:S(2)}) collective-permute-start(s16[32,1152]{1,0:T(8,128)(2,1)S(1)} %get-tuple-element.65), channel_id=1, source_target_pairs={{0,3},{128,131},{1,0},{129,128},{2,1},{130,129},{3,2},{131,130},{4... | collective-permute-start | bytes 221192 | tf_op jit(solution)/shard_map/ppermute | solution.py:252
  86.6 4.6 %collective-permute-done.15.half_below = s16[32,1152]{1,0:T(8,128)(2,1)S(1)} collective-permute-done((s16[32,1152]{1,0:T(8,128)(2,1)S(1)}, s16[32,1152]{1,0:T(8,128)(2,1)S(1)}, u32[]{:S(2)}, u32[]{:S(2)}) %collective-permute-start.15) | collective-permute-done | bytes 73760 | tf_op jit(solution)/shard_map/ppermute | solution.py:252
  91.7 3.8 %collective-permute-start.17 = (s16[64,1152]{1,0:T(8,128)(2,1)S(1)}, s16[64,1152]{1,0:T(8,128)(2,1)S(1)}, u32[]{:S(2)}, u32[]{:S(2)}) collective-permute-start(s16[64,1152]{1,0:T(8,128)(2,1)S(1)} %get-tuple-element.66), channel_id=1, source_target_pairs={{0,1},{128,129},{1,2},{129,130},{2,3},{130,131},{3,0},{131,128},{4... | collective-permute-start | bytes 442376 | tf_op jit(solution)/shard_map/ppermute | solution.py:252
  95.9 4.2 %collective-permute-done.17.far_below = s16[64,1152]{1,0:T(8,128)(2,1)S(1)} collective-permute-done((s16[64,1152]{1,0:T(8,128)(2,1)S(1)}, s16[64,1152]{1,0:T(8,128)(2,1)S(1)}, u32[]{:S(2)}, u32[]{:S(2)}) %collective-permute-start.17) | collective-permute-done | bytes 147488 | tf_op jit(solution)/shard_map/ppermute | solution.py:252
  100.1 2.2 %collective-permute-done.18.far_above = s16[64,1152]{1,0:T(8,128)(2,1)S(1)} collective-permute-done((s16[64,1152]{1,0:T(8,128)(2,1)S(1)}, s16[64,1152]{1,0:T(8,128)(2,1)S(1)}, u32[]{:S(2)}, u32[]{:S(2)}) %collective-permute-start.18) | collective-permute-done | bytes 147488 | tf_op jit(solution)/shard_map/ppermute | solution.py:252
  102.3 1.1 %add_up.1 = (f32[1,64]{1,0:T(1,128)}, f32[64,1024]{1,0:T(8,128)}) custom-call(f32[192,1024]{1,0:T(8,128)S(1)} %get-tuple-element.60.gradient, f32[192,128]{1,0:T(8,128)S(1)} %get-tuple-element.61.proof, s16[128,1152]{1,0:T(8,128)(2,1)S(1)} %collective-permute-done.13.from_below, s16[128,1152]{1,0:T(8,128)(2,1)S(1)} %collective-permute-done.14.from_above, ...), custom_call_target="tpu_custom_call" | custom-call | bytes 1048576 | tf_op jit(solution)/shard_map/add_up/pallas_call | solution.py:29
  (31 shorter events, 2.1 us)
Async XLA Ops:
  2.8 13.5 %copy-start.3 = (bf16[144,1024]{1,0:T(8,128)(2,1)S(1)}, bf16[144,1024]{1,0:T(8,128)(2,1)}, u32[]{:S(2)}) copy-start(bf16[144,1024]{1,0:T(8,128)(2,1)} %get-tuple-element.37.refs_0_) | copy-start | bytes 884740
  2.8 13.5 %collective-permute-start.2 = (bf16[144,1024]{1,0:T(8,128)(2,1)}, bf16[144,1024]{1,0:T(8,128)(2,1)S(1)}, u32[]{:S(2)}, u32[]{:S(2)}) collective-permute-start(bf16[144,1024]{1,0:T(8,128)(2,1)} %get-tuple-element.37.refs_0_), channel_id=1, source_target_pairs={{0,64},{16,24},{4,68},{20,28},{8,72},{24,16},{12,76},{28,20},{32,9... | collective-permute-start | bytes 884744 | tf_op jit(solution)/shard_map/ppermute | solution.py:262
  5.8 10.5 %collective-permute-start.1 = (bf16[144,1024]{1,0:T(8,128)(2,1)}, bf16[144,1024]{1,0:T(8,128)(2,1)S(1)}, u32[]{:S(2)}, u32[]{:S(2)}) collective-permute-start(bf16[144,1024]{1,0:T(8,128)(2,1)} %get-tuple-element.37.refs_0_), channel_id=1, source_target_pairs={{0,96},{16,28},{4,100},{20,16},{8,104},{24,20},{12,108},{28,24},{3... | collective-permute-start | bytes 884744 | tf_op jit(solution)/shard_map/ppermute | solution.py:262
  7.0 9.4 %collective-permute-start = (bf16[144,1024]{1,0:T(8,128)(2,1)}, bf16[144,1024]{1,0:T(8,128)(2,1)S(1)}, u32[]{:S(2)}, u32[]{:S(2)}) collective-permute-start(bf16[144,1024]{1,0:T(8,128)(2,1)} %get-tuple-element.37.refs_0_), channel_id=1, source_target_pairs={{0,32},{16,20},{4,36},{20,24},{8,40},{24,28},{12,44},{28,16},{32,6... | collective-permute-start | bytes 884744 | tf_op jit(solution)/shard_map/ppermute | solution.py:262
  7.9 38.8 %all-to-all-start = ((bf16[8,64,1024]{2,1,0:T(8,128)(2,1)}), bf16[8,64,1024]{2,1,0:T(8,128)(2,1)}, u32[]{:S(2)}, u32[]{:S(2)}) async-start(bf16[8,64,1024]{2,1,0:T(8,128)(2,1)} %get-tuple-element.36), calls=%async_computation | async-start | bytes 2097152 | tf_op jit(solution)/shard_map/all_to_all | solution.py:286
  16.5 15.3 %collective-permute-start.8 = (bf16[528,1024]{1,0:T(8,128)(2,1)S(1)}, bf16[528,1024]{1,0:T(8,128)(2,1)}, u32[]{:S(2)}, u32[]{:S(2)}) collective-permute-start(bf16[528,1024]{1,0:T(8,128)(2,1)S(1)} %pack_line.1.refs_0_), channel_id=1, source_target_pairs={{0,4},{16,48},{4,8},{20,52},{8,12},{24,56},{12,0},{28,60},{32,36},... | collective-permute-start | bytes 3244040 | tf_op jit(solution)/shard_map/ppermute | solution.py:262
  18.1 15.3 %collective-permute-start.6 = (bf16[528,1024]{1,0:T(8,128)(2,1)S(1)}, bf16[528,1024]{1,0:T(8,128)(2,1)}, u32[]{:S(2)}, u32[]{:S(2)}) collective-permute-start(bf16[528,1024]{1,0:T(8,128)(2,1)S(1)} %pack_line.1.refs_0_), channel_id=1, source_target_pairs={{0,12},{16,112},{4,0},{20,116},{8,4},{24,120},{12,8},{28,124},{32,... | collective-permute-start | bytes 3244040 | tf_op jit(solution)/shard_map/ppermute | solution.py:262
  18.6 27.1 %collective-permute-start.4 = (bf16[528,1024]{1,0:T(8,128)(2,1)S(1)}, bf16[528,1024]{1,0:T(8,128)(2,1)}, u32[]{:S(2)}, u32[]{:S(2)}) collective-permute-start(bf16[528,1024]{1,0:T(8,128)(2,1)S(1)} %pack_line.1.refs_0_), channel_id=1, source_target_pairs={{0,8},{16,80},{4,12},{20,84},{8,0},{24,88},{12,4},{28,92},{32,40},... | collective-permute-start | bytes 3244040 | tf_op jit(solution)/shard_map/ppermute | solution.py:262
  20.9 24.8 %collective-permute-start.3 = (bf16[528,1024]{1,0:T(8,128)(2,1)S(1)}, bf16[528,1024]{1,0:T(8,128)(2,1)S(1)}, u32[]{:S(2)}, u32[]{:S(2)}) collective-permute-start(bf16[528,1024]{1,0:T(8,128)(2,1)S(1)} %pack_line.1.refs_0_), channel_id=1, source_target_pairs={{0,16},{16,0},{1,17},{17,1},{2,18},{18,2},{3,19},{19,3},{4,20},{20... | collective-permute-start | bytes 3244040 | tf_op jit(solution)/shard_map/ppermute | solution.py:270
  31.8 24.4 %collective-permute-start.9 = (bf16[528,1024]{1,0:T(8,128)(2,1)}, bf16[528,1024]{1,0:T(8,128)(2,1)}, u32[]{:S(2)}, u32[]{:S(2)}) collective-permute-start(bf16[528,1024]{1,0:T(8,128)(2,1)} %collective-permute-done.8.refs_0_.refs_1_), channel_id=1, source_target_pairs={{0,16},{16,0},{1,17},{17,1},{2,18},{18,2},{3,19},{19,3},{4,20},{20... | collective-permute-start | bytes 3244040 | tf_op jit(solution)/shard_map/ppermute | solution.py:270
  33.4 22.8 %collective-permute-start.7 = (bf16[528,1024]{1,0:T(8,128)(2,1)}, bf16[528,1024]{1,0:T(8,128)(2,1)S(1)}, u32[]{:S(2)}, u32[]{:S(2)}) collective-permute-start(bf16[528,1024]{1,0:T(8,128)(2,1)} %collective-permute-done.6.refs_1_.refs_2_), channel_id=1, source_target_pairs={{0,16},{16,0},{1,17},{17,1},{2,18},{18,2},{3,19},{19,3},{4,20},{20... | collective-permute-start | bytes 3244040 | tf_op jit(solution)/shard_map/ppermute | solution.py:270
  45.7 10.5 %collective-permute-start.5 = (bf16[528,1024]{1,0:T(8,128)(2,1)}, bf16[528,1024]{1,0:T(8,128)(2,1)S(1)}, u32[]{:S(2)}, u32[]{:S(2)}) collective-permute-start(bf16[528,1024]{1,0:T(8,128)(2,1)} %collective-permute-done.4.refs_0_.refs_3_), channel_id=1, source_target_pairs={{0,16},{16,0},{1,17},{17,1},{2,18},{18,2},{3,19},{19,3},{4,20},{20... | collective-permute-start | bytes 3244040 | tf_op jit(solution)/shard_map/ppermute | solution.py:270
  45.7 1.0 copy-start
  46.7 1.2 %copy-start.1 = (bf16[528,1024]{1,0:T(8,128)(2,1)S(1)}, bf16[528,1024]{1,0:T(8,128)(2,1)}, u32[]{:S(2)}) copy-start(bf16[528,1024]{1,0:T(8,128)(2,1)} %copy-done) | copy-start | bytes 3244036
  51.8 4.4 %copy-start.2 = (bf16[528,1024]{1,0:T(8,128)(2,1)S(1)}, bf16[528,1024]{1,0:T(8,128)(2,1)}, u32[]{:S(2)}) copy-start(bf16[528,1024]{1,0:T(8,128)(2,1)} %copy-done) | copy-start | bytes 3244036
  58.6 6.5 %collective-permute-start.10 = (f32[8,128]{1,0:T(8,128)S(1)}, f32[8,128]{1,0:T(8,128)S(1)}, u32[]{:S(2)}, u32[]{:S(2)}) collective-permute-start(f32[8,128]{1,0:T(8,128)S(1)} %count_chosen.1), channel_id=1, source_target_pairs={{0,128},{128,0},{1,129},{129,1},{2,130},{130,2},{3,131},{131,3},{4... | collective-permute-start | bytes 12296 | tf_op jit(solution)/shard_map/ppermute | solution.py:321
  65.1 4.6 %collective-permute-start.11 = (f32[8,128]{1,0:T(8,128)S(1)}, f32[8,128]{1,0:T(8,128)S(1)}, u32[]{:S(2)}, u32[]{:S(2)}) collective-permute-start(f32[8,128]{1,0:T(8,128)S(1)} %add.9), channel_id=1, source_target_pairs={{0,1},{128,129},{1,0},{129,128},{2,3},{130,131},{3,2},{131,130},{4... | collective-permute-start | bytes 12296 | tf_op jit(solution)/shard_map/ppermute | solution.py:321
  69.7 7.5 %collective-permute-start.12 = (f32[8,128]{1,0:T(8,128)S(1)}, f32[8,128]{1,0:T(8,128)S(1)}, u32[]{:S(2)}, u32[]{:S(2)}) collective-permute-start(f32[8,128]{1,0:T(8,128)S(1)} %add.10), channel_id=1, source_target_pairs={{0,2},{128,130},{1,3},{129,131},{2,0},{130,128},{3,1},{131,129},{4... | collective-permute-start | bytes 12296 | tf_op jit(solution)/shard_map/ppermute | solution.py:321
  78.2 12.9 %collective-permute-start.13 = (s16[128,1152]{1,0:T(8,128)(2,1)S(1)}, s16[128,1152]{1,0:T(8,128)(2,1)S(1)}, u32[]{:S(2)}, u32[]{:S(2)}) collective-permute-start(s16[128,1152]{1,0:T(8,128)(2,1)S(1)} %get-tuple-element.62), channel_id=1, source_target_pairs={{0,128},{128,1},{1,129},{129,2},{2,130},{130,3},{3,131},{131,0},{4... | collective-permute-start | bytes 884744 | tf_op jit(solution)/shard_map/ppermute | solution.py:252
  78.4 12.8 %collective-permute-start.14 = (s16[128,1152]{1,0:T(8,128)(2,1)S(1)}, s16[128,1152]{1,0:T(8,128)(2,1)S(1)}, u32[]{:S(2)}, u32[]{:S(2)}) collective-permute-start(s16[128,1152]{1,0:T(8,128)(2,1)S(1)} %get-tuple-element.63), channel_id=1, source_target_pairs={{0,131},{128,0},{1,128},{129,1},{2,129},{130,2},{3,130},{131,3},{4... | collective-permute-start | bytes 884744 | tf_op jit(solution)/shard_map/ppermute | solution.py:252
  82.0 9.1 %collective-permute-start.15 = (s16[32,1152]{1,0:T(8,128)(2,1)S(1)}, s16[32,1152]{1,0:T(8,128)(2,1)S(1)}, u32[]{:S(2)}, u32[]{:S(2)}) collective-permute-start(s16[32,1152]{1,0:T(8,128)(2,1)S(1)} %get-tuple-element.64), channel_id=1, source_target_pairs={{0,1},{128,129},{1,2},{129,130},{2,3},{130,131},{3,0},{131,128},{4... | collective-permute-start | bytes 221192 | tf_op jit(solution)/shard_map/ppermute | solution.py:252
  82.8 8.4 %collective-permute-start.16 = (s16[32,1152]{1,0:T(8,128)(2,1)S(1)}, s16[32,1152]{1,0:T(8,128)(2,1)S(1)}, u32[]{:S(2)}, u32[]{:S(2)}) collective-permute-start(s16[32,1152]{1,0:T(8,128)(2,1)S(1)} %get-tuple-element.65), channel_id=1, source_target_pairs={{0,3},{128,131},{1,0},{129,128},{2,1},{130,129},{3,2},{131,130},{4... | collective-permute-start | bytes 221192 | tf_op jit(solution)/shard_map/ppermute | solution.py:252
  91.7 8.5 %collective-permute-start.17 = (s16[64,1152]{1,0:T(8,128)(2,1)S(1)}, s16[64,1152]{1,0:T(8,128)(2,1)S(1)}, u32[]{:S(2)}, u32[]{:S(2)}) collective-permute-start(s16[64,1152]{1,0:T(8,128)(2,1)S(1)} %get-tuple-element.66), channel_id=1, source_target_pairs={{0,1},{128,129},{1,2},{129,130},{2,3},{130,131},{3,0},{131,128},{4... | collective-permute-start | bytes 442376 | tf_op jit(solution)/shard_map/ppermute | solution.py:252
  95.5 6.8 %collective-permute-start.18 = (s16[64,1152]{1,0:T(8,128)(2,1)S(1)}, s16[64,1152]{1,0:T(8,128)(2,1)S(1)}, u32[]{:S(2)}, u32[]{:S(2)}) collective-permute-start(s16[64,1152]{1,0:T(8,128)(2,1)S(1)} %get-tuple-element.67), channel_id=1, source_target_pairs={{0,3},{128,131},{1,0},{129,128},{2,1},{130,129},{3,2},{131,130},{4... | collective-permute-start | bytes 442376 | tf_op jit(solution)/shard_map/ppermute | solution.py:252

commit v4 on v3

--- a/solution.py
+++ b/solution.py
@@ -22,7 +22,7 @@
     return jax.ShapeDtypeStruct(dims, dtype)
 
 
-def in_vmem(body, name, out_shape, flops=0, traffic=1 << 20, scratch=(), limit=16, aliases=None):
+def in_vmem(body, name, out_shape, flops=0, traffic=1 << 20, scratch=(), limit=12, aliases=None):
     spec = pl.BlockSpec(memory_space=pltpu.VMEM)
 
     def call(*args):
@@ -61,7 +61,7 @@
     return jnp.concatenate([a, b], axis=1)
 
 
-def pack_block(pool, targets, counts, block, copies):
+def pack_block(pool, targets, counts, block):
     height = pool.shape[0]
     block[:height, :] = pool[...]
     block[height : 2 * height, :] = targets[...]
@@ -74,12 +74,13 @@
     block[2 * height :, :] = jnp.concatenate(
         [meta, jnp.zeros((META, block.shape[1] - LANES), F32)], axis=1
     ).astype(BF16)
-    for i in range(copies.shape[0]):
-        copies[i] = pool[...]
 
 
 def pack_line(*refs):
-    blocks, piece = refs[:-1], refs[-1]
+    blocks, (own, below, above, opposite, piece, up_pair, down_pair, across) = refs[:-8], refs[-8:]
+    across[...] = opposite[...]
+    up_pair[...] = jnp.concatenate([own[...], below[...]], axis=0)
+    down_pair[...] = jnp.concatenate([own[...], above[...]], axis=0)
     count, height = len(blocks), (blocks[0].shape[0] - META) // 2
     for j, block in enumerate(blocks):
         piece[j * height : (j + 1) * height, :] = block[:height, :]
@@ -93,7 +94,7 @@
     ).astype(BF16)
 
 
-def add_columns(panel, norms, pieces, pulls, masses, weights, rows, first):
+def add_columns(panel, norms, pieces, old, pulls, masses, weights, rows):
     height, width = panel.shape
     size = (pieces[0].shape[0] - META) // 2
     for half in range(2):
@@ -110,15 +111,17 @@
                 kernel = jnp.exp(-squared * (0.5 / width))
                 if half == 0:
                     kernel = kernel * meta[:1]
-                if first and i == 0:
-                    masses[half][part, :] = lane_sums(kernel)
-                else:
-                    masses[half][part, :] += lane_sums(kernel)
+                mass = lane_sums(kernel)
+                if i > 0:
+                    mass = masses[half][part, :] + mass
+                elif old:
+                    mass = old[2 + half][part, :] + mass
+                masses[half][part, :] = mass
                 weights[half][part, i * size : (i + 1) * size] = kernel.astype(BF16)
     for half in range(2):
         for at in range(0, height, rows):
             part = slice(at, at + rows)
-            total = None if first else pulls[half][part, :]
+            total = old[half][part, :] if old else None
             for i, piece in enumerate(pieces):
                 one = jnp.dot(
                     weights[half][part, i * size : (i + 1) * size],
@@ -129,32 +132,32 @@
             pulls[half][part, :] = total
 
 
-def first_columns(rows, lines, panel, *refs):
+def first_columns(rows, lines, own, below, above, opposite, pair_below, pair_above, *refs):
     pieces, refs = refs[:lines], refs[lines:]
     ordered, norms, pp, tp, pm, tm, *weights = refs
-    ring, height, _ = panel.shape
-    z = 2 * lax.axis_index("zh") + lax.axis_index("zl")
+    height = own.shape[0]
+    found = {0: own, 1: above, 7: below, 4: opposite}
     for i, offset in enumerate(OFFSETS):
         part = slice(i * height, (i + 1) * height)
-        there = lax.rem(z + offset, ring)
-        block = panel[lax.rem(there, 2) * 4 + lax.div(there, 2)]
+        if offset in found:
+            block = found[offset][...]
+        else:
+            pair, at = (pair_above, offset - 2) if offset < 4 else (pair_below, 6 - offset)
+            block = pair[at * height : (at + 1) * height, :]
         ordered[part, :] = block
         norms[part, :] = jnp.broadcast_to(square_norms(block), (height, LANES))
-    add_columns(ordered, norms, pieces, (pp, tp), (pm, tm), weights, rows, True)
+    add_columns(ordered, norms, pieces, (), (pp, tp), (pm, tm), weights, rows)
 
 
 def more_columns(rows, lines, panel, norms, *refs):
-    pieces, refs = refs[:lines], refs[lines + 4 :]
+    pieces, old, refs = refs[:lines], refs[lines : lines + 4], refs[lines + 4 :]
     pp, tp, pm, tm, *weights = refs
-    add_columns(panel, norms, pieces, (pp, tp), (pm, tm), weights, rows, False)
+    add_columns(panel, norms, pieces, old, (pp, tp), (pm, tm), weights, rows)
 
 
 def count_chosen(*refs):
-    pieces, chosen = refs[:-1], refs[-1]
-    size = (pieces[0].shape[0] - META) // 2
-    total = jnp.zeros((1, size), F32)
-    for piece in pieces:
-        total = total + piece[2 * size :, :size].astype(F32)[:1]
+    metas, chosen = refs[:-1], refs[-1]
+    total = sum(meta[...].astype(F32)[:1] for meta in metas)
     chosen[...] = jnp.full(chosen.shape, jnp.sum(total), F32)
 
 
@@ -247,6 +250,19 @@
     return z % 2 * 4 + z // 2
 
 
+def handed_on(array, awaited):
+    there = pl.BlockSpec(memory_space=pl.ANY)
+    return pl.pallas_call(
+        lambda *refs: None,
+        out_shape=shape(array.shape, array.dtype),
+        in_specs=[there, pl.BlockSpec(memory_space=pltpu.VMEM)],
+        out_specs=there,
+        input_output_aliases={0: 0},
+        compiler_params=pltpu.CompilerParams(vmem_limit_bytes=4 << 20),
+        name="handed_on",
+    )(array, awaited)
+
+
 def up_the_ring(x, step):
     ring = lax.axis_size(RING)
     return lax.ppermute(x, RING, [(place(i), place((i + step) % ring)) for i in range(ring)])
@@ -276,19 +292,20 @@
     rows = ring * height
     target_count = float(height * lax.axis_size(AXES))
 
-    block, copies = in_vmem(
-        pack_block,
-        "pack_block",
-        (shape((2 * height + META, width), BF16), shape((ring, height, width), BF16)),
-        limit=56,
-    )(pool, targets, counts.reshape(1, height))
+    block = in_vmem(pack_block, "pack_block", shape((2 * height + META, width), BF16), limit=56)(
+        pool, targets, counts.reshape(1, height)
+    )
     blocks = line(block, 0)
-    panel = lax.all_to_all(copies, RING, split_axis=0, concat_axis=0, tiled=True)
-    piece = in_vmem(
-        pack_line, "pack_line", shape((2 * height * len(blocks) + META, width), BF16)
-    )(*blocks)
+    below, above, opposite = (up_the_ring(pool, step) for step in (1, ring - 1, ring // 2))
+    pair = shape((2 * height, width), BF16)
+    piece, up_pair, down_pair, opposite = in_vmem(
+        pack_line,
+        "pack_line",
+        (shape((2 * height * len(blocks) + META, width), BF16), pair, pair, shape(pool.shape, BF16)),
+    )(*blocks, pool, below, above, opposite)
     pieces = line(piece, 1)
-    others = [other_core(p) for p in pieces]
+    pairs = up_the_ring(up_pair, 2), up_the_ring(down_pair, ring - 2)
+    others = [other_core(p) for p in pieces[:3]]
 
     size = height * len(blocks)
     sums = (shape((rows, width), F32),) * 2 + (shape((rows, LANES), F32),) * 2
@@ -300,7 +317,7 @@
             out_shape,
             flops=8 * rows * len(some) * size * width,
             scratch=[pltpu.VMEM((rows, len(some) * size), BF16)] * 2,
-            limit=20,
+            limit=12,
             aliases=aliases,
         )(*arrays, *some, *state)
 
@@ -309,17 +326,27 @@
 
     panel, norms, *state = add(
         first_columns,
-        (panel,),
-        (pieces[0], others[0]),
+        (pool, below, above, opposite, *pairs),
+        pieces[:1],
         (),
         (shape((rows, width), BF16), shape((rows, LANES), F32), *sums),
         {},
     )
     state = more(pieces[1:3], state)
-    total = in_vmem(count_chosen, "count_chosen", shape((8, LANES), F32))(*pieces, *others)
+    pieces[3] = handed_on(pieces[3], state[2])
+    others.append(other_core(pieces[3]))
+    total = pl.pallas_call(
+        count_chosen,
+        grid=(1,),
+        out_shape=shape((8, LANES), F32),
+        in_specs=[pl.BlockSpec((META, size), lambda i: (2 * size // META, 0))] * 2 * len(pieces),
+        out_specs=pl.BlockSpec((8, LANES), lambda i: (0, 0)),
+        name="count_chosen",
+        compiler_params=pltpu.CompilerParams(vmem_limit_bytes=4 << 20),
+    )(*pieces, *others)
     for bit in (1, 2, 4):
         total = total + lax.ppermute(total, RING, [(place(i), place(i ^ bit)) for i in range(ring)])
-    for some in ((pieces[3], others[1]), others[2:3], others[3:]):
+    for some in (pieces[3:], others[:2], others[2:3], others[3:]):
         state = more(some, state)
 
     inputs = panel, *state, total

time: 104 us -> 109 us (1.048)
  the two profiles are of different devices: /device:TPU:8 before, /device:TPU:6 now
where the time goes in v4:
time: 109 us
  waiting for transfers between devices  50.4 us (46%)
  starting transfers between devices  37.6 us (34%)
  Pallas kernels  18.4 us (17%)
  local copies, waits for them, and re-layouts  1.86 us (2%)
    ppermute x11, waiting for transfers between devices, up_the_ring(): lax.ppermute(x, RING, [(place(i), place((i + step) % ring)) for i in rang...  34.1 us
    ppermute x11, starting transfers between devices, up_the_ring(): lax.ppermute(x, RING, [(place(i), place((i + step) % ring)) for i in rang...  25.9 us
    pallas_call x12, Pallas kernels, call(): pl.pallas_call(body, out_shape=out_shape, in_specs=[spec] * len(args), ou...  18.3 us
    ppermute x6, waiting for transfers between devices, along_line(): return lax.ppermute(x, PLANE, pairs)  9.05 us
    ppermute x6, starting transfers between devices, along_line(): return lax.ppermute(x, PLANE, pairs)  5.91 us
    ppermute x3, starting transfers between devices, on_device(): lax.ppermute(total, RING, [(place(i), place(i ^ bit)) for i in range(ring)])  5.12 us
    ppermute x3, waiting for transfers between devices, on_device(): lax.ppermute(total, RING, [(place(i), place(i ^ bit)) for i in range(ring)])  3.82 us
    ppermute x4, waiting for transfers between devices, other_core(): return lax.ppermute(x, 'c', [(0, 1), (1, 0)])  3.36 us
  transfers between devices with their start and end apart: 24, of which 13 were waited for; matrix products, arithmetic and copies ran while one was open for 0% of the time, Pallas kernels for 12%

profile of v4, /device:TPU:6, one launch (start us, length us, event | category | flops | bytes accessed | tf_op | source)
XLA Modules:
  0.0 109.1 jit_solution(5237827521264729906)
XLA Ops:
  0.6 2.0 %pack_block.1.refs_0_ = bf16[144,1024]{1,0:T(8,128)(2,1)} custom-call(bf16[64,1024]{1,0:T(8,128)(2,1)} %own.1, bf16[64,1024]{1,0:T(8,128)(2,1)} %targets.1, s32[1,64]{1,0:T(1,128)} %bitcast.2), custom_call_target="tpu_custom_call" | custom-call | bytes 1048576 | tf_op jit(solution)/shard_map/pack_block/pallas_call | solution.py:29
  2.6 2.2 %collective-permute-start.2 = (bf16[144,1024]{1,0:T(8,128)(2,1)}, bf16[144,1024]{1,0:T(8,128)(2,1)S(1)}, u32[]{:S(2)}, u32[]{:S(2)}) collective-permute-start(bf16[144,1024]{1,0:T(8,128)(2,1)} %pack_block.1.refs_0_), channel_id=1, source_target_pairs={{0,32},{16,20},{4,36},{20,24},{8,40},{24,28},{12,44},{28,16},{32,6... | collective-permute-start | bytes 884744 | tf_op jit(solution)/shard_map/ppermute | solution.py:278
  4.8 1.5 %collective-permute-start.4 = (bf16[144,1024]{1,0:T(8,128)(2,1)}, bf16[144,1024]{1,0:T(8,128)(2,1)S(1)}, u32[]{:S(2)}, u32[]{:S(2)}) collective-permute-start(bf16[144,1024]{1,0:T(8,128)(2,1)} %pack_block.1.refs_0_), channel_id=1, source_target_pairs={{0,64},{16,24},{4,68},{20,28},{8,72},{24,16},{12,76},{28,20},{32,9... | collective-permute-start | bytes 884744 | tf_op jit(solution)/shard_map/ppermute | solution.py:278
  6.3 1.7 %collective-permute-start = (bf16[64,1024]{1,0:T(8,128)(2,1)}, bf16[64,1024]{1,0:T(8,128)(2,1)S(1)}, u32[]{:S(2)}, u32[]{:S(2)}) collective-permute-start(bf16[64,1024]{1,0:T(8,128)(2,1)} %own.1), channel_id=1, source_target_pairs={{0,128},{128,1},{1,129},{129,2},{2,130},{130,3},{3,131},{131,0},{4... | collective-permute-start | bytes 393224 | tf_op jit(solution)/shard_map/ppermute | solution.py:268
  8.0 3.9 %collective-permute-start.1 = (bf16[64,1024]{1,0:T(8,128)(2,1)}, bf16[64,1024]{1,0:T(8,128)(2,1)S(1)}, u32[]{:S(2)}, u32[]{:S(2)}) collective-permute-start(bf16[64,1024]{1,0:T(8,128)(2,1)} %own.1), channel_id=1, source_target_pairs={{0,131},{128,0},{1,128},{129,1},{2,129},{130,2},{3,130},{131,3},{4... | collective-permute-start | bytes 393224 | tf_op jit(solution)/shard_map/ppermute | solution.py:268
  11.9 4.5 %collective-permute-done.refs_5_.below = bf16[64,1024]{1,0:T(8,128)(2,1)S(1)} collective-permute-done((bf16[64,1024]{1,0:T(8,128)(2,1)}, bf16[64,1024]{1,0:T(8,128)(2,1)S(1)}, u32[]{:S(2)}, u32[]{:S(2)}) %collective-permute-start) | collective-permute-done | bytes 131104 | tf_op jit(solution)/shard_map/ppermute | solution.py:268
  16.4 4.5 %collective-permute-start.5 = (bf16[64,1024]{1,0:T(8,128)(2,1)}, bf16[64,1024]{1,0:T(8,128)(2,1)S(1)}, u32[]{:S(2)}, u32[]{:S(2)}) collective-permute-start(bf16[64,1024]{1,0:T(8,128)(2,1)} %own.1), channel_id=1, source_target_pairs={{0,2},{128,130},{1,3},{129,131},{2,0},{130,128},{3,1},{131,129},{4... | collective-permute-start | bytes 393224 | tf_op jit(solution)/shard_map/ppermute | solution.py:268
  20.9 8.0 %collective-permute-done.5.refs_7_ = bf16[64,1024]{1,0:T(8,128)(2,1)S(1)} collective-permute-done((bf16[64,1024]{1,0:T(8,128)(2,1)}, bf16[64,1024]{1,0:T(8,128)(2,1)S(1)}, u32[]{:S(2)}, u32[]{:S(2)}) %collective-permute-start.5) | collective-permute-done | bytes 131104 | tf_op jit(solution)/shard_map/ppermute | solution.py:268
  30.9 2.0 %collective-permute-start.9 = (bf16[528,1024]{1,0:T(8,128)(2,1)S(1)}, bf16[528,1024]{1,0:T(8,128)(2,1)S(1)}, u32[]{:S(2)}, u32[]{:S(2)}) collective-permute-start(bf16[528,1024]{1,0:T(8,128)(2,1)S(1)} %get-tuple-element.45.refs_0_), channel_id=1, source_target_pairs={{0,4},{16,48},{4,8},{20,52},{8,12},{24,56},{12,0},{28,60},{32,36},... | collective-permute-start | bytes 3244040 | tf_op jit(solution)/shard_map/ppermute | solution.py:278
  33.1 4.1 %collective-permute-start.7 = (bf16[128,1024]{1,0:T(8,128)(2,1)S(1)}, bf16[128,1024]{1,0:T(8,128)(2,1)S(1)}, u32[]{:S(2)}, u32[]{:S(2)}) collective-permute-start(bf16[128,1024]{1,0:T(8,128)(2,1)S(1)} %get-tuple-element.44), channel_id=1, source_target_pairs={{0,3},{128,131},{1,0},{129,128},{2,1},{130,129},{3,2},{131,130},{4... | collective-permute-start | bytes 786440 | tf_op jit(solution)/shard_map/ppermute | solution.py:268
  37.2 11.2 %collective-permute-done.6.pair_below = bf16[128,1024]{1,0:T(8,128)(2,1)S(1)} collective-permute-done((bf16[128,1024]{1,0:T(8,128)(2,1)S(1)}, bf16[128,1024]{1,0:T(8,128)(2,1)S(1)}, u32[]{:S(2)}, u32[]{:S(2)}) %collective-permute-start.6) | collective-permute-done | bytes 262176 | tf_op jit(solution)/shard_map/ppermute | solution.py:268
  48.4 1.5 %first_columns.1 = (bf16[512,1024]{1,0:T(8,128)(2,1)S(1)}, f32[512,128]{1,0:T(8,128)S(1)}, f32[512,1024]{1,0:T(8,128)S(1)}, f32[512,1024]{1,0:T(8,128)S(1)}, f32...) custom-call(bf16[64,1024]{1,0:T(8,128)(2,1)S(1)} %copy-done.2, bf16[64,1024]{1,0:T(8,128)(2,1)S(1)} %collective-permute-done.refs_5_.below, ...), custom_call_target="tpu_custom_call" | custom-call | flops 1073741824 | bytes 1048576 | tf_op jit(solution)/shard_map/first_columns/pallas_call | solution.py:29
  49.9 9.0 %collective-permute-done.9.refs_0_.refs_1_ = bf16[528,1024]{1,0:T(8,128)(2,1)S(1)} collective-permute-done((bf16[528,1024]{1,0:T(8,128)(2,1)S(1)}, bf16[528,1024]{1,0:T(8,128)(2,1)S(1)}, u32[]{:S(2)}, u32[]{:S(2)}) %collective-permute-start.9) | collective-permute-done | bytes 1081376 | tf_op jit(solution)/shard_map/ppermute | solution.py:278
  58.9 3.1 %more_columns.5 = (f32[512,1024]{1,0:T(8,128)S(1)}, f32[512,1024]{1,0:T(8,128)S(1)}, f32[512,128]{1,0:T(8,128)S(1)}, f32[512,128]{1,0:T(8,128)S(1)}) custom-call(bf16[512,1024]{1,0:T(8,128)(2,1)S(1)} %get-tuple-element.46.panel.refs_0_, ...), custom_call_target="tpu_custom_call", output_to_operand_aliasing={{0}: (4, {}), {1}: (5, {}), {2}: (6, {}), {3}: (7, {})} | custom-call | flops 2147483648 | bytes 1048576 | tf_op jit(solution)/shard_map/more_columns/pallas_call | solution.py:29
  62.8 1.8 %more_columns.6 = (f32[512,1024]{1,0:T(8,128)S(1)}, f32[512,1024]{1,0:T(8,128)S(1)}, f32[512,128]{1,0:T(8,128)S(1)}, f32[512,128]{1,0:T(8,128)S(1)}) custom-call(bf16[512,1024]{1,0:T(8,128)(2,1)S(1)} %get-tuple-element.46.panel.refs_0_, ...), custom_call_target="tpu_custom_call", output_to_operand_aliasing={{0}: (3, {}), {1}: (4, {}), {2}: (5, {}), {3}: (6, {})} | custom-call | flops 1073741824 | bytes 1048576 | tf_op jit(solution)/shard_map/more_columns/pallas_call | solution.py:29
  64.9 1.5 %collective-permute-done.12.refs_0_.refs_6_ = bf16[528,1024]{1,0:T(8,128)(2,1)S(1)} collective-permute-done((bf16[528,1024]{1,0:T(8,128)(2,1)S(1)}, bf16[528,1024]{1,0:T(8,128)(2,1)S(1)}, u32[]{:S(2)}, u32[]{:S(2)}) %collective-permute-start.12) | collective-permute-done | bytes 1081376 | tf_op jit(solution)/shard_map/ppermute | solution.py:286
  66.4 1.5 %collective-permute-done.14.refs_1_.refs_5_ = bf16[528,1024]{1,0:T(8,128)(2,1)S(1)} collective-permute-done((bf16[528,1024]{1,0:T(8,128)(2,1)S(1)}, bf16[528,1024]{1,0:T(8,128)(2,1)S(1)}, u32[]{:S(2)}, u32[]{:S(2)}) %collective-permute-start.14) | collective-permute-done | bytes 1081376 | tf_op jit(solution)/shard_map/ppermute | solution.py:286
  68.2 3.1 %more_columns.7 = (f32[512,1024]{1,0:T(8,128)S(1)}, f32[512,1024]{1,0:T(8,128)S(1)}, f32[512,128]{1,0:T(8,128)S(1)}, f32[512,128]{1,0:T(8,128)S(1)}) custom-call(bf16[512,1024]{1,0:T(8,128)(2,1)S(1)} %get-tuple-element.46.panel.refs_0_, ...), custom_call_target="tpu_custom_call", output_to_operand_aliasing={{0}: (4, {}), {1}: (5, {}), {2}: (6, {}), {3}: (7, {})} | custom-call | flops 2147483648 | bytes 1048576 | tf_op jit(solution)/shard_map/more_columns/pallas_call | solution.py:29
  71.8 1.5 %collective-permute-start.16 = (f32[8,128]{1,0:T(8,128)S(1)}, f32[8,128]{1,0:T(8,128)S(1)}, u32[]{:S(2)}, u32[]{:S(2)}) collective-permute-start(f32[8,128]{1,0:T(8,128)S(1)} %add.9), channel_id=1, source_target_pairs={{0,1},{128,129},{1,0},{129,128},{2,3},{130,131},{3,2},{131,130},{4... | collective-permute-start | bytes 12296 | tf_op jit(solution)/shard_map/ppermute | solution.py:348
  73.3 1.8 %more_columns.8 = (f32[512,1024]{1,0:T(8,128)S(1)}, f32[512,1024]{1,0:T(8,128)S(1)}, f32[512,128]{1,0:T(8,128)S(1)}, f32[512,128]{1,0:T(8,128)S(1)}) custom-call(bf16[512,1024]{1,0:T(8,128)(2,1)S(1)} %get-tuple-element.46.panel.refs_0_, ...), custom_call_target="tpu_custom_call", output_to_operand_aliasing={{0}: (3, {}), {1}: (4, {}), {2}: (5, {}), {3}: (6, {})} | custom-call | flops 1073741824 | bytes 1048576 | tf_op jit(solution)/shard_map/more_columns/pallas_call | solution.py:29
  75.1 1.2 %collective-permute-done.16 = f32[8,128]{1,0:T(8,128)S(1)} collective-permute-done((f32[8,128]{1,0:T(8,128)S(1)}, f32[8,128]{1,0:T(8,128)S(1)}, u32[]{:S(2)}, u32[]{:S(2)}) %collective-permute-start.16) | collective-permute-done | bytes 4128 | tf_op jit(solution)/shard_map/ppermute | solution.py:348
  76.3 3.5 %collective-permute-start.17 = (f32[8,128]{1,0:T(8,128)S(1)}, f32[8,128]{1,0:T(8,128)S(1)}, u32[]{:S(2)}, u32[]{:S(2)}) collective-permute-start(f32[8,128]{1,0:T(8,128)S(1)} %add.10), channel_id=1, source_target_pairs={{0,2},{128,130},{1,3},{129,131},{2,0},{130,128},{3,1},{131,129},{4... | collective-permute-start | bytes 12296 | tf_op jit(solution)/shard_map/ppermute | solution.py:348
  79.8 1.8 %more_columns.9 = (f32[512,1024]{1,0:T(8,128)S(1)}, f32[512,1024]{1,0:T(8,128)S(1)}, f32[512,128]{1,0:T(8,128)S(1)}, f32[512,128]{1,0:T(8,128)S(1)}) custom-call(bf16[512,1024]{1,0:T(8,128)(2,1)S(1)} %get-tuple-element.46.panel.refs_0_, ...), custom_call_target="tpu_custom_call", output_to_operand_aliasing={{0}: (3, {}), {1}: (4, {}), {2}: (5, {}), {3}: (6, {})} | custom-call | flops 1073741824 | bytes 1048576 | tf_op jit(solution)/shard_map/more_columns/pallas_call | solution.py:29
  81.6 2.2 %collective-permute-done.17 = f32[8,128]{1,0:T(8,128)S(1)} collective-permute-done((f32[8,128]{1,0:T(8,128)S(1)}, f32[8,128]{1,0:T(8,128)S(1)}, u32[]{:S(2)}, u32[]{:S(2)}) %collective-permute-start.17) | collective-permute-done | bytes 4128 | tf_op jit(solution)/shard_map/ppermute | solution.py:348
  84.8 2.0 %collective-permute-start.18 = (s16[128,1152]{1,0:T(8,128)(2,1)S(1)}, s16[128,1152]{1,0:T(8,128)(2,1)S(1)}, u32[]{:S(2)}, u32[]{:S(2)}) collective-permute-start(s16[128,1152]{1,0:T(8,128)(2,1)S(1)} %get-tuple-element.74), channel_id=1, source_target_pairs={{0,128},{128,1},{1,129},{129,2},{2,130},{130,3},{3,131},{131,0},{4... | collective-permute-start | bytes 884744 | tf_op jit(solution)/shard_map/ppermute | solution.py:268
  86.8 1.4 %collective-permute-start.19 = (s16[128,1152]{1,0:T(8,128)(2,1)S(1)}, s16[128,1152]{1,0:T(8,128)(2,1)S(1)}, u32[]{:S(2)}, u32[]{:S(2)}) collective-permute-start(s16[128,1152]{1,0:T(8,128)(2,1)S(1)} %get-tuple-element.75), channel_id=1, source_target_pairs={{0,131},{128,0},{1,128},{129,1},{2,129},{130,2},{3,130},{131,3},{4... | collective-permute-start | bytes 884744 | tf_op jit(solution)/shard_map/ppermute | solution.py:268
  88.4 3.8 %collective-permute-start.21 = (s16[32,1152]{1,0:T(8,128)(2,1)S(1)}, s16[32,1152]{1,0:T(8,128)(2,1)S(1)}, u32[]{:S(2)}, u32[]{:S(2)}) collective-permute-start(s16[32,1152]{1,0:T(8,128)(2,1)S(1)} %get-tuple-element.77), channel_id=1, source_target_pairs={{0,3},{128,131},{1,0},{129,128},{2,1},{130,129},{3,2},{131,130},{4... | collective-permute-start | bytes 221192 | tf_op jit(solution)/shard_map/ppermute | solution.py:268
  92.7 4.1 %collective-permute-done.20.half_below = s16[32,1152]{1,0:T(8,128)(2,1)S(1)} collective-permute-done((s16[32,1152]{1,0:T(8,128)(2,1)S(1)}, s16[32,1152]{1,0:T(8,128)(2,1)S(1)}, u32[]{:S(2)}, u32[]{:S(2)}) %collective-permute-start.20) | collective-permute-done | bytes 73760 | tf_op jit(solution)/shard_map/ppermute | solution.py:268
  97.3 3.4 %collective-permute-start.22 = (s16[64,1152]{1,0:T(8,128)(2,1)S(1)}, s16[64,1152]{1,0:T(8,128)(2,1)S(1)}, u32[]{:S(2)}, u32[]{:S(2)}) collective-permute-start(s16[64,1152]{1,0:T(8,128)(2,1)S(1)} %get-tuple-element.78), channel_id=1, source_target_pairs={{0,1},{128,129},{1,2},{129,130},{2,3},{130,131},{3,0},{131,128},{4... | collective-permute-start | bytes 442376 | tf_op jit(solution)/shard_map/ppermute | solution.py:268
  101.6 4.3 %collective-permute-done.22.far_below = s16[64,1152]{1,0:T(8,128)(2,1)S(1)} collective-permute-done((s16[64,1152]{1,0:T(8,128)(2,1)S(1)}, s16[64,1152]{1,0:T(8,128)(2,1)S(1)}, u32[]{:S(2)}, u32[]{:S(2)}) %collective-permute-start.22) | collective-permute-done | bytes 147488 | tf_op jit(solution)/shard_map/ppermute | solution.py:268
  105.9 2.1 %collective-permute-done.23.far_above = s16[64,1152]{1,0:T(8,128)(2,1)S(1)} collective-permute-done((s16[64,1152]{1,0:T(8,128)(2,1)S(1)}, s16[64,1152]{1,0:T(8,128)(2,1)S(1)}, u32[]{:S(2)}, u32[]{:S(2)}) %collective-permute-start.23) | collective-permute-done | bytes 147488 | tf_op jit(solution)/shard_map/ppermute | solution.py:268
  108.0 1.1 add_up.1
  (39 shorter events, 6.9 us)
Async XLA Ops:
  0.6 47.7 %copy-start.2 = (bf16[64,1024]{1,0:T(8,128)(2,1)S(1)}, bf16[64,1024]{1,0:T(8,128)(2,1)}, u32[]{:S(2)}) copy-start(bf16[64,1024]{1,0:T(8,128)(2,1)} %own.1) | copy-start | bytes 393220
  2.6 26.2 %collective-permute-start.2 = (bf16[144,1024]{1,0:T(8,128)(2,1)}, bf16[144,1024]{1,0:T(8,128)(2,1)S(1)}, u32[]{:S(2)}, u32[]{:S(2)}) collective-permute-start(bf16[144,1024]{1,0:T(8,128)(2,1)} %pack_block.1.refs_0_), channel_id=1, source_target_pairs={{0,32},{16,20},{4,36},{20,24},{8,40},{24,28},{12,44},{28,16},{32,6... | collective-permute-start | bytes 884744 | tf_op jit(solution)/shard_map/ppermute | solution.py:278
  4.8 24.0 %collective-permute-start.3 = (bf16[144,1024]{1,0:T(8,128)(2,1)}, bf16[144,1024]{1,0:T(8,128)(2,1)S(1)}, u32[]{:S(2)}, u32[]{:S(2)}) collective-permute-start(bf16[144,1024]{1,0:T(8,128)(2,1)} %pack_block.1.refs_0_), channel_id=1, source_target_pairs={{0,96},{16,28},{4,100},{20,16},{8,104},{24,20},{12,108},{28,24},{3... | collective-permute-start | bytes 884744 | tf_op jit(solution)/shard_map/ppermute | solution.py:278
  4.8 24.0 %collective-permute-start.4 = (bf16[144,1024]{1,0:T(8,128)(2,1)}, bf16[144,1024]{1,0:T(8,128)(2,1)S(1)}, u32[]{:S(2)}, u32[]{:S(2)}) collective-permute-start(bf16[144,1024]{1,0:T(8,128)(2,1)} %pack_block.1.refs_0_), channel_id=1, source_target_pairs={{0,64},{16,24},{4,68},{20,28},{8,72},{24,16},{12,76},{28,20},{32,9... | collective-permute-start | bytes 884744 | tf_op jit(solution)/shard_map/ppermute | solution.py:278
  6.3 10.1 %collective-permute-start = (bf16[64,1024]{1,0:T(8,128)(2,1)}, bf16[64,1024]{1,0:T(8,128)(2,1)S(1)}, u32[]{:S(2)}, u32[]{:S(2)}) collective-permute-start(bf16[64,1024]{1,0:T(8,128)(2,1)} %own.1), channel_id=1, source_target_pairs={{0,128},{128,1},{1,129},{129,2},{2,130},{130,3},{3,131},{131,0},{4... | collective-permute-start | bytes 393224 | tf_op jit(solution)/shard_map/ppermute | solution.py:268
  8.0 12.9 %collective-permute-start.1 = (bf16[64,1024]{1,0:T(8,128)(2,1)}, bf16[64,1024]{1,0:T(8,128)(2,1)S(1)}, u32[]{:S(2)}, u32[]{:S(2)}) collective-permute-start(bf16[64,1024]{1,0:T(8,128)(2,1)} %own.1), channel_id=1, source_target_pairs={{0,131},{128,0},{1,128},{129,1},{2,129},{130,2},{3,130},{131,3},{4... | collective-permute-start | bytes 393224 | tf_op jit(solution)/shard_map/ppermute | solution.py:268
  16.4 12.4 %collective-permute-start.5 = (bf16[64,1024]{1,0:T(8,128)(2,1)}, bf16[64,1024]{1,0:T(8,128)(2,1)S(1)}, u32[]{:S(2)}, u32[]{:S(2)}) collective-permute-start(bf16[64,1024]{1,0:T(8,128)(2,1)} %own.1), channel_id=1, source_target_pairs={{0,2},{128,130},{1,3},{129,131},{2,0},{130,128},{3,1},{131,129},{4... | collective-permute-start | bytes 393224 | tf_op jit(solution)/shard_map/ppermute | solution.py:268
  28.8 1.0 copy-start
  29.8 0.9 copy-start.1
  30.8 19.1 %collective-permute-start.10 = (bf16[528,1024]{1,0:T(8,128)(2,1)S(1)}, bf16[528,1024]{1,0:T(8,128)(2,1)S(1)}, u32[]{:S(2)}, u32[]{:S(2)}) collective-permute-start(bf16[528,1024]{1,0:T(8,128)(2,1)S(1)} %get-tuple-element.45.refs_0_), channel_id=1, source_target_pairs={{0,12},{16,112},{4,0},{20,116},{8,4},{24,120},{12,8},{28,124},{32,... | collective-permute-start | bytes 3244040 | tf_op jit(solution)/shard_map/ppermute | solution.py:278
  30.9 28.0 %collective-permute-start.9 = (bf16[528,1024]{1,0:T(8,128)(2,1)S(1)}, bf16[528,1024]{1,0:T(8,128)(2,1)S(1)}, u32[]{:S(2)}, u32[]{:S(2)}) collective-permute-start(bf16[528,1024]{1,0:T(8,128)(2,1)S(1)} %get-tuple-element.45.refs_0_), channel_id=1, source_target_pairs={{0,4},{16,48},{4,8},{20,52},{8,12},{24,56},{12,0},{28,60},{32,36},... | collective-permute-start | bytes 3244040 | tf_op jit(solution)/shard_map/ppermute | solution.py:278
  32.9 29.2 %collective-permute-start.8 = (bf16[528,1024]{1,0:T(8,128)(2,1)S(1)}, bf16[528,1024]{1,0:T(8,128)(2,1)S(1)}, u32[]{:S(2)}, u32[]{:S(2)}) collective-permute-start(bf16[528,1024]{1,0:T(8,128)(2,1)S(1)} %get-tuple-element.45.refs_0_), channel_id=1, source_target_pairs={{0,8},{16,80},{4,12},{20,84},{8,0},{24,88},{12,4},{28,92},{32,40},... | collective-permute-start | bytes 3244040 | tf_op jit(solution)/shard_map/ppermute | solution.py:278
  33.1 15.3 %collective-permute-start.6 = (bf16[128,1024]{1,0:T(8,128)(2,1)S(1)}, bf16[128,1024]{1,0:T(8,128)(2,1)S(1)}, u32[]{:S(2)}, u32[]{:S(2)}) collective-permute-start(bf16[128,1024]{1,0:T(8,128)(2,1)S(1)} %get-tuple-element.43), channel_id=1, source_target_pairs={{0,1},{128,129},{1,2},{129,130},{2,3},{130,131},{3,0},{131,128},{4... | collective-permute-start | bytes 786440 | tf_op jit(solution)/shard_map/ppermute | solution.py:268
  33.1 15.3 %collective-permute-start.7 = (bf16[128,1024]{1,0:T(8,128)(2,1)S(1)}, bf16[128,1024]{1,0:T(8,128)(2,1)S(1)}, u32[]{:S(2)}, u32[]{:S(2)}) collective-permute-start(bf16[128,1024]{1,0:T(8,128)(2,1)S(1)} %get-tuple-element.44), channel_id=1, source_target_pairs={{0,3},{128,131},{1,0},{129,128},{2,1},{130,129},{3,2},{131,130},{4... | collective-permute-start | bytes 786440 | tf_op jit(solution)/shard_map/ppermute | solution.py:268
  48.4 16.3 %collective-permute-start.13 = (bf16[528,1024]{1,0:T(8,128)(2,1)S(1)}, bf16[528,1024]{1,0:T(8,128)(2,1)S(1)}, u32[]{:S(2)}, u32[]{:S(2)}) collective-permute-start(bf16[528,1024]{1,0:T(8,128)(2,1)S(1)} %get-tuple-element.45.refs_0_), channel_id=1, source_target_pairs={{0,16},{16,0},{1,17},{17,1},{2,18},{18,2},{3,19},{19,3},{4,20},{20... | collective-permute-start | bytes 3244040 | tf_op jit(solution)/shard_map/ppermute | solution.py:286
  62.1 2.8 %collective-permute-start.11 = (bf16[528,1024]{1,0:T(8,128)(2,1)S(1)}, bf16[528,1024]{1,0:T(8,128)(2,1)S(1)}, u32[]{:S(2)}, u32[]{:S(2)}) collective-permute-start(bf16[528,1024]{1,0:T(8,128)(2,1)S(1)} %handed_on.1.refs_0_.refs_3_), channel_id=1, source_target_pairs={{0,16},{16,0},{1,17},{17,1},{2,18},{18,2},{3,19},{19,3},{4,20},{20... | collective-permute-start | bytes 3244040 | tf_op jit(solution)/shard_map/ppermute | solution.py:286
  62.2 4.2 %collective-permute-start.12 = (bf16[528,1024]{1,0:T(8,128)(2,1)S(1)}, bf16[528,1024]{1,0:T(8,128)(2,1)S(1)}, u32[]{:S(2)}, u32[]{:S(2)}) collective-permute-start(bf16[528,1024]{1,0:T(8,128)(2,1)S(1)} %collective-permute-done.10.refs_1_.refs_2_), channel_id=1, source_target_pairs={{0,16},{16,0},{1,17},{17,1},{2,18},{18,2},{3,19},{19,3},{4,20},{20... | collective-permute-start | bytes 3244040 | tf_op jit(solution)/shard_map/ppermute | solution.py:286
  62.7 5.3 %collective-permute-start.14 = (bf16[528,1024]{1,0:T(8,128)(2,1)S(1)}, bf16[528,1024]{1,0:T(8,128)(2,1)S(1)}, u32[]{:S(2)}, u32[]{:S(2)}) collective-permute-start(bf16[528,1024]{1,0:T(8,128)(2,1)S(1)} %collective-permute-done.9.refs_0_.refs_1_), channel_id=1, source_target_pairs={{0,16},{16,0},{1,17},{17,1},{2,18},{18,2},{3,19},{19,3},{4,20},{20... | collective-permute-start | bytes 3244040 | tf_op jit(solution)/shard_map/ppermute | solution.py:286
  68.1 3.7 %collective-permute-start.15 = (f32[8,128]{1,0:T(8,128)S(1)}, f32[8,128]{1,0:T(8,128)S(1)}, u32[]{:S(2)}, u32[]{:S(2)}) collective-permute-start(f32[8,128]{1,0:T(8,128)S(1)} %count_chosen.1), channel_id=1, source_target_pairs={{0,128},{128,0},{1,129},{129,1},{2,130},{130,2},{3,131},{131,3},{4... | collective-permute-start | bytes 12296 | tf_op jit(solution)/shard_map/ppermute | solution.py:348
  71.8 4.5 %collective-permute-start.16 = (f32[8,128]{1,0:T(8,128)S(1)}, f32[8,128]{1,0:T(8,128)S(1)}, u32[]{:S(2)}, u32[]{:S(2)}) collective-permute-start(f32[8,128]{1,0:T(8,128)S(1)} %add.9), channel_id=1, source_target_pairs={{0,1},{128,129},{1,0},{129,128},{2,3},{130,131},{3,2},{131,130},{4... | collective-permute-start | bytes 12296 | tf_op jit(solution)/shard_map/ppermute | solution.py:348
  76.3 7.5 %collective-permute-start.17 = (f32[8,128]{1,0:T(8,128)S(1)}, f32[8,128]{1,0:T(8,128)S(1)}, u32[]{:S(2)}, u32[]{:S(2)}) collective-permute-start(f32[8,128]{1,0:T(8,128)S(1)} %add.10), channel_id=1, source_target_pairs={{0,2},{128,130},{1,3},{129,131},{2,0},{130,128},{3,1},{131,129},{4... | collective-permute-start | bytes 12296 | tf_op jit(solution)/shard_map/ppermute | solution.py:348
  84.8 12.0 %collective-permute-start.18 = (s16[128,1152]{1,0:T(8,128)(2,1)S(1)}, s16[128,1152]{1,0:T(8,128)(2,1)S(1)}, u32[]{:S(2)}, u32[]{:S(2)}) collective-permute-start(s16[128,1152]{1,0:T(8,128)(2,1)S(1)} %get-tuple-element.74), channel_id=1, source_target_pairs={{0,128},{128,1},{1,129},{129,2},{2,130},{130,3},{3,131},{131,0},{4... | collective-permute-start | bytes 884744 | tf_op jit(solution)/shard_map/ppermute | solution.py:268
  86.8 10.0 %collective-permute-start.19 = (s16[128,1152]{1,0:T(8,128)(2,1)S(1)}, s16[128,1152]{1,0:T(8,128)(2,1)S(1)}, u32[]{:S(2)}, u32[]{:S(2)}) collective-permute-start(s16[128,1152]{1,0:T(8,128)(2,1)S(1)} %get-tuple-element.75), channel_id=1, source_target_pairs={{0,131},{128,0},{1,128},{129,1},{2,129},{130,2},{3,130},{131,3},{4... | collective-permute-start | bytes 884744 | tf_op jit(solution)/shard_map/ppermute | solution.py:268
  88.1 8.6 %collective-permute-start.20 = (s16[32,1152]{1,0:T(8,128)(2,1)S(1)}, s16[32,1152]{1,0:T(8,128)(2,1)S(1)}, u32[]{:S(2)}, u32[]{:S(2)}) collective-permute-start(s16[32,1152]{1,0:T(8,128)(2,1)S(1)} %get-tuple-element.76), channel_id=1, source_target_pairs={{0,1},{128,129},{1,2},{129,130},{2,3},{130,131},{3,0},{131,128},{4... | collective-permute-start | bytes 221192 | tf_op jit(solution)/shard_map/ppermute | solution.py:268
  88.4 8.3 %collective-permute-start.21 = (s16[32,1152]{1,0:T(8,128)(2,1)S(1)}, s16[32,1152]{1,0:T(8,128)(2,1)S(1)}, u32[]{:S(2)}, u32[]{:S(2)}) collective-permute-start(s16[32,1152]{1,0:T(8,128)(2,1)S(1)} %get-tuple-element.77), channel_id=1, source_target_pairs={{0,3},{128,131},{1,0},{129,128},{2,1},{130,129},{3,2},{131,130},{4... | collective-permute-start | bytes 221192 | tf_op jit(solution)/shard_map/ppermute | solution.py:268
  97.3 8.6 %collective-permute-start.22 = (s16[64,1152]{1,0:T(8,128)(2,1)S(1)}, s16[64,1152]{1,0:T(8,128)(2,1)S(1)}, u32[]{:S(2)}, u32[]{:S(2)}) collective-permute-start(s16[64,1152]{1,0:T(8,128)(2,1)S(1)} %get-tuple-element.78), channel_id=1, source_target_pairs={{0,1},{128,129},{1,2},{129,130},{2,3},{130,131},{3,0},{131,128},{4... | collective-permute-start | bytes 442376 | tf_op jit(solution)/shard_map/ppermute | solution.py:268
  100.7 7.3 %collective-permute-start.23 = (s16[64,1152]{1,0:T(8,128)(2,1)S(1)}, s16[64,1152]{1,0:T(8,128)(2,1)S(1)}, u32[]{:S(2)}, u32[]{:S(2)}) collective-permute-start(s16[64,1152]{1,0:T(8,128)(2,1)S(1)} %get-tuple-element.79), channel_id=1, source_target_pairs={{0,3},{128,131},{1,0},{129,128},{2,1},{130,129},{3,2},{131,130},{4... | collective-permute-start | bytes 442376 | tf_op jit(solution)/shard_map/ppermute | solution.py:268

commit v5 on v4

--- a/solution.py
+++ b/solution.py
@@ -77,10 +77,10 @@
 
 
 def pack_line(*refs):
-    blocks, (own, below, above, opposite, piece, up_pair, down_pair, across) = refs[:-8], refs[-8:]
-    across[...] = opposite[...]
-    up_pair[...] = jnp.concatenate([own[...], below[...]], axis=0)
-    down_pair[...] = jnp.concatenate([own[...], above[...]], axis=0)
+    blocks, (own, below, above, piece, up_pair, down_pair) = refs[:-6], refs[-6:]
+    half = own.shape[0] // 2
+    up_pair[...] = jnp.concatenate([own[...], above[...], below[:half, :]], axis=0)
+    down_pair[...] = jnp.concatenate([own[...], below[...], above[half:, :]], axis=0)
     count, height = len(blocks), (blocks[0].shape[0] - META) // 2
     for j, block in enumerate(blocks):
         piece[j * height : (j + 1) * height, :] = block[:height, :]
@@ -132,18 +132,23 @@
             pulls[half][part, :] = total
 
 
-def first_columns(rows, lines, own, below, above, opposite, pair_below, pair_above, *refs):
+def first_columns(rows, lines, own, below, above, far_below, far_above, *refs):
     pieces, refs = refs[:lines], refs[lines:]
     ordered, norms, pp, tp, pm, tm, *weights = refs
     height = own.shape[0]
-    found = {0: own, 1: above, 7: below, 4: opposite}
+    found = {
+        0: own[...],
+        1: above[...],
+        7: below[...],
+        3: far_above[:height, :],
+        2: far_above[height : 2 * height, :],
+        5: far_below[:height, :],
+        6: far_below[height : 2 * height, :],
+        4: jnp.concatenate([far_below[2 * height :, :], far_above[2 * height :, :]], axis=0),
+    }
     for i, offset in enumerate(OFFSETS):
         part = slice(i * height, (i + 1) * height)
-        if offset in found:
-            block = found[offset][...]
-        else:
-            pair, at = (pair_above, offset - 2) if offset < 4 else (pair_below, 6 - offset)
-            block = pair[at * height : (at + 1) * height, :]
+        block = found[offset]
         ordered[part, :] = block
         norms[part, :] = jnp.broadcast_to(square_norms(block), (height, LANES))
     add_columns(ordered, norms, pieces, (), (pp, tp), (pm, tm), weights, rows)
@@ -250,17 +255,17 @@
     return z % 2 * 4 + z // 2
 
 
-def handed_on(array, awaited):
+def handed_on(arrays, *awaited):
     there = pl.BlockSpec(memory_space=pl.ANY)
     return pl.pallas_call(
         lambda *refs: None,
-        out_shape=shape(array.shape, array.dtype),
-        in_specs=[there, pl.BlockSpec(memory_space=pltpu.VMEM)],
-        out_specs=there,
-        input_output_aliases={0: 0},
+        out_shape=[shape(a.shape, a.dtype) for a in arrays],
+        in_specs=[there] * (len(arrays) + len(awaited)),
+        out_specs=[there] * len(arrays),
+        input_output_aliases={i: i for i in range(len(arrays))},
         compiler_params=pltpu.CompilerParams(vmem_limit_bytes=4 << 20),
         name="handed_on",
-    )(array, awaited)
+    )(*arrays, *awaited)
 
 
 def up_the_ring(x, step):
@@ -296,16 +301,14 @@
         pool, targets, counts.reshape(1, height)
     )
     blocks = line(block, 0)
-    below, above, opposite = (up_the_ring(pool, step) for step in (1, ring - 1, ring // 2))
-    pair = shape((2 * height, width), BF16)
-    piece, up_pair, down_pair, opposite = in_vmem(
-        pack_line,
-        "pack_line",
-        (shape((2 * height * len(blocks) + META, width), BF16), pair, pair, shape(pool.shape, BF16)),
-    )(*blocks, pool, below, above, opposite)
+    below, above = up_the_ring(pool, 1), up_the_ring(pool, ring - 1)
+    pair = shape((5 * height // 2, width), BF16)
+    piece, up_pair, down_pair = in_vmem(
+        pack_line, "pack_line", (shape((2 * height * len(blocks) + META, width), BF16), pair, pair)
+    )(*blocks, pool, below, above)
     pieces = line(piece, 1)
-    pairs = up_the_ring(up_pair, 2), up_the_ring(down_pair, ring - 2)
-    others = [other_core(p) for p in pieces[:3]]
+    pairs = up_the_ring(up_pair, 3), up_the_ring(down_pair, ring - 3)
+    others = [other_core(piece)]
 
     size = height * len(blocks)
     sums = (shape((rows, width), F32),) * 2 + (shape((rows, LANES), F32),) * 2
@@ -326,14 +329,16 @@
 
     panel, norms, *state = add(
         first_columns,
-        (pool, below, above, opposite, *pairs),
+        (pool, below, above, *pairs),
         pieces[:1],
         (),
         (shape((rows, width), BF16), shape((rows, LANES), F32), *sums),
         {},
     )
+    pieces[1:3] = handed_on(pieces[1:3], norms)
+    others += [other_core(p) for p in pieces[1:3]]
     state = more(pieces[1:3], state)
-    pieces[3] = handed_on(pieces[3], state[2])
+    pieces[3:] = handed_on(pieces[3:], state[2], *others[1:3])
     others.append(other_core(pieces[3]))
     total = pl.pallas_call(
         count_chosen,

time: 109 us -> 99.4 us (0.912)
  the two profiles are of different devices: /device:TPU:6 before, /device:TPU:8 now
where the time goes in v5:
time: 99.4 us; the launch traced here: 99.3 us
  starting transfers between devices  41.8 us (42%)
  waiting for transfers between devices  36.4 us (37%)
  Pallas kernels  18.4 us (19%)
  local copies, waits for them, and re-layouts  1.86 us (2%)
    ppermute x10, waiting for transfers between devices, up_the_ring(): lax.ppermute(x, RING, [(place(i), place((i + step) % ring)) for i in rang...  29.3 us
    ppermute x10, starting transfers between devices, up_the_ring(): lax.ppermute(x, RING, [(place(i), place((i + step) % ring)) for i in rang...  22.6 us
    pallas_call x12, Pallas kernels, call(): pl.pallas_call(body, out_shape=out_shape, in_specs=[spec] * len(args), ou...  18.2 us
    ppermute x6, starting transfers between devices, along_line(): return lax.ppermute(x, PLANE, pairs)  9.45 us
    ppermute x3, starting transfers between devices, on_device(): lax.ppermute(total, RING, [(place(i), place(i ^ bit)) for i in range(ring)])  8.89 us
    ppermute x3, waiting for transfers between devices, on_device(): lax.ppermute(total, RING, [(place(i), place(i ^ bit)) for i in range(ring)])  5.46 us
  transfers between devices with their start and end apart: 23, of which 11 were waited for; matrix products, arithmetic and copies ran while one was open for 0% of the time, Pallas kernels for 14%

profile of v5, /device:TPU:8, one launch (start us, length us, event | category | flops | bytes accessed | tf_op | source)
XLA Modules:
  0.0 99.3 jit_solution(12543407645583060213)
XLA Ops:
  0.6 2.0 %pack_block.1.refs_0_ = bf16[144,1024]{1,0:T(8,128)(2,1)} custom-call(bf16[64,1024]{1,0:T(8,128)(2,1)} %own.1, bf16[64,1024]{1,0:T(8,128)(2,1)} %targets.1, s32[1,64]{1,0:T(1,128)} %bitcast.2), custom_call_target="tpu_custom_call" | custom-call | bytes 1048576 | tf_op jit(solution)/shard_map/pack_block/pallas_call | solution.py:29
  2.6 1.5 %collective-permute-start.2 = (bf16[144,1024]{1,0:T(8,128)(2,1)}, bf16[144,1024]{1,0:T(8,128)(2,1)S(1)}, u32[]{:S(2)}, u32[]{:S(2)}) collective-permute-start(bf16[144,1024]{1,0:T(8,128)(2,1)} %pack_block.1.refs_0_), channel_id=1, source_target_pairs={{0,32},{16,20},{4,36},{20,24},{8,40},{24,28},{12,44},{28,16},{32,6... | collective-permute-start | bytes 884744 | tf_op jit(solution)/shard_map/ppermute | solution.py:283
  4.1 1.7 %collective-permute-start.3 = (bf16[144,1024]{1,0:T(8,128)(2,1)}, bf16[144,1024]{1,0:T(8,128)(2,1)S(1)}, u32[]{:S(2)}, u32[]{:S(2)}) collective-permute-start(bf16[144,1024]{1,0:T(8,128)(2,1)} %pack_block.1.refs_0_), channel_id=1, source_target_pairs={{0,96},{16,28},{4,100},{20,16},{8,104},{24,20},{12,108},{28,24},{3... | collective-permute-start | bytes 884744 | tf_op jit(solution)/shard_map/ppermute | solution.py:283
  5.9 1.8 %collective-permute-start.4 = (bf16[144,1024]{1,0:T(8,128)(2,1)}, bf16[144,1024]{1,0:T(8,128)(2,1)S(1)}, u32[]{:S(2)}, u32[]{:S(2)}) collective-permute-start(bf16[144,1024]{1,0:T(8,128)(2,1)} %pack_block.1.refs_0_), channel_id=1, source_target_pairs={{0,64},{16,24},{4,68},{20,28},{8,72},{24,16},{12,76},{28,20},{32,9... | collective-permute-start | bytes 884744 | tf_op jit(solution)/shard_map/ppermute | solution.py:283
  7.7 1.9 %collective-permute-start = (bf16[64,1024]{1,0:T(8,128)(2,1)}, bf16[64,1024]{1,0:T(8,128)(2,1)S(1)}, u32[]{:S(2)}, u32[]{:S(2)}) collective-permute-start(bf16[64,1024]{1,0:T(8,128)(2,1)} %own.1), channel_id=1, source_target_pairs={{0,128},{128,1},{1,129},{129,2},{2,130},{130,3},{3,131},{131,0},{4... | collective-permute-start | bytes 393224 | tf_op jit(solution)/shard_map/ppermute | solution.py:273
  9.6 3.9 %collective-permute-start.1 = (bf16[64,1024]{1,0:T(8,128)(2,1)}, bf16[64,1024]{1,0:T(8,128)(2,1)S(1)}, u32[]{:S(2)}, u32[]{:S(2)}) collective-permute-start(bf16[64,1024]{1,0:T(8,128)(2,1)} %own.1), channel_id=1, source_target_pairs={{0,131},{128,0},{1,128},{129,1},{2,129},{130,2},{3,130},{131,3},{4... | collective-permute-start | bytes 393224 | tf_op jit(solution)/shard_map/ppermute | solution.py:273
  13.5 3.2 %collective-permute-done.refs_5_.below = bf16[64,1024]{1,0:T(8,128)(2,1)S(1)} collective-permute-done((bf16[64,1024]{1,0:T(8,128)(2,1)}, bf16[64,1024]{1,0:T(8,128)(2,1)S(1)}, u32[]{:S(2)}, u32[]{:S(2)}) %collective-permute-start) | collective-permute-done | bytes 131104 | tf_op jit(solution)/shard_map/ppermute | solution.py:273
  16.7 1.0 copy-done
  18.7 1.7 %collective-permute-start.8 = (bf16[528,1024]{1,0:T(8,128)(2,1)S(1)}, bf16[528,1024]{1,0:T(8,128)(2,1)S(1)}, u32[]{:S(2)}, u32[]{:S(2)}) collective-permute-start(bf16[528,1024]{1,0:T(8,128)(2,1)S(1)} %get-tuple-element.45.refs_0_), channel_id=1, source_target_pairs={{0,4},{16,48},{4,8},{20,52},{8,12},{24,56},{12,0},{28,60},{32,36},... | collective-permute-start | bytes 3244040 | tf_op jit(solution)/shard_map/ppermute | solution.py:283
  20.8 5.1 %collective-permute-start.5 = (bf16[160,1024]{1,0:T(8,128)(2,1)S(1)}, bf16[160,1024]{1,0:T(8,128)(2,1)S(1)}, u32[]{:S(2)}, u32[]{:S(2)}) collective-permute-start(bf16[160,1024]{1,0:T(8,128)(2,1)S(1)} %get-tuple-element.43), channel_id=1, source_target_pairs={{0,129},{128,2},{1,130},{129,3},{2,131},{130,0},{3,128},{131,1},{4... | collective-permute-start | bytes 983048 | tf_op jit(solution)/shard_map/ppermute | solution.py:273
  25.9 2.3 %collective-permute-start.7 = (bf16[528,1024]{1,0:T(8,128)(2,1)S(1)}, bf16[528,1024]{1,0:T(8,128)(2,1)S(1)}, u32[]{:S(2)}, u32[]{:S(2)}) collective-permute-start(bf16[528,1024]{1,0:T(8,128)(2,1)S(1)} %get-tuple-element.45.refs_0_), channel_id=1, source_target_pairs={{0,8},{16,80},{4,12},{20,84},{8,0},{24,88},{12,4},{28,92},{32,40},... | collective-permute-start | bytes 3244040 | tf_op jit(solution)/shard_map/ppermute | solution.py:283
  28.2 15.6 %collective-permute-done.5.far_below = bf16[160,1024]{1,0:T(8,128)(2,1)S(1)} collective-permute-done((bf16[160,1024]{1,0:T(8,128)(2,1)S(1)}, bf16[160,1024]{1,0:T(8,128)(2,1)S(1)}, u32[]{:S(2)}, u32[]{:S(2)}) %collective-permute-start.5) | collective-permute-done | bytes 327712 | tf_op jit(solution)/shard_map/ppermute | solution.py:273
  43.8 1.9 %collective-permute-done.6.far_above = bf16[160,1024]{1,0:T(8,128)(2,1)S(1)} collective-permute-done((bf16[160,1024]{1,0:T(8,128)(2,1)S(1)}, bf16[160,1024]{1,0:T(8,128)(2,1)S(1)}, u32[]{:S(2)}, u32[]{:S(2)}) %collective-permute-start.6) | collective-permute-done | bytes 327712 | tf_op jit(solution)/shard_map/ppermute | solution.py:273
  45.7 1.5 %first_columns.1 = (bf16[512,1024]{1,0:T(8,128)(2,1)S(1)}, f32[512,128]{1,0:T(8,128)S(1)}, f32[512,1024]{1,0:T(8,128)S(1)}, f32[512,1024]{1,0:T(8,128)S(1)}, f32...) custom-call(bf16[64,1024]{1,0:T(8,128)(2,1)S(1)} %copy-done.2, bf16[64,1024]{1,0:T(8,128)(2,1)S(1)} %collective-permute-done.refs_5_.below, ...), custom_call_target="tpu_custom_call" | custom-call | flops 1073741824 | bytes 1048576 | tf_op jit(solution)/shard_map/first_columns/pallas_call | solution.py:29
  47.9 3.1 %more_columns.5 = (f32[512,1024]{1,0:T(8,128)S(1)}, f32[512,1024]{1,0:T(8,128)S(1)}, f32[512,128]{1,0:T(8,128)S(1)}, f32[512,128]{1,0:T(8,128)S(1)}) custom-call(bf16[512,1024]{1,0:T(8,128)(2,1)S(1)} %get-tuple-element.46.panel.refs_0_, ...), custom_call_target="tpu_custom_call", output_to_operand_aliasing={{0}: (4, {}), {1}: (5, {}), {2}: (6, {}), {3}: (7, {})} | custom-call | flops 2147483648 | bytes 1048576 | tf_op jit(solution)/shard_map/more_columns/pallas_call | solution.py:29
  51.7 1.8 %more_columns.6 = (f32[512,1024]{1,0:T(8,128)S(1)}, f32[512,1024]{1,0:T(8,128)S(1)}, f32[512,128]{1,0:T(8,128)S(1)}, f32[512,128]{1,0:T(8,128)S(1)}) custom-call(bf16[512,1024]{1,0:T(8,128)(2,1)S(1)} %get-tuple-element.46.panel.refs_0_, ...), custom_call_target="tpu_custom_call", output_to_operand_aliasing={{0}: (3, {}), {1}: (4, {}), {2}: (5, {}), {3}: (6, {})} | custom-call | flops 1073741824 | bytes 1048576 | tf_op jit(solution)/shard_map/more_columns/pallas_call | solution.py:29
  53.5 1.1 %collective-permute-done.12.refs_0_.refs_7_ = bf16[528,1024]{1,0:T(8,128)(2,1)S(1)} collective-permute-done((bf16[528,1024]{1,0:T(8,128)(2,1)S(1)}, bf16[528,1024]{1,0:T(8,128)(2,1)S(1)}, u32[]{:S(2)}, u32[]{:S(2)}) %collective-permute-start.12) | collective-permute-done | bytes 1081376 | tf_op jit(solution)/shard_map/ppermute | solution.py:291
  54.8 5.8 %collective-permute-start.14 = (f32[8,128]{1,0:T(8,128)S(1)}, f32[8,128]{1,0:T(8,128)S(1)}, u32[]{:S(2)}, u32[]{:S(2)}) collective-permute-start(f32[8,128]{1,0:T(8,128)S(1)} %count_chosen.1), channel_id=1, source_target_pairs={{0,128},{128,0},{1,129},{129,1},{2,130},{130,2},{3,131},{131,3},{4... | collective-permute-start | bytes 12296 | tf_op jit(solution)/shard_map/ppermute | solution.py:353
  60.6 3.1 %more_columns.7 = (f32[512,1024]{1,0:T(8,128)S(1)}, f32[512,1024]{1,0:T(8,128)S(1)}, f32[512,128]{1,0:T(8,128)S(1)}, f32[512,128]{1,0:T(8,128)S(1)}) custom-call(bf16[512,1024]{1,0:T(8,128)(2,1)S(1)} %get-tuple-element.46.panel.refs_0_, ...), custom_call_target="tpu_custom_call", output_to_operand_aliasing={{0}: (4, {}), {1}: (5, {}), {2}: (6, {}), {3}: (7, {})} | custom-call | flops 2147483648 | bytes 1048576 | tf_op jit(solution)/shard_map/more_columns/pallas_call | solution.py:29
  63.8 2.2 %collective-permute-start.15 = (f32[8,128]{1,0:T(8,128)S(1)}, f32[8,128]{1,0:T(8,128)S(1)}, u32[]{:S(2)}, u32[]{:S(2)}) collective-permute-start(f32[8,128]{1,0:T(8,128)S(1)} %add.9), channel_id=1, source_target_pairs={{0,1},{128,129},{1,0},{129,128},{2,3},{130,131},{3,2},{131,130},{4... | collective-permute-start | bytes 12296 | tf_op jit(solution)/shard_map/ppermute | solution.py:353
  66.0 1.8 %more_columns.8 = (f32[512,1024]{1,0:T(8,128)S(1)}, f32[512,1024]{1,0:T(8,128)S(1)}, f32[512,128]{1,0:T(8,128)S(1)}, f32[512,128]{1,0:T(8,128)S(1)}) custom-call(bf16[512,1024]{1,0:T(8,128)(2,1)S(1)} %get-tuple-element.46.panel.refs_0_, ...), custom_call_target="tpu_custom_call", output_to_operand_aliasing={{0}: (3, {}), {1}: (4, {}), {2}: (5, {}), {3}: (6, {})} | custom-call | flops 1073741824 | bytes 1048576 | tf_op jit(solution)/shard_map/more_columns/pallas_call | solution.py:29
  69.2 1.8 %more_columns.9 = (f32[512,1024]{1,0:T(8,128)S(1)}, f32[512,1024]{1,0:T(8,128)S(1)}, f32[512,128]{1,0:T(8,128)S(1)}, f32[512,128]{1,0:T(8,128)S(1)}) custom-call(bf16[512,1024]{1,0:T(8,128)(2,1)S(1)} %get-tuple-element.46.panel.refs_0_, ...), custom_call_target="tpu_custom_call", output_to_operand_aliasing={{0}: (3, {}), {1}: (4, {}), {2}: (5, {}), {3}: (6, {})} | custom-call | flops 1073741824 | bytes 1048576 | tf_op jit(solution)/shard_map/more_columns/pallas_call | solution.py:29
  71.0 4.9 %collective-permute-done.16 = f32[8,128]{1,0:T(8,128)S(1)} collective-permute-done((f32[8,128]{1,0:T(8,128)S(1)}, f32[8,128]{1,0:T(8,128)S(1)}, u32[]{:S(2)}, u32[]{:S(2)}) %collective-permute-start.16) | collective-permute-done | bytes 4128 | tf_op jit(solution)/shard_map/ppermute | solution.py:353
  75.9 1.0 far_terms.1
  77.3 2.9 %collective-permute-start.18 = (s16[128,1152]{1,0:T(8,128)(2,1)S(1)}, s16[128,1152]{1,0:T(8,128)(2,1)S(1)}, u32[]{:S(2)}, u32[]{:S(2)}) collective-permute-start(s16[128,1152]{1,0:T(8,128)(2,1)S(1)} %get-tuple-element.77), channel_id=1, source_target_pairs={{0,131},{128,0},{1,128},{129,1},{2,129},{130,2},{3,130},{131,3},{4... | collective-permute-start | bytes 884744 | tf_op jit(solution)/shard_map/ppermute | solution.py:273
  81.1 3.2 %collective-permute-start.20 = (s16[32,1152]{1,0:T(8,128)(2,1)S(1)}, s16[32,1152]{1,0:T(8,128)(2,1)S(1)}, u32[]{:S(2)}, u32[]{:S(2)}) collective-permute-start(s16[32,1152]{1,0:T(8,128)(2,1)S(1)} %get-tuple-element.79), channel_id=1, source_target_pairs={{0,3},{128,131},{1,0},{129,128},{2,1},{130,129},{3,2},{131,130},{4... | collective-permute-start | bytes 221192 | tf_op jit(solution)/shard_map/ppermute | solution.py:273
  84.7 2.2 %collective-permute-done.19.half_below = s16[32,1152]{1,0:T(8,128)(2,1)S(1)} collective-permute-done((s16[32,1152]{1,0:T(8,128)(2,1)S(1)}, s16[32,1152]{1,0:T(8,128)(2,1)S(1)}, u32[]{:S(2)}, u32[]{:S(2)}) %collective-permute-start.19) | collective-permute-done | bytes 73760 | tf_op jit(solution)/shard_map/ppermute | solution.py:273
  87.0 1.5 %collective-permute-done.20.half_above = s16[32,1152]{1,0:T(8,128)(2,1)S(1)} collective-permute-done((s16[32,1152]{1,0:T(8,128)(2,1)S(1)}, s16[32,1152]{1,0:T(8,128)(2,1)S(1)}, u32[]{:S(2)}, u32[]{:S(2)}) %collective-permute-start.20) | collective-permute-done | bytes 73760 | tf_op jit(solution)/shard_map/ppermute | solution.py:273
  89.0 1.5 %collective-permute-start.21 = (s16[64,1152]{1,0:T(8,128)(2,1)S(1)}, s16[64,1152]{1,0:T(8,128)(2,1)S(1)}, u32[]{:S(2)}, u32[]{:S(2)}) collective-permute-start(s16[64,1152]{1,0:T(8,128)(2,1)S(1)} %get-tuple-element.80), channel_id=1, source_target_pairs={{0,1},{128,129},{1,2},{129,130},{2,3},{130,131},{3,0},{131,128},{4... | collective-permute-start | bytes 442376 | tf_op jit(solution)/shard_map/ppermute | solution.py:273
  90.5 2.7 %collective-permute-start.22 = (s16[64,1152]{1,0:T(8,128)(2,1)S(1)}, s16[64,1152]{1,0:T(8,128)(2,1)S(1)}, u32[]{:S(2)}, u32[]{:S(2)}) collective-permute-start(s16[64,1152]{1,0:T(8,128)(2,1)S(1)} %get-tuple-element.81), channel_id=1, source_target_pairs={{0,3},{128,131},{1,0},{129,128},{2,1},{130,129},{3,2},{131,130},{4... | collective-permute-start | bytes 442376 | tf_op jit(solution)/shard_map/ppermute | solution.py:273
  93.2 4.7 %collective-permute-done.21.far_below = s16[64,1152]{1,0:T(8,128)(2,1)S(1)} collective-permute-done((s16[64,1152]{1,0:T(8,128)(2,1)S(1)}, s16[64,1152]{1,0:T(8,128)(2,1)S(1)}, u32[]{:S(2)}, u32[]{:S(2)}) %collective-permute-start.21) | collective-permute-done | bytes 147488 | tf_op jit(solution)/shard_map/ppermute | solution.py:273
  98.2 1.1 %add_up.1 = (f32[1,64]{1,0:T(1,128)}, f32[64,1024]{1,0:T(8,128)}) custom-call(f32[192,1024]{1,0:T(8,128)S(1)} %get-tuple-element.74.gradient, f32[192,128]{1,0:T(8,128)S(1)} %get-tuple-element.75.proof, s16[128,1152]{1,0:T(8,128)(2,1)S(1)} %collective-permute-done.17.from_below, s16[128,1152]{1,0:T(8,128)(2,1)S(1)} %collective-permute-done.18.from_above, ...), custom_call_target="tpu_custom_call" | custom-call | bytes 1048576 | tf_op jit(solution)/shard_map/add_up/pallas_call | solution.py:29
  (38 shorter events, 6.9 us)
Async XLA Ops:
  0.6 45.0 %copy-start.2 = (bf16[64,1024]{1,0:T(8,128)(2,1)S(1)}, bf16[64,1024]{1,0:T(8,128)(2,1)}, u32[]{:S(2)}) copy-start(bf16[64,1024]{1,0:T(8,128)(2,1)} %own.1) | copy-start | bytes 393220
  2.6 14.1 %collective-permute-start.2 = (bf16[144,1024]{1,0:T(8,128)(2,1)}, bf16[144,1024]{1,0:T(8,128)(2,1)S(1)}, u32[]{:S(2)}, u32[]{:S(2)}) collective-permute-start(bf16[144,1024]{1,0:T(8,128)(2,1)} %pack_block.1.refs_0_), channel_id=1, source_target_pairs={{0,32},{16,20},{4,36},{20,24},{8,40},{24,28},{12,44},{28,16},{32,6... | collective-permute-start | bytes 884744 | tf_op jit(solution)/shard_map/ppermute | solution.py:283
  4.1 12.6 %collective-permute-start.3 = (bf16[144,1024]{1,0:T(8,128)(2,1)}, bf16[144,1024]{1,0:T(8,128)(2,1)S(1)}, u32[]{:S(2)}, u32[]{:S(2)}) collective-permute-start(bf16[144,1024]{1,0:T(8,128)(2,1)} %pack_block.1.refs_0_), channel_id=1, source_target_pairs={{0,96},{16,28},{4,100},{20,16},{8,104},{24,20},{12,108},{28,24},{3... | collective-permute-start | bytes 884744 | tf_op jit(solution)/shard_map/ppermute | solution.py:283
  5.9 10.8 %collective-permute-start.4 = (bf16[144,1024]{1,0:T(8,128)(2,1)}, bf16[144,1024]{1,0:T(8,128)(2,1)S(1)}, u32[]{:S(2)}, u32[]{:S(2)}) collective-permute-start(bf16[144,1024]{1,0:T(8,128)(2,1)} %pack_block.1.refs_0_), channel_id=1, source_target_pairs={{0,64},{16,24},{4,68},{20,28},{8,72},{24,16},{12,76},{28,20},{32,9... | collective-permute-start | bytes 884744 | tf_op jit(solution)/shard_map/ppermute | solution.py:283
  7.7 9.0 %collective-permute-start = (bf16[64,1024]{1,0:T(8,128)(2,1)}, bf16[64,1024]{1,0:T(8,128)(2,1)S(1)}, u32[]{:S(2)}, u32[]{:S(2)}) collective-permute-start(bf16[64,1024]{1,0:T(8,128)(2,1)} %own.1), channel_id=1, source_target_pairs={{0,128},{128,1},{1,129},{129,2},{2,130},{130,3},{3,131},{131,0},{4... | collective-permute-start | bytes 393224 | tf_op jit(solution)/shard_map/ppermute | solution.py:273
  9.6 7.1 %collective-permute-start.1 = (bf16[64,1024]{1,0:T(8,128)(2,1)}, bf16[64,1024]{1,0:T(8,128)(2,1)S(1)}, u32[]{:S(2)}, u32[]{:S(2)}) collective-permute-start(bf16[64,1024]{1,0:T(8,128)(2,1)} %own.1), channel_id=1, source_target_pairs={{0,131},{128,0},{1,128},{129,1},{2,129},{130,2},{3,130},{131,3},{4... | collective-permute-start | bytes 393224 | tf_op jit(solution)/shard_map/ppermute | solution.py:273
  16.7 1.0 copy-start
  17.7 0.9 copy-start.1
  18.7 28.5 %collective-permute-start.8 = (bf16[528,1024]{1,0:T(8,128)(2,1)S(1)}, bf16[528,1024]{1,0:T(8,128)(2,1)S(1)}, u32[]{:S(2)}, u32[]{:S(2)}) collective-permute-start(bf16[528,1024]{1,0:T(8,128)(2,1)S(1)} %get-tuple-element.45.refs_0_), channel_id=1, source_target_pairs={{0,4},{16,48},{4,8},{20,52},{8,12},{24,56},{12,0},{28,60},{32,36},... | collective-permute-start | bytes 3244040 | tf_op jit(solution)/shard_map/ppermute | solution.py:283
  20.3 26.8 %collective-permute-start.9 = (bf16[528,1024]{1,0:T(8,128)(2,1)S(1)}, bf16[528,1024]{1,0:T(8,128)(2,1)S(1)}, u32[]{:S(2)}, u32[]{:S(2)}) collective-permute-start(bf16[528,1024]{1,0:T(8,128)(2,1)S(1)} %get-tuple-element.45.refs_0_), channel_id=1, source_target_pairs={{0,12},{16,112},{4,0},{20,116},{8,4},{24,120},{12,8},{28,124},{32,... | collective-permute-start | bytes 3244040 | tf_op jit(solution)/shard_map/ppermute | solution.py:283
  20.8 23.0 %collective-permute-start.5 = (bf16[160,1024]{1,0:T(8,128)(2,1)S(1)}, bf16[160,1024]{1,0:T(8,128)(2,1)S(1)}, u32[]{:S(2)}, u32[]{:S(2)}) collective-permute-start(bf16[160,1024]{1,0:T(8,128)(2,1)S(1)} %get-tuple-element.43), channel_id=1, source_target_pairs={{0,129},{128,2},{1,130},{129,3},{2,131},{130,0},{3,128},{131,1},{4... | collective-permute-start | bytes 983048 | tf_op jit(solution)/shard_map/ppermute | solution.py:273
  25.9 19.8 %collective-permute-start.6 = (bf16[160,1024]{1,0:T(8,128)(2,1)S(1)}, bf16[160,1024]{1,0:T(8,128)(2,1)S(1)}, u32[]{:S(2)}, u32[]{:S(2)}) collective-permute-start(bf16[160,1024]{1,0:T(8,128)(2,1)S(1)} %get-tuple-element.44), channel_id=1, source_target_pairs={{0,130},{128,3},{1,131},{129,0},{2,128},{130,1},{3,129},{131,2},{4... | collective-permute-start | bytes 983048 | tf_op jit(solution)/shard_map/ppermute | solution.py:273
  25.9 25.1 %collective-permute-start.7 = (bf16[528,1024]{1,0:T(8,128)(2,1)S(1)}, bf16[528,1024]{1,0:T(8,128)(2,1)S(1)}, u32[]{:S(2)}, u32[]{:S(2)}) collective-permute-start(bf16[528,1024]{1,0:T(8,128)(2,1)S(1)} %get-tuple-element.45.refs_0_), channel_id=1, source_target_pairs={{0,8},{16,80},{4,12},{20,84},{8,0},{24,88},{12,4},{28,92},{32,40},... | collective-permute-start | bytes 3244040 | tf_op jit(solution)/shard_map/ppermute | solution.py:283
  47.2 3.9 %collective-permute-start.10 = (bf16[528,1024]{1,0:T(8,128)(2,1)S(1)}, bf16[528,1024]{1,0:T(8,128)(2,1)S(1)}, u32[]{:S(2)}, u32[]{:S(2)}) collective-permute-start(bf16[528,1024]{1,0:T(8,128)(2,1)S(1)} %get-tuple-element.48.refs_0_.refs_1_), channel_id=1, source_target_pairs={{0,16},{16,0},{1,17},{17,1},{2,18},{18,2},{3,19},{19,3},{4,20},{20... | collective-permute-start | bytes 3244040 | tf_op jit(solution)/shard_map/ppermute | solution.py:291
  47.3 4.2 %collective-permute-start.11 = (bf16[528,1024]{1,0:T(8,128)(2,1)S(1)}, bf16[528,1024]{1,0:T(8,128)(2,1)S(1)}, u32[]{:S(2)}, u32[]{:S(2)}) collective-permute-start(bf16[528,1024]{1,0:T(8,128)(2,1)S(1)} %get-tuple-element.49.refs_1_.refs_2_), channel_id=1, source_target_pairs={{0,16},{16,0},{1,17},{17,1},{2,18},{18,2},{3,19},{19,3},{4,20},{20... | collective-permute-start | bytes 3244040 | tf_op jit(solution)/shard_map/ppermute | solution.py:291
  47.8 5.7 %collective-permute-start.13 = (bf16[528,1024]{1,0:T(8,128)(2,1)S(1)}, bf16[528,1024]{1,0:T(8,128)(2,1)S(1)}, u32[]{:S(2)}, u32[]{:S(2)}) collective-permute-start(bf16[528,1024]{1,0:T(8,128)(2,1)S(1)} %get-tuple-element.45.refs_0_), channel_id=1, source_target_pairs={{0,16},{16,0},{1,17},{17,1},{2,18},{18,2},{3,19},{19,3},{4,20},{20... | collective-permute-start | bytes 3244040 | tf_op jit(solution)/shard_map/ppermute | solution.py:291
  51.5 3.1 %collective-permute-start.12 = (bf16[528,1024]{1,0:T(8,128)(2,1)S(1)}, bf16[528,1024]{1,0:T(8,128)(2,1)S(1)}, u32[]{:S(2)}, u32[]{:S(2)}) collective-permute-start(bf16[528,1024]{1,0:T(8,128)(2,1)S(1)} %handed_on.3.refs_0_.refs_3_), channel_id=1, source_target_pairs={{0,16},{16,0},{1,17},{17,1},{2,18},{18,2},{3,19},{19,3},{4,20},{20... | collective-permute-start | bytes 3244040 | tf_op jit(solution)/shard_map/ppermute | solution.py:291
  54.8 9.0 %collective-permute-start.14 = (f32[8,128]{1,0:T(8,128)S(1)}, f32[8,128]{1,0:T(8,128)S(1)}, u32[]{:S(2)}, u32[]{:S(2)}) collective-permute-start(f32[8,128]{1,0:T(8,128)S(1)} %count_chosen.1), channel_id=1, source_target_pairs={{0,128},{128,0},{1,129},{129,1},{2,130},{130,2},{3,131},{131,3},{4... | collective-permute-start | bytes 12296 | tf_op jit(solution)/shard_map/ppermute | solution.py:353
  63.8 4.6 %collective-permute-start.15 = (f32[8,128]{1,0:T(8,128)S(1)}, f32[8,128]{1,0:T(8,128)S(1)}, u32[]{:S(2)}, u32[]{:S(2)}) collective-permute-start(f32[8,128]{1,0:T(8,128)S(1)} %add.9), channel_id=1, source_target_pairs={{0,1},{128,129},{1,0},{129,128},{2,3},{130,131},{3,2},{131,130},{4... | collective-permute-start | bytes 12296 | tf_op jit(solution)/shard_map/ppermute | solution.py:353
  68.4 7.5 %collective-permute-start.16 = (f32[8,128]{1,0:T(8,128)S(1)}, f32[8,128]{1,0:T(8,128)S(1)}, u32[]{:S(2)}, u32[]{:S(2)}) collective-permute-start(f32[8,128]{1,0:T(8,128)S(1)} %add.10), channel_id=1, source_target_pairs={{0,2},{128,130},{1,3},{129,131},{2,0},{130,128},{3,1},{131,129},{4... | collective-permute-start | bytes 12296 | tf_op jit(solution)/shard_map/ppermute | solution.py:353
  76.9 11.6 %collective-permute-start.17 = (s16[128,1152]{1,0:T(8,128)(2,1)S(1)}, s16[128,1152]{1,0:T(8,128)(2,1)S(1)}, u32[]{:S(2)}, u32[]{:S(2)}) collective-permute-start(s16[128,1152]{1,0:T(8,128)(2,1)S(1)} %get-tuple-element.76), channel_id=1, source_target_pairs={{0,128},{128,1},{1,129},{129,2},{2,130},{130,3},{3,131},{131,0},{4... | collective-permute-start | bytes 884744 | tf_op jit(solution)/shard_map/ppermute | solution.py:273
  77.3 11.1 %collective-permute-start.18 = (s16[128,1152]{1,0:T(8,128)(2,1)S(1)}, s16[128,1152]{1,0:T(8,128)(2,1)S(1)}, u32[]{:S(2)}, u32[]{:S(2)}) collective-permute-start(s16[128,1152]{1,0:T(8,128)(2,1)S(1)} %get-tuple-element.77), channel_id=1, source_target_pairs={{0,131},{128,0},{1,128},{129,1},{2,129},{130,2},{3,130},{131,3},{4... | collective-permute-start | bytes 884744 | tf_op jit(solution)/shard_map/ppermute | solution.py:273
  80.2 6.8 %collective-permute-start.19 = (s16[32,1152]{1,0:T(8,128)(2,1)S(1)}, s16[32,1152]{1,0:T(8,128)(2,1)S(1)}, u32[]{:S(2)}, u32[]{:S(2)}) collective-permute-start(s16[32,1152]{1,0:T(8,128)(2,1)S(1)} %get-tuple-element.78), channel_id=1, source_target_pairs={{0,1},{128,129},{1,2},{129,130},{2,3},{130,131},{3,0},{131,128},{4... | collective-permute-start | bytes 221192 | tf_op jit(solution)/shard_map/ppermute | solution.py:273
  81.1 7.3 %collective-permute-start.20 = (s16[32,1152]{1,0:T(8,128)(2,1)S(1)}, s16[32,1152]{1,0:T(8,128)(2,1)S(1)}, u32[]{:S(2)}, u32[]{:S(2)}) collective-permute-start(s16[32,1152]{1,0:T(8,128)(2,1)S(1)} %get-tuple-element.79), channel_id=1, source_target_pairs={{0,3},{128,131},{1,0},{129,128},{2,1},{130,129},{3,2},{131,130},{4... | collective-permute-start | bytes 221192 | tf_op jit(solution)/shard_map/ppermute | solution.py:273
  89.0 8.9 %collective-permute-start.21 = (s16[64,1152]{1,0:T(8,128)(2,1)S(1)}, s16[64,1152]{1,0:T(8,128)(2,1)S(1)}, u32[]{:S(2)}, u32[]{:S(2)}) collective-permute-start(s16[64,1152]{1,0:T(8,128)(2,1)S(1)} %get-tuple-element.80), channel_id=1, source_target_pairs={{0,1},{128,129},{1,2},{129,130},{2,3},{130,131},{3,0},{131,128},{4... | collective-permute-start | bytes 442376 | tf_op jit(solution)/shard_map/ppermute | solution.py:273
  90.5 7.7 %collective-permute-start.22 = (s16[64,1152]{1,0:T(8,128)(2,1)S(1)}, s16[64,1152]{1,0:T(8,128)(2,1)S(1)}, u32[]{:S(2)}, u32[]{:S(2)}) collective-permute-start(s16[64,1152]{1,0:T(8,128)(2,1)S(1)} %get-tuple-element.81), channel_id=1, source_target_pairs={{0,3},{128,131},{1,0},{129,128},{2,1},{130,129},{3,2},{131,130},{4... | collective-permute-start | bytes 442376 | tf_op jit(solution)/shard_map/ppermute | solution.py:273

commit v6 on v5

--- a/solution.py
+++ b/solution.py
@@ -132,9 +132,10 @@
             pulls[half][part, :] = total
 
 
-def first_columns(rows, lines, own, below, above, far_below, far_above, *refs):
+def first_columns(rows, lines, own, below, above, far_below, far_above, chosen, *refs):
     pieces, refs = refs[:lines], refs[lines:]
-    ordered, norms, pp, tp, pm, tm, *weights = refs
+    ordered, norms, total, pp, tp, pm, tm, *weights = refs
+    total[...] = jnp.broadcast_to(jnp.sum(chosen[...], axis=0), total.shape)
     height = own.shape[0]
     found = {
         0: own[...],
@@ -160,12 +161,6 @@
     add_columns(panel, norms, pieces, old, (pp, tp), (pm, tm), weights, rows)
 
 
-def count_chosen(*refs):
-    metas, chosen = refs[:-1], refs[-1]
-    total = sum(meta[...].astype(F32)[:1] for meta in metas)
-    chosen[...] = jnp.full(chosen.shape, jnp.sum(total), F32)
-
-
 def terms(target_count, panel, pp, tp, pm, tm, total, part):
     weight = total[:1, :1]
     pool_mass = jnp.sum(pm[part, :], axis=1, keepdims=True)
@@ -297,6 +292,9 @@
     rows = ring * height
     target_count = float(height * lax.axis_size(AXES))
 
+    devices = lax.axis_size(AXES)
+    chosen = jnp.broadcast_to(jnp.sum(counts).astype(F32), (devices, 1, LANES))
+    chosen = lax.all_to_all(chosen, AXES, split_axis=0, concat_axis=0, tiled=True)
     block = in_vmem(pack_block, "pack_block", shape((2 * height + META, width), BF16), limit=56)(
         pool, targets, counts.reshape(1, height)
     )
@@ -327,31 +325,17 @@
     def more(some, state):
         return add(more_columns, (panel, norms), some, state, sums, {2 + len(some) + i: i for i in range(4)})
 
-    panel, norms, *state = add(
+    panel, norms, total, *state = add(
         first_columns,
-        (pool, below, above, *pairs),
+        (pool, below, above, *pairs, chosen),
         pieces[:1],
         (),
-        (shape((rows, width), BF16), shape((rows, LANES), F32), *sums),
+        (shape((rows, width), BF16), shape((rows, LANES), F32), shape((8, LANES), F32), *sums),
         {},
     )
-    pieces[1:3] = handed_on(pieces[1:3], norms)
-    others += [other_core(p) for p in pieces[1:3]]
-    state = more(pieces[1:3], state)
-    pieces[3:] = handed_on(pieces[3:], state[2], *others[1:3])
-    others.append(other_core(pieces[3]))
-    total = pl.pallas_call(
-        count_chosen,
-        grid=(1,),
-        out_shape=shape((8, LANES), F32),
-        in_specs=[pl.BlockSpec((META, size), lambda i: (2 * size // META, 0))] * 2 * len(pieces),
-        out_specs=pl.BlockSpec((8, LANES), lambda i: (0, 0)),
-        name="count_chosen",
-        compiler_params=pltpu.CompilerParams(vmem_limit_bytes=4 << 20),
-    )(*pieces, *others)
-    for bit in (1, 2, 4):
-        total = total + lax.ppermute(total, RING, [(place(i), place(i ^ bit)) for i in range(ring)])
-    for some in (pieces[3:], others[:2], others[2:3], others[3:]):
+    pieces[1:] = handed_on(pieces[1:], norms)
+    others += [other_core(p) for p in pieces[1:]]
+    for some in (pieces[1:3], (pieces[3], others[0]), others[1:]):
         state = more(some, state)
 
     inputs = panel, *state, total

time: 99.4 us -> 104 us (1.046); the launches traced: 99.3 us -> 102 us
  waiting for transfers between devices: 36.4 us -> 32.1 us
  Pallas kernels: 18.4 us -> 21.2 us
  local copies, waits for them, and re-layouts: 1.86 us -> 3.54 us
  starting transfers between devices: 41.8 us -> 43.2 us
    all_to_all x0 -> x1, starting transfers between devices: none -> 9.81 us  [on_device(): lax.all_to_all(chosen, AXES, split_axis=0, concat_axis=0, tiled=True)]
    ppermute x3 -> x0, starting transfers between devices: 8.89 us -> none  [on_device(): lax.ppermute(total, RING, [(place(i), place(i ^ bit)) for i in range(ring)])]
    ppermute x3 -> x0, waiting for transfers between devices: 5.46 us -> none  [on_device(): lax.ppermute(total, RING, [(place(i), place(i ^ bit)) for i in range(ring)])]
    all_to_all x0 -> x1, waiting for transfers between devices: none -> 3.26 us  [on_device(): lax.all_to_all(chosen, AXES, split_axis=0, concat_axis=0, tiled=True)]
    pallas_call x12 -> x10, Pallas kernels: 18.2 us -> 21.2 us  [call(): pl.pallas_call(body, out_shape=out_shape, in_specs=[spec] * len(args), ou...]
    ppermute x4, waiting for transfers between devices: 1.62 us -> 0.01 us  [other_core(): return lax.ppermute(x, 'c', [(0, 1), (1, 0)])]
    unnamed x6 -> x12, local copies, waits for them, and re-layouts: 1.86 us -> 2.82 us
  transfers between devices with their start and end apart: 23 -> 21, of which waited for: 11 -> 7; matrix products, arithmetic and copies ran while one was open for 0% -> 1% of each run, Pallas kernels for 14% -> 11%
where the time goes in v6:
time: 104 us; the launch traced here: 102 us
  starting transfers between devices  43.2 us (42%)
  waiting for transfers between devices  32.1 us (31%)
  Pallas kernels  21.2 us (20%)
  local copies, waits for them, and re-layouts  3.54 us (3%)
  between operations  1.46 us (1%)
    ppermute x10, waiting for transfers between devices, up_the_ring(): lax.ppermute(x, RING, [(place(i), place((i + step) % ring)) for i in rang...  28.8 us
    ppermute x10, starting transfers between devices, up_the_ring(): lax.ppermute(x, RING, [(place(i), place((i + step) % ring)) for i in rang...  23.3 us
    pallas_call x10, Pallas kernels, call(): pl.pallas_call(body, out_shape=out_shape, in_specs=[spec] * len(args), ou...  21.2 us
    all_to_all x1, starting transfers between devices, on_device(): lax.all_to_all(chosen, AXES, split_axis=0, concat_axis=0, tiled=True)  9.81 us
    ppermute x6, starting transfers between devices, along_line(): return lax.ppermute(x, PLANE, pairs)  9.37 us
    all_to_all x1, waiting for transfers between devices, on_device(): lax.all_to_all(chosen, AXES, split_axis=0, concat_axis=0, tiled=True)  3.26 us
    unnamed x12, local copies, waits for them, and re-layouts  2.82 us
  transfers between devices with their start and end apart: 21, of which 7 were waited for; matrix products, arithmetic and copies ran while one was open for 1% of the time, Pallas kernels for 11%

profile of v6, /device:TPU:8, one launch (start us, length us, event | category | flops | bytes accessed | tf_op | source)
XLA Modules:
  0.0 102.1 jit_solution(6654498696839339992)
XLA Ops:
  0.7 2.0 %pack_block.1.refs_0_ = bf16[144,1024]{1,0:T(8,128)(2,1)} custom-call(bf16[64,1024]{1,0:T(8,128)(2,1)} %own.1, bf16[64,1024]{1,0:T(8,128)(2,1)} %targets.1, s32[1,64]{1,0:T(1,128)} %bitcast.2), custom_call_target="tpu_custom_call" | custom-call | bytes 1048576 | tf_op jit(solution)/shard_map/pack_block/pallas_call | solution.py:29
  2.6 3.0 %collective-permute-start.4 = (bf16[144,1024]{1,0:T(8,128)(2,1)}, bf16[144,1024]{1,0:T(8,128)(2,1)S(1)}, u32[]{:S(2)}, u32[]{:S(2)}) collective-permute-start(bf16[144,1024]{1,0:T(8,128)(2,1)} %pack_block.1.refs_0_), channel_id=1, source_target_pairs={{0,64},{16,24},{4,68},{20,28},{8,72},{24,16},{12,76},{28,20},{32,9... | collective-permute-start | bytes 884744 | tf_op jit(solution)/shard_map/ppermute | solution.py:278
  5.7 1.1 %collective-permute-start.3 = (bf16[144,1024]{1,0:T(8,128)(2,1)}, bf16[144,1024]{1,0:T(8,128)(2,1)S(1)}, u32[]{:S(2)}, u32[]{:S(2)}) collective-permute-start(bf16[144,1024]{1,0:T(8,128)(2,1)} %pack_block.1.refs_0_), channel_id=1, source_target_pairs={{0,96},{16,28},{4,100},{20,16},{8,104},{24,20},{12,108},{28,24},{3... | collective-permute-start | bytes 884744 | tf_op jit(solution)/shard_map/ppermute | solution.py:278
  6.8 0.9 collective-permute-start.2
  7.7 5.9 %collective-permute-start.1 = (bf16[64,1024]{1,0:T(8,128)(2,1)}, bf16[64,1024]{1,0:T(8,128)(2,1)S(1)}, u32[]{:S(2)}, u32[]{:S(2)}) collective-permute-start(bf16[64,1024]{1,0:T(8,128)(2,1)} %own.1), channel_id=1, source_target_pairs={{0,131},{128,0},{1,128},{129,1},{2,129},{130,2},{3,130},{131,3},{4... | collective-permute-start | bytes 393224 | tf_op jit(solution)/shard_map/ppermute | solution.py:268
  13.5 2.8 %collective-permute-done.1.refs_6_.above = bf16[64,1024]{1,0:T(8,128)(2,1)S(1)} collective-permute-done((bf16[64,1024]{1,0:T(8,128)(2,1)}, bf16[64,1024]{1,0:T(8,128)(2,1)S(1)}, u32[]{:S(2)}, u32[]{:S(2)}) %collective-permute-start.1) | collective-permute-done | bytes 131104 | tf_op jit(solution)/shard_map/ppermute | solution.py:268
  16.4 3.6 %collective-permute-done.refs_5_.below = bf16[64,1024]{1,0:T(8,128)(2,1)S(1)} collective-permute-done((bf16[64,1024]{1,0:T(8,128)(2,1)}, bf16[64,1024]{1,0:T(8,128)(2,1)S(1)}, u32[]{:S(2)}, u32[]{:S(2)}) %collective-permute-start) | collective-permute-done | bytes 131104 | tf_op jit(solution)/shard_map/ppermute | solution.py:268
  20.0 1.0 copy-done
  21.0 0.9 copy-done.1
  21.9 1.3 %pack_line.1 = (bf16[528,1024]{1,0:T(8,128)(2,1)}, bf16[160,1024]{1,0:T(8,128)(2,1)}, bf16[160,1024]{1,0:T(8,128)(2,1)}) custom-call(bf16[144,1024]{1,0:T(8,128)(2,1)S(1)} %copy-done, bf16[144,1024]{1,0:T(8,128)(2,1)S(1)} %collective-permute-done.2.refs_1_, bf16[144,1024]{1,0:T(8,128)(2,1)S(1)} %collective-permute-done.3.refs_2_, ...), custom_call_target="tpu_custom_call" | custom-call | bytes 1048576 | tf_op jit(solution)/shard_map/pack_line/pallas_call | solution.py:29
  23.1 2.3 %collective-permute-start.9 = (bf16[528,1024]{1,0:T(8,128)(2,1)}, bf16[528,1024]{1,0:T(8,128)(2,1)S(1)}, u32[]{:S(2)}, u32[]{:S(2)}) collective-permute-start(bf16[528,1024]{1,0:T(8,128)(2,1)} %get-tuple-element.39.refs_0_), channel_id=1, source_target_pairs={{0,8},{16,80},{4,12},{20,84},{8,0},{24,88},{12,4},{28,92},{32,40},... | collective-permute-start | bytes 3244040 | tf_op jit(solution)/shard_map/ppermute | solution.py:278
  25.4 1.3 %collective-permute-start.8 = (bf16[528,1024]{1,0:T(8,128)(2,1)}, bf16[528,1024]{1,0:T(8,128)(2,1)S(1)}, u32[]{:S(2)}, u32[]{:S(2)}) collective-permute-start(bf16[528,1024]{1,0:T(8,128)(2,1)} %get-tuple-element.39.refs_0_), channel_id=1, source_target_pairs={{0,12},{16,112},{4,0},{20,116},{8,4},{24,120},{12,8},{28,124},{32,... | collective-permute-start | bytes 3244040 | tf_op jit(solution)/shard_map/ppermute | solution.py:278
  27.4 5.0 %collective-permute-start.6 = (bf16[160,1024]{1,0:T(8,128)(2,1)}, bf16[160,1024]{1,0:T(8,128)(2,1)}, u32[]{:S(2)}, u32[]{:S(2)}) collective-permute-start(bf16[160,1024]{1,0:T(8,128)(2,1)} %get-tuple-element.38), channel_id=1, source_target_pairs={{0,130},{128,3},{1,131},{129,0},{2,128},{130,1},{3,129},{131,2},{4... | collective-permute-start | bytes 983048 | tf_op jit(solution)/shard_map/ppermute | solution.py:268
  33.8 0.7 broadcast_in_dim.3
  34.5 9.8 %all-to-all-start = ((f32[256,1,128]{2,1,0:T(1,128)}), f32[256,1,128]{2,1,0:T(1,128)}, u32[]{:S(2)}, u32[]{:S(2)}) async-start(f32[256,1,128]{2,1,0:T(1,128)} %broadcast_in_dim.3), calls=%async_computation | async-start | bytes 262144 | tf_op jit(solution)/shard_map/all_to_all | solution.py:297
  44.3 9.2 %collective-permute-done.5.far_below = bf16[160,1024]{1,0:T(8,128)(2,1)} collective-permute-done((bf16[160,1024]{1,0:T(8,128)(2,1)}, bf16[160,1024]{1,0:T(8,128)(2,1)}, u32[]{:S(2)}, u32[]{:S(2)}) %collective-permute-start.5) | collective-permute-done | bytes 327712 | tf_op jit(solution)/shard_map/ppermute | solution.py:268
  53.5 3.3 %all-to-all-done.chosen = f32[256,1,128]{2,1,0:T(1,128)} async-done(((f32[256,1,128]{2,1,0:T(1,128)}), f32[256,1,128]{2,1,0:T(1,128)}, u32[]{:S(2)}, u32[]{:S(2)}) %all-to-all-start) | async-done | bytes 131104 | tf_op jit(solution)/shard_map/all_to_all | solution.py:297
  56.8 0.9 copy-done.4
  57.7 3.0 %first_columns.1 = (bf16[512,1024]{1,0:T(8,128)(2,1)S(1)}, f32[512,128]{1,0:T(8,128)S(1)}, f32[8,128]{1,0:T(8,128)S(1)}, f32[512,1024]{1,0:T(8,128)S(1)}, f32[51...) custom-call(bf16[64,1024]{1,0:T(8,128)(2,1)S(1)} %copy-done.2, bf16[64,1024]{1,0:T(8,128)(2,1)S(1)} %copy-done.4, ...), custom_call_target="tpu_custom_call" | custom-call | flops 1073741824 | bytes 1048576 | tf_op jit(solution)/shard_map/first_columns/pallas_call | solution.py:29
  61.5 3.1 %more_columns.3 = (f32[512,1024]{1,0:T(8,128)S(1)}, f32[512,1024]{1,0:T(8,128)S(1)}, f32[512,128]{1,0:T(8,128)S(1)}, f32[512,128]{1,0:T(8,128)S(1)}) custom-call(bf16[512,1024]{1,0:T(8,128)(2,1)S(1)} %get-tuple-element.40.panel.refs_0_, ...), custom_call_target="tpu_custom_call", output_to_operand_aliasing={{0}: (4, {}), {1}: (5, {}), {2}: (6, {}), {3}: (7, {})} | custom-call | flops 2147483648 | bytes 1048576 | tf_op jit(solution)/shard_map/more_columns/pallas_call | solution.py:29
  64.6 4.4 %more_columns.4 = (f32[512,1024]{1,0:T(8,128)S(1)}, f32[512,1024]{1,0:T(8,128)S(1)}, f32[512,128]{1,0:T(8,128)S(1)}, f32[512,128]{1,0:T(8,128)S(1)}) custom-call(bf16[512,1024]{1,0:T(8,128)(2,1)S(1)} %get-tuple-element.40.panel.refs_0_, ...), custom_call_target="tpu_custom_call", output_to_operand_aliasing={{0}: (4, {}), {1}: (5, {}), {2}: (6, {}), {3}: (7, {})} | custom-call | flops 2147483648 | bytes 1048576 | tf_op jit(solution)/shard_map/more_columns/pallas_call | solution.py:29
  69.1 4.4 %more_columns.5 = (f32[512,1024]{1,0:T(8,128)S(1)}, f32[512,1024]{1,0:T(8,128)S(1)}, f32[512,128]{1,0:T(8,128)S(1)}, f32[512,128]{1,0:T(8,128)S(1)}) custom-call(bf16[512,1024]{1,0:T(8,128)(2,1)S(1)} %get-tuple-element.40.panel.refs_0_, ...), custom_call_target="tpu_custom_call", output_to_operand_aliasing={{0}: (5, {}), {1}: (6, {}), {2}: (7, {}), {3}: (8, {})} | custom-call | flops 3221225472 | bytes 1048576 | tf_op jit(solution)/shard_map/more_columns/pallas_call | solution.py:29
  73.5 1.0 far_terms.1
  74.5 4.1 %collective-permute-start.14 = (s16[128,1152]{1,0:T(8,128)(2,1)S(1)}, s16[128,1152]{1,0:T(8,128)(2,1)S(1)}, u32[]{:S(2)}, u32[]{:S(2)}) collective-permute-start(s16[128,1152]{1,0:T(8,128)(2,1)S(1)} %get-tuple-element.64), channel_id=1, source_target_pairs={{0,128},{128,1},{1,129},{129,2},{2,130},{130,3},{3,131},{131,0},{4... | collective-permute-start | bytes 884744 | tf_op jit(solution)/shard_map/ppermute | solution.py:268
  78.5 2.5 %collective-permute-start.16 = (s16[32,1152]{1,0:T(8,128)(2,1)S(1)}, s16[32,1152]{1,0:T(8,128)(2,1)S(1)}, u32[]{:S(2)}, u32[]{:S(2)}) collective-permute-start(s16[32,1152]{1,0:T(8,128)(2,1)S(1)} %get-tuple-element.66), channel_id=1, source_target_pairs={{0,1},{128,129},{1,2},{129,130},{2,3},{130,131},{3,0},{131,128},{4... | collective-permute-start | bytes 221192 | tf_op jit(solution)/shard_map/ppermute | solution.py:268
  81.0 1.7 %collective-permute-start.17 = (s16[32,1152]{1,0:T(8,128)(2,1)S(1)}, s16[32,1152]{1,0:T(8,128)(2,1)S(1)}, u32[]{:S(2)}, u32[]{:S(2)}) collective-permute-start(s16[32,1152]{1,0:T(8,128)(2,1)S(1)} %get-tuple-element.67), channel_id=1, source_target_pairs={{0,3},{128,131},{1,0},{129,128},{2,1},{130,129},{3,2},{131,130},{4... | collective-permute-start | bytes 221192 | tf_op jit(solution)/shard_map/ppermute | solution.py:268
  83.1 6.8 %collective-permute-done.16.half_below = s16[32,1152]{1,0:T(8,128)(2,1)S(1)} collective-permute-done((s16[32,1152]{1,0:T(8,128)(2,1)S(1)}, s16[32,1152]{1,0:T(8,128)(2,1)S(1)}, u32[]{:S(2)}, u32[]{:S(2)}) %collective-permute-start.16) | collective-permute-done | bytes 73760 | tf_op jit(solution)/shard_map/ppermute | solution.py:268
  89.9 1.3 %collective-permute-done.17.half_above = s16[32,1152]{1,0:T(8,128)(2,1)S(1)} collective-permute-done((s16[32,1152]{1,0:T(8,128)(2,1)S(1)}, s16[32,1152]{1,0:T(8,128)(2,1)S(1)}, u32[]{:S(2)}, u32[]{:S(2)}) %collective-permute-start.17) | collective-permute-done | bytes 73760 | tf_op jit(solution)/shard_map/ppermute | solution.py:268
  91.7 0.8 collective-permute-start.18
  92.5 3.4 %collective-permute-start.19 = (s16[64,1152]{1,0:T(8,128)(2,1)S(1)}, s16[64,1152]{1,0:T(8,128)(2,1)S(1)}, u32[]{:S(2)}, u32[]{:S(2)}) collective-permute-start(s16[64,1152]{1,0:T(8,128)(2,1)S(1)} %get-tuple-element.69), channel_id=1, source_target_pairs={{0,3},{128,131},{1,0},{129,128},{2,1},{130,129},{3,2},{131,130},{4... | collective-permute-start | bytes 442376 | tf_op jit(solution)/shard_map/ppermute | solution.py:268
  95.9 5.1 %collective-permute-done.18.far_below = s16[64,1152]{1,0:T(8,128)(2,1)S(1)} collective-permute-done((s16[64,1152]{1,0:T(8,128)(2,1)S(1)}, s16[64,1152]{1,0:T(8,128)(2,1)S(1)}, u32[]{:S(2)}, u32[]{:S(2)}) %collective-permute-start.18) | collective-permute-done | bytes 147488 | tf_op jit(solution)/shard_map/ppermute | solution.py:268
  101.1 1.1 %add_up.1 = (f32[1,64]{1,0:T(1,128)}, f32[64,1024]{1,0:T(8,128)}) custom-call(f32[192,1024]{1,0:T(8,128)S(1)} %get-tuple-element.62.gradient, f32[192,128]{1,0:T(8,128)S(1)} %get-tuple-element.63.proof, s16[128,1152]{1,0:T(8,128)(2,1)S(1)} %collective-permute-done.14.from_below, s16[128,1152]{1,0:T(8,128)(2,1)S(1)} %collective-permute-done.15.from_above, ...), custom_call_target="tpu_custom_call" | custom-call | bytes 1048576 | tf_op jit(solution)/shard_map/add_up/pallas_call | solution.py:29
  (35 shorter events, 3.0 us)
Async XLA Ops:
  0.6 31.9 %copy-start.5 = (s32[64]{0:T(128)S(1)}, s32[64]{0:T(128)}, u32[]{:S(2)}) copy-start(s32[64]{0:T(128)} %param.5) | copy-start | bytes 772
  0.6 56.1 %copy-start.2 = (bf16[64,1024]{1,0:T(8,128)(2,1)S(1)}, bf16[64,1024]{1,0:T(8,128)(2,1)}, u32[]{:S(2)}) copy-start(bf16[64,1024]{1,0:T(8,128)(2,1)} %own.1) | copy-start | bytes 393220
  2.6 17.3 %collective-permute-start.4 = (bf16[144,1024]{1,0:T(8,128)(2,1)}, bf16[144,1024]{1,0:T(8,128)(2,1)S(1)}, u32[]{:S(2)}, u32[]{:S(2)}) collective-permute-start(bf16[144,1024]{1,0:T(8,128)(2,1)} %pack_block.1.refs_0_), channel_id=1, source_target_pairs={{0,64},{16,24},{4,68},{20,28},{8,72},{24,16},{12,76},{28,20},{32,9... | collective-permute-start | bytes 884744 | tf_op jit(solution)/shard_map/ppermute | solution.py:278
  5.7 14.3 %collective-permute-start.3 = (bf16[144,1024]{1,0:T(8,128)(2,1)}, bf16[144,1024]{1,0:T(8,128)(2,1)S(1)}, u32[]{:S(2)}, u32[]{:S(2)}) collective-permute-start(bf16[144,1024]{1,0:T(8,128)(2,1)} %pack_block.1.refs_0_), channel_id=1, source_target_pairs={{0,96},{16,28},{4,100},{20,16},{8,104},{24,20},{12,108},{28,24},{3... | collective-permute-start | bytes 884744 | tf_op jit(solution)/shard_map/ppermute | solution.py:278
  6.8 13.1 %collective-permute-start.2 = (bf16[144,1024]{1,0:T(8,128)(2,1)}, bf16[144,1024]{1,0:T(8,128)(2,1)S(1)}, u32[]{:S(2)}, u32[]{:S(2)}) collective-permute-start(bf16[144,1024]{1,0:T(8,128)(2,1)} %pack_block.1.refs_0_), channel_id=1, source_target_pairs={{0,32},{16,20},{4,36},{20,24},{8,40},{24,28},{12,44},{28,16},{32,6... | collective-permute-start | bytes 884744 | tf_op jit(solution)/shard_map/ppermute | solution.py:278
  7.7 8.7 %collective-permute-start.1 = (bf16[64,1024]{1,0:T(8,128)(2,1)}, bf16[64,1024]{1,0:T(8,128)(2,1)S(1)}, u32[]{:S(2)}, u32[]{:S(2)}) collective-permute-start(bf16[64,1024]{1,0:T(8,128)(2,1)} %own.1), channel_id=1, source_target_pairs={{0,131},{128,0},{1,128},{129,1},{2,129},{130,2},{3,130},{131,3},{4... | collective-permute-start | bytes 393224 | tf_op jit(solution)/shard_map/ppermute | solution.py:268
  13.5 6.4 %collective-permute-start = (bf16[64,1024]{1,0:T(8,128)(2,1)}, bf16[64,1024]{1,0:T(8,128)(2,1)S(1)}, u32[]{:S(2)}, u32[]{:S(2)}) collective-permute-start(bf16[64,1024]{1,0:T(8,128)(2,1)} %own.1), channel_id=1, source_target_pairs={{0,128},{128,1},{1,129},{129,2},{2,130},{130,3},{3,131},{131,0},{4... | collective-permute-start | bytes 393224 | tf_op jit(solution)/shard_map/ppermute | solution.py:268
  19.9 5.5 %copy-start.3 = (bf16[64,1024]{1,0:T(8,128)(2,1)}, bf16[64,1024]{1,0:T(8,128)(2,1)S(1)}, u32[]{:S(2)}) copy-start(bf16[64,1024]{1,0:T(8,128)(2,1)S(1)} %collective-permute-done.refs_5_.below) | copy-start | bytes 393220
  19.9 1.0 copy-start
  21.0 0.9 copy-start.1
  23.1 37.6 %collective-permute-start.9 = (bf16[528,1024]{1,0:T(8,128)(2,1)}, bf16[528,1024]{1,0:T(8,128)(2,1)S(1)}, u32[]{:S(2)}, u32[]{:S(2)}) collective-permute-start(bf16[528,1024]{1,0:T(8,128)(2,1)} %get-tuple-element.39.refs_0_), channel_id=1, source_target_pairs={{0,8},{16,80},{4,12},{20,84},{8,0},{24,88},{12,4},{28,92},{32,40},... | collective-permute-start | bytes 3244040 | tf_op jit(solution)/shard_map/ppermute | solution.py:278
  25.4 35.3 %collective-permute-start.8 = (bf16[528,1024]{1,0:T(8,128)(2,1)}, bf16[528,1024]{1,0:T(8,128)(2,1)S(1)}, u32[]{:S(2)}, u32[]{:S(2)}) collective-permute-start(bf16[528,1024]{1,0:T(8,128)(2,1)} %get-tuple-element.39.refs_0_), channel_id=1, source_target_pairs={{0,12},{16,112},{4,0},{20,116},{8,4},{24,120},{12,8},{28,124},{32,... | collective-permute-start | bytes 3244040 | tf_op jit(solution)/shard_map/ppermute | solution.py:278
  26.8 34.0 %collective-permute-start.7 = (bf16[528,1024]{1,0:T(8,128)(2,1)}, bf16[528,1024]{1,0:T(8,128)(2,1)S(1)}, u32[]{:S(2)}, u32[]{:S(2)}) collective-permute-start(bf16[528,1024]{1,0:T(8,128)(2,1)} %get-tuple-element.39.refs_0_), channel_id=1, source_target_pairs={{0,4},{16,48},{4,8},{20,52},{8,12},{24,56},{12,0},{28,60},{32,36},... | collective-permute-start | bytes 3244040 | tf_op jit(solution)/shard_map/ppermute | solution.py:278
  27.4 26.1 %collective-permute-start.5 = (bf16[160,1024]{1,0:T(8,128)(2,1)}, bf16[160,1024]{1,0:T(8,128)(2,1)}, u32[]{:S(2)}, u32[]{:S(2)}) collective-permute-start(bf16[160,1024]{1,0:T(8,128)(2,1)} %get-tuple-element.37), channel_id=1, source_target_pairs={{0,129},{128,2},{1,130},{129,3},{2,131},{130,0},{3,128},{131,1},{4... | collective-permute-start | bytes 983048 | tf_op jit(solution)/shard_map/ppermute | solution.py:268
  27.4 29.3 %collective-permute-start.6 = (bf16[160,1024]{1,0:T(8,128)(2,1)}, bf16[160,1024]{1,0:T(8,128)(2,1)}, u32[]{:S(2)}, u32[]{:S(2)}) collective-permute-start(bf16[160,1024]{1,0:T(8,128)(2,1)} %get-tuple-element.38), channel_id=1, source_target_pairs={{0,130},{128,3},{1,131},{129,0},{2,128},{130,1},{3,129},{131,2},{4... | collective-permute-start | bytes 983048 | tf_op jit(solution)/shard_map/ppermute | solution.py:268
  34.5 22.3 %all-to-all-start = ((f32[256,1,128]{2,1,0:T(1,128)}), f32[256,1,128]{2,1,0:T(1,128)}, u32[]{:S(2)}, u32[]{:S(2)}) async-start(f32[256,1,128]{2,1,0:T(1,128)} %broadcast_in_dim.3), calls=%async_computation | async-start | bytes 262144 | tf_op jit(solution)/shard_map/all_to_all | solution.py:297
  53.5 11.1 %collective-permute-start.13 = (bf16[528,1024]{1,0:T(8,128)(2,1)}, bf16[528,1024]{1,0:T(8,128)(2,1)}, u32[]{:S(2)}, u32[]{:S(2)}) collective-permute-start(bf16[528,1024]{1,0:T(8,128)(2,1)} %get-tuple-element.39.refs_0_), channel_id=1, source_target_pairs={{0,16},{16,0},{1,17},{17,1},{2,18},{18,2},{3,19},{19,3},{4,20},{20... | collective-permute-start | bytes 3244040 | tf_op jit(solution)/shard_map/ppermute | solution.py:286
  56.8 0.9 copy-start.4
  60.8 8.3 %collective-permute-start.10 = (bf16[528,1024]{1,0:T(8,128)(2,1)S(1)}, bf16[528,1024]{1,0:T(8,128)(2,1)S(1)}, u32[]{:S(2)}, u32[]{:S(2)}) collective-permute-start(bf16[528,1024]{1,0:T(8,128)(2,1)S(1)} %get-tuple-element.42.refs_0_), channel_id=1, source_target_pairs={{0,16},{16,0},{1,17},{17,1},{2,18},{18,2},{3,19},{19,3},{4,20},{20... | collective-permute-start | bytes 3244040 | tf_op jit(solution)/shard_map/ppermute | solution.py:286
  60.9 8.2 %collective-permute-start.11 = (bf16[528,1024]{1,0:T(8,128)(2,1)S(1)}, bf16[528,1024]{1,0:T(8,128)(2,1)S(1)}, u32[]{:S(2)}, u32[]{:S(2)}) collective-permute-start(bf16[528,1024]{1,0:T(8,128)(2,1)S(1)} %get-tuple-element.43.refs_1_), channel_id=1, source_target_pairs={{0,16},{16,0},{1,17},{17,1},{2,18},{18,2},{3,19},{19,3},{4,20},{20... | collective-permute-start | bytes 3244040 | tf_op jit(solution)/shard_map/ppermute | solution.py:286
  61.4 7.7 %collective-permute-start.12 = (bf16[528,1024]{1,0:T(8,128)(2,1)S(1)}, bf16[528,1024]{1,0:T(8,128)(2,1)S(1)}, u32[]{:S(2)}, u32[]{:S(2)}) collective-permute-start(bf16[528,1024]{1,0:T(8,128)(2,1)S(1)} %get-tuple-element.44.refs_0_), channel_id=1, source_target_pairs={{0,16},{16,0},{1,17},{17,1},{2,18},{18,2},{3,19},{19,3},{4,20},{20... | collective-permute-start | bytes 3244040 | tf_op jit(solution)/shard_map/ppermute | solution.py:286
  74.5 16.7 %collective-permute-start.14 = (s16[128,1152]{1,0:T(8,128)(2,1)S(1)}, s16[128,1152]{1,0:T(8,128)(2,1)S(1)}, u32[]{:S(2)}, u32[]{:S(2)}) collective-permute-start(s16[128,1152]{1,0:T(8,128)(2,1)S(1)} %get-tuple-element.64), channel_id=1, source_target_pairs={{0,128},{128,1},{1,129},{129,2},{2,130},{130,3},{3,131},{131,0},{4... | collective-permute-start | bytes 884744 | tf_op jit(solution)/shard_map/ppermute | solution.py:268
  78.5 12.6 %collective-permute-start.15 = (s16[128,1152]{1,0:T(8,128)(2,1)S(1)}, s16[128,1152]{1,0:T(8,128)(2,1)S(1)}, u32[]{:S(2)}, u32[]{:S(2)}) collective-permute-start(s16[128,1152]{1,0:T(8,128)(2,1)S(1)} %get-tuple-element.65), channel_id=1, source_target_pairs={{0,131},{128,0},{1,128},{129,1},{2,129},{130,2},{3,130},{131,3},{4... | collective-permute-start | bytes 884744 | tf_op jit(solution)/shard_map/ppermute | solution.py:268
  78.5 11.4 %collective-permute-start.16 = (s16[32,1152]{1,0:T(8,128)(2,1)S(1)}, s16[32,1152]{1,0:T(8,128)(2,1)S(1)}, u32[]{:S(2)}, u32[]{:S(2)}) collective-permute-start(s16[32,1152]{1,0:T(8,128)(2,1)S(1)} %get-tuple-element.66), channel_id=1, source_target_pairs={{0,1},{128,129},{1,2},{129,130},{2,3},{130,131},{3,0},{131,128},{4... | collective-permute-start | bytes 221192 | tf_op jit(solution)/shard_map/ppermute | solution.py:268
  81.0 10.1 %collective-permute-start.17 = (s16[32,1152]{1,0:T(8,128)(2,1)S(1)}, s16[32,1152]{1,0:T(8,128)(2,1)S(1)}, u32[]{:S(2)}, u32[]{:S(2)}) collective-permute-start(s16[32,1152]{1,0:T(8,128)(2,1)S(1)} %get-tuple-element.67), channel_id=1, source_target_pairs={{0,3},{128,131},{1,0},{129,128},{2,1},{130,129},{3,2},{131,130},{4... | collective-permute-start | bytes 221192 | tf_op jit(solution)/shard_map/ppermute | solution.py:268
  91.7 9.3 %collective-permute-start.18 = (s16[64,1152]{1,0:T(8,128)(2,1)S(1)}, s16[64,1152]{1,0:T(8,128)(2,1)S(1)}, u32[]{:S(2)}, u32[]{:S(2)}) collective-permute-start(s16[64,1152]{1,0:T(8,128)(2,1)S(1)} %get-tuple-element.68), channel_id=1, source_target_pairs={{0,1},{128,129},{1,2},{129,130},{2,3},{130,131},{3,0},{131,128},{4... | collective-permute-start | bytes 442376 | tf_op jit(solution)/shard_map/ppermute | solution.py:268
  92.5 8.5 %collective-permute-start.19 = (s16[64,1152]{1,0:T(8,128)(2,1)S(1)}, s16[64,1152]{1,0:T(8,128)(2,1)S(1)}, u32[]{:S(2)}, u32[]{:S(2)}) collective-permute-start(s16[64,1152]{1,0:T(8,128)(2,1)S(1)} %get-tuple-element.69), channel_id=1, source_target_pairs={{0,3},{128,131},{1,0},{129,128},{2,1},{130,129},{3,2},{131,130},{4... | collective-permute-start | bytes 442376 | tf_op jit(solution)/shard_map/ppermute | solution.py:268

commit v7 on v6

--- a/solution.py
+++ b/solution.py
@@ -10,6 +10,7 @@
 
 AXES = ("zl", "x", "c", "y", "zh")
 RING = ("zl", "zh")
+CHIPS = ("zl", "x", "y", "zh")
 PLANE = ("x", "c", "y")
 LANES = 128
 META = 16
@@ -61,8 +62,9 @@
     return jnp.concatenate([a, b], axis=1)
 
 
-def pack_block(pool, targets, counts, block):
+def pack_block(pool, targets, counts, block, chosen):
     height = pool.shape[0]
+    chosen[...] = jnp.full(chosen.shape, jnp.sum(counts[...].astype(F32)), F32)
     block[:height, :] = pool[...]
     block[height : 2 * height, :] = targets[...]
     norms = along_lanes(jnp.concatenate([square_norms(pool[...]), square_norms(targets[...])], axis=0))
@@ -161,8 +163,8 @@
     add_columns(panel, norms, pieces, old, (pp, tp), (pm, tm), weights, rows)
 
 
-def terms(target_count, panel, pp, tp, pm, tm, total, part):
-    weight = total[:1, :1]
+def terms(target_count, panel, pp, tp, pm, tm, total, other_total, part):
+    weight = total[:1, :1] + other_total[:1, :1]
     pool_mass = jnp.sum(pm[part, :], axis=1, keepdims=True)
     target_mass = jnp.sum(tm[part, :], axis=1, keepdims=True)
     own = panel[part, :].astype(F32)
@@ -174,7 +176,7 @@
 
 
 def far_terms(target_count, height, *refs):
-    inputs, (up, down, up_half, down_half) = refs[:6], refs[6:]
+    inputs, (up, down, up_half, down_half) = refs[:7], refs[7:]
     for i in range(4):
         code = encode(*terms(target_count, *inputs, slice(i * height, (i + 1) * height)))
         (up, down)[i // 2][i % 2 * height : (i % 2 + 1) * height, :] = code
@@ -184,7 +186,7 @@
 
 
 def near_terms(target_count, height, *refs):
-    inputs, (gradient, proof) = refs[:6], refs[6:]
+    inputs, (gradient, proof) = refs[:7], refs[7:]
     for i in range(5, 8):
         part = slice((i - 5) * height, (i - 4) * height)
         gradient[part, :], small = terms(target_count, *inputs, slice(i * height, (i + 1) * height))
@@ -292,12 +294,13 @@
     rows = ring * height
     target_count = float(height * lax.axis_size(AXES))
 
-    devices = lax.axis_size(AXES)
-    chosen = jnp.broadcast_to(jnp.sum(counts).astype(F32), (devices, 1, LANES))
-    chosen = lax.all_to_all(chosen, AXES, split_axis=0, concat_axis=0, tiled=True)
-    block = in_vmem(pack_block, "pack_block", shape((2 * height + META, width), BF16), limit=56)(
-        pool, targets, counts.reshape(1, height)
-    )
+    block, chosen = in_vmem(
+        pack_block,
+        "pack_block",
+        (shape((2 * height + META, width), BF16), shape((lax.axis_size(CHIPS), 1, LANES), F32)),
+        limit=56,
+    )(pool, targets, counts.reshape(1, height))
+    chosen = lax.all_to_all(chosen, CHIPS, split_axis=0, concat_axis=0, tiled=True)
     blocks = line(block, 0)
     below, above = up_the_ring(pool, 1), up_the_ring(pool, ring - 1)
     pair = shape((5 * height // 2, width), BF16)
@@ -306,7 +309,6 @@
     )(*blocks, pool, below, above)
     pieces = line(piece, 1)
     pairs = up_the_ring(up_pair, 3), up_the_ring(down_pair, ring - 3)
-    others = [other_core(piece)]
 
     size = height * len(blocks)
     sums = (shape((rows, width), F32),) * 2 + (shape((rows, LANES), F32),) * 2
@@ -333,12 +335,13 @@
         (shape((rows, width), BF16), shape((rows, LANES), F32), shape((8, LANES), F32), *sums),
         {},
     )
-    pieces[1:] = handed_on(pieces[1:], norms)
-    others += [other_core(p) for p in pieces[1:]]
+    totals = total, other_core(total)
+    pieces = handed_on(pieces, norms)
+    others = [other_core(p) for p in pieces]
     for some in (pieces[1:3], (pieces[3], others[0]), others[1:]):
         state = more(some, state)
 
-    inputs = panel, *state, total
+    inputs = panel, *state, *totals
     whole, half = (shape((n, width + LANES), jnp.int16) for n in (2 * height, height // 2))
     up, down, up_half, down_half = in_vmem(
         functools.partial(far_terms, target_count, height),

time: 104 us -> 97.1 us (0.934)
  blocking collectives: 0 us -> 24.7 us
  waiting for transfers between devices: 32.1 us -> 16.6 us
  starting transfers between devices: 43.2 us -> 34.3 us
  Pallas kernels: 21.2 us -> 17.3 us
  local copies, waits for them, and re-layouts: 3.54 us -> 1.86 us
    all_to_all x0 -> x1, blocking collectives: none -> 24.7 us  [on_device(): lax.all_to_all(chosen, CHIPS, split_axis=0, concat_axis=0, tiled=True)]
    ppermute x10, waiting for transfers between devices: 28.8 us -> 16.5 us  [up_the_ring(): lax.ppermute(x, RING, [(place(i), place((i + step) % ring)) for i in rang...]
    all_to_all x1 -> x0, starting transfers between devices: 9.81 us -> none  [on_device(): lax.all_to_all(chosen, AXES, split_axis=0, concat_axis=0, tiled=True)]
    pallas_call x10, Pallas kernels: 21.2 us -> 17.3 us  [call(): pl.pallas_call(body, out_shape=out_shape, in_specs=[spec] * len(args), ou...]
    all_to_all x1 -> x0, waiting for transfers between devices: 3.26 us -> none  [on_device(): lax.all_to_all(chosen, AXES, split_axis=0, concat_axis=0, tiled=True)]
    unnamed x12 -> x6, local copies, waits for them, and re-layouts: 2.82 us -> 1.86 us
  transfers between devices with their start and end apart: 21 -> 21, of which waited for: 7 -> 4; matrix products, arithmetic and copies ran while one was open for 1% -> 0% of each run, Pallas kernels for 11% -> 13%
where the time goes in v7:
time: 97.1 us; the launch traced here: 95.6 us
  starting transfers between devices  34.3 us (35%)
  blocking collectives  24.7 us (25%)
  Pallas kernels  17.3 us (18%)
  waiting for transfers between devices  16.6 us (17%)
  local copies, waits for them, and re-layouts  1.86 us (2%)
    all_to_all x1, blocking collectives, on_device(): lax.all_to_all(chosen, CHIPS, split_axis=0, concat_axis=0, tiled=True)  24.7 us
    ppermute x10, starting transfers between devices, up_the_ring(): lax.ppermute(x, RING, [(place(i), place((i + step) % ring)) for i in rang...  23.6 us
    pallas_call x10, Pallas kernels, call(): pl.pallas_call(body, out_shape=out_shape, in_specs=[spec] * len(args), ou...  17.3 us
    ppermute x10, waiting for transfers between devices, up_the_ring(): lax.ppermute(x, RING, [(place(i), place((i + step) % ring)) for i in rang...  16.5 us
    ppermute x6, starting transfers between devices, along_line(): return lax.ppermute(x, PLANE, pairs)  9.45 us
  transfers between devices with their start and end apart: 21, of which 4 were waited for; matrix products, arithmetic and copies ran while one was open for 0% of the time, Pallas kernels for 13%

profile of v7, /device:TPU:8, one launch (start us, length us, event | category | flops | bytes accessed | tf_op | source)
XLA Modules:
  0.0 95.6 jit_solution(7814676337592771488)
XLA Ops:
  0.6 2.0 %pack_block.1 = (bf16[144,1024]{1,0:T(8,128)(2,1)}, f32[128,1,128]{2,1,0:T(1,128)}) custom-call(bf16[64,1024]{1,0:T(8,128)(2,1)} %own.1, bf16[64,1024]{1,0:T(8,128)(2,1)} %targets.1, s32[1,64]{1,0:T(1,128)} %bitcast.2), custom_call_target="tpu_custom_call" | custom-call | bytes 1048576 | tf_op jit(solution)/shard_map/pack_block/pallas_call | solution.py:30
  2.6 1.5 %collective-permute-start.2 = (bf16[144,1024]{1,0:T(8,128)(2,1)}, bf16[144,1024]{1,0:T(8,128)(2,1)S(1)}, u32[]{:S(2)}, u32[]{:S(2)}) collective-permute-start(bf16[144,1024]{1,0:T(8,128)(2,1)} %get-tuple-element.40.refs_0_), channel_id=1, source_target_pairs={{0,32},{16,20},{4,36},{20,24},{8,40},{24,28},{12,44},{28,16},{32,6... | collective-permute-start | bytes 884744 | tf_op jit(solution)/shard_map/ppermute | solution.py:280
  4.1 1.7 %collective-permute-start.3 = (bf16[144,1024]{1,0:T(8,128)(2,1)}, bf16[144,1024]{1,0:T(8,128)(2,1)S(1)}, u32[]{:S(2)}, u32[]{:S(2)}) collective-permute-start(bf16[144,1024]{1,0:T(8,128)(2,1)} %get-tuple-element.40.refs_0_), channel_id=1, source_target_pairs={{0,96},{16,28},{4,100},{20,16},{8,104},{24,20},{12,108},{28,24},{3... | collective-permute-start | bytes 884744 | tf_op jit(solution)/shard_map/ppermute | solution.py:280
  5.8 1.8 %collective-permute-start.4 = (bf16[144,1024]{1,0:T(8,128)(2,1)}, bf16[144,1024]{1,0:T(8,128)(2,1)S(1)}, u32[]{:S(2)}, u32[]{:S(2)}) collective-permute-start(bf16[144,1024]{1,0:T(8,128)(2,1)} %get-tuple-element.40.refs_0_), channel_id=1, source_target_pairs={{0,64},{16,24},{4,68},{20,28},{8,72},{24,16},{12,76},{28,20},{32,9... | collective-permute-start | bytes 884744 | tf_op jit(solution)/shard_map/ppermute | solution.py:280
  7.7 1.9 %collective-permute-start = (bf16[64,1024]{1,0:T(8,128)(2,1)}, bf16[64,1024]{1,0:T(8,128)(2,1)S(1)}, u32[]{:S(2)}, u32[]{:S(2)}) collective-permute-start(bf16[64,1024]{1,0:T(8,128)(2,1)} %own.1), channel_id=1, source_target_pairs={{0,128},{128,1},{1,129},{129,2},{2,130},{130,3},{3,131},{131,0},{4... | collective-permute-start | bytes 393224 | tf_op jit(solution)/shard_map/ppermute | solution.py:270
  9.6 3.9 %collective-permute-start.1 = (bf16[64,1024]{1,0:T(8,128)(2,1)}, bf16[64,1024]{1,0:T(8,128)(2,1)S(1)}, u32[]{:S(2)}, u32[]{:S(2)}) collective-permute-start(bf16[64,1024]{1,0:T(8,128)(2,1)} %own.1), channel_id=1, source_target_pairs={{0,131},{128,0},{1,128},{129,1},{2,129},{130,2},{3,130},{131,3},{4... | collective-permute-start | bytes 393224 | tf_op jit(solution)/shard_map/ppermute | solution.py:270
  13.5 3.2 %collective-permute-done.refs_5_.below = bf16[64,1024]{1,0:T(8,128)(2,1)S(1)} collective-permute-done((bf16[64,1024]{1,0:T(8,128)(2,1)}, bf16[64,1024]{1,0:T(8,128)(2,1)S(1)}, u32[]{:S(2)}, u32[]{:S(2)}) %collective-permute-start) | collective-permute-done | bytes 131104 | tf_op jit(solution)/shard_map/ppermute | solution.py:270
  16.7 0.9 copy-done
  17.6 1.0 %copy-done.1 = bf16[144,1024]{1,0:T(8,128)(2,1)S(1)} copy-done((bf16[144,1024]{1,0:T(8,128)(2,1)S(1)}, bf16[144,1024]{1,0:T(8,128)(2,1)}, u32[]{:S(2)}) %copy-start.1) | copy-done | bytes 294936
  18.7 1.7 %collective-permute-start.7 = (bf16[528,1024]{1,0:T(8,128)(2,1)S(1)}, bf16[528,1024]{1,0:T(8,128)(2,1)S(1)}, u32[]{:S(2)}, u32[]{:S(2)}) collective-permute-start(bf16[528,1024]{1,0:T(8,128)(2,1)S(1)} %get-tuple-element.44.refs_0_), channel_id=1, source_target_pairs={{0,4},{16,48},{4,8},{20,52},{8,12},{24,56},{12,0},{28,60},{32,36},... | collective-permute-start | bytes 3244040 | tf_op jit(solution)/shard_map/ppermute | solution.py:280
  20.3 0.4 collective-permute-start.8
  20.8 2.3 %collective-permute-start.9 = (bf16[528,1024]{1,0:T(8,128)(2,1)S(1)}, bf16[528,1024]{1,0:T(8,128)(2,1)S(1)}, u32[]{:S(2)}, u32[]{:S(2)}) collective-permute-start(bf16[528,1024]{1,0:T(8,128)(2,1)S(1)} %get-tuple-element.44.refs_0_), channel_id=1, source_target_pairs={{0,8},{16,80},{4,12},{20,84},{8,0},{24,88},{12,4},{28,92},{32,40},... | collective-permute-start | bytes 3244040 | tf_op jit(solution)/shard_map/ppermute | solution.py:280
  23.1 5.1 %collective-permute-start.5 = (bf16[160,1024]{1,0:T(8,128)(2,1)S(1)}, bf16[160,1024]{1,0:T(8,128)(2,1)S(1)}, u32[]{:S(2)}, u32[]{:S(2)}) collective-permute-start(bf16[160,1024]{1,0:T(8,128)(2,1)S(1)} %get-tuple-element.41), channel_id=1, source_target_pairs={{0,129},{128,2},{1,130},{129,3},{2,131},{130,0},{3,128},{131,1},{4... | collective-permute-start | bytes 983048 | tf_op jit(solution)/shard_map/ppermute | solution.py:270
  28.2 24.7 %all_to_all.5.chosen = f32[128,1,128]{2,1,0:T(1,128)S(1)} all-to-all(f32[128,1,128]{2,1,0:T(1,128)S(1)} %copy-done.2), channel_id=1, replica_groups=mesh['zl'=2,'x'=4,'c'=2,'y'=4,'zh'=4] {'zl','x','y','zh'}, dimensions={0} | all-to-all | bytes 131072 | tf_op jit(solution)/shard_map/all_to_all | solution.py:303
  53.0 1.5 %first_columns.1 = (bf16[512,1024]{1,0:T(8,128)(2,1)S(1)}, f32[512,128]{1,0:T(8,128)S(1)}, f32[8,128]{1,0:T(8,128)S(1)}, f32[512,1024]{1,0:T(8,128)S(1)}, f32[51...) custom-call(bf16[64,1024]{1,0:T(8,128)(2,1)S(1)} %copy-done, ...), custom_call_target="tpu_custom_call" | custom-call | flops 1073741824 | bytes 1048576 | tf_op jit(solution)/shard_map/first_columns/pallas_call | solution.py:30
  54.6 0.5 collective-permute-start.10
  55.2 0.4 collective-permute-start.12
  55.7 3.2 %more_columns.3 = (f32[512,1024]{1,0:T(8,128)S(1)}, f32[512,1024]{1,0:T(8,128)S(1)}, f32[512,128]{1,0:T(8,128)S(1)}, f32[512,128]{1,0:T(8,128)S(1)}) custom-call(bf16[512,1024]{1,0:T(8,128)(2,1)S(1)} %get-tuple-element.45.panel.refs_0_, ...), custom_call_target="tpu_custom_call", output_to_operand_aliasing={{0}: (4, {}), {1}: (5, {}), {2}: (6, {}), {3}: (7, {})} | custom-call | flops 2147483648 | bytes 1048576 | tf_op jit(solution)/shard_map/more_columns/pallas_call | solution.py:30
  59.0 3.2 %more_columns.4 = (f32[512,1024]{1,0:T(8,128)S(1)}, f32[512,1024]{1,0:T(8,128)S(1)}, f32[512,128]{1,0:T(8,128)S(1)}, f32[512,128]{1,0:T(8,128)S(1)}) custom-call(bf16[512,1024]{1,0:T(8,128)(2,1)S(1)} %get-tuple-element.45.panel.refs_0_, ...), custom_call_target="tpu_custom_call", output_to_operand_aliasing={{0}: (4, {}), {1}: (5, {}), {2}: (6, {}), {3}: (7, {})} | custom-call | flops 2147483648 | bytes 1048576 | tf_op jit(solution)/shard_map/more_columns/pallas_call | solution.py:30
  62.2 4.4 %more_columns.5 = (f32[512,1024]{1,0:T(8,128)S(1)}, f32[512,1024]{1,0:T(8,128)S(1)}, f32[512,128]{1,0:T(8,128)S(1)}, f32[512,128]{1,0:T(8,128)S(1)}) custom-call(bf16[512,1024]{1,0:T(8,128)(2,1)S(1)} %get-tuple-element.45.panel.refs_0_, ...), custom_call_target="tpu_custom_call", output_to_operand_aliasing={{0}: (5, {}), {1}: (6, {}), {2}: (7, {}), {3}: (8, {})} | custom-call | flops 3221225472 | bytes 1048576 | tf_op jit(solution)/shard_map/more_columns/pallas_call | solution.py:30
  66.5 1.0 %far_terms.1 = (s16[128,1152]{1,0:T(8,128)(2,1)S(1)}, s16[128,1152]{1,0:T(8,128)(2,1)S(1)}, s16[32,1152]{1,0:T(8,128)(2,1)S(1)}, s16[32,1152]{1,0:T(8,128)(2,1)S(1)}) custom-call(bf16[512,1024]{1,0:T(8,128)(2,1)S(1)} %get-tuple-element.45.panel.refs_0_, f32[512,1024]{1,0:T(8,128)S(1)} %get-tuple-element.63.refs_1_, ...), custom_call_target="tpu_custom_call" | custom-call | bytes 1048576 | tf_op jit(solution)/shard_map/far_terms/pallas_call | solution.py:30
  67.5 4.3 %collective-permute-start.15 = (s16[128,1152]{1,0:T(8,128)(2,1)S(1)}, s16[128,1152]{1,0:T(8,128)(2,1)S(1)}, u32[]{:S(2)}, u32[]{:S(2)}) collective-permute-start(s16[128,1152]{1,0:T(8,128)(2,1)S(1)} %get-tuple-element.70), channel_id=1, source_target_pairs={{0,128},{128,1},{1,129},{129,2},{2,130},{130,3},{3,131},{131,0},{4... | collective-permute-start | bytes 884744 | tf_op jit(solution)/shard_map/ppermute | solution.py:270
  71.8 2.2 %collective-permute-start.17 = (s16[32,1152]{1,0:T(8,128)(2,1)S(1)}, s16[32,1152]{1,0:T(8,128)(2,1)S(1)}, u32[]{:S(2)}, u32[]{:S(2)}) collective-permute-start(s16[32,1152]{1,0:T(8,128)(2,1)S(1)} %get-tuple-element.72), channel_id=1, source_target_pairs={{0,1},{128,129},{1,2},{129,130},{2,3},{130,131},{3,0},{131,128},{4... | collective-permute-start | bytes 221192 | tf_op jit(solution)/shard_map/ppermute | solution.py:270
  74.0 1.9 %collective-permute-start.18 = (s16[32,1152]{1,0:T(8,128)(2,1)S(1)}, s16[32,1152]{1,0:T(8,128)(2,1)S(1)}, u32[]{:S(2)}, u32[]{:S(2)}) collective-permute-start(s16[32,1152]{1,0:T(8,128)(2,1)S(1)} %get-tuple-element.73), channel_id=1, source_target_pairs={{0,3},{128,131},{1,0},{129,128},{2,1},{130,129},{3,2},{131,130},{4... | collective-permute-start | bytes 221192 | tf_op jit(solution)/shard_map/ppermute | solution.py:270
  75.9 0.4 near_terms.1
  76.3 5.5 %collective-permute-done.17.half_below = s16[32,1152]{1,0:T(8,128)(2,1)S(1)} collective-permute-done((s16[32,1152]{1,0:T(8,128)(2,1)S(1)}, s16[32,1152]{1,0:T(8,128)(2,1)S(1)}, u32[]{:S(2)}, u32[]{:S(2)}) %collective-permute-start.17) | collective-permute-done | bytes 73760 | tf_op jit(solution)/shard_map/ppermute | solution.py:270
  81.8 2.4 %collective-permute-done.18.half_above = s16[32,1152]{1,0:T(8,128)(2,1)S(1)} collective-permute-done((s16[32,1152]{1,0:T(8,128)(2,1)S(1)}, s16[32,1152]{1,0:T(8,128)(2,1)S(1)}, u32[]{:S(2)}, u32[]{:S(2)}) %collective-permute-start.18) | collective-permute-done | bytes 73760 | tf_op jit(solution)/shard_map/ppermute | solution.py:270
  84.3 0.5 pass_on.1
  84.8 2.2 %collective-permute-start.19 = (s16[64,1152]{1,0:T(8,128)(2,1)S(1)}, s16[64,1152]{1,0:T(8,128)(2,1)S(1)}, u32[]{:S(2)}, u32[]{:S(2)}) collective-permute-start(s16[64,1152]{1,0:T(8,128)(2,1)S(1)} %get-tuple-element.74), channel_id=1, source_target_pairs={{0,1},{128,129},{1,2},{129,130},{2,3},{130,131},{3,0},{131,128},{4... | collective-permute-start | bytes 442376 | tf_op jit(solution)/shard_map/ppermute | solution.py:270
  87.0 2.0 %collective-permute-start.20 = (s16[64,1152]{1,0:T(8,128)(2,1)S(1)}, s16[64,1152]{1,0:T(8,128)(2,1)S(1)}, u32[]{:S(2)}, u32[]{:S(2)}) collective-permute-start(s16[64,1152]{1,0:T(8,128)(2,1)S(1)} %get-tuple-element.75), channel_id=1, source_target_pairs={{0,3},{128,131},{1,0},{129,128},{2,1},{130,129},{3,2},{131,130},{4... | collective-permute-start | bytes 442376 | tf_op jit(solution)/shard_map/ppermute | solution.py:270
  89.0 5.5 %collective-permute-done.19.far_below = s16[64,1152]{1,0:T(8,128)(2,1)S(1)} collective-permute-done((s16[64,1152]{1,0:T(8,128)(2,1)S(1)}, s16[64,1152]{1,0:T(8,128)(2,1)S(1)}, u32[]{:S(2)}, u32[]{:S(2)}) %collective-permute-start.19) | collective-permute-done | bytes 147488 | tf_op jit(solution)/shard_map/ppermute | solution.py:270
  94.5 1.1 %add_up.1 = (f32[1,64]{1,0:T(1,128)}, f32[64,1024]{1,0:T(8,128)}) custom-call(f32[192,1024]{1,0:T(8,128)S(1)} %get-tuple-element.68.gradient, f32[192,128]{1,0:T(8,128)S(1)} %get-tuple-element.69.proof, s16[128,1152]{1,0:T(8,128)(2,1)S(1)} %collective-permute-done.15.from_below, s16[128,1152]{1,0:T(8,128)(2,1)S(1)} %collective-permute-done.16.from_above, ...), custom_call_target="tpu_custom_call" | custom-call | bytes 1048576 | tf_op jit(solution)/shard_map/add_up/pallas_call | solution.py:30
  (28 shorter events, 0.5 us)
Async XLA Ops:
  2.6 14.1 %collective-permute-start.2 = (bf16[144,1024]{1,0:T(8,128)(2,1)}, bf16[144,1024]{1,0:T(8,128)(2,1)S(1)}, u32[]{:S(2)}, u32[]{:S(2)}) collective-permute-start(bf16[144,1024]{1,0:T(8,128)(2,1)} %get-tuple-element.40.refs_0_), channel_id=1, source_target_pairs={{0,32},{16,20},{4,36},{20,24},{8,40},{24,28},{12,44},{28,16},{32,6... | collective-permute-start | bytes 884744 | tf_op jit(solution)/shard_map/ppermute | solution.py:280
  4.1 12.6 %collective-permute-start.3 = (bf16[144,1024]{1,0:T(8,128)(2,1)}, bf16[144,1024]{1,0:T(8,128)(2,1)S(1)}, u32[]{:S(2)}, u32[]{:S(2)}) collective-permute-start(bf16[144,1024]{1,0:T(8,128)(2,1)} %get-tuple-element.40.refs_0_), channel_id=1, source_target_pairs={{0,96},{16,28},{4,100},{20,16},{8,104},{24,20},{12,108},{28,24},{3... | collective-permute-start | bytes 884744 | tf_op jit(solution)/shard_map/ppermute | solution.py:280
  5.8 10.8 %collective-permute-start.4 = (bf16[144,1024]{1,0:T(8,128)(2,1)}, bf16[144,1024]{1,0:T(8,128)(2,1)S(1)}, u32[]{:S(2)}, u32[]{:S(2)}) collective-permute-start(bf16[144,1024]{1,0:T(8,128)(2,1)} %get-tuple-element.40.refs_0_), channel_id=1, source_target_pairs={{0,64},{16,24},{4,68},{20,28},{8,72},{24,16},{12,76},{28,20},{32,9... | collective-permute-start | bytes 884744 | tf_op jit(solution)/shard_map/ppermute | solution.py:280
  7.7 9.0 %collective-permute-start = (bf16[64,1024]{1,0:T(8,128)(2,1)}, bf16[64,1024]{1,0:T(8,128)(2,1)S(1)}, u32[]{:S(2)}, u32[]{:S(2)}) collective-permute-start(bf16[64,1024]{1,0:T(8,128)(2,1)} %own.1), channel_id=1, source_target_pairs={{0,128},{128,1},{1,129},{129,2},{2,130},{130,3},{3,131},{131,0},{4... | collective-permute-start | bytes 393224 | tf_op jit(solution)/shard_map/ppermute | solution.py:270
  9.6 7.1 %collective-permute-start.1 = (bf16[64,1024]{1,0:T(8,128)(2,1)}, bf16[64,1024]{1,0:T(8,128)(2,1)S(1)}, u32[]{:S(2)}, u32[]{:S(2)}) collective-permute-start(bf16[64,1024]{1,0:T(8,128)(2,1)} %own.1), channel_id=1, source_target_pairs={{0,131},{128,0},{1,128},{129,1},{2,129},{130,2},{3,130},{131,3},{4... | collective-permute-start | bytes 393224 | tf_op jit(solution)/shard_map/ppermute | solution.py:270
  16.7 0.9 copy-start
  17.6 1.0 %copy-start.1 = (bf16[144,1024]{1,0:T(8,128)(2,1)S(1)}, bf16[144,1024]{1,0:T(8,128)(2,1)}, u32[]{:S(2)}) copy-start(bf16[144,1024]{1,0:T(8,128)(2,1)} %get-tuple-element.40.refs_0_) | copy-start | bytes 884740
  18.6 9.6 %copy-start.2 = (f32[128,1,128]{2,1,0:T(1,128)S(1)}, f32[128,1,128]{2,1,0:T(1,128)}, u32[]{:S(2)}) copy-start(f32[128,1,128]{2,1,0:T(1,128)} %get-tuple-element.43) | copy-start | bytes 196612
  18.7 35.8 %collective-permute-start.7 = (bf16[528,1024]{1,0:T(8,128)(2,1)S(1)}, bf16[528,1024]{1,0:T(8,128)(2,1)S(1)}, u32[]{:S(2)}, u32[]{:S(2)}) collective-permute-start(bf16[528,1024]{1,0:T(8,128)(2,1)S(1)} %get-tuple-element.44.refs_0_), channel_id=1, source_target_pairs={{0,4},{16,48},{4,8},{20,52},{8,12},{24,56},{12,0},{28,60},{32,36},... | collective-permute-start | bytes 3244040 | tf_op jit(solution)/shard_map/ppermute | solution.py:280
  20.3 34.2 %collective-permute-start.8 = (bf16[528,1024]{1,0:T(8,128)(2,1)S(1)}, bf16[528,1024]{1,0:T(8,128)(2,1)S(1)}, u32[]{:S(2)}, u32[]{:S(2)}) collective-permute-start(bf16[528,1024]{1,0:T(8,128)(2,1)S(1)} %get-tuple-element.44.refs_0_), channel_id=1, source_target_pairs={{0,12},{16,112},{4,0},{20,116},{8,4},{24,120},{12,8},{28,124},{32,... | collective-permute-start | bytes 3244040 | tf_op jit(solution)/shard_map/ppermute | solution.py:280
  20.8 33.7 %collective-permute-start.9 = (bf16[528,1024]{1,0:T(8,128)(2,1)S(1)}, bf16[528,1024]{1,0:T(8,128)(2,1)S(1)}, u32[]{:S(2)}, u32[]{:S(2)}) collective-permute-start(bf16[528,1024]{1,0:T(8,128)(2,1)S(1)} %get-tuple-element.44.refs_0_), channel_id=1, source_target_pairs={{0,8},{16,80},{4,12},{20,84},{8,0},{24,88},{12,4},{28,92},{32,40},... | collective-permute-start | bytes 3244040 | tf_op jit(solution)/shard_map/ppermute | solution.py:280
  23.1 29.9 %collective-permute-start.5 = (bf16[160,1024]{1,0:T(8,128)(2,1)S(1)}, bf16[160,1024]{1,0:T(8,128)(2,1)S(1)}, u32[]{:S(2)}, u32[]{:S(2)}) collective-permute-start(bf16[160,1024]{1,0:T(8,128)(2,1)S(1)} %get-tuple-element.41), channel_id=1, source_target_pairs={{0,129},{128,2},{1,130},{129,3},{2,131},{130,0},{3,128},{131,1},{4... | collective-permute-start | bytes 983048 | tf_op jit(solution)/shard_map/ppermute | solution.py:270
  28.2 24.8 %collective-permute-start.6 = (bf16[160,1024]{1,0:T(8,128)(2,1)S(1)}, bf16[160,1024]{1,0:T(8,128)(2,1)S(1)}, u32[]{:S(2)}, u32[]{:S(2)}) collective-permute-start(bf16[160,1024]{1,0:T(8,128)(2,1)S(1)} %get-tuple-element.42), channel_id=1, source_target_pairs={{0,130},{128,3},{1,131},{129,0},{2,128},{130,1},{3,129},{131,2},{4... | collective-permute-start | bytes 983048 | tf_op jit(solution)/shard_map/ppermute | solution.py:270
  54.5 4.4 %collective-permute-start.13 = (bf16[528,1024]{1,0:T(8,128)(2,1)S(1)}, bf16[528,1024]{1,0:T(8,128)(2,1)S(1)}, u32[]{:S(2)}, u32[]{:S(2)}) collective-permute-start(bf16[528,1024]{1,0:T(8,128)(2,1)S(1)} %get-tuple-element.50), channel_id=1, source_target_pairs={{0,16},{16,0},{1,17},{17,1},{2,18},{18,2},{3,19},{19,3},{4,20},{20... | collective-permute-start | bytes 3244040 | tf_op jit(solution)/shard_map/ppermute | solution.py:288
  54.6 7.5 %collective-permute-start.10 = (bf16[528,1024]{1,0:T(8,128)(2,1)S(1)}, bf16[528,1024]{1,0:T(8,128)(2,1)S(1)}, u32[]{:S(2)}, u32[]{:S(2)}) collective-permute-start(bf16[528,1024]{1,0:T(8,128)(2,1)S(1)} %get-tuple-element.47.refs_0_), channel_id=1, source_target_pairs={{0,16},{16,0},{1,17},{17,1},{2,18},{18,2},{3,19},{19,3},{4,20},{20... | collective-permute-start | bytes 3244040 | tf_op jit(solution)/shard_map/ppermute | solution.py:288
  55.1 7.0 %collective-permute-start.11 = (bf16[528,1024]{1,0:T(8,128)(2,1)S(1)}, bf16[528,1024]{1,0:T(8,128)(2,1)S(1)}, u32[]{:S(2)}, u32[]{:S(2)}) collective-permute-start(bf16[528,1024]{1,0:T(8,128)(2,1)S(1)} %get-tuple-element.48.refs_1_), channel_id=1, source_target_pairs={{0,16},{16,0},{1,17},{17,1},{2,18},{18,2},{3,19},{19,3},{4,20},{20... | collective-permute-start | bytes 3244040 | tf_op jit(solution)/shard_map/ppermute | solution.py:288
  55.2 6.9 %collective-permute-start.12 = (bf16[528,1024]{1,0:T(8,128)(2,1)S(1)}, bf16[528,1024]{1,0:T(8,128)(2,1)S(1)}, u32[]{:S(2)}, u32[]{:S(2)}) collective-permute-start(bf16[528,1024]{1,0:T(8,128)(2,1)S(1)} %get-tuple-element.49.refs_0_), channel_id=1, source_target_pairs={{0,16},{16,0},{1,17},{17,1},{2,18},{18,2},{3,19},{19,3},{4,20},{20... | collective-permute-start | bytes 3244040 | tf_op jit(solution)/shard_map/ppermute | solution.py:288
  55.6 10.9 %collective-permute-start.14 = (f32[8,128]{1,0:T(8,128)S(1)}, f32[8,128]{1,0:T(8,128)S(1)}, u32[]{:S(2)}, u32[]{:S(2)}) collective-permute-start(f32[8,128]{1,0:T(8,128)S(1)} %get-tuple-element.67.refs_5_), channel_id=1, source_target_pairs={{0,16},{16,0},{1,17},{17,1},{2,18},{18,2},{3,19},{19,3},{4,20},{20... | collective-permute-start | bytes 12296 | tf_op jit(solution)/shard_map/ppermute | solution.py:288
  67.5 16.7 %collective-permute-start.15 = (s16[128,1152]{1,0:T(8,128)(2,1)S(1)}, s16[128,1152]{1,0:T(8,128)(2,1)S(1)}, u32[]{:S(2)}, u32[]{:S(2)}) collective-permute-start(s16[128,1152]{1,0:T(8,128)(2,1)S(1)} %get-tuple-element.70), channel_id=1, source_target_pairs={{0,128},{128,1},{1,129},{129,2},{2,130},{130,3},{3,131},{131,0},{4... | collective-permute-start | bytes 884744 | tf_op jit(solution)/shard_map/ppermute | solution.py:270
  71.8 12.4 %collective-permute-start.16 = (s16[128,1152]{1,0:T(8,128)(2,1)S(1)}, s16[128,1152]{1,0:T(8,128)(2,1)S(1)}, u32[]{:S(2)}, u32[]{:S(2)}) collective-permute-start(s16[128,1152]{1,0:T(8,128)(2,1)S(1)} %get-tuple-element.71), channel_id=1, source_target_pairs={{0,131},{128,0},{1,128},{129,1},{2,129},{130,2},{3,130},{131,3},{4... | collective-permute-start | bytes 884744 | tf_op jit(solution)/shard_map/ppermute | solution.py:270
  71.8 10.0 %collective-permute-start.17 = (s16[32,1152]{1,0:T(8,128)(2,1)S(1)}, s16[32,1152]{1,0:T(8,128)(2,1)S(1)}, u32[]{:S(2)}, u32[]{:S(2)}) collective-permute-start(s16[32,1152]{1,0:T(8,128)(2,1)S(1)} %get-tuple-element.72), channel_id=1, source_target_pairs={{0,1},{128,129},{1,2},{129,130},{2,3},{130,131},{3,0},{131,128},{4... | collective-permute-start | bytes 221192 | tf_op jit(solution)/shard_map/ppermute | solution.py:270
  74.0 10.2 %collective-permute-start.18 = (s16[32,1152]{1,0:T(8,128)(2,1)S(1)}, s16[32,1152]{1,0:T(8,128)(2,1)S(1)}, u32[]{:S(2)}, u32[]{:S(2)}) collective-permute-start(s16[32,1152]{1,0:T(8,128)(2,1)S(1)} %get-tuple-element.73), channel_id=1, source_target_pairs={{0,3},{128,131},{1,0},{129,128},{2,1},{130,129},{3,2},{131,130},{4... | collective-permute-start | bytes 221192 | tf_op jit(solution)/shard_map/ppermute | solution.py:270
  84.8 9.7 %collective-permute-start.19 = (s16[64,1152]{1,0:T(8,128)(2,1)S(1)}, s16[64,1152]{1,0:T(8,128)(2,1)S(1)}, u32[]{:S(2)}, u32[]{:S(2)}) collective-permute-start(s16[64,1152]{1,0:T(8,128)(2,1)S(1)} %get-tuple-element.74), channel_id=1, source_target_pairs={{0,1},{128,129},{1,2},{129,130},{2,3},{130,131},{3,0},{131,128},{4... | collective-permute-start | bytes 442376 | tf_op jit(solution)/shard_map/ppermute | solution.py:270
  87.0 7.5 %collective-permute-start.20 = (s16[64,1152]{1,0:T(8,128)(2,1)S(1)}, s16[64,1152]{1,0:T(8,128)(2,1)S(1)}, u32[]{:S(2)}, u32[]{:S(2)}) collective-permute-start(s16[64,1152]{1,0:T(8,128)(2,1)S(1)} %get-tuple-element.75), channel_id=1, source_target_pairs={{0,3},{128,131},{1,0},{129,128},{2,1},{130,129},{3,2},{131,130},{4... | collective-permute-start | bytes 442376 | tf_op jit(solution)/shard_map/ppermute | solution.py:270

commit v8 on v7

--- a/solution.py
+++ b/solution.py
@@ -79,7 +79,8 @@
 
 
 def pack_line(*refs):
-    blocks, (own, below, above, piece, up_pair, down_pair) = refs[:-6], refs[-6:]
+    blocks, (own, below, above, chosen, piece, up_pair, down_pair, total) = refs[:-8], refs[-8:]
+    total[...] = jnp.broadcast_to(jnp.sum(chosen[...], axis=0), total.shape)
     half = own.shape[0] // 2
     up_pair[...] = jnp.concatenate([own[...], above[...], below[:half, :]], axis=0)
     down_pair[...] = jnp.concatenate([own[...], below[...], above[half:, :]], axis=0)
@@ -134,10 +135,9 @@
             pulls[half][part, :] = total
 
 
-def first_columns(rows, lines, own, below, above, far_below, far_above, chosen, *refs):
+def first_columns(rows, lines, own, below, above, far_below, far_above, *refs):
     pieces, refs = refs[:lines], refs[lines:]
-    ordered, norms, total, pp, tp, pm, tm, *weights = refs
-    total[...] = jnp.broadcast_to(jnp.sum(chosen[...], axis=0), total.shape)
+    ordered, norms, pp, tp, pm, tm, *weights = refs
     height = own.shape[0]
     found = {
         0: own[...],
@@ -175,8 +175,17 @@
     return gradient, proof
 
 
-def far_terms(target_count, height, *refs):
-    inputs, (up, down, up_half, down_half) = refs[:7], refs[7:]
+def last_columns(lines, start, stop, panel, norms, *refs):
+    pieces, old, totals, outs = refs[:lines], refs[lines : lines + 4], refs[lines + 4 : lines + 6], refs[lines + 6 :]
+    outs, (pp, tp, pm, tm, *weights) = outs[:-6], outs[-6:]
+    rows = slice(start, stop)
+    panel, norms, *old = (ref.at[rows] for ref in (panel, norms, *old))
+    add_columns(panel, norms, pieces, old, (pp, tp), (pm, tm), weights, stop - start)
+    return (panel, pp, tp, pm, tm, *totals), outs
+
+
+def far_terms(target_count, lines, height, *refs):
+    inputs, (up, down, up_half, down_half) = last_columns(lines, 0, 5 * height, *refs)
     for i in range(4):
         code = encode(*terms(target_count, *inputs, slice(i * height, (i + 1) * height)))
         (up, down)[i // 2][i % 2 * height : (i % 2 + 1) * height, :] = code
@@ -185,11 +194,11 @@
     up_half[...] = code[height // 2 :, :]
 
 
-def near_terms(target_count, height, *refs):
-    inputs, (gradient, proof) = refs[:7], refs[7:]
-    for i in range(5, 8):
-        part = slice((i - 5) * height, (i - 4) * height)
-        gradient[part, :], small = terms(target_count, *inputs, slice(i * height, (i + 1) * height))
+def near_terms(target_count, lines, height, *refs):
+    inputs, (gradient, proof) = last_columns(lines, 5 * height, 8 * height, *refs)
+    for i in range(3):
+        part = slice(i * height, (i + 1) * height)
+        gradient[part, :], small = terms(target_count, *inputs, part)
         proof[part, :] = jnp.broadcast_to(small, (height, LANES))
 
 
@@ -304,9 +313,11 @@
     blocks = line(block, 0)
     below, above = up_the_ring(pool, 1), up_the_ring(pool, ring - 1)
     pair = shape((5 * height // 2, width), BF16)
-    piece, up_pair, down_pair = in_vmem(
-        pack_line, "pack_line", (shape((2 * height * len(blocks) + META, width), BF16), pair, pair)
-    )(*blocks, pool, below, above)
+    piece, up_pair, down_pair, total = in_vmem(
+        pack_line,
+        "pack_line",
+        (shape((2 * height * len(blocks) + META, width), BF16), pair, pair, shape((8, LANES), F32)),
+    )(*blocks, pool, below, above, chosen)
     pieces = line(piece, 1)
     pairs = up_the_ring(up_pair, 3), up_the_ring(down_pair, ring - 3)
 
@@ -327,34 +338,40 @@
     def more(some, state):
         return add(more_columns, (panel, norms), some, state, sums, {2 + len(some) + i: i for i in range(4)})
 
-    panel, norms, total, *state = add(
+    panel, norms, *state = add(
         first_columns,
-        (pool, below, above, *pairs, chosen),
+        (pool, below, above, *pairs),
         pieces[:1],
         (),
-        (shape((rows, width), BF16), shape((rows, LANES), F32), shape((8, LANES), F32), *sums),
+        (shape((rows, width), BF16), shape((rows, LANES), F32), *sums),
         {},
     )
     totals = total, other_core(total)
     pieces = handed_on(pieces, norms)
     others = [other_core(p) for p in pieces]
-    for some in (pieces[1:3], (pieces[3], others[0]), others[1:]):
+    for some in (pieces[1:3], (pieces[3], others[0])):
         state = more(some, state)
 
-    inputs = panel, *state, *totals
+    inputs = panel, norms, *others[1:], *state, *totals
+
+    def last(body, count, out_shape):
+        return in_vmem(
+            functools.partial(body, target_count, 3, height),
+            body.__name__,
+            out_shape,
+            flops=8 * count * 3 * size * width,
+            scratch=[pltpu.VMEM((count, n), F32) for n in (width, width, LANES, LANES)]
+            + [pltpu.VMEM((count, 3 * size), BF16)] * 2,
+            limit=16,
+        )(*inputs)
+
     whole, half = (shape((n, width + LANES), jnp.int16) for n in (2 * height, height // 2))
-    up, down, up_half, down_half = in_vmem(
-        functools.partial(far_terms, target_count, height),
-        "far_terms",
-        (whole, whole, half, half),
-    )(*inputs)
+    up, down, up_half, down_half = last(far_terms, 5 * height, (whole, whole, half, half))
     from_above, from_below = up_the_ring(down, ring - 1), up_the_ring(up, 1)
     half_above, half_below = up_the_ring(down_half, ring - 2), up_the_ring(up_half, 2)
-    near = in_vmem(
-        functools.partial(near_terms, target_count, height),
-        "near_terms",
-        (shape((3 * height, width), F32), shape((3 * height, LANES), F32)),
-    )(*inputs)
+    near = last(
+        near_terms, 3 * height, (shape((3 * height, width), F32), shape((3 * height, LANES), F32))
+    )
     up, down = in_vmem(pass_on, "pass_on", (shape((height, width + LANES), jnp.int16),) * 2)(
         *near, from_below, from_above, half_below, half_above
     )

time: 97.1 us -> 105 us (1.081)
  the two profiles are of different devices: /device:TPU:8 before, /device:TPU:36 now
where the time goes in v8:
time: 105 us
  waiting for transfers between devices  32 us (30%)
  starting transfers between devices  27.8 us (26%)
  blocking collectives  25.7 us (24%)
  Pallas kernels  17 us (16%)
  local copies, waits for them, and re-layouts  1.86 us (2%)
    ppermute x10, waiting for transfers between devices, up_the_ring(): lax.ppermute(x, RING, [(place(i), place((i + step) % ring)) for i in rang...  31.7 us
    all_to_all x1, blocking collectives, on_device(): lax.all_to_all(chosen, CHIPS, split_axis=0, concat_axis=0, tiled=True)  25.7 us
    ppermute x10, starting transfers between devices, up_the_ring(): lax.ppermute(x, RING, [(place(i), place((i + step) % ring)) for i in rang...  19.6 us
    pallas_call x9, Pallas kernels, call(): pl.pallas_call(body, out_shape=out_shape, in_specs=[spec] * len(args), ou...  17 us
    ppermute x6, starting transfers between devices, along_line(): return lax.ppermute(x, PLANE, pairs)  7.06 us
  transfers between devices with their start and end apart: 21, of which 5 were waited for; matrix products, arithmetic and copies ran while one was open for 0% of the time, Pallas kernels for 9%

profile of v8, /device:TPU:36, one launch (start us, length us, event | category | flops | bytes accessed | tf_op | source)
XLA Modules:
  0.0 105.1 jit_solution(8455276747754762497)
XLA Ops:
  0.6 2.0 %pack_block.1 = (bf16[144,1024]{1,0:T(8,128)(2,1)}, f32[128,1,128]{2,1,0:T(1,128)}) custom-call(bf16[64,1024]{1,0:T(8,128)(2,1)} %own.1, bf16[64,1024]{1,0:T(8,128)(2,1)} %targets.1, s32[1,64]{1,0:T(1,128)} %bitcast.2), custom_call_target="tpu_custom_call" | custom-call | bytes 1048576 | tf_op jit(solution)/shard_map/pack_block/pallas_call | solution.py:30
  2.6 1.2 %collective-permute-start.2 = (bf16[144,1024]{1,0:T(8,128)(2,1)}, bf16[144,1024]{1,0:T(8,128)(2,1)S(1)}, u32[]{:S(2)}, u32[]{:S(2)}) collective-permute-start(bf16[144,1024]{1,0:T(8,128)(2,1)} %get-tuple-element.36.refs_0_), channel_id=1, source_target_pairs={{0,32},{16,20},{4,36},{20,24},{8,40},{24,28},{12,44},{28,16},{32,6... | collective-permute-start | bytes 884744 | tf_op jit(solution)/shard_map/ppermute | solution.py:289
  3.8 0.8 collective-permute-start.3
  4.6 1.7 %collective-permute-start.4 = (bf16[144,1024]{1,0:T(8,128)(2,1)}, bf16[144,1024]{1,0:T(8,128)(2,1)S(1)}, u32[]{:S(2)}, u32[]{:S(2)}) collective-permute-start(bf16[144,1024]{1,0:T(8,128)(2,1)} %get-tuple-element.36.refs_0_), channel_id=1, source_target_pairs={{0,64},{16,24},{4,68},{20,28},{8,72},{24,16},{12,76},{28,20},{32,9... | collective-permute-start | bytes 884744 | tf_op jit(solution)/shard_map/ppermute | solution.py:289
  6.4 1.9 %collective-permute-start = (bf16[64,1024]{1,0:T(8,128)(2,1)}, bf16[64,1024]{1,0:T(8,128)(2,1)S(1)}, u32[]{:S(2)}, u32[]{:S(2)}) collective-permute-start(bf16[64,1024]{1,0:T(8,128)(2,1)} %own.1), channel_id=1, source_target_pairs={{0,128},{128,1},{1,129},{129,2},{2,130},{130,3},{3,131},{131,0},{4... | collective-permute-start | bytes 393224 | tf_op jit(solution)/shard_map/ppermute | solution.py:279
  8.3 0.1 collective-permute-start.1
  8.4 25.7 %all_to_all.5.refs_7_ = f32[128,1,128]{2,1,0:T(1,128)S(1)} all-to-all(f32[128,1,128]{2,1,0:T(1,128)} %get-tuple-element.37), channel_id=1, replica_groups=mesh['zl'=2,'x'=4,'c'=2,'y'=4,'zh'=4] {'zl','x','y','zh'}, dimensions={0} | all-to-all | bytes 131072 | tf_op jit(solution)/shard_map/all_to_all | solution.py:312
  34.1 0.9 copy-done
  35.0 1.0 copy-done.1
  36.0 0.2 pack_line.1
  36.2 0.7 collective-permute-start.7
  36.8 2.6 %collective-permute-start.8 = (bf16[528,1024]{1,0:T(8,128)(2,1)S(1)}, bf16[528,1024]{1,0:T(8,128)(2,1)S(1)}, u32[]{:S(2)}, u32[]{:S(2)}) collective-permute-start(bf16[528,1024]{1,0:T(8,128)(2,1)S(1)} %get-tuple-element.40.refs_0_), channel_id=1, source_target_pairs={{0,12},{16,112},{4,0},{20,116},{8,4},{24,120},{12,8},{28,124},{32,... | collective-permute-start | bytes 3244040 | tf_op jit(solution)/shard_map/ppermute | solution.py:289
  39.5 0.8 collective-permute-start.5
  40.3 4.2 %collective-permute-start.6 = (bf16[160,1024]{1,0:T(8,128)(2,1)S(1)}, bf16[160,1024]{1,0:T(8,128)(2,1)S(1)}, u32[]{:S(2)}, u32[]{:S(2)}) collective-permute-start(bf16[160,1024]{1,0:T(8,128)(2,1)S(1)} %get-tuple-element.39), channel_id=1, source_target_pairs={{0,130},{128,3},{1,131},{129,0},{2,128},{130,1},{3,129},{131,2},{4... | collective-permute-start | bytes 983048 | tf_op jit(solution)/shard_map/ppermute | solution.py:279
  44.5 17.9 %collective-permute-done.5.far_below = bf16[160,1024]{1,0:T(8,128)(2,1)S(1)} collective-permute-done((bf16[160,1024]{1,0:T(8,128)(2,1)S(1)}, bf16[160,1024]{1,0:T(8,128)(2,1)S(1)}, u32[]{:S(2)}, u32[]{:S(2)}) %collective-permute-start.5) | collective-permute-done | bytes 327712 | tf_op jit(solution)/shard_map/ppermute | solution.py:279
  62.4 1.5 %first_columns.1 = (bf16[512,1024]{1,0:T(8,128)(2,1)S(1)}, f32[512,128]{1,0:T(8,128)S(1)}, f32[512,1024]{1,0:T(8,128)S(1)}, f32[512,1024]{1,0:T(8,128)S(1)}, f32...) custom-call(bf16[64,1024]{1,0:T(8,128)(2,1)S(1)} %copy-done, bf16[64,1024]{1,0:T(8,128)(2,1)S(1)} %collective-permute-done.refs_5_.below, ...), custom_call_target="tpu_custom_call" | custom-call | flops 1073741824 | bytes 1048576 | tf_op jit(solution)/shard_map/first_columns/pallas_call | solution.py:30
  63.9 0.2 collective-permute-done.7.refs_1_
  64.3 0.5 collective-permute-start.10
  64.9 0.4 collective-permute-start.12
  65.4 3.1 %more_columns.2 = (f32[512,1024]{1,0:T(8,128)S(1)}, f32[512,1024]{1,0:T(8,128)S(1)}, f32[512,128]{1,0:T(8,128)S(1)}, f32[512,128]{1,0:T(8,128)S(1)}) custom-call(bf16[512,1024]{1,0:T(8,128)(2,1)S(1)} %get-tuple-element.41.panel.refs_0_, ...), custom_call_target="tpu_custom_call", output_to_operand_aliasing={{0}: (4, {}), {1}: (5, {}), {2}: (6, {}), {3}: (7, {})} | custom-call | flops 2147483648 | bytes 1048576 | tf_op jit(solution)/shard_map/more_columns/pallas_call | solution.py:30
  68.6 3.2 %more_columns.3 = (f32[512,1024]{1,0:T(8,128)S(1)}, f32[512,1024]{1,0:T(8,128)S(1)}, f32[512,128]{1,0:T(8,128)S(1)}, f32[512,128]{1,0:T(8,128)S(1)}) custom-call(bf16[512,1024]{1,0:T(8,128)(2,1)S(1)} %get-tuple-element.41.panel.refs_0_, ...), custom_call_target="tpu_custom_call", output_to_operand_aliasing={{0}: (4, {}), {1}: (5, {}), {2}: (6, {}), {3}: (7, {})} | custom-call | flops 2147483648 | bytes 1048576 | tf_op jit(solution)/shard_map/more_columns/pallas_call | solution.py:30
  71.8 3.2 %far_terms.1 = (s16[128,1152]{1,0:T(8,128)(2,1)S(1)}, s16[128,1152]{1,0:T(8,128)(2,1)S(1)}, s16[32,1152]{1,0:T(8,128)(2,1)S(1)}, s16[32,1152]{1,0:T(8,128)(2,1)S(1)}) custom-call(bf16[512,1024]{1,0:T(8,128)(2,1)S(1)} %get-tuple-element.41.panel.refs_0_, f32[512,128]{1,0:T(8,128)S(1)} %get-tuple-element.42.refs_4_.norms.refs_1_, ...), custom_call_target="tpu_custom_call" | custom-call | flops 2013265920 | bytes 1048576 | tf_op jit(solution)/shard_map/far_terms/pallas_call | solution.py:30
  75.1 3.7 %collective-permute-start.15 = (s16[128,1152]{1,0:T(8,128)(2,1)S(1)}, s16[128,1152]{1,0:T(8,128)(2,1)S(1)}, u32[]{:S(2)}, u32[]{:S(2)}) collective-permute-start(s16[128,1152]{1,0:T(8,128)(2,1)S(1)} %get-tuple-element.62), channel_id=1, source_target_pairs={{0,128},{128,1},{1,129},{129,2},{2,130},{130,3},{3,131},{131,0},{4... | collective-permute-start | bytes 884744 | tf_op jit(solution)/shard_map/ppermute | solution.py:279
  78.7 2.0 %collective-permute-start.17 = (s16[32,1152]{1,0:T(8,128)(2,1)S(1)}, s16[32,1152]{1,0:T(8,128)(2,1)S(1)}, u32[]{:S(2)}, u32[]{:S(2)}) collective-permute-start(s16[32,1152]{1,0:T(8,128)(2,1)S(1)} %get-tuple-element.64), channel_id=1, source_target_pairs={{0,1},{128,129},{1,2},{129,130},{2,3},{130,131},{3,0},{131,128},{4... | collective-permute-start | bytes 221192 | tf_op jit(solution)/shard_map/ppermute | solution.py:279
  80.7 2.1 %collective-permute-start.18 = (s16[32,1152]{1,0:T(8,128)(2,1)S(1)}, s16[32,1152]{1,0:T(8,128)(2,1)S(1)}, u32[]{:S(2)}, u32[]{:S(2)}) collective-permute-start(s16[32,1152]{1,0:T(8,128)(2,1)S(1)} %get-tuple-element.65), channel_id=1, source_target_pairs={{0,3},{128,131},{1,0},{129,128},{2,1},{130,129},{3,2},{131,130},{4... | collective-permute-start | bytes 221192 | tf_op jit(solution)/shard_map/ppermute | solution.py:279
  82.9 2.1 %near_terms.1 = (f32[192,1024]{1,0:T(8,128)S(1)}, f32[192,128]{1,0:T(8,128)S(1)}) custom-call(bf16[512,1024]{1,0:T(8,128)(2,1)S(1)} %get-tuple-element.41.panel.refs_0_, f32[512,128]{1,0:T(8,128)S(1)} %get-tuple-element.42.refs_4_.norms.refs_1_, bf16[528,1024]{1,0:T(8,128)(2,1)S(1)} %collective-permute-done.10.refs_2_, ...), custom_call_target="tpu_custom_call" | custom-call | flops 1207959552 | bytes 1048576 | tf_op jit(solution)/shard_map/near_terms/pallas_call | solution.py:30
  85.0 5.2 %collective-permute-done.17.half_below = s16[32,1152]{1,0:T(8,128)(2,1)S(1)} collective-permute-done((s16[32,1152]{1,0:T(8,128)(2,1)S(1)}, s16[32,1152]{1,0:T(8,128)(2,1)S(1)}, u32[]{:S(2)}, u32[]{:S(2)}) %collective-permute-start.17) | collective-permute-done | bytes 73760 | tf_op jit(solution)/shard_map/ppermute | solution.py:279
  90.2 0.5 pass_on.1
  90.8 4.7 %collective-permute-start.19 = (s16[64,1152]{1,0:T(8,128)(2,1)S(1)}, s16[64,1152]{1,0:T(8,128)(2,1)S(1)}, u32[]{:S(2)}, u32[]{:S(2)}) collective-permute-start(s16[64,1152]{1,0:T(8,128)(2,1)S(1)} %get-tuple-element.66), channel_id=1, source_target_pairs={{0,1},{128,129},{1,2},{129,130},{2,3},{130,131},{3,0},{131,128},{4... | collective-permute-start | bytes 442376 | tf_op jit(solution)/shard_map/ppermute | solution.py:279
  95.5 4.8 %collective-permute-done.19.far_below = s16[64,1152]{1,0:T(8,128)(2,1)S(1)} collective-permute-done((s16[64,1152]{1,0:T(8,128)(2,1)S(1)}, s16[64,1152]{1,0:T(8,128)(2,1)S(1)}, u32[]{:S(2)}, u32[]{:S(2)}) %collective-permute-start.19) | collective-permute-done | bytes 147488 | tf_op jit(solution)/shard_map/ppermute | solution.py:279
  100.3 3.8 %collective-permute-done.20.far_above = s16[64,1152]{1,0:T(8,128)(2,1)S(1)} collective-permute-done((s16[64,1152]{1,0:T(8,128)(2,1)S(1)}, s16[64,1152]{1,0:T(8,128)(2,1)S(1)}, u32[]{:S(2)}, u32[]{:S(2)}) %collective-permute-start.20) | collective-permute-done | bytes 147488 | tf_op jit(solution)/shard_map/ppermute | solution.py:279
  104.1 1.1 %add_up.1 = (f32[1,64]{1,0:T(1,128)}, f32[64,1024]{1,0:T(8,128)}) custom-call(f32[192,1024]{1,0:T(8,128)S(1)} %get-tuple-element.60.gradient, f32[192,128]{1,0:T(8,128)S(1)} %get-tuple-element.61.proof, s16[128,1152]{1,0:T(8,128)(2,1)S(1)} %collective-permute-done.15.from_below, s16[128,1152]{1,0:T(8,128)(2,1)S(1)} %collective-permute-done.16.from_above, ...), custom_call_target="tpu_custom_call" | custom-call | bytes 1048576 | tf_op jit(solution)/shard_map/add_up/pallas_call | solution.py:30
  (25 shorter events, 0.3 us)
Async XLA Ops:
  2.6 31.5 %collective-permute-start.2 = (bf16[144,1024]{1,0:T(8,128)(2,1)}, bf16[144,1024]{1,0:T(8,128)(2,1)S(1)}, u32[]{:S(2)}, u32[]{:S(2)}) collective-permute-start(bf16[144,1024]{1,0:T(8,128)(2,1)} %get-tuple-element.36.refs_0_), channel_id=1, source_target_pairs={{0,32},{16,20},{4,36},{20,24},{8,40},{24,28},{12,44},{28,16},{32,6... | collective-permute-start | bytes 884744 | tf_op jit(solution)/shard_map/ppermute | solution.py:289
  3.8 30.3 %collective-permute-start.3 = (bf16[144,1024]{1,0:T(8,128)(2,1)}, bf16[144,1024]{1,0:T(8,128)(2,1)S(1)}, u32[]{:S(2)}, u32[]{:S(2)}) collective-permute-start(bf16[144,1024]{1,0:T(8,128)(2,1)} %get-tuple-element.36.refs_0_), channel_id=1, source_target_pairs={{0,96},{16,28},{4,100},{20,16},{8,104},{24,20},{12,108},{28,24},{3... | collective-permute-start | bytes 884744 | tf_op jit(solution)/shard_map/ppermute | solution.py:289
  4.6 29.5 %collective-permute-start.4 = (bf16[144,1024]{1,0:T(8,128)(2,1)}, bf16[144,1024]{1,0:T(8,128)(2,1)S(1)}, u32[]{:S(2)}, u32[]{:S(2)}) collective-permute-start(bf16[144,1024]{1,0:T(8,128)(2,1)} %get-tuple-element.36.refs_0_), channel_id=1, source_target_pairs={{0,64},{16,24},{4,68},{20,28},{8,72},{24,16},{12,76},{28,20},{32,9... | collective-permute-start | bytes 884744 | tf_op jit(solution)/shard_map/ppermute | solution.py:289
  6.4 27.7 %collective-permute-start = (bf16[64,1024]{1,0:T(8,128)(2,1)}, bf16[64,1024]{1,0:T(8,128)(2,1)S(1)}, u32[]{:S(2)}, u32[]{:S(2)}) collective-permute-start(bf16[64,1024]{1,0:T(8,128)(2,1)} %own.1), channel_id=1, source_target_pairs={{0,128},{128,1},{1,129},{129,2},{2,130},{130,3},{3,131},{131,0},{4... | collective-permute-start | bytes 393224 | tf_op jit(solution)/shard_map/ppermute | solution.py:279
  8.3 25.8 %collective-permute-start.1 = (bf16[64,1024]{1,0:T(8,128)(2,1)}, bf16[64,1024]{1,0:T(8,128)(2,1)S(1)}, u32[]{:S(2)}, u32[]{:S(2)}) collective-permute-start(bf16[64,1024]{1,0:T(8,128)(2,1)} %own.1), channel_id=1, source_target_pairs={{0,131},{128,0},{1,128},{129,1},{2,129},{130,2},{3,130},{131,3},{4... | collective-permute-start | bytes 393224 | tf_op jit(solution)/shard_map/ppermute | solution.py:279
  34.1 0.9 copy-start
  35.0 1.0 copy-start.1
  36.2 28.0 %collective-permute-start.7 = (bf16[528,1024]{1,0:T(8,128)(2,1)S(1)}, bf16[528,1024]{1,0:T(8,128)(2,1)S(1)}, u32[]{:S(2)}, u32[]{:S(2)}) collective-permute-start(bf16[528,1024]{1,0:T(8,128)(2,1)S(1)} %get-tuple-element.40.refs_0_), channel_id=1, source_target_pairs={{0,4},{16,48},{4,8},{20,52},{8,12},{24,56},{12,0},{28,60},{32,36},... | collective-permute-start | bytes 3244040 | tf_op jit(solution)/shard_map/ppermute | solution.py:289
  36.8 27.4 %collective-permute-start.8 = (bf16[528,1024]{1,0:T(8,128)(2,1)S(1)}, bf16[528,1024]{1,0:T(8,128)(2,1)S(1)}, u32[]{:S(2)}, u32[]{:S(2)}) collective-permute-start(bf16[528,1024]{1,0:T(8,128)(2,1)S(1)} %get-tuple-element.40.refs_0_), channel_id=1, source_target_pairs={{0,12},{16,112},{4,0},{20,116},{8,4},{24,120},{12,8},{28,124},{32,... | collective-permute-start | bytes 3244040 | tf_op jit(solution)/shard_map/ppermute | solution.py:289
  39.5 24.7 %collective-permute-start.9 = (bf16[528,1024]{1,0:T(8,128)(2,1)S(1)}, bf16[528,1024]{1,0:T(8,128)(2,1)S(1)}, u32[]{:S(2)}, u32[]{:S(2)}) collective-permute-start(bf16[528,1024]{1,0:T(8,128)(2,1)S(1)} %get-tuple-element.40.refs_0_), channel_id=1, source_target_pairs={{0,8},{16,80},{4,12},{20,84},{8,0},{24,88},{12,4},{28,92},{32,40},... | collective-permute-start | bytes 3244040 | tf_op jit(solution)/shard_map/ppermute | solution.py:289
  39.5 23.0 %collective-permute-start.5 = (bf16[160,1024]{1,0:T(8,128)(2,1)S(1)}, bf16[160,1024]{1,0:T(8,128)(2,1)S(1)}, u32[]{:S(2)}, u32[]{:S(2)}) collective-permute-start(bf16[160,1024]{1,0:T(8,128)(2,1)S(1)} %get-tuple-element.38), channel_id=1, source_target_pairs={{0,129},{128,2},{1,130},{129,3},{2,131},{130,0},{3,128},{131,1},{4... | collective-permute-start | bytes 983048 | tf_op jit(solution)/shard_map/ppermute | solution.py:279
  40.3 22.1 %collective-permute-start.6 = (bf16[160,1024]{1,0:T(8,128)(2,1)S(1)}, bf16[160,1024]{1,0:T(8,128)(2,1)S(1)}, u32[]{:S(2)}, u32[]{:S(2)}) collective-permute-start(bf16[160,1024]{1,0:T(8,128)(2,1)S(1)} %get-tuple-element.39), channel_id=1, source_target_pairs={{0,130},{128,3},{1,131},{129,0},{2,128},{130,1},{3,129},{131,2},{4... | collective-permute-start | bytes 983048 | tf_op jit(solution)/shard_map/ppermute | solution.py:279
  64.2 4.4 %collective-permute-start.13 = (bf16[528,1024]{1,0:T(8,128)(2,1)S(1)}, bf16[528,1024]{1,0:T(8,128)(2,1)S(1)}, u32[]{:S(2)}, u32[]{:S(2)}) collective-permute-start(bf16[528,1024]{1,0:T(8,128)(2,1)S(1)} %get-tuple-element.46), channel_id=1, source_target_pairs={{0,16},{16,0},{1,17},{17,1},{2,18},{18,2},{3,19},{19,3},{4,20},{20... | collective-permute-start | bytes 3244040 | tf_op jit(solution)/shard_map/ppermute | solution.py:297
  64.3 7.5 %collective-permute-start.10 = (bf16[528,1024]{1,0:T(8,128)(2,1)S(1)}, bf16[528,1024]{1,0:T(8,128)(2,1)S(1)}, u32[]{:S(2)}, u32[]{:S(2)}) collective-permute-start(bf16[528,1024]{1,0:T(8,128)(2,1)S(1)} %get-tuple-element.43.refs_0_), channel_id=1, source_target_pairs={{0,16},{16,0},{1,17},{17,1},{2,18},{18,2},{3,19},{19,3},{4,20},{20... | collective-permute-start | bytes 3244040 | tf_op jit(solution)/shard_map/ppermute | solution.py:297
  64.8 7.0 %collective-permute-start.11 = (bf16[528,1024]{1,0:T(8,128)(2,1)S(1)}, bf16[528,1024]{1,0:T(8,128)(2,1)S(1)}, u32[]{:S(2)}, u32[]{:S(2)}) collective-permute-start(bf16[528,1024]{1,0:T(8,128)(2,1)S(1)} %get-tuple-element.44.refs_1_), channel_id=1, source_target_pairs={{0,16},{16,0},{1,17},{17,1},{2,18},{18,2},{3,19},{19,3},{4,20},{20... | collective-permute-start | bytes 3244040 | tf_op jit(solution)/shard_map/ppermute | solution.py:297
  64.9 6.9 %collective-permute-start.12 = (bf16[528,1024]{1,0:T(8,128)(2,1)S(1)}, bf16[528,1024]{1,0:T(8,128)(2,1)S(1)}, u32[]{:S(2)}, u32[]{:S(2)}) collective-permute-start(bf16[528,1024]{1,0:T(8,128)(2,1)S(1)} %get-tuple-element.45.refs_0_), channel_id=1, source_target_pairs={{0,16},{16,0},{1,17},{17,1},{2,18},{18,2},{3,19},{19,3},{4,20},{20... | collective-permute-start | bytes 3244040 | tf_op jit(solution)/shard_map/ppermute | solution.py:297
  65.3 6.5 %collective-permute-start.14 = (f32[8,128]{1,0:T(8,128)S(1)}, f32[8,128]{1,0:T(8,128)S(1)}, u32[]{:S(2)}, u32[]{:S(2)}) collective-permute-start(f32[8,128]{1,0:T(8,128)S(1)} %get-tuple-element.59.refs_9_), channel_id=1, source_target_pairs={{0,16},{16,0},{1,17},{17,1},{2,18},{18,2},{3,19},{19,3},{4,20},{20... | collective-permute-start | bytes 12296 | tf_op jit(solution)/shard_map/ppermute | solution.py:297
  75.1 15.1 %collective-permute-start.15 = (s16[128,1152]{1,0:T(8,128)(2,1)S(1)}, s16[128,1152]{1,0:T(8,128)(2,1)S(1)}, u32[]{:S(2)}, u32[]{:S(2)}) collective-permute-start(s16[128,1152]{1,0:T(8,128)(2,1)S(1)} %get-tuple-element.62), channel_id=1, source_target_pairs={{0,128},{128,1},{1,129},{129,2},{2,130},{130,3},{3,131},{131,0},{4... | collective-permute-start | bytes 884744 | tf_op jit(solution)/shard_map/ppermute | solution.py:279
  78.7 11.5 %collective-permute-start.16 = (s16[128,1152]{1,0:T(8,128)(2,1)S(1)}, s16[128,1152]{1,0:T(8,128)(2,1)S(1)}, u32[]{:S(2)}, u32[]{:S(2)}) collective-permute-start(s16[128,1152]{1,0:T(8,128)(2,1)S(1)} %get-tuple-element.63), channel_id=1, source_target_pairs={{0,131},{128,0},{1,128},{129,1},{2,129},{130,2},{3,130},{131,3},{4... | collective-permute-start | bytes 884744 | tf_op jit(solution)/shard_map/ppermute | solution.py:279
  78.7 11.5 %collective-permute-start.17 = (s16[32,1152]{1,0:T(8,128)(2,1)S(1)}, s16[32,1152]{1,0:T(8,128)(2,1)S(1)}, u32[]{:S(2)}, u32[]{:S(2)}) collective-permute-start(s16[32,1152]{1,0:T(8,128)(2,1)S(1)} %get-tuple-element.64), channel_id=1, source_target_pairs={{0,1},{128,129},{1,2},{129,130},{2,3},{130,131},{3,0},{131,128},{4... | collective-permute-start | bytes 221192 | tf_op jit(solution)/shard_map/ppermute | solution.py:279
  80.7 9.5 %collective-permute-start.18 = (s16[32,1152]{1,0:T(8,128)(2,1)S(1)}, s16[32,1152]{1,0:T(8,128)(2,1)S(1)}, u32[]{:S(2)}, u32[]{:S(2)}) collective-permute-start(s16[32,1152]{1,0:T(8,128)(2,1)S(1)} %get-tuple-element.65), channel_id=1, source_target_pairs={{0,3},{128,131},{1,0},{129,128},{2,1},{130,129},{3,2},{131,130},{4... | collective-permute-start | bytes 221192 | tf_op jit(solution)/shard_map/ppermute | solution.py:279
  90.8 9.6 %collective-permute-start.19 = (s16[64,1152]{1,0:T(8,128)(2,1)S(1)}, s16[64,1152]{1,0:T(8,128)(2,1)S(1)}, u32[]{:S(2)}, u32[]{:S(2)}) collective-permute-start(s16[64,1152]{1,0:T(8,128)(2,1)S(1)} %get-tuple-element.66), channel_id=1, source_target_pairs={{0,1},{128,129},{1,2},{129,130},{2,3},{130,131},{3,0},{131,128},{4... | collective-permute-start | bytes 442376 | tf_op jit(solution)/shard_map/ppermute | solution.py:279
  95.5 8.6 %collective-permute-start.20 = (s16[64,1152]{1,0:T(8,128)(2,1)S(1)}, s16[64,1152]{1,0:T(8,128)(2,1)S(1)}, u32[]{:S(2)}, u32[]{:S(2)}) collective-permute-start(s16[64,1152]{1,0:T(8,128)(2,1)S(1)} %get-tuple-element.67), channel_id=1, source_target_pairs={{0,3},{128,131},{1,0},{129,128},{2,1},{130,129},{3,2},{131,130},{4... | collective-permute-start | bytes 442376 | tf_op jit(solution)/shard_map/ppermute | solution.py:279

commit v9 on v8

--- a/solution.py
+++ b/solution.py
@@ -79,8 +79,8 @@
 
 
 def pack_line(*refs):
-    blocks, (own, below, above, chosen, piece, up_pair, down_pair, total) = refs[:-8], refs[-8:]
-    total[...] = jnp.broadcast_to(jnp.sum(chosen[...], axis=0), total.shape)
+    blocks, (below, above, piece, up_pair, down_pair) = refs[:-5], refs[-5:]
+    own = blocks[0].at[: below.shape[0]]
     half = own.shape[0] // 2
     up_pair[...] = jnp.concatenate([own[...], above[...], below[:half, :]], axis=0)
     down_pair[...] = jnp.concatenate([own[...], below[...], above[half:, :]], axis=0)
@@ -135,12 +135,13 @@
             pulls[half][part, :] = total
 
 
-def first_columns(rows, lines, own, below, above, far_below, far_above, *refs):
+def first_columns(rows, lines, block, below, above, far_below, far_above, chosen, *refs):
     pieces, refs = refs[:lines], refs[lines:]
-    ordered, norms, pp, tp, pm, tm, *weights = refs
-    height = own.shape[0]
+    ordered, norms, total, pp, tp, pm, tm, *weights = refs
+    total[...] = jnp.broadcast_to(jnp.sum(chosen[...], axis=0), total.shape)
+    height = below.shape[0]
     found = {
-        0: own[...],
+        0: block[:height, :],
         1: above[...],
         7: below[...],
         3: far_above[:height, :],
@@ -313,11 +314,9 @@
     blocks = line(block, 0)
     below, above = up_the_ring(pool, 1), up_the_ring(pool, ring - 1)
     pair = shape((5 * height // 2, width), BF16)
-    piece, up_pair, down_pair, total = in_vmem(
-        pack_line,
-        "pack_line",
-        (shape((2 * height * len(blocks) + META, width), BF16), pair, pair, shape((8, LANES), F32)),
-    )(*blocks, pool, below, above, chosen)
+    piece, up_pair, down_pair = in_vmem(
+        pack_line, "pack_line", (shape((2 * height * len(blocks) + META, width), BF16), pair, pair)
+    )(*blocks, below, above)
     pieces = line(piece, 1)
     pairs = up_the_ring(up_pair, 3), up_the_ring(down_pair, ring - 3)
 
@@ -338,12 +337,12 @@
     def more(some, state):
         return add(more_columns, (panel, norms), some, state, sums, {2 + len(some) + i: i for i in range(4)})
 
-    panel, norms, *state = add(
+    panel, norms, total, *state = add(
         first_columns,
-        (pool, below, above, *pairs),
+        (block, below, above, *pairs, chosen),
         pieces[:1],
         (),
-        (shape((rows, width), BF16), shape((rows, LANES), F32), *sums),
+        (shape((rows, width), BF16), shape((rows, LANES), F32), shape((8, LANES), F32), *sums),
         {},
     )
     totals = total, other_core(total)

time: 105 us -> 94.5 us (0.900)
  the two profiles are of different devices: /device:TPU:36 before, /device:TPU:8 now
where the time goes in v9:
time: 94.5 us; the launch traced here: 93 us
  starting transfers between devices  34.3 us (36%)
  blocking collectives  24.7 us (26%)
  Pallas kernels  17.3 us (18%)
  waiting for transfers between devices  15 us (16%)
  local copies, waits for them, and re-layouts  0.96 us (1%)
    all_to_all x1, blocking collectives, on_device(): lax.all_to_all(chosen, CHIPS, split_axis=0, concat_axis=0, tiled=True)  24.7 us
    ppermute x10, starting transfers between devices, up_the_ring(): lax.ppermute(x, RING, [(place(i), place((i + step) % ring)) for i in rang...  23.6 us
    pallas_call x9, Pallas kernels, call(): pl.pallas_call(body, out_shape=out_shape, in_specs=[spec] * len(args), ou...  17.3 us
    ppermute x10, waiting for transfers between devices, up_the_ring(): lax.ppermute(x, RING, [(place(i), place((i + step) % ring)) for i in rang...  15 us
    ppermute x6, starting transfers between devices, along_line(): return lax.ppermute(x, PLANE, pairs)  9.45 us
  transfers between devices with their start and end apart: 21, of which 4 were waited for; matrix products, arithmetic and copies ran while one was open for 0% of the time, Pallas kernels for 11%

profile of v9, /device:TPU:8, one launch (start us, length us, event | category | flops | bytes accessed | tf_op | source)
XLA Modules:
  0.0 93.0 jit_solution(5952983985410794861)
XLA Ops:
  0.6 2.0 %pack_block.1 = (bf16[144,1024]{1,0:T(8,128)(2,1)}, f32[128,1,128]{2,1,0:T(1,128)}) custom-call(bf16[64,1024]{1,0:T(8,128)(2,1)} %pool.1, bf16[64,1024]{1,0:T(8,128)(2,1)} %targets.1, s32[1,64]{1,0:T(1,128)} %bitcast.2), custom_call_target="tpu_custom_call" | custom-call | bytes 1048576 | tf_op jit(solution)/shard_map/pack_block/pallas_call | solution.py:30
  2.6 1.5 %collective-permute-start.2 = (bf16[144,1024]{1,0:T(8,128)(2,1)}, bf16[144,1024]{1,0:T(8,128)(2,1)S(1)}, u32[]{:S(2)}, u32[]{:S(2)}) collective-permute-start(bf16[144,1024]{1,0:T(8,128)(2,1)} %get-tuple-element.36.refs_0_.block), channel_id=1, source_target_pairs={{0,32},{16,20},{4,36},{20,24},{8,40},{24,28},{12,44},{28,16},{32,6... | collective-permute-start | bytes 884744 | tf_op jit(solution)/shard_map/ppermute | solution.py:290
  4.1 1.7 %collective-permute-start.3 = (bf16[144,1024]{1,0:T(8,128)(2,1)}, bf16[144,1024]{1,0:T(8,128)(2,1)S(1)}, u32[]{:S(2)}, u32[]{:S(2)}) collective-permute-start(bf16[144,1024]{1,0:T(8,128)(2,1)} %get-tuple-element.36.refs_0_.block), channel_id=1, source_target_pairs={{0,96},{16,28},{4,100},{20,16},{8,104},{24,20},{12,108},{28,24},{3... | collective-permute-start | bytes 884744 | tf_op jit(solution)/shard_map/ppermute | solution.py:290
  5.8 1.8 %collective-permute-start.4 = (bf16[144,1024]{1,0:T(8,128)(2,1)}, bf16[144,1024]{1,0:T(8,128)(2,1)S(1)}, u32[]{:S(2)}, u32[]{:S(2)}) collective-permute-start(bf16[144,1024]{1,0:T(8,128)(2,1)} %get-tuple-element.36.refs_0_.block), channel_id=1, source_target_pairs={{0,64},{16,24},{4,68},{20,28},{8,72},{24,16},{12,76},{28,20},{32,9... | collective-permute-start | bytes 884744 | tf_op jit(solution)/shard_map/ppermute | solution.py:290
  7.7 1.9 %collective-permute-start = (bf16[64,1024]{1,0:T(8,128)(2,1)}, bf16[64,1024]{1,0:T(8,128)(2,1)S(1)}, u32[]{:S(2)}, u32[]{:S(2)}) collective-permute-start(bf16[64,1024]{1,0:T(8,128)(2,1)} %pool.1), channel_id=1, source_target_pairs={{0,128},{128,1},{1,129},{129,2},{2,130},{130,3},{3,131},{131,0},{4... | collective-permute-start | bytes 393224 | tf_op jit(solution)/shard_map/ppermute | solution.py:280
  9.6 3.9 %collective-permute-start.1 = (bf16[64,1024]{1,0:T(8,128)(2,1)}, bf16[64,1024]{1,0:T(8,128)(2,1)S(1)}, u32[]{:S(2)}, u32[]{:S(2)}) collective-permute-start(bf16[64,1024]{1,0:T(8,128)(2,1)} %pool.1), channel_id=1, source_target_pairs={{0,131},{128,0},{1,128},{129,1},{2,129},{130,2},{3,130},{131,3},{4... | collective-permute-start | bytes 393224 | tf_op jit(solution)/shard_map/ppermute | solution.py:280
  13.5 3.2 %collective-permute-done.refs_4_.below = bf16[64,1024]{1,0:T(8,128)(2,1)S(1)} collective-permute-done((bf16[64,1024]{1,0:T(8,128)(2,1)}, bf16[64,1024]{1,0:T(8,128)(2,1)S(1)}, u32[]{:S(2)}, u32[]{:S(2)}) %collective-permute-start) | collective-permute-done | bytes 131104 | tf_op jit(solution)/shard_map/ppermute | solution.py:280
  16.7 1.0 %copy-done = bf16[144,1024]{1,0:T(8,128)(2,1)S(1)} copy-done((bf16[144,1024]{1,0:T(8,128)(2,1)S(1)}, bf16[144,1024]{1,0:T(8,128)(2,1)}, u32[]{:S(2)}) %copy-start) | copy-done | bytes 294936
  17.7 0.1 pack_line.1
  17.8 1.7 %collective-permute-start.7 = (bf16[528,1024]{1,0:T(8,128)(2,1)S(1)}, bf16[528,1024]{1,0:T(8,128)(2,1)S(1)}, u32[]{:S(2)}, u32[]{:S(2)}) collective-permute-start(bf16[528,1024]{1,0:T(8,128)(2,1)S(1)} %get-tuple-element.40.refs_0_), channel_id=1, source_target_pairs={{0,4},{16,48},{4,8},{20,52},{8,12},{24,56},{12,0},{28,60},{32,36},... | collective-permute-start | bytes 3244040 | tf_op jit(solution)/shard_map/ppermute | solution.py:290
  19.4 0.4 collective-permute-start.8
  19.9 2.3 %collective-permute-start.9 = (bf16[528,1024]{1,0:T(8,128)(2,1)S(1)}, bf16[528,1024]{1,0:T(8,128)(2,1)S(1)}, u32[]{:S(2)}, u32[]{:S(2)}) collective-permute-start(bf16[528,1024]{1,0:T(8,128)(2,1)S(1)} %get-tuple-element.40.refs_0_), channel_id=1, source_target_pairs={{0,8},{16,80},{4,12},{20,84},{8,0},{24,88},{12,4},{28,92},{32,40},... | collective-permute-start | bytes 3244040 | tf_op jit(solution)/shard_map/ppermute | solution.py:290
  22.2 5.1 %collective-permute-start.5 = (bf16[160,1024]{1,0:T(8,128)(2,1)S(1)}, bf16[160,1024]{1,0:T(8,128)(2,1)S(1)}, u32[]{:S(2)}, u32[]{:S(2)}) collective-permute-start(bf16[160,1024]{1,0:T(8,128)(2,1)S(1)} %get-tuple-element.37), channel_id=1, source_target_pairs={{0,129},{128,2},{1,130},{129,3},{2,131},{130,0},{3,128},{131,1},{4... | collective-permute-start | bytes 983048 | tf_op jit(solution)/shard_map/ppermute | solution.py:280
  27.3 24.7 %all_to_all.5.chosen = f32[128,1,128]{2,1,0:T(1,128)S(1)} all-to-all(f32[128,1,128]{2,1,0:T(1,128)S(1)} %copy-done.1), channel_id=1, replica_groups=mesh['zl'=2,'x'=4,'c'=2,'y'=4,'zh'=4] {'zl','x','y','zh'}, dimensions={0} | all-to-all | bytes 131072 | tf_op jit(solution)/shard_map/all_to_all | solution.py:313
  52.1 1.6 %first_columns.1 = (bf16[512,1024]{1,0:T(8,128)(2,1)S(1)}, f32[512,128]{1,0:T(8,128)S(1)}, f32[8,128]{1,0:T(8,128)S(1)}, f32[512,1024]{1,0:T(8,128)S(1)}, f32[51...) custom-call(bf16[144,1024]{1,0:T(8,128)(2,1)S(1)} %copy-done, ...), custom_call_target="tpu_custom_call" | custom-call | flops 1073741824 | bytes 1048576 | tf_op jit(solution)/shard_map/first_columns/pallas_call | solution.py:30
  53.8 0.5 collective-permute-start.10
  54.3 0.1 collective-permute-start.11
  54.4 0.4 collective-permute-start.12
  54.9 3.3 %more_columns.2 = (f32[512,1024]{1,0:T(8,128)S(1)}, f32[512,1024]{1,0:T(8,128)S(1)}, f32[512,128]{1,0:T(8,128)S(1)}, f32[512,128]{1,0:T(8,128)S(1)}) custom-call(bf16[512,1024]{1,0:T(8,128)(2,1)S(1)} %get-tuple-element.41.panel.refs_0_, ...), custom_call_target="tpu_custom_call", output_to_operand_aliasing={{0}: (4, {}), {1}: (5, {}), {2}: (6, {}), {3}: (7, {})} | custom-call | flops 2147483648 | bytes 1048576 | tf_op jit(solution)/shard_map/more_columns/pallas_call | solution.py:30
  58.2 3.3 %more_columns.3 = (f32[512,1024]{1,0:T(8,128)S(1)}, f32[512,1024]{1,0:T(8,128)S(1)}, f32[512,128]{1,0:T(8,128)S(1)}, f32[512,128]{1,0:T(8,128)S(1)}) custom-call(bf16[512,1024]{1,0:T(8,128)(2,1)S(1)} %get-tuple-element.41.panel.refs_0_, ...), custom_call_target="tpu_custom_call", output_to_operand_aliasing={{0}: (4, {}), {1}: (5, {}), {2}: (6, {}), {3}: (7, {})} | custom-call | flops 2147483648 | bytes 1048576 | tf_op jit(solution)/shard_map/more_columns/pallas_call | solution.py:30
  61.5 3.3 %far_terms.1 = (s16[128,1152]{1,0:T(8,128)(2,1)S(1)}, s16[128,1152]{1,0:T(8,128)(2,1)S(1)}, s16[32,1152]{1,0:T(8,128)(2,1)S(1)}, s16[32,1152]{1,0:T(8,128)(2,1)S(1)}) custom-call(bf16[512,1024]{1,0:T(8,128)(2,1)S(1)} %get-tuple-element.41.panel.refs_0_, f32[512,128]{1,0:T(8,128)S(1)} %get-tuple-element.42.refs_4_.norms.refs_1_, ...), custom_call_target="tpu_custom_call" | custom-call | flops 2013265920 | bytes 1048576 | tf_op jit(solution)/shard_map/far_terms/pallas_call | solution.py:30
  64.8 4.3 %collective-permute-start.15 = (s16[128,1152]{1,0:T(8,128)(2,1)S(1)}, s16[128,1152]{1,0:T(8,128)(2,1)S(1)}, u32[]{:S(2)}, u32[]{:S(2)}) collective-permute-start(s16[128,1152]{1,0:T(8,128)(2,1)S(1)} %get-tuple-element.62), channel_id=1, source_target_pairs={{0,128},{128,1},{1,129},{129,2},{2,130},{130,3},{3,131},{131,0},{4... | collective-permute-start | bytes 884744 | tf_op jit(solution)/shard_map/ppermute | solution.py:280
  69.1 2.2 %collective-permute-start.17 = (s16[32,1152]{1,0:T(8,128)(2,1)S(1)}, s16[32,1152]{1,0:T(8,128)(2,1)S(1)}, u32[]{:S(2)}, u32[]{:S(2)}) collective-permute-start(s16[32,1152]{1,0:T(8,128)(2,1)S(1)} %get-tuple-element.64), channel_id=1, source_target_pairs={{0,1},{128,129},{1,2},{129,130},{2,3},{130,131},{3,0},{131,128},{4... | collective-permute-start | bytes 221192 | tf_op jit(solution)/shard_map/ppermute | solution.py:280
  71.3 1.9 %collective-permute-start.18 = (s16[32,1152]{1,0:T(8,128)(2,1)S(1)}, s16[32,1152]{1,0:T(8,128)(2,1)S(1)}, u32[]{:S(2)}, u32[]{:S(2)}) collective-permute-start(s16[32,1152]{1,0:T(8,128)(2,1)S(1)} %get-tuple-element.65), channel_id=1, source_target_pairs={{0,3},{128,131},{1,0},{129,128},{2,1},{130,129},{3,2},{131,130},{4... | collective-permute-start | bytes 221192 | tf_op jit(solution)/shard_map/ppermute | solution.py:280
  73.2 2.1 %near_terms.1 = (f32[192,1024]{1,0:T(8,128)S(1)}, f32[192,128]{1,0:T(8,128)S(1)}) custom-call(bf16[512,1024]{1,0:T(8,128)(2,1)S(1)} %get-tuple-element.41.panel.refs_0_, f32[512,128]{1,0:T(8,128)S(1)} %get-tuple-element.42.refs_4_.norms.refs_1_, bf16[528,1024]{1,0:T(8,128)(2,1)S(1)} %collective-permute-done.10.refs_2_, ...), custom_call_target="tpu_custom_call" | custom-call | flops 1207959552 | bytes 1048576 | tf_op jit(solution)/shard_map/near_terms/pallas_call | solution.py:30
  75.4 3.7 %collective-permute-done.17.half_below = s16[32,1152]{1,0:T(8,128)(2,1)S(1)} collective-permute-done((s16[32,1152]{1,0:T(8,128)(2,1)S(1)}, s16[32,1152]{1,0:T(8,128)(2,1)S(1)}, u32[]{:S(2)}, u32[]{:S(2)}) %collective-permute-start.17) | collective-permute-done | bytes 73760 | tf_op jit(solution)/shard_map/ppermute | solution.py:280
  79.1 2.4 %collective-permute-done.18.half_above = s16[32,1152]{1,0:T(8,128)(2,1)S(1)} collective-permute-done((s16[32,1152]{1,0:T(8,128)(2,1)S(1)}, s16[32,1152]{1,0:T(8,128)(2,1)S(1)}, u32[]{:S(2)}, u32[]{:S(2)}) %collective-permute-start.18) | collective-permute-done | bytes 73760 | tf_op jit(solution)/shard_map/ppermute | solution.py:280
  81.5 0.5 pass_on.1
  82.1 2.2 %collective-permute-start.19 = (s16[64,1152]{1,0:T(8,128)(2,1)S(1)}, s16[64,1152]{1,0:T(8,128)(2,1)S(1)}, u32[]{:S(2)}, u32[]{:S(2)}) collective-permute-start(s16[64,1152]{1,0:T(8,128)(2,1)S(1)} %get-tuple-element.66), channel_id=1, source_target_pairs={{0,1},{128,129},{1,2},{129,130},{2,3},{130,131},{3,0},{131,128},{4... | collective-permute-start | bytes 442376 | tf_op jit(solution)/shard_map/ppermute | solution.py:280
  84.3 2.0 %collective-permute-start.20 = (s16[64,1152]{1,0:T(8,128)(2,1)S(1)}, s16[64,1152]{1,0:T(8,128)(2,1)S(1)}, u32[]{:S(2)}, u32[]{:S(2)}) collective-permute-start(s16[64,1152]{1,0:T(8,128)(2,1)S(1)} %get-tuple-element.67), channel_id=1, source_target_pairs={{0,3},{128,131},{1,0},{129,128},{2,1},{130,129},{3,2},{131,130},{4... | collective-permute-start | bytes 442376 | tf_op jit(solution)/shard_map/ppermute | solution.py:280
  86.3 5.6 %collective-permute-done.19.far_below = s16[64,1152]{1,0:T(8,128)(2,1)S(1)} collective-permute-done((s16[64,1152]{1,0:T(8,128)(2,1)S(1)}, s16[64,1152]{1,0:T(8,128)(2,1)S(1)}, u32[]{:S(2)}, u32[]{:S(2)}) %collective-permute-start.19) | collective-permute-done | bytes 147488 | tf_op jit(solution)/shard_map/ppermute | solution.py:280
  92.0 1.1 %add_up.1 = (f32[1,64]{1,0:T(1,128)}, f32[64,1024]{1,0:T(8,128)}) custom-call(f32[192,1024]{1,0:T(8,128)S(1)} %get-tuple-element.60.gradient, f32[192,128]{1,0:T(8,128)S(1)} %get-tuple-element.61.proof, s16[128,1152]{1,0:T(8,128)(2,1)S(1)} %collective-permute-done.15.from_below, s16[128,1152]{1,0:T(8,128)(2,1)S(1)} %collective-permute-done.16.from_above, ...), custom_call_target="tpu_custom_call" | custom-call | bytes 1048576 | tf_op jit(solution)/shard_map/add_up/pallas_call | solution.py:30
  (25 shorter events, 0.3 us)
Async XLA Ops:
  2.6 14.1 %collective-permute-start.2 = (bf16[144,1024]{1,0:T(8,128)(2,1)}, bf16[144,1024]{1,0:T(8,128)(2,1)S(1)}, u32[]{:S(2)}, u32[]{:S(2)}) collective-permute-start(bf16[144,1024]{1,0:T(8,128)(2,1)} %get-tuple-element.36.refs_0_.block), channel_id=1, source_target_pairs={{0,32},{16,20},{4,36},{20,24},{8,40},{24,28},{12,44},{28,16},{32,6... | collective-permute-start | bytes 884744 | tf_op jit(solution)/shard_map/ppermute | solution.py:290
  4.1 12.6 %collective-permute-start.3 = (bf16[144,1024]{1,0:T(8,128)(2,1)}, bf16[144,1024]{1,0:T(8,128)(2,1)S(1)}, u32[]{:S(2)}, u32[]{:S(2)}) collective-permute-start(bf16[144,1024]{1,0:T(8,128)(2,1)} %get-tuple-element.36.refs_0_.block), channel_id=1, source_target_pairs={{0,96},{16,28},{4,100},{20,16},{8,104},{24,20},{12,108},{28,24},{3... | collective-permute-start | bytes 884744 | tf_op jit(solution)/shard_map/ppermute | solution.py:290
  5.8 10.8 %collective-permute-start.4 = (bf16[144,1024]{1,0:T(8,128)(2,1)}, bf16[144,1024]{1,0:T(8,128)(2,1)S(1)}, u32[]{:S(2)}, u32[]{:S(2)}) collective-permute-start(bf16[144,1024]{1,0:T(8,128)(2,1)} %get-tuple-element.36.refs_0_.block), channel_id=1, source_target_pairs={{0,64},{16,24},{4,68},{20,28},{8,72},{24,16},{12,76},{28,20},{32,9... | collective-permute-start | bytes 884744 | tf_op jit(solution)/shard_map/ppermute | solution.py:290
  7.7 9.0 %collective-permute-start = (bf16[64,1024]{1,0:T(8,128)(2,1)}, bf16[64,1024]{1,0:T(8,128)(2,1)S(1)}, u32[]{:S(2)}, u32[]{:S(2)}) collective-permute-start(bf16[64,1024]{1,0:T(8,128)(2,1)} %pool.1), channel_id=1, source_target_pairs={{0,128},{128,1},{1,129},{129,2},{2,130},{130,3},{3,131},{131,0},{4... | collective-permute-start | bytes 393224 | tf_op jit(solution)/shard_map/ppermute | solution.py:280
  9.6 7.1 %collective-permute-start.1 = (bf16[64,1024]{1,0:T(8,128)(2,1)}, bf16[64,1024]{1,0:T(8,128)(2,1)S(1)}, u32[]{:S(2)}, u32[]{:S(2)}) collective-permute-start(bf16[64,1024]{1,0:T(8,128)(2,1)} %pool.1), channel_id=1, source_target_pairs={{0,131},{128,0},{1,128},{129,1},{2,129},{130,2},{3,130},{131,3},{4... | collective-permute-start | bytes 393224 | tf_op jit(solution)/shard_map/ppermute | solution.py:280
  16.7 1.0 %copy-start = (bf16[144,1024]{1,0:T(8,128)(2,1)S(1)}, bf16[144,1024]{1,0:T(8,128)(2,1)}, u32[]{:S(2)}) copy-start(bf16[144,1024]{1,0:T(8,128)(2,1)} %get-tuple-element.36.refs_0_.block) | copy-start | bytes 884740
  17.7 9.6 %copy-start.1 = (f32[128,1,128]{2,1,0:T(1,128)S(1)}, f32[128,1,128]{2,1,0:T(1,128)}, u32[]{:S(2)}) copy-start(f32[128,1,128]{2,1,0:T(1,128)} %get-tuple-element.39) | copy-start | bytes 196612
  17.8 35.9 %collective-permute-start.7 = (bf16[528,1024]{1,0:T(8,128)(2,1)S(1)}, bf16[528,1024]{1,0:T(8,128)(2,1)S(1)}, u32[]{:S(2)}, u32[]{:S(2)}) collective-permute-start(bf16[528,1024]{1,0:T(8,128)(2,1)S(1)} %get-tuple-element.40.refs_0_), channel_id=1, source_target_pairs={{0,4},{16,48},{4,8},{20,52},{8,12},{24,56},{12,0},{28,60},{32,36},... | collective-permute-start | bytes 3244040 | tf_op jit(solution)/shard_map/ppermute | solution.py:290
  19.4 34.2 %collective-permute-start.8 = (bf16[528,1024]{1,0:T(8,128)(2,1)S(1)}, bf16[528,1024]{1,0:T(8,128)(2,1)S(1)}, u32[]{:S(2)}, u32[]{:S(2)}) collective-permute-start(bf16[528,1024]{1,0:T(8,128)(2,1)S(1)} %get-tuple-element.40.refs_0_), channel_id=1, source_target_pairs={{0,12},{16,112},{4,0},{20,116},{8,4},{24,120},{12,8},{28,124},{32,... | collective-permute-start | bytes 3244040 | tf_op jit(solution)/shard_map/ppermute | solution.py:290
  19.9 33.8 %collective-permute-start.9 = (bf16[528,1024]{1,0:T(8,128)(2,1)S(1)}, bf16[528,1024]{1,0:T(8,128)(2,1)S(1)}, u32[]{:S(2)}, u32[]{:S(2)}) collective-permute-start(bf16[528,1024]{1,0:T(8,128)(2,1)S(1)} %get-tuple-element.40.refs_0_), channel_id=1, source_target_pairs={{0,8},{16,80},{4,12},{20,84},{8,0},{24,88},{12,4},{28,92},{32,40},... | collective-permute-start | bytes 3244040 | tf_op jit(solution)/shard_map/ppermute | solution.py:290
  22.2 29.9 %collective-permute-start.5 = (bf16[160,1024]{1,0:T(8,128)(2,1)S(1)}, bf16[160,1024]{1,0:T(8,128)(2,1)S(1)}, u32[]{:S(2)}, u32[]{:S(2)}) collective-permute-start(bf16[160,1024]{1,0:T(8,128)(2,1)S(1)} %get-tuple-element.37), channel_id=1, source_target_pairs={{0,129},{128,2},{1,130},{129,3},{2,131},{130,0},{3,128},{131,1},{4... | collective-permute-start | bytes 983048 | tf_op jit(solution)/shard_map/ppermute | solution.py:280
  27.3 24.8 %collective-permute-start.6 = (bf16[160,1024]{1,0:T(8,128)(2,1)S(1)}, bf16[160,1024]{1,0:T(8,128)(2,1)S(1)}, u32[]{:S(2)}, u32[]{:S(2)}) collective-permute-start(bf16[160,1024]{1,0:T(8,128)(2,1)S(1)} %get-tuple-element.38), channel_id=1, source_target_pairs={{0,130},{128,3},{1,131},{129,0},{2,128},{130,1},{3,129},{131,2},{4... | collective-permute-start | bytes 983048 | tf_op jit(solution)/shard_map/ppermute | solution.py:280
  53.7 4.5 %collective-permute-start.13 = (bf16[528,1024]{1,0:T(8,128)(2,1)S(1)}, bf16[528,1024]{1,0:T(8,128)(2,1)S(1)}, u32[]{:S(2)}, u32[]{:S(2)}) collective-permute-start(bf16[528,1024]{1,0:T(8,128)(2,1)S(1)} %get-tuple-element.46), channel_id=1, source_target_pairs={{0,16},{16,0},{1,17},{17,1},{2,18},{18,2},{3,19},{19,3},{4,20},{20... | collective-permute-start | bytes 3244040 | tf_op jit(solution)/shard_map/ppermute | solution.py:298
  53.8 7.7 %collective-permute-start.10 = (bf16[528,1024]{1,0:T(8,128)(2,1)S(1)}, bf16[528,1024]{1,0:T(8,128)(2,1)S(1)}, u32[]{:S(2)}, u32[]{:S(2)}) collective-permute-start(bf16[528,1024]{1,0:T(8,128)(2,1)S(1)} %get-tuple-element.43.refs_0_), channel_id=1, source_target_pairs={{0,16},{16,0},{1,17},{17,1},{2,18},{18,2},{3,19},{19,3},{4,20},{20... | collective-permute-start | bytes 3244040 | tf_op jit(solution)/shard_map/ppermute | solution.py:298
  54.3 7.2 %collective-permute-start.11 = (bf16[528,1024]{1,0:T(8,128)(2,1)S(1)}, bf16[528,1024]{1,0:T(8,128)(2,1)S(1)}, u32[]{:S(2)}, u32[]{:S(2)}) collective-permute-start(bf16[528,1024]{1,0:T(8,128)(2,1)S(1)} %get-tuple-element.44.refs_1_), channel_id=1, source_target_pairs={{0,16},{16,0},{1,17},{17,1},{2,18},{18,2},{3,19},{19,3},{4,20},{20... | collective-permute-start | bytes 3244040 | tf_op jit(solution)/shard_map/ppermute | solution.py:298
  54.4 7.1 %collective-permute-start.12 = (bf16[528,1024]{1,0:T(8,128)(2,1)S(1)}, bf16[528,1024]{1,0:T(8,128)(2,1)S(1)}, u32[]{:S(2)}, u32[]{:S(2)}) collective-permute-start(bf16[528,1024]{1,0:T(8,128)(2,1)S(1)} %get-tuple-element.45.refs_0_), channel_id=1, source_target_pairs={{0,16},{16,0},{1,17},{17,1},{2,18},{18,2},{3,19},{19,3},{4,20},{20... | collective-permute-start | bytes 3244040 | tf_op jit(solution)/shard_map/ppermute | solution.py:298
  54.8 6.7 %collective-permute-start.14 = (f32[8,128]{1,0:T(8,128)S(1)}, f32[8,128]{1,0:T(8,128)S(1)}, u32[]{:S(2)}, u32[]{:S(2)}) collective-permute-start(f32[8,128]{1,0:T(8,128)S(1)} %get-tuple-element.59.refs_9_), channel_id=1, source_target_pairs={{0,16},{16,0},{1,17},{17,1},{2,18},{18,2},{3,19},{19,3},{4,20},{20... | collective-permute-start | bytes 12296 | tf_op jit(solution)/shard_map/ppermute | solution.py:298
  64.8 16.7 %collective-permute-start.15 = (s16[128,1152]{1,0:T(8,128)(2,1)S(1)}, s16[128,1152]{1,0:T(8,128)(2,1)S(1)}, u32[]{:S(2)}, u32[]{:S(2)}) collective-permute-start(s16[128,1152]{1,0:T(8,128)(2,1)S(1)} %get-tuple-element.62), channel_id=1, source_target_pairs={{0,128},{128,1},{1,129},{129,2},{2,130},{130,3},{3,131},{131,0},{4... | collective-permute-start | bytes 884744 | tf_op jit(solution)/shard_map/ppermute | solution.py:280
  69.1 12.4 %collective-permute-start.16 = (s16[128,1152]{1,0:T(8,128)(2,1)S(1)}, s16[128,1152]{1,0:T(8,128)(2,1)S(1)}, u32[]{:S(2)}, u32[]{:S(2)}) collective-permute-start(s16[128,1152]{1,0:T(8,128)(2,1)S(1)} %get-tuple-element.63), channel_id=1, source_target_pairs={{0,131},{128,0},{1,128},{129,1},{2,129},{130,2},{3,130},{131,3},{4... | collective-permute-start | bytes 884744 | tf_op jit(solution)/shard_map/ppermute | solution.py:280
  69.1 10.0 %collective-permute-start.17 = (s16[32,1152]{1,0:T(8,128)(2,1)S(1)}, s16[32,1152]{1,0:T(8,128)(2,1)S(1)}, u32[]{:S(2)}, u32[]{:S(2)}) collective-permute-start(s16[32,1152]{1,0:T(8,128)(2,1)S(1)} %get-tuple-element.64), channel_id=1, source_target_pairs={{0,1},{128,129},{1,2},{129,130},{2,3},{130,131},{3,0},{131,128},{4... | collective-permute-start | bytes 221192 | tf_op jit(solution)/shard_map/ppermute | solution.py:280
  71.3 10.2 %collective-permute-start.18 = (s16[32,1152]{1,0:T(8,128)(2,1)S(1)}, s16[32,1152]{1,0:T(8,128)(2,1)S(1)}, u32[]{:S(2)}, u32[]{:S(2)}) collective-permute-start(s16[32,1152]{1,0:T(8,128)(2,1)S(1)} %get-tuple-element.65), channel_id=1, source_target_pairs={{0,3},{128,131},{1,0},{129,128},{2,1},{130,129},{3,2},{131,130},{4... | collective-permute-start | bytes 221192 | tf_op jit(solution)/shard_map/ppermute | solution.py:280
  82.1 9.9 %collective-permute-start.19 = (s16[64,1152]{1,0:T(8,128)(2,1)S(1)}, s16[64,1152]{1,0:T(8,128)(2,1)S(1)}, u32[]{:S(2)}, u32[]{:S(2)}) collective-permute-start(s16[64,1152]{1,0:T(8,128)(2,1)S(1)} %get-tuple-element.66), channel_id=1, source_target_pairs={{0,1},{128,129},{1,2},{129,130},{2,3},{130,131},{3,0},{131,128},{4... | collective-permute-start | bytes 442376 | tf_op jit(solution)/shard_map/ppermute | solution.py:280
  84.3 7.7 %collective-permute-start.20 = (s16[64,1152]{1,0:T(8,128)(2,1)S(1)}, s16[64,1152]{1,0:T(8,128)(2,1)S(1)}, u32[]{:S(2)}, u32[]{:S(2)}) collective-permute-start(s16[64,1152]{1,0:T(8,128)(2,1)S(1)} %get-tuple-element.67), channel_id=1, source_target_pairs={{0,3},{128,131},{1,0},{129,128},{2,1},{130,129},{3,2},{131,130},{4... | collective-permute-start | bytes 442376 | tf_op jit(solution)/shard_map/ppermute | solution.py:280

commit v10 on v9

--- a/solution.py
+++ b/solution.py
@@ -135,10 +135,13 @@
             pulls[half][part, :] = total
 
 
-def first_columns(rows, lines, block, below, above, far_below, far_above, chosen, *refs):
+def add_counts(chosen, total):
+    total[...] = jnp.broadcast_to(jnp.sum(chosen[...], axis=0), total.shape)
+
+
+def first_columns(rows, lines, block, below, above, far_below, far_above, *refs):
     pieces, refs = refs[:lines], refs[lines:]
-    ordered, norms, total, pp, tp, pm, tm, *weights = refs
-    total[...] = jnp.broadcast_to(jnp.sum(chosen[...], axis=0), total.shape)
+    ordered, norms, pp, tp, pm, tm, *weights = refs
     height = below.shape[0]
     found = {
         0: block[:height, :],
@@ -158,12 +161,6 @@
     add_columns(ordered, norms, pieces, (), (pp, tp), (pm, tm), weights, rows)
 
 
-def more_columns(rows, lines, panel, norms, *refs):
-    pieces, old, refs = refs[:lines], refs[lines : lines + 4], refs[lines + 4 :]
-    pp, tp, pm, tm, *weights = refs
-    add_columns(panel, norms, pieces, old, (pp, tp), (pm, tm), weights, rows)
-
-
 def terms(target_count, panel, pp, tp, pm, tm, total, other_total, part):
     weight = total[:1, :1] + other_total[:1, :1]
     pool_mass = jnp.sum(pm[part, :], axis=1, keepdims=True)
@@ -334,33 +331,28 @@
             aliases=aliases,
         )(*arrays, *some, *state)
 
-    def more(some, state):
-        return add(more_columns, (panel, norms), some, state, sums, {2 + len(some) + i: i for i in range(4)})
-
-    panel, norms, total, *state = add(
+    pieces = handed_on(pieces, chosen, *pairs)
+    total = in_vmem(add_counts, "add_counts", shape((8, LANES), F32))(chosen)
+    others = [other_core(p) for p in pieces]
+    panel, norms, *state = add(
         first_columns,
-        (block, below, above, *pairs, chosen),
-        pieces[:1],
+        (block, below, above, *pairs),
+        pieces,
         (),
-        (shape((rows, width), BF16), shape((rows, LANES), F32), shape((8, LANES), F32), *sums),
+        (shape((rows, width), BF16), shape((rows, LANES), F32), *sums),
         {},
     )
     totals = total, other_core(total)
-    pieces = handed_on(pieces, norms)
-    others = [other_core(p) for p in pieces]
-    for some in (pieces[1:3], (pieces[3], others[0])):
-        state = more(some, state)
-
-    inputs = panel, norms, *others[1:], *state, *totals
+    inputs = panel, norms, *others, *state, *totals
 
     def last(body, count, out_shape):
         return in_vmem(
-            functools.partial(body, target_count, 3, height),
+            functools.partial(body, target_count, len(others), height),
             body.__name__,
             out_shape,
-            flops=8 * count * 3 * size * width,
+            flops=8 * count * len(others) * size * width,
             scratch=[pltpu.VMEM((count, n), F32) for n in (width, width, LANES, LANES)]
-            + [pltpu.VMEM((count, 3 * size), BF16)] * 2,
+            + [pltpu.VMEM((count, len(others) * size), BF16)] * 2,
             limit=16,
         )(*inputs)
 

time: 94.5 us -> 92 us (0.974)
  Pallas kernels: 17.3 us -> 15.7 us
    pallas_call x9 -> x8, Pallas kernels: 17.3 us -> 15.7 us  [call(): pl.pallas_call(body, out_shape=out_shape, in_specs=[spec] * len(args), ou...]
    ppermute x10, waiting for transfers between devices: 15 us -> 13.5 us  [up_the_ring(): lax.ppermute(x, RING, [(place(i), place((i + step) % ring)) for i in rang...]
  transfers between devices with their start and end apart: 21 -> 21, of which waited for: 4 -> 6; matrix products, arithmetic and copies ran while one was open for 0% -> 0% of each run, Pallas kernels for 11% -> 9%
where the time goes in v10:
time: 92 us; the launch traced here: 90.9 us
  starting transfers between devices  34.5 us (38%)
  blocking collectives  24.7 us (27%)
  Pallas kernels  15.7 us (17%)
  waiting for transfers between devices  14.2 us (15%)
  local copies, waits for them, and re-layouts  0.96 us (1%)
    all_to_all x1, blocking collectives, on_device(): lax.all_to_all(chosen, CHIPS, split_axis=0, concat_axis=0, tiled=True)  24.7 us
    ppermute x10, starting transfers between devices, up_the_ring(): lax.ppermute(x, RING, [(place(i), place((i + step) % ring)) for i in rang...  23.6 us
    pallas_call x8, Pallas kernels, call(): pl.pallas_call(body, out_shape=out_shape, in_specs=[spec] * len(args), ou...  15.7 us
    ppermute x10, waiting for transfers between devices, up_the_ring(): lax.ppermute(x, RING, [(place(i), place((i + step) % ring)) for i in rang...  13.5 us
    ppermute x6, starting transfers between devices, along_line(): return lax.ppermute(x, PLANE, pairs)  9.45 us
  transfers between devices with their start and end apart: 21, of which 6 were waited for; matrix products, arithmetic and copies ran while one was open for 0% of the time, Pallas kernels for 9%

profile of v10, /device:TPU:8, one launch (start us, length us, event | category | flops | bytes accessed | tf_op | source)
XLA Modules:
  0.0 90.9 jit_solution(9064840513964897194)
XLA Ops:
  0.6 2.0 %pack_block.1 = (bf16[144,1024]{1,0:T(8,128)(2,1)}, f32[128,1,128]{2,1,0:T(1,128)}) custom-call(bf16[64,1024]{1,0:T(8,128)(2,1)} %pool.1, bf16[64,1024]{1,0:T(8,128)(2,1)} %targets.1, s32[1,64]{1,0:T(1,128)} %bitcast.2), custom_call_target="tpu_custom_call" | custom-call | bytes 1048576 | tf_op jit(solution)/shard_map/pack_block/pallas_call | solution.py:30
  2.6 1.5 %collective-permute-start.2 = (bf16[144,1024]{1,0:T(8,128)(2,1)}, bf16[144,1024]{1,0:T(8,128)(2,1)S(1)}, u32[]{:S(2)}, u32[]{:S(2)}) collective-permute-start(bf16[144,1024]{1,0:T(8,128)(2,1)} %get-tuple-element.27.refs_0_.block), channel_id=1, source_target_pairs={{0,32},{16,20},{4,36},{20,24},{8,40},{24,28},{12,44},{28,16},{32,6... | collective-permute-start | bytes 884744 | tf_op jit(solution)/shard_map/ppermute | solution.py:287
  4.1 1.7 %collective-permute-start.3 = (bf16[144,1024]{1,0:T(8,128)(2,1)}, bf16[144,1024]{1,0:T(8,128)(2,1)S(1)}, u32[]{:S(2)}, u32[]{:S(2)}) collective-permute-start(bf16[144,1024]{1,0:T(8,128)(2,1)} %get-tuple-element.27.refs_0_.block), channel_id=1, source_target_pairs={{0,96},{16,28},{4,100},{20,16},{8,104},{24,20},{12,108},{28,24},{3... | collective-permute-start | bytes 884744 | tf_op jit(solution)/shard_map/ppermute | solution.py:287
  5.8 1.8 %collective-permute-start.4 = (bf16[144,1024]{1,0:T(8,128)(2,1)}, bf16[144,1024]{1,0:T(8,128)(2,1)S(1)}, u32[]{:S(2)}, u32[]{:S(2)}) collective-permute-start(bf16[144,1024]{1,0:T(8,128)(2,1)} %get-tuple-element.27.refs_0_.block), channel_id=1, source_target_pairs={{0,64},{16,24},{4,68},{20,28},{8,72},{24,16},{12,76},{28,20},{32,9... | collective-permute-start | bytes 884744 | tf_op jit(solution)/shard_map/ppermute | solution.py:287
  7.7 1.9 %collective-permute-start = (bf16[64,1024]{1,0:T(8,128)(2,1)}, bf16[64,1024]{1,0:T(8,128)(2,1)S(1)}, u32[]{:S(2)}, u32[]{:S(2)}) collective-permute-start(bf16[64,1024]{1,0:T(8,128)(2,1)} %pool.1), channel_id=1, source_target_pairs={{0,128},{128,1},{1,129},{129,2},{2,130},{130,3},{3,131},{131,0},{4... | collective-permute-start | bytes 393224 | tf_op jit(solution)/shard_map/ppermute | solution.py:277
  9.6 3.9 %collective-permute-start.1 = (bf16[64,1024]{1,0:T(8,128)(2,1)}, bf16[64,1024]{1,0:T(8,128)(2,1)S(1)}, u32[]{:S(2)}, u32[]{:S(2)}) collective-permute-start(bf16[64,1024]{1,0:T(8,128)(2,1)} %pool.1), channel_id=1, source_target_pairs={{0,131},{128,0},{1,128},{129,1},{2,129},{130,2},{3,130},{131,3},{4... | collective-permute-start | bytes 393224 | tf_op jit(solution)/shard_map/ppermute | solution.py:277
  13.5 3.2 %collective-permute-done.refs_4_.below = bf16[64,1024]{1,0:T(8,128)(2,1)S(1)} collective-permute-done((bf16[64,1024]{1,0:T(8,128)(2,1)}, bf16[64,1024]{1,0:T(8,128)(2,1)S(1)}, u32[]{:S(2)}, u32[]{:S(2)}) %collective-permute-start) | collective-permute-done | bytes 131104 | tf_op jit(solution)/shard_map/ppermute | solution.py:277
  16.7 1.0 %copy-done = bf16[144,1024]{1,0:T(8,128)(2,1)S(1)} copy-done((bf16[144,1024]{1,0:T(8,128)(2,1)S(1)}, bf16[144,1024]{1,0:T(8,128)(2,1)}, u32[]{:S(2)}) %copy-start) | copy-done | bytes 294936
  17.8 1.7 %collective-permute-start.7 = (bf16[528,1024]{1,0:T(8,128)(2,1)S(1)}, bf16[528,1024]{1,0:T(8,128)(2,1)S(1)}, u32[]{:S(2)}, u32[]{:S(2)}) collective-permute-start(bf16[528,1024]{1,0:T(8,128)(2,1)S(1)} %get-tuple-element.30.refs_0_), channel_id=1, source_target_pairs={{0,4},{16,48},{4,8},{20,52},{8,12},{24,56},{12,0},{28,60},{32,36},... | collective-permute-start | bytes 3244040 | tf_op jit(solution)/shard_map/ppermute | solution.py:287
  19.4 0.4 collective-permute-start.8
  19.9 2.3 %collective-permute-start.9 = (bf16[528,1024]{1,0:T(8,128)(2,1)S(1)}, bf16[528,1024]{1,0:T(8,128)(2,1)S(1)}, u32[]{:S(2)}, u32[]{:S(2)}) collective-permute-start(bf16[528,1024]{1,0:T(8,128)(2,1)S(1)} %get-tuple-element.30.refs_0_), channel_id=1, source_target_pairs={{0,8},{16,80},{4,12},{20,84},{8,0},{24,88},{12,4},{28,92},{32,40},... | collective-permute-start | bytes 3244040 | tf_op jit(solution)/shard_map/ppermute | solution.py:287
  22.2 5.1 %collective-permute-start.5 = (bf16[160,1024]{1,0:T(8,128)(2,1)S(1)}, bf16[160,1024]{1,0:T(8,128)(2,1)S(1)}, u32[]{:S(2)}, u32[]{:S(2)}) collective-permute-start(bf16[160,1024]{1,0:T(8,128)(2,1)S(1)} %get-tuple-element.28), channel_id=1, source_target_pairs={{0,129},{128,2},{1,130},{129,3},{2,131},{130,0},{3,128},{131,1},{4... | collective-permute-start | bytes 983048 | tf_op jit(solution)/shard_map/ppermute | solution.py:277
  27.3 24.7 %all_to_all.5.refs_4_.chosen = f32[128,1,128]{2,1,0:T(1,128)S(1)} all-to-all(f32[128,1,128]{2,1,0:T(1,128)S(1)} %copy-done.2), channel_id=1, replica_groups=mesh['zl'=2,'x'=4,'c'=2,'y'=4,'zh'=4] {'zl','x','y','zh'}, dimensions={0} | all-to-all | bytes 131072 | tf_op jit(solution)/shard_map/all_to_all | solution.py:310
  52.2 0.5 collective-permute-start.11
  52.8 0.4 collective-permute-start.13
  53.2 0.1 add_counts.1.refs_10_
  53.4 0.4 collective-permute-start.14
  53.7 5.1 %first_columns.1 = (bf16[512,1024]{1,0:T(8,128)(2,1)S(1)}, f32[512,128]{1,0:T(8,128)S(1)}, f32[512,1024]{1,0:T(8,128)S(1)}, f32[512,1024]{1,0:T(8,128)S(1)}, f32...) custom-call(bf16[144,1024]{1,0:T(8,128)(2,1)S(1)} %copy-done.1, bf16[64,1024]{1,0:T(8,128)(2,1)S(1)} %collective-permute-done.refs_4_.below, ...), custom_call_target="tpu_custom_call" | custom-call | flops 4294967296 | bytes 1048576 | tf_op jit(solution)/shard_map/first_columns/pallas_call | solution.py:30
  58.9 0.7 collective-permute-done.14.refs_11_
  59.6 4.0 %far_terms.1 = (s16[128,1152]{1,0:T(8,128)(2,1)S(1)}, s16[128,1152]{1,0:T(8,128)(2,1)S(1)}, s16[32,1152]{1,0:T(8,128)(2,1)S(1)}, s16[32,1152]{1,0:T(8,128)(2,1)S(1)}) custom-call(bf16[512,1024]{1,0:T(8,128)(2,1)S(1)} %get-tuple-element.36.refs_0_, f32[512,128]{1,0:T(8,128)S(1)} %get-tuple-element.37.refs_1_, ...), custom_call_target="tpu_custom_call" | custom-call | flops 2684354560 | bytes 1048576 | tf_op jit(solution)/shard_map/far_terms/pallas_call | solution.py:30
  63.6 4.3 %collective-permute-start.15 = (s16[128,1152]{1,0:T(8,128)(2,1)S(1)}, s16[128,1152]{1,0:T(8,128)(2,1)S(1)}, u32[]{:S(2)}, u32[]{:S(2)}) collective-permute-start(s16[128,1152]{1,0:T(8,128)(2,1)S(1)} %get-tuple-element.44), channel_id=1, source_target_pairs={{0,128},{128,1},{1,129},{129,2},{2,130},{130,3},{3,131},{131,0},{4... | collective-permute-start | bytes 884744 | tf_op jit(solution)/shard_map/ppermute | solution.py:277
  67.9 2.2 %collective-permute-start.17 = (s16[32,1152]{1,0:T(8,128)(2,1)S(1)}, s16[32,1152]{1,0:T(8,128)(2,1)S(1)}, u32[]{:S(2)}, u32[]{:S(2)}) collective-permute-start(s16[32,1152]{1,0:T(8,128)(2,1)S(1)} %get-tuple-element.46), channel_id=1, source_target_pairs={{0,1},{128,129},{1,2},{129,130},{2,3},{130,131},{3,0},{131,128},{4... | collective-permute-start | bytes 221192 | tf_op jit(solution)/shard_map/ppermute | solution.py:277
  70.1 1.9 %collective-permute-start.18 = (s16[32,1152]{1,0:T(8,128)(2,1)S(1)}, s16[32,1152]{1,0:T(8,128)(2,1)S(1)}, u32[]{:S(2)}, u32[]{:S(2)}) collective-permute-start(s16[32,1152]{1,0:T(8,128)(2,1)S(1)} %get-tuple-element.47), channel_id=1, source_target_pairs={{0,3},{128,131},{1,0},{129,128},{2,1},{130,129},{3,2},{131,130},{4... | collective-permute-start | bytes 221192 | tf_op jit(solution)/shard_map/ppermute | solution.py:277
  72.0 2.7 %near_terms.1 = (f32[192,1024]{1,0:T(8,128)S(1)}, f32[192,128]{1,0:T(8,128)S(1)}) custom-call(bf16[512,1024]{1,0:T(8,128)(2,1)S(1)} %get-tuple-element.36.refs_0_, f32[512,128]{1,0:T(8,128)S(1)} %get-tuple-element.37.refs_1_, bf16[528,1024]{1,0:T(8,128)(2,1)S(1)} %collective-permute-done.10.refs_2_, bf16[528,1024]{1,0:T(8,128)(2,1)S(1)} %collective-permute-done.11.refs_3_, ...), custom_call_target="tpu_custom_call" | custom-call | flops 1610612736 | bytes 1048576 | tf_op jit(solution)/shard_map/near_terms/pallas_call | solution.py:30
  74.7 2.9 %collective-permute-done.17.half_below = s16[32,1152]{1,0:T(8,128)(2,1)S(1)} collective-permute-done((s16[32,1152]{1,0:T(8,128)(2,1)S(1)}, s16[32,1152]{1,0:T(8,128)(2,1)S(1)}, u32[]{:S(2)}, u32[]{:S(2)}) %collective-permute-start.17) | collective-permute-done | bytes 73760 | tf_op jit(solution)/shard_map/ppermute | solution.py:277
  77.6 2.4 %collective-permute-done.18.half_above = s16[32,1152]{1,0:T(8,128)(2,1)S(1)} collective-permute-done((s16[32,1152]{1,0:T(8,128)(2,1)S(1)}, s16[32,1152]{1,0:T(8,128)(2,1)S(1)}, u32[]{:S(2)}, u32[]{:S(2)}) %collective-permute-start.18) | collective-permute-done | bytes 73760 | tf_op jit(solution)/shard_map/ppermute | solution.py:277
  80.0 0.5 pass_on.1
  80.6 2.2 %collective-permute-start.19 = (s16[64,1152]{1,0:T(8,128)(2,1)S(1)}, s16[64,1152]{1,0:T(8,128)(2,1)S(1)}, u32[]{:S(2)}, u32[]{:S(2)}) collective-permute-start(s16[64,1152]{1,0:T(8,128)(2,1)S(1)} %get-tuple-element.48), channel_id=1, source_target_pairs={{0,1},{128,129},{1,2},{129,130},{2,3},{130,131},{3,0},{131,128},{4... | collective-permute-start | bytes 442376 | tf_op jit(solution)/shard_map/ppermute | solution.py:277
  82.8 2.0 %collective-permute-start.20 = (s16[64,1152]{1,0:T(8,128)(2,1)S(1)}, s16[64,1152]{1,0:T(8,128)(2,1)S(1)}, u32[]{:S(2)}, u32[]{:S(2)}) collective-permute-start(s16[64,1152]{1,0:T(8,128)(2,1)S(1)} %get-tuple-element.49), channel_id=1, source_target_pairs={{0,3},{128,131},{1,0},{129,128},{2,1},{130,129},{3,2},{131,130},{4... | collective-permute-start | bytes 442376 | tf_op jit(solution)/shard_map/ppermute | solution.py:277
  84.8 3.3 %collective-permute-done.19.far_below = s16[64,1152]{1,0:T(8,128)(2,1)S(1)} collective-permute-done((s16[64,1152]{1,0:T(8,128)(2,1)S(1)}, s16[64,1152]{1,0:T(8,128)(2,1)S(1)}, u32[]{:S(2)}, u32[]{:S(2)}) %collective-permute-start.19) | collective-permute-done | bytes 147488 | tf_op jit(solution)/shard_map/ppermute | solution.py:277
  88.1 1.7 %collective-permute-done.20.far_above = s16[64,1152]{1,0:T(8,128)(2,1)S(1)} collective-permute-done((s16[64,1152]{1,0:T(8,128)(2,1)S(1)}, s16[64,1152]{1,0:T(8,128)(2,1)S(1)}, u32[]{:S(2)}, u32[]{:S(2)}) %collective-permute-start.20) | collective-permute-done | bytes 147488 | tf_op jit(solution)/shard_map/ppermute | solution.py:277
  89.8 1.1 %add_up.1 = (f32[1,64]{1,0:T(1,128)}, f32[64,1024]{1,0:T(8,128)}) custom-call(f32[192,1024]{1,0:T(8,128)S(1)} %get-tuple-element.42.gradient, f32[192,128]{1,0:T(8,128)S(1)} %get-tuple-element.43.proof, s16[128,1152]{1,0:T(8,128)(2,1)S(1)} %collective-permute-done.15.from_below, s16[128,1152]{1,0:T(8,128)(2,1)S(1)} %collective-permute-done.16.from_above, ...), custom_call_target="tpu_custom_call" | custom-call | bytes 1048576 | tf_op jit(solution)/shard_map/add_up/pallas_call | solution.py:30
  (26 shorter events, 0.4 us)
Async XLA Ops:
  2.6 14.1 %collective-permute-start.2 = (bf16[144,1024]{1,0:T(8,128)(2,1)}, bf16[144,1024]{1,0:T(8,128)(2,1)S(1)}, u32[]{:S(2)}, u32[]{:S(2)}) collective-permute-start(bf16[144,1024]{1,0:T(8,128)(2,1)} %get-tuple-element.27.refs_0_.block), channel_id=1, source_target_pairs={{0,32},{16,20},{4,36},{20,24},{8,40},{24,28},{12,44},{28,16},{32,6... | collective-permute-start | bytes 884744 | tf_op jit(solution)/shard_map/ppermute | solution.py:287
  4.1 12.6 %collective-permute-start.3 = (bf16[144,1024]{1,0:T(8,128)(2,1)}, bf16[144,1024]{1,0:T(8,128)(2,1)S(1)}, u32[]{:S(2)}, u32[]{:S(2)}) collective-permute-start(bf16[144,1024]{1,0:T(8,128)(2,1)} %get-tuple-element.27.refs_0_.block), channel_id=1, source_target_pairs={{0,96},{16,28},{4,100},{20,16},{8,104},{24,20},{12,108},{28,24},{3... | collective-permute-start | bytes 884744 | tf_op jit(solution)/shard_map/ppermute | solution.py:287
  5.8 10.8 %collective-permute-start.4 = (bf16[144,1024]{1,0:T(8,128)(2,1)}, bf16[144,1024]{1,0:T(8,128)(2,1)S(1)}, u32[]{:S(2)}, u32[]{:S(2)}) collective-permute-start(bf16[144,1024]{1,0:T(8,128)(2,1)} %get-tuple-element.27.refs_0_.block), channel_id=1, source_target_pairs={{0,64},{16,24},{4,68},{20,28},{8,72},{24,16},{12,76},{28,20},{32,9... | collective-permute-start | bytes 884744 | tf_op jit(solution)/shard_map/ppermute | solution.py:287
  7.7 9.0 %collective-permute-start = (bf16[64,1024]{1,0:T(8,128)(2,1)}, bf16[64,1024]{1,0:T(8,128)(2,1)S(1)}, u32[]{:S(2)}, u32[]{:S(2)}) collective-permute-start(bf16[64,1024]{1,0:T(8,128)(2,1)} %pool.1), channel_id=1, source_target_pairs={{0,128},{128,1},{1,129},{129,2},{2,130},{130,3},{3,131},{131,0},{4... | collective-permute-start | bytes 393224 | tf_op jit(solution)/shard_map/ppermute | solution.py:277
  9.6 7.1 %collective-permute-start.1 = (bf16[64,1024]{1,0:T(8,128)(2,1)}, bf16[64,1024]{1,0:T(8,128)(2,1)S(1)}, u32[]{:S(2)}, u32[]{:S(2)}) collective-permute-start(bf16[64,1024]{1,0:T(8,128)(2,1)} %pool.1), channel_id=1, source_target_pairs={{0,131},{128,0},{1,128},{129,1},{2,129},{130,2},{3,130},{131,3},{4... | collective-permute-start | bytes 393224 | tf_op jit(solution)/shard_map/ppermute | solution.py:277
  16.7 1.0 %copy-start = (bf16[144,1024]{1,0:T(8,128)(2,1)S(1)}, bf16[144,1024]{1,0:T(8,128)(2,1)}, u32[]{:S(2)}) copy-start(bf16[144,1024]{1,0:T(8,128)(2,1)} %get-tuple-element.27.refs_0_.block) | copy-start | bytes 884740
  17.7 9.6 %copy-start.2 = (f32[128,1,128]{2,1,0:T(1,128)S(1)}, f32[128,1,128]{2,1,0:T(1,128)}, u32[]{:S(2)}) copy-start(f32[128,1,128]{2,1,0:T(1,128)} %get-tuple-element.31) | copy-start | bytes 196612
  17.8 34.3 %collective-permute-start.7 = (bf16[528,1024]{1,0:T(8,128)(2,1)S(1)}, bf16[528,1024]{1,0:T(8,128)(2,1)S(1)}, u32[]{:S(2)}, u32[]{:S(2)}) collective-permute-start(bf16[528,1024]{1,0:T(8,128)(2,1)S(1)} %get-tuple-element.30.refs_0_), channel_id=1, source_target_pairs={{0,4},{16,48},{4,8},{20,52},{8,12},{24,56},{12,0},{28,60},{32,36},... | collective-permute-start | bytes 3244040 | tf_op jit(solution)/shard_map/ppermute | solution.py:287
  19.4 32.6 %collective-permute-start.8 = (bf16[528,1024]{1,0:T(8,128)(2,1)S(1)}, bf16[528,1024]{1,0:T(8,128)(2,1)S(1)}, u32[]{:S(2)}, u32[]{:S(2)}) collective-permute-start(bf16[528,1024]{1,0:T(8,128)(2,1)S(1)} %get-tuple-element.30.refs_0_), channel_id=1, source_target_pairs={{0,12},{16,112},{4,0},{20,116},{8,4},{24,120},{12,8},{28,124},{32,... | collective-permute-start | bytes 3244040 | tf_op jit(solution)/shard_map/ppermute | solution.py:287
  19.9 32.2 %collective-permute-start.9 = (bf16[528,1024]{1,0:T(8,128)(2,1)S(1)}, bf16[528,1024]{1,0:T(8,128)(2,1)S(1)}, u32[]{:S(2)}, u32[]{:S(2)}) collective-permute-start(bf16[528,1024]{1,0:T(8,128)(2,1)S(1)} %get-tuple-element.30.refs_0_), channel_id=1, source_target_pairs={{0,8},{16,80},{4,12},{20,84},{8,0},{24,88},{12,4},{28,92},{32,40},... | collective-permute-start | bytes 3244040 | tf_op jit(solution)/shard_map/ppermute | solution.py:287
  22.2 29.9 %collective-permute-start.5 = (bf16[160,1024]{1,0:T(8,128)(2,1)S(1)}, bf16[160,1024]{1,0:T(8,128)(2,1)S(1)}, u32[]{:S(2)}, u32[]{:S(2)}) collective-permute-start(bf16[160,1024]{1,0:T(8,128)(2,1)S(1)} %get-tuple-element.28), channel_id=1, source_target_pairs={{0,129},{128,2},{1,130},{129,3},{2,131},{130,0},{3,128},{131,1},{4... | collective-permute-start | bytes 983048 | tf_op jit(solution)/shard_map/ppermute | solution.py:277
  27.3 24.8 %collective-permute-start.6 = (bf16[160,1024]{1,0:T(8,128)(2,1)S(1)}, bf16[160,1024]{1,0:T(8,128)(2,1)S(1)}, u32[]{:S(2)}, u32[]{:S(2)}) collective-permute-start(bf16[160,1024]{1,0:T(8,128)(2,1)S(1)} %get-tuple-element.29), channel_id=1, source_target_pairs={{0,130},{128,3},{1,131},{129,0},{2,128},{130,1},{3,129},{131,2},{4... | collective-permute-start | bytes 983048 | tf_op jit(solution)/shard_map/ppermute | solution.py:277
  52.1 1.7 %copy-start.1 = (bf16[144,1024]{1,0:T(8,128)(2,1)S(1)}, bf16[144,1024]{1,0:T(8,128)(2,1)}, u32[]{:S(2)}) copy-start(bf16[144,1024]{1,0:T(8,128)(2,1)} %get-tuple-element.27.refs_0_.block) | copy-start | bytes 884740
  52.1 7.4 %collective-permute-start.10 = (bf16[528,1024]{1,0:T(8,128)(2,1)S(1)}, bf16[528,1024]{1,0:T(8,128)(2,1)S(1)}, u32[]{:S(2)}, u32[]{:S(2)}) collective-permute-start(bf16[528,1024]{1,0:T(8,128)(2,1)S(1)} %get-tuple-element.32.refs_0_), channel_id=1, source_target_pairs={{0,16},{16,0},{1,17},{17,1},{2,18},{18,2},{3,19},{19,3},{4,20},{20... | collective-permute-start | bytes 3244040 | tf_op jit(solution)/shard_map/ppermute | solution.py:295
  52.2 7.3 %collective-permute-start.11 = (bf16[528,1024]{1,0:T(8,128)(2,1)S(1)}, bf16[528,1024]{1,0:T(8,128)(2,1)S(1)}, u32[]{:S(2)}, u32[]{:S(2)}) collective-permute-start(bf16[528,1024]{1,0:T(8,128)(2,1)S(1)} %get-tuple-element.33.refs_1_), channel_id=1, source_target_pairs={{0,16},{16,0},{1,17},{17,1},{2,18},{18,2},{3,19},{19,3},{4,20},{20... | collective-permute-start | bytes 3244040 | tf_op jit(solution)/shard_map/ppermute | solution.py:295
  52.7 6.9 %collective-permute-start.12 = (bf16[528,1024]{1,0:T(8,128)(2,1)S(1)}, bf16[528,1024]{1,0:T(8,128)(2,1)S(1)}, u32[]{:S(2)}, u32[]{:S(2)}) collective-permute-start(bf16[528,1024]{1,0:T(8,128)(2,1)S(1)} %get-tuple-element.34.refs_2_), channel_id=1, source_target_pairs={{0,16},{16,0},{1,17},{17,1},{2,18},{18,2},{3,19},{19,3},{4,20},{20... | collective-permute-start | bytes 3244040 | tf_op jit(solution)/shard_map/ppermute | solution.py:295
  52.8 6.8 %collective-permute-start.13 = (bf16[528,1024]{1,0:T(8,128)(2,1)S(1)}, bf16[528,1024]{1,0:T(8,128)(2,1)S(1)}, u32[]{:S(2)}, u32[]{:S(2)}) collective-permute-start(bf16[528,1024]{1,0:T(8,128)(2,1)S(1)} %get-tuple-element.35.refs_3_), channel_id=1, source_target_pairs={{0,16},{16,0},{1,17},{17,1},{2,18},{18,2},{3,19},{19,3},{4,20},{20... | collective-permute-start | bytes 3244040 | tf_op jit(solution)/shard_map/ppermute | solution.py:295
  53.4 6.2 %collective-permute-start.14 = (f32[8,128]{1,0:T(8,128)S(1)}, f32[8,128]{1,0:T(8,128)S(1)}, u32[]{:S(2)}, u32[]{:S(2)}) collective-permute-start(f32[8,128]{1,0:T(8,128)S(1)} %add_counts.1.refs_10_), channel_id=1, source_target_pairs={{0,16},{16,0},{1,17},{17,1},{2,18},{18,2},{3,19},{19,3},{4,20},{20... | collective-permute-start | bytes 12296 | tf_op jit(solution)/shard_map/ppermute | solution.py:295
  63.6 16.4 %collective-permute-start.15 = (s16[128,1152]{1,0:T(8,128)(2,1)S(1)}, s16[128,1152]{1,0:T(8,128)(2,1)S(1)}, u32[]{:S(2)}, u32[]{:S(2)}) collective-permute-start(s16[128,1152]{1,0:T(8,128)(2,1)S(1)} %get-tuple-element.44), channel_id=1, source_target_pairs={{0,128},{128,1},{1,129},{129,2},{2,130},{130,3},{3,131},{131,0},{4... | collective-permute-start | bytes 884744 | tf_op jit(solution)/shard_map/ppermute | solution.py:277
  67.9 12.2 %collective-permute-start.16 = (s16[128,1152]{1,0:T(8,128)(2,1)S(1)}, s16[128,1152]{1,0:T(8,128)(2,1)S(1)}, u32[]{:S(2)}, u32[]{:S(2)}) collective-permute-start(s16[128,1152]{1,0:T(8,128)(2,1)S(1)} %get-tuple-element.45), channel_id=1, source_target_pairs={{0,131},{128,0},{1,128},{129,1},{2,129},{130,2},{3,130},{131,3},{4... | collective-permute-start | bytes 884744 | tf_op jit(solution)/shard_map/ppermute | solution.py:277
  67.9 9.7 %collective-permute-start.17 = (s16[32,1152]{1,0:T(8,128)(2,1)S(1)}, s16[32,1152]{1,0:T(8,128)(2,1)S(1)}, u32[]{:S(2)}, u32[]{:S(2)}) collective-permute-start(s16[32,1152]{1,0:T(8,128)(2,1)S(1)} %get-tuple-element.46), channel_id=1, source_target_pairs={{0,1},{128,129},{1,2},{129,130},{2,3},{130,131},{3,0},{131,128},{4... | collective-permute-start | bytes 221192 | tf_op jit(solution)/shard_map/ppermute | solution.py:277
  70.1 9.9 %collective-permute-start.18 = (s16[32,1152]{1,0:T(8,128)(2,1)S(1)}, s16[32,1152]{1,0:T(8,128)(2,1)S(1)}, u32[]{:S(2)}, u32[]{:S(2)}) collective-permute-start(s16[32,1152]{1,0:T(8,128)(2,1)S(1)} %get-tuple-element.47), channel_id=1, source_target_pairs={{0,3},{128,131},{1,0},{129,128},{2,1},{130,129},{3,2},{131,130},{4... | collective-permute-start | bytes 221192 | tf_op jit(solution)/shard_map/ppermute | solution.py:277
  80.6 7.6 %collective-permute-start.19 = (s16[64,1152]{1,0:T(8,128)(2,1)S(1)}, s16[64,1152]{1,0:T(8,128)(2,1)S(1)}, u32[]{:S(2)}, u32[]{:S(2)}) collective-permute-start(s16[64,1152]{1,0:T(8,128)(2,1)S(1)} %get-tuple-element.48), channel_id=1, source_target_pairs={{0,1},{128,129},{1,2},{129,130},{2,3},{130,131},{3,0},{131,128},{4... | collective-permute-start | bytes 442376 | tf_op jit(solution)/shard_map/ppermute | solution.py:277
  82.8 7.0 %collective-permute-start.20 = (s16[64,1152]{1,0:T(8,128)(2,1)S(1)}, s16[64,1152]{1,0:T(8,128)(2,1)S(1)}, u32[]{:S(2)}, u32[]{:S(2)}) collective-permute-start(s16[64,1152]{1,0:T(8,128)(2,1)S(1)} %get-tuple-element.49), channel_id=1, source_target_pairs={{0,3},{128,131},{1,0},{129,128},{2,1},{130,129},{3,2},{131,130},{4... | collective-permute-start | bytes 442376 | tf_op jit(solution)/shard_map/ppermute | solution.py:277

commit v11 on v10

--- a/solution.py
+++ b/solution.py
@@ -10,7 +10,6 @@
 
 AXES = ("zl", "x", "c", "y", "zh")
 RING = ("zl", "zh")
-CHIPS = ("zl", "x", "y", "zh")
 PLANE = ("x", "c", "y")
 LANES = 128
 META = 16
@@ -161,8 +160,8 @@
     add_columns(ordered, norms, pieces, (), (pp, tp), (pm, tm), weights, rows)
 
 
-def terms(target_count, panel, pp, tp, pm, tm, total, other_total, part):
-    weight = total[:1, :1] + other_total[:1, :1]
+def terms(target_count, panel, pp, tp, pm, tm, total, part):
+    weight = total[:1, :1]
     pool_mass = jnp.sum(pm[part, :], axis=1, keepdims=True)
     target_mass = jnp.sum(tm[part, :], axis=1, keepdims=True)
     own = panel[part, :].astype(F32)
@@ -174,12 +173,12 @@
 
 
 def last_columns(lines, start, stop, panel, norms, *refs):
-    pieces, old, totals, outs = refs[:lines], refs[lines : lines + 4], refs[lines + 4 : lines + 6], refs[lines + 6 :]
+    pieces, old, total, outs = refs[:lines], refs[lines : lines + 4], refs[lines + 4], refs[lines + 5 :]
     outs, (pp, tp, pm, tm, *weights) = outs[:-6], outs[-6:]
     rows = slice(start, stop)
     panel, norms, *old = (ref.at[rows] for ref in (panel, norms, *old))
     add_columns(panel, norms, pieces, old, (pp, tp), (pm, tm), weights, stop - start)
-    return (panel, pp, tp, pm, tm, *totals), outs
+    return (panel, pp, tp, pm, tm, total), outs
 
 
 def far_terms(target_count, lines, height, *refs):
@@ -304,10 +303,10 @@
     block, chosen = in_vmem(
         pack_block,
         "pack_block",
-        (shape((2 * height + META, width), BF16), shape((lax.axis_size(CHIPS), 1, LANES), F32)),
+        (shape((2 * height + META, width), BF16), shape((lax.axis_size(AXES), 1, LANES), F32)),
         limit=56,
     )(pool, targets, counts.reshape(1, height))
-    chosen = lax.all_to_all(chosen, CHIPS, split_axis=0, concat_axis=0, tiled=True)
+    chosen = lax.all_to_all(chosen, AXES, split_axis=0, concat_axis=0, tiled=True)
     blocks = line(block, 0)
     below, above = up_the_ring(pool, 1), up_the_ring(pool, ring - 1)
     pair = shape((5 * height // 2, width), BF16)
@@ -342,8 +341,7 @@
         (shape((rows, width), BF16), shape((rows, LANES), F32), *sums),
         {},
     )
-    totals = total, other_core(total)
-    inputs = panel, norms, *others, *state, *totals
+    inputs = panel, norms, *others, *state, total
 
     def last(body, count, out_shape):
         return in_vmem(

time: 92 us -> 92.9 us (level)
  blocking collectives: 24.7 us -> 25.7 us
    all_to_all x1, blocking collectives: 24.7 us -> 25.7 us  [on_device(): lax.all_to_all(chosen, AXES, split_axis=0, concat_axis=0, tiled=True)]
  transfers between devices with their start and end apart: 21 -> 20, of which waited for: 6 -> 6; matrix products, arithmetic and copies ran while one was open for 0% -> 0% of each run, Pallas kernels for 9% -> 9%
where the time goes in v11:
time: 92.9 us; the launch traced here: 92.3 us
  starting transfers between devices  34.6 us (37%)
  blocking collectives  25.7 us (28%)
  Pallas kernels  15.9 us (17%)
  waiting for transfers between devices  14.4 us (16%)
  local copies, waits for them, and re-layouts  0.96 us (1%)
    all_to_all x1, blocking collectives, on_device(): lax.all_to_all(chosen, AXES, split_axis=0, concat_axis=0, tiled=True)  25.7 us
    ppermute x10, starting transfers between devices, up_the_ring(): lax.ppermute(x, RING, [(place(i), place((i + step) % ring)) for i in rang...  24 us
    pallas_call x8, Pallas kernels, call(): pl.pallas_call(body, out_shape=out_shape, in_specs=[spec] * len(args), ou...  15.9 us
    ppermute x10, waiting for transfers between devices, up_the_ring(): lax.ppermute(x, RING, [(place(i), place((i + step) % ring)) for i in rang...  13.5 us
    ppermute x6, starting transfers between devices, along_line(): return lax.ppermute(x, PLANE, pairs)  9.45 us
  transfers between devices with their start and end apart: 20, of which 6 were waited for; matrix products, arithmetic and copies ran while one was open for 0% of the time, Pallas kernels for 9%

profile of v11, /device:TPU:8, one launch (start us, length us, event | category | flops | bytes accessed | tf_op | source)
XLA Modules:
  0.0 92.3 jit_solution(8559987485366852029)
XLA Ops:
  0.6 2.0 %pack_block.1 = (bf16[144,1024]{1,0:T(8,128)(2,1)}, f32[256,1,128]{2,1,0:T(1,128)}) custom-call(bf16[64,1024]{1,0:T(8,128)(2,1)} %pool.1, bf16[64,1024]{1,0:T(8,128)(2,1)} %targets.1, s32[1,64]{1,0:T(1,128)} %bitcast.2), custom_call_target="tpu_custom_call" | custom-call | bytes 1048576 | tf_op jit(solution)/shard_map/pack_block/pallas_call | solution.py:29
  2.7 1.5 %collective-permute-start.2 = (bf16[144,1024]{1,0:T(8,128)(2,1)}, bf16[144,1024]{1,0:T(8,128)(2,1)S(1)}, u32[]{:S(2)}, u32[]{:S(2)}) collective-permute-start(bf16[144,1024]{1,0:T(8,128)(2,1)} %get-tuple-element.27.refs_0_.block), channel_id=1, source_target_pairs={{0,32},{16,20},{4,36},{20,24},{8,40},{24,28},{12,44},{28,16},{32,6... | collective-permute-start | bytes 884744 | tf_op jit(solution)/shard_map/ppermute | solution.py:286
  4.2 1.7 %collective-permute-start.3 = (bf16[144,1024]{1,0:T(8,128)(2,1)}, bf16[144,1024]{1,0:T(8,128)(2,1)S(1)}, u32[]{:S(2)}, u32[]{:S(2)}) collective-permute-start(bf16[144,1024]{1,0:T(8,128)(2,1)} %get-tuple-element.27.refs_0_.block), channel_id=1, source_target_pairs={{0,96},{16,28},{4,100},{20,16},{8,104},{24,20},{12,108},{28,24},{3... | collective-permute-start | bytes 884744 | tf_op jit(solution)/shard_map/ppermute | solution.py:286
  5.9 1.8 %collective-permute-start.4 = (bf16[144,1024]{1,0:T(8,128)(2,1)}, bf16[144,1024]{1,0:T(8,128)(2,1)S(1)}, u32[]{:S(2)}, u32[]{:S(2)}) collective-permute-start(bf16[144,1024]{1,0:T(8,128)(2,1)} %get-tuple-element.27.refs_0_.block), channel_id=1, source_target_pairs={{0,64},{16,24},{4,68},{20,28},{8,72},{24,16},{12,76},{28,20},{32,9... | collective-permute-start | bytes 884744 | tf_op jit(solution)/shard_map/ppermute | solution.py:286
  7.7 1.9 %collective-permute-start = (bf16[64,1024]{1,0:T(8,128)(2,1)}, bf16[64,1024]{1,0:T(8,128)(2,1)S(1)}, u32[]{:S(2)}, u32[]{:S(2)}) collective-permute-start(bf16[64,1024]{1,0:T(8,128)(2,1)} %pool.1), channel_id=1, source_target_pairs={{0,128},{128,1},{1,129},{129,2},{2,130},{130,3},{3,131},{131,0},{4... | collective-permute-start | bytes 393224 | tf_op jit(solution)/shard_map/ppermute | solution.py:276
  9.6 3.9 %collective-permute-start.1 = (bf16[64,1024]{1,0:T(8,128)(2,1)}, bf16[64,1024]{1,0:T(8,128)(2,1)S(1)}, u32[]{:S(2)}, u32[]{:S(2)}) collective-permute-start(bf16[64,1024]{1,0:T(8,128)(2,1)} %pool.1), channel_id=1, source_target_pairs={{0,131},{128,0},{1,128},{129,1},{2,129},{130,2},{3,130},{131,3},{4... | collective-permute-start | bytes 393224 | tf_op jit(solution)/shard_map/ppermute | solution.py:276
  13.6 3.2 %collective-permute-done.refs_4_.below = bf16[64,1024]{1,0:T(8,128)(2,1)S(1)} collective-permute-done((bf16[64,1024]{1,0:T(8,128)(2,1)}, bf16[64,1024]{1,0:T(8,128)(2,1)S(1)}, u32[]{:S(2)}, u32[]{:S(2)}) %collective-permute-start) | collective-permute-done | bytes 131104 | tf_op jit(solution)/shard_map/ppermute | solution.py:276
  16.8 1.0 %copy-done = bf16[144,1024]{1,0:T(8,128)(2,1)S(1)} copy-done((bf16[144,1024]{1,0:T(8,128)(2,1)S(1)}, bf16[144,1024]{1,0:T(8,128)(2,1)}, u32[]{:S(2)}) %copy-start) | copy-done | bytes 294936
  17.7 0.1 pack_line.1
  17.8 1.7 %collective-permute-start.7 = (bf16[528,1024]{1,0:T(8,128)(2,1)S(1)}, bf16[528,1024]{1,0:T(8,128)(2,1)S(1)}, u32[]{:S(2)}, u32[]{:S(2)}) collective-permute-start(bf16[528,1024]{1,0:T(8,128)(2,1)S(1)} %get-tuple-element.30.refs_0_), channel_id=1, source_target_pairs={{0,4},{16,48},{4,8},{20,52},{8,12},{24,56},{12,0},{28,60},{32,36},... | collective-permute-start | bytes 3244040 | tf_op jit(solution)/shard_map/ppermute | solution.py:286
  19.5 0.4 collective-permute-start.8
  19.9 2.3 %collective-permute-start.9 = (bf16[528,1024]{1,0:T(8,128)(2,1)S(1)}, bf16[528,1024]{1,0:T(8,128)(2,1)S(1)}, u32[]{:S(2)}, u32[]{:S(2)}) collective-permute-start(bf16[528,1024]{1,0:T(8,128)(2,1)S(1)} %get-tuple-element.30.refs_0_), channel_id=1, source_target_pairs={{0,8},{16,80},{4,12},{20,84},{8,0},{24,88},{12,4},{28,92},{32,40},... | collective-permute-start | bytes 3244040 | tf_op jit(solution)/shard_map/ppermute | solution.py:286
  22.2 5.1 %collective-permute-start.5 = (bf16[160,1024]{1,0:T(8,128)(2,1)S(1)}, bf16[160,1024]{1,0:T(8,128)(2,1)S(1)}, u32[]{:S(2)}, u32[]{:S(2)}) collective-permute-start(bf16[160,1024]{1,0:T(8,128)(2,1)S(1)} %get-tuple-element.28), channel_id=1, source_target_pairs={{0,129},{128,2},{1,130},{129,3},{2,131},{130,0},{3,128},{131,1},{4... | collective-permute-start | bytes 983048 | tf_op jit(solution)/shard_map/ppermute | solution.py:276
  27.4 25.7 %all_to_all.5.refs_4_.chosen = f32[256,1,128]{2,1,0:T(1,128)S(1)} all-to-all(f32[256,1,128]{2,1,0:T(1,128)S(1)} %copy-done.2), channel_id=1, replica_groups=mesh['zl'=2,'x'=4,'c'=2,'y'=4,'zh'=4] {'zl','x','c','y','zh'}, dimensions={0} | all-to-all | bytes 262144 | tf_op jit(solution)/shard_map/all_to_all | solution.py:309
  53.3 0.5 collective-permute-start.11
  53.9 0.4 collective-permute-start.13
  54.3 0.3 add_counts.1.refs_10_
  54.5 5.2 %first_columns.1 = (bf16[512,1024]{1,0:T(8,128)(2,1)S(1)}, f32[512,128]{1,0:T(8,128)S(1)}, f32[512,1024]{1,0:T(8,128)S(1)}, f32[512,1024]{1,0:T(8,128)S(1)}, f32...) custom-call(bf16[144,1024]{1,0:T(8,128)(2,1)S(1)} %copy-done.1, bf16[64,1024]{1,0:T(8,128)(2,1)S(1)} %collective-permute-done.refs_4_.below, ...), custom_call_target="tpu_custom_call" | custom-call | flops 4294967296 | bytes 1048576 | tf_op jit(solution)/shard_map/first_columns/pallas_call | solution.py:29
  59.8 0.8 collective-permute-done.13.refs_5_
  60.6 4.0 %far_terms.1 = (s16[128,1152]{1,0:T(8,128)(2,1)S(1)}, s16[128,1152]{1,0:T(8,128)(2,1)S(1)}, s16[32,1152]{1,0:T(8,128)(2,1)S(1)}, s16[32,1152]{1,0:T(8,128)(2,1)S(1)}) custom-call(bf16[512,1024]{1,0:T(8,128)(2,1)S(1)} %get-tuple-element.36.refs_0_, f32[512,128]{1,0:T(8,128)S(1)} %get-tuple-element.37.refs_1_, ...), custom_call_target="tpu_custom_call" | custom-call | flops 2684354560 | bytes 1048576 | tf_op jit(solution)/shard_map/far_terms/pallas_call | solution.py:29
  64.6 4.7 %collective-permute-start.14 = (s16[128,1152]{1,0:T(8,128)(2,1)S(1)}, s16[128,1152]{1,0:T(8,128)(2,1)S(1)}, u32[]{:S(2)}, u32[]{:S(2)}) collective-permute-start(s16[128,1152]{1,0:T(8,128)(2,1)S(1)} %get-tuple-element.44), channel_id=1, source_target_pairs={{0,128},{128,1},{1,129},{129,2},{2,130},{130,3},{3,131},{131,0},{4... | collective-permute-start | bytes 884744 | tf_op jit(solution)/shard_map/ppermute | solution.py:276
  69.3 2.0 %collective-permute-start.16 = (s16[32,1152]{1,0:T(8,128)(2,1)S(1)}, s16[32,1152]{1,0:T(8,128)(2,1)S(1)}, u32[]{:S(2)}, u32[]{:S(2)}) collective-permute-start(s16[32,1152]{1,0:T(8,128)(2,1)S(1)} %get-tuple-element.46), channel_id=1, source_target_pairs={{0,1},{128,129},{1,2},{129,130},{2,3},{130,131},{3,0},{131,128},{4... | collective-permute-start | bytes 221192 | tf_op jit(solution)/shard_map/ppermute | solution.py:276
  71.2 2.2 %collective-permute-start.17 = (s16[32,1152]{1,0:T(8,128)(2,1)S(1)}, s16[32,1152]{1,0:T(8,128)(2,1)S(1)}, u32[]{:S(2)}, u32[]{:S(2)}) collective-permute-start(s16[32,1152]{1,0:T(8,128)(2,1)S(1)} %get-tuple-element.47), channel_id=1, source_target_pairs={{0,3},{128,131},{1,0},{129,128},{2,1},{130,129},{3,2},{131,130},{4... | collective-permute-start | bytes 221192 | tf_op jit(solution)/shard_map/ppermute | solution.py:276
  73.4 2.7 %near_terms.1 = (f32[192,1024]{1,0:T(8,128)S(1)}, f32[192,128]{1,0:T(8,128)S(1)}) custom-call(bf16[512,1024]{1,0:T(8,128)(2,1)S(1)} %get-tuple-element.36.refs_0_, f32[512,128]{1,0:T(8,128)S(1)} %get-tuple-element.37.refs_1_, bf16[528,1024]{1,0:T(8,128)(2,1)S(1)} %collective-permute-done.10.refs_2_, bf16[528,1024]{1,0:T(8,128)(2,1)S(1)} %collective-permute-done.11.refs_3_, ...), custom_call_target="tpu_custom_call" | custom-call | flops 1610612736 | bytes 1048576 | tf_op jit(solution)/shard_map/near_terms/pallas_call | solution.py:29
  76.1 3.7 %collective-permute-done.16.half_below = s16[32,1152]{1,0:T(8,128)(2,1)S(1)} collective-permute-done((s16[32,1152]{1,0:T(8,128)(2,1)S(1)}, s16[32,1152]{1,0:T(8,128)(2,1)S(1)}, u32[]{:S(2)}, u32[]{:S(2)}) %collective-permute-start.16) | collective-permute-done | bytes 73760 | tf_op jit(solution)/shard_map/ppermute | solution.py:276
  79.8 1.3 %collective-permute-done.17.half_above = s16[32,1152]{1,0:T(8,128)(2,1)S(1)} collective-permute-done((s16[32,1152]{1,0:T(8,128)(2,1)S(1)}, s16[32,1152]{1,0:T(8,128)(2,1)S(1)}, u32[]{:S(2)}, u32[]{:S(2)}) %collective-permute-start.17) | collective-permute-done | bytes 73760 | tf_op jit(solution)/shard_map/ppermute | solution.py:276
  81.2 0.5 pass_on.1
  81.7 2.5 %collective-permute-start.18 = (s16[64,1152]{1,0:T(8,128)(2,1)S(1)}, s16[64,1152]{1,0:T(8,128)(2,1)S(1)}, u32[]{:S(2)}, u32[]{:S(2)}) collective-permute-start(s16[64,1152]{1,0:T(8,128)(2,1)S(1)} %get-tuple-element.48), channel_id=1, source_target_pairs={{0,1},{128,129},{1,2},{129,130},{2,3},{130,131},{3,0},{131,128},{4... | collective-permute-start | bytes 442376 | tf_op jit(solution)/shard_map/ppermute | solution.py:276
  84.2 1.8 %collective-permute-start.19 = (s16[64,1152]{1,0:T(8,128)(2,1)S(1)}, s16[64,1152]{1,0:T(8,128)(2,1)S(1)}, u32[]{:S(2)}, u32[]{:S(2)}) collective-permute-start(s16[64,1152]{1,0:T(8,128)(2,1)S(1)} %get-tuple-element.49), channel_id=1, source_target_pairs={{0,3},{128,131},{1,0},{129,128},{2,1},{130,129},{3,2},{131,130},{4... | collective-permute-start | bytes 442376 | tf_op jit(solution)/shard_map/ppermute | solution.py:276
  85.9 3.7 %collective-permute-done.18.far_below = s16[64,1152]{1,0:T(8,128)(2,1)S(1)} collective-permute-done((s16[64,1152]{1,0:T(8,128)(2,1)S(1)}, s16[64,1152]{1,0:T(8,128)(2,1)S(1)}, u32[]{:S(2)}, u32[]{:S(2)}) %collective-permute-start.18) | collective-permute-done | bytes 147488 | tf_op jit(solution)/shard_map/ppermute | solution.py:276
  89.6 1.7 %collective-permute-done.19.far_above = s16[64,1152]{1,0:T(8,128)(2,1)S(1)} collective-permute-done((s16[64,1152]{1,0:T(8,128)(2,1)S(1)}, s16[64,1152]{1,0:T(8,128)(2,1)S(1)}, u32[]{:S(2)}, u32[]{:S(2)}) %collective-permute-start.19) | collective-permute-done | bytes 147488 | tf_op jit(solution)/shard_map/ppermute | solution.py:276
  91.3 1.1 %add_up.1 = (f32[1,64]{1,0:T(1,128)}, f32[64,1024]{1,0:T(8,128)}) custom-call(f32[192,1024]{1,0:T(8,128)S(1)} %get-tuple-element.42.gradient, f32[192,128]{1,0:T(8,128)S(1)} %get-tuple-element.43.proof, s16[128,1152]{1,0:T(8,128)(2,1)S(1)} %collective-permute-done.14.from_below, s16[128,1152]{1,0:T(8,128)(2,1)S(1)} %collective-permute-done.15.from_above, ...), custom_call_target="tpu_custom_call" | custom-call | bytes 1048576 | tf_op jit(solution)/shard_map/add_up/pallas_call | solution.py:29
  (24 shorter events, 0.2 us)
Async XLA Ops:
  2.7 14.1 %collective-permute-start.2 = (bf16[144,1024]{1,0:T(8,128)(2,1)}, bf16[144,1024]{1,0:T(8,128)(2,1)S(1)}, u32[]{:S(2)}, u32[]{:S(2)}) collective-permute-start(bf16[144,1024]{1,0:T(8,128)(2,1)} %get-tuple-element.27.refs_0_.block), channel_id=1, source_target_pairs={{0,32},{16,20},{4,36},{20,24},{8,40},{24,28},{12,44},{28,16},{32,6... | collective-permute-start | bytes 884744 | tf_op jit(solution)/shard_map/ppermute | solution.py:286
  4.2 12.6 %collective-permute-start.3 = (bf16[144,1024]{1,0:T(8,128)(2,1)}, bf16[144,1024]{1,0:T(8,128)(2,1)S(1)}, u32[]{:S(2)}, u32[]{:S(2)}) collective-permute-start(bf16[144,1024]{1,0:T(8,128)(2,1)} %get-tuple-element.27.refs_0_.block), channel_id=1, source_target_pairs={{0,96},{16,28},{4,100},{20,16},{8,104},{24,20},{12,108},{28,24},{3... | collective-permute-start | bytes 884744 | tf_op jit(solution)/shard_map/ppermute | solution.py:286
  5.9 10.8 %collective-permute-start.4 = (bf16[144,1024]{1,0:T(8,128)(2,1)}, bf16[144,1024]{1,0:T(8,128)(2,1)S(1)}, u32[]{:S(2)}, u32[]{:S(2)}) collective-permute-start(bf16[144,1024]{1,0:T(8,128)(2,1)} %get-tuple-element.27.refs_0_.block), channel_id=1, source_target_pairs={{0,64},{16,24},{4,68},{20,28},{8,72},{24,16},{12,76},{28,20},{32,9... | collective-permute-start | bytes 884744 | tf_op jit(solution)/shard_map/ppermute | solution.py:286
  7.7 9.0 %collective-permute-start = (bf16[64,1024]{1,0:T(8,128)(2,1)}, bf16[64,1024]{1,0:T(8,128)(2,1)S(1)}, u32[]{:S(2)}, u32[]{:S(2)}) collective-permute-start(bf16[64,1024]{1,0:T(8,128)(2,1)} %pool.1), channel_id=1, source_target_pairs={{0,128},{128,1},{1,129},{129,2},{2,130},{130,3},{3,131},{131,0},{4... | collective-permute-start | bytes 393224 | tf_op jit(solution)/shard_map/ppermute | solution.py:276
  9.6 7.1 %collective-permute-start.1 = (bf16[64,1024]{1,0:T(8,128)(2,1)}, bf16[64,1024]{1,0:T(8,128)(2,1)S(1)}, u32[]{:S(2)}, u32[]{:S(2)}) collective-permute-start(bf16[64,1024]{1,0:T(8,128)(2,1)} %pool.1), channel_id=1, source_target_pairs={{0,131},{128,0},{1,128},{129,1},{2,129},{130,2},{3,130},{131,3},{4... | collective-permute-start | bytes 393224 | tf_op jit(solution)/shard_map/ppermute | solution.py:276
  16.8 1.0 %copy-start = (bf16[144,1024]{1,0:T(8,128)(2,1)S(1)}, bf16[144,1024]{1,0:T(8,128)(2,1)}, u32[]{:S(2)}) copy-start(bf16[144,1024]{1,0:T(8,128)(2,1)} %get-tuple-element.27.refs_0_.block) | copy-start | bytes 884740
  17.7 9.6 %copy-start.2 = (f32[256,1,128]{2,1,0:T(1,128)S(1)}, f32[256,1,128]{2,1,0:T(1,128)}, u32[]{:S(2)}) copy-start(f32[256,1,128]{2,1,0:T(1,128)} %get-tuple-element.31) | copy-start | bytes 393220
  17.8 35.3 %collective-permute-start.7 = (bf16[528,1024]{1,0:T(8,128)(2,1)S(1)}, bf16[528,1024]{1,0:T(8,128)(2,1)S(1)}, u32[]{:S(2)}, u32[]{:S(2)}) collective-permute-start(bf16[528,1024]{1,0:T(8,128)(2,1)S(1)} %get-tuple-element.30.refs_0_), channel_id=1, source_target_pairs={{0,4},{16,48},{4,8},{20,52},{8,12},{24,56},{12,0},{28,60},{32,36},... | collective-permute-start | bytes 3244040 | tf_op jit(solution)/shard_map/ppermute | solution.py:286
  19.5 33.6 %collective-permute-start.8 = (bf16[528,1024]{1,0:T(8,128)(2,1)S(1)}, bf16[528,1024]{1,0:T(8,128)(2,1)S(1)}, u32[]{:S(2)}, u32[]{:S(2)}) collective-permute-start(bf16[528,1024]{1,0:T(8,128)(2,1)S(1)} %get-tuple-element.30.refs_0_), channel_id=1, source_target_pairs={{0,12},{16,112},{4,0},{20,116},{8,4},{24,120},{12,8},{28,124},{32,... | collective-permute-start | bytes 3244040 | tf_op jit(solution)/shard_map/ppermute | solution.py:286
  19.9 33.2 %collective-permute-start.9 = (bf16[528,1024]{1,0:T(8,128)(2,1)S(1)}, bf16[528,1024]{1,0:T(8,128)(2,1)S(1)}, u32[]{:S(2)}, u32[]{:S(2)}) collective-permute-start(bf16[528,1024]{1,0:T(8,128)(2,1)S(1)} %get-tuple-element.30.refs_0_), channel_id=1, source_target_pairs={{0,8},{16,80},{4,12},{20,84},{8,0},{24,88},{12,4},{28,92},{32,40},... | collective-permute-start | bytes 3244040 | tf_op jit(solution)/shard_map/ppermute | solution.py:286
  22.2 30.9 %collective-permute-start.5 = (bf16[160,1024]{1,0:T(8,128)(2,1)S(1)}, bf16[160,1024]{1,0:T(8,128)(2,1)S(1)}, u32[]{:S(2)}, u32[]{:S(2)}) collective-permute-start(bf16[160,1024]{1,0:T(8,128)(2,1)S(1)} %get-tuple-element.28), channel_id=1, source_target_pairs={{0,129},{128,2},{1,130},{129,3},{2,131},{130,0},{3,128},{131,1},{4... | collective-permute-start | bytes 983048 | tf_op jit(solution)/shard_map/ppermute | solution.py:276
  27.4 25.8 %collective-permute-start.6 = (bf16[160,1024]{1,0:T(8,128)(2,1)S(1)}, bf16[160,1024]{1,0:T(8,128)(2,1)S(1)}, u32[]{:S(2)}, u32[]{:S(2)}) collective-permute-start(bf16[160,1024]{1,0:T(8,128)(2,1)S(1)} %get-tuple-element.29), channel_id=1, source_target_pairs={{0,130},{128,3},{1,131},{129,0},{2,128},{130,1},{3,129},{131,2},{4... | collective-permute-start | bytes 983048 | tf_op jit(solution)/shard_map/ppermute | solution.py:276
  53.1 1.4 %copy-start.1 = (bf16[144,1024]{1,0:T(8,128)(2,1)S(1)}, bf16[144,1024]{1,0:T(8,128)(2,1)}, u32[]{:S(2)}) copy-start(bf16[144,1024]{1,0:T(8,128)(2,1)} %get-tuple-element.27.refs_0_.block) | copy-start | bytes 884740
  53.2 6.6 %collective-permute-start.10 = (bf16[528,1024]{1,0:T(8,128)(2,1)S(1)}, bf16[528,1024]{1,0:T(8,128)(2,1)S(1)}, u32[]{:S(2)}, u32[]{:S(2)}) collective-permute-start(bf16[528,1024]{1,0:T(8,128)(2,1)S(1)} %get-tuple-element.32.refs_0_), channel_id=1, source_target_pairs={{0,16},{16,0},{1,17},{17,1},{2,18},{18,2},{3,19},{19,3},{4,20},{20... | collective-permute-start | bytes 3244040 | tf_op jit(solution)/shard_map/ppermute | solution.py:294
  53.3 6.5 %collective-permute-start.11 = (bf16[528,1024]{1,0:T(8,128)(2,1)S(1)}, bf16[528,1024]{1,0:T(8,128)(2,1)S(1)}, u32[]{:S(2)}, u32[]{:S(2)}) collective-permute-start(bf16[528,1024]{1,0:T(8,128)(2,1)S(1)} %get-tuple-element.33.refs_1_), channel_id=1, source_target_pairs={{0,16},{16,0},{1,17},{17,1},{2,18},{18,2},{3,19},{19,3},{4,20},{20... | collective-permute-start | bytes 3244040 | tf_op jit(solution)/shard_map/ppermute | solution.py:294
  53.8 6.0 %collective-permute-start.12 = (bf16[528,1024]{1,0:T(8,128)(2,1)S(1)}, bf16[528,1024]{1,0:T(8,128)(2,1)S(1)}, u32[]{:S(2)}, u32[]{:S(2)}) collective-permute-start(bf16[528,1024]{1,0:T(8,128)(2,1)S(1)} %get-tuple-element.34.refs_2_), channel_id=1, source_target_pairs={{0,16},{16,0},{1,17},{17,1},{2,18},{18,2},{3,19},{19,3},{4,20},{20... | collective-permute-start | bytes 3244040 | tf_op jit(solution)/shard_map/ppermute | solution.py:294
  53.9 6.7 %collective-permute-start.13 = (bf16[528,1024]{1,0:T(8,128)(2,1)S(1)}, bf16[528,1024]{1,0:T(8,128)(2,1)S(1)}, u32[]{:S(2)}, u32[]{:S(2)}) collective-permute-start(bf16[528,1024]{1,0:T(8,128)(2,1)S(1)} %get-tuple-element.35.refs_3_), channel_id=1, source_target_pairs={{0,16},{16,0},{1,17},{17,1},{2,18},{18,2},{3,19},{19,3},{4,20},{20... | collective-permute-start | bytes 3244040 | tf_op jit(solution)/shard_map/ppermute | solution.py:294
  64.6 16.5 %collective-permute-start.14 = (s16[128,1152]{1,0:T(8,128)(2,1)S(1)}, s16[128,1152]{1,0:T(8,128)(2,1)S(1)}, u32[]{:S(2)}, u32[]{:S(2)}) collective-permute-start(s16[128,1152]{1,0:T(8,128)(2,1)S(1)} %get-tuple-element.44), channel_id=1, source_target_pairs={{0,128},{128,1},{1,129},{129,2},{2,130},{130,3},{3,131},{131,0},{4... | collective-permute-start | bytes 884744 | tf_op jit(solution)/shard_map/ppermute | solution.py:276
  69.3 11.9 %collective-permute-start.15 = (s16[128,1152]{1,0:T(8,128)(2,1)S(1)}, s16[128,1152]{1,0:T(8,128)(2,1)S(1)}, u32[]{:S(2)}, u32[]{:S(2)}) collective-permute-start(s16[128,1152]{1,0:T(8,128)(2,1)S(1)} %get-tuple-element.45), channel_id=1, source_target_pairs={{0,131},{128,0},{1,128},{129,1},{2,129},{130,2},{3,130},{131,3},{4... | collective-permute-start | bytes 884744 | tf_op jit(solution)/shard_map/ppermute | solution.py:276
  69.3 10.5 %collective-permute-start.16 = (s16[32,1152]{1,0:T(8,128)(2,1)S(1)}, s16[32,1152]{1,0:T(8,128)(2,1)S(1)}, u32[]{:S(2)}, u32[]{:S(2)}) collective-permute-start(s16[32,1152]{1,0:T(8,128)(2,1)S(1)} %get-tuple-element.46), channel_id=1, source_target_pairs={{0,1},{128,129},{1,2},{129,130},{2,3},{130,131},{3,0},{131,128},{4... | collective-permute-start | bytes 221192 | tf_op jit(solution)/shard_map/ppermute | solution.py:276
  71.2 9.9 %collective-permute-start.17 = (s16[32,1152]{1,0:T(8,128)(2,1)S(1)}, s16[32,1152]{1,0:T(8,128)(2,1)S(1)}, u32[]{:S(2)}, u32[]{:S(2)}) collective-permute-start(s16[32,1152]{1,0:T(8,128)(2,1)S(1)} %get-tuple-element.47), channel_id=1, source_target_pairs={{0,3},{128,131},{1,0},{129,128},{2,1},{130,129},{3,2},{131,130},{4... | collective-permute-start | bytes 221192 | tf_op jit(solution)/shard_map/ppermute | solution.py:276
  81.7 7.9 %collective-permute-start.18 = (s16[64,1152]{1,0:T(8,128)(2,1)S(1)}, s16[64,1152]{1,0:T(8,128)(2,1)S(1)}, u32[]{:S(2)}, u32[]{:S(2)}) collective-permute-start(s16[64,1152]{1,0:T(8,128)(2,1)S(1)} %get-tuple-element.48), channel_id=1, source_target_pairs={{0,1},{128,129},{1,2},{129,130},{2,3},{130,131},{3,0},{131,128},{4... | collective-permute-start | bytes 442376 | tf_op jit(solution)/shard_map/ppermute | solution.py:276
  84.2 7.1 %collective-permute-start.19 = (s16[64,1152]{1,0:T(8,128)(2,1)S(1)}, s16[64,1152]{1,0:T(8,128)(2,1)S(1)}, u32[]{:S(2)}, u32[]{:S(2)}) collective-permute-start(s16[64,1152]{1,0:T(8,128)(2,1)S(1)} %get-tuple-element.49), channel_id=1, source_target_pairs={{0,3},{128,131},{1,0},{129,128},{2,1},{130,129},{3,2},{131,130},{4... | collective-permute-start | bytes 442376 | tf_op jit(solution)/shard_map/ppermute | solution.py:276

commit v12 on v10

--- a/solution.py
+++ b/solution.py
@@ -183,13 +183,11 @@
 
 
 def far_terms(target_count, lines, height, *refs):
-    inputs, (up, down, up_half, down_half) = last_columns(lines, 0, 5 * height, *refs)
+    inputs, (up, down, across) = last_columns(lines, 0, 5 * height, *refs)
     for i in range(4):
         code = encode(*terms(target_count, *inputs, slice(i * height, (i + 1) * height)))
         (up, down)[i // 2][i % 2 * height : (i % 2 + 1) * height, :] = code
-    code = encode(*terms(target_count, *inputs, slice(4 * height, 5 * height)))
-    down_half[...] = code[: height // 2, :]
-    up_half[...] = code[height // 2 :, :]
+    across[...] = encode(*terms(target_count, *inputs, slice(4 * height, 5 * height)))
 
 
 def near_terms(target_count, lines, height, *refs):
@@ -200,27 +198,19 @@
         proof[part, :] = jnp.broadcast_to(small, (height, LANES))
 
 
-def pass_on(gradient, proof, from_below, from_above, half_below, half_above, up, down):
+def pass_on(gradient, proof, from_below, from_above, up, down):
     width, height = gradient.shape[1], gradient.shape[0] // 3
-    for i, near, half, out in ((0, from_below, half_below, up), (1, from_above, half_above, down)):
+    for i, near, out in ((0, from_below, up), (1, from_above, down)):
         part = slice(i * height, (i + 1) * height)
         near_gradient, near_proof = decode(near[:height, :], width)
-        half_gradient, half_proof = decode(half[...], width)
-        zeros = jnp.zeros((height // 2, width), F32), jnp.zeros((height // 2, 1), F32)
-        both = [(half_gradient, zeros[0]), (half_proof, zeros[1])]
-        if i == 0:
-            both = [pair[::-1] for pair in both]
-        half_gradient, half_proof = (jnp.concatenate(pair, axis=0) for pair in both)
-        out[...] = encode(
-            gradient[part, :] + near_gradient + half_gradient,
-            proof[part, :1] + near_proof + half_proof,
-        )
-
-
-def add_up(gradient, proof, from_below, from_above, far_below, far_above, out_proof, out):
+        out[...] = encode(gradient[part, :] + near_gradient, proof[part, :1] + near_proof)
+
+
+def add_up(gradient, proof, from_below, from_above, opposite, far_below, far_above, out_proof, out):
     width, height = gradient.shape[1], gradient.shape[0] // 3
     total, small = gradient[2 * height :, :], proof[2 * height :, :1]
-    for coded in (from_below[height:, :], from_above[height:, :], far_below[...], far_above[...]):
+    near = from_below[height:, :], from_above[height:, :]
+    for coded in (*near, opposite[...], far_below[...], far_above[...]):
         one, part = decode(coded, width)
         total, small = total + one, small + part
     out[...] = total
@@ -356,20 +346,20 @@
             limit=16,
         )(*inputs)
 
-    whole, half = (shape((n, width + LANES), jnp.int16) for n in (2 * height, height // 2))
-    up, down, up_half, down_half = last(far_terms, 5 * height, (whole, whole, half, half))
+    two, one = (shape((n, width + LANES), jnp.int16) for n in (2 * height, height))
+    up, down, across = last(far_terms, 5 * height, (two, two, one))
     from_above, from_below = up_the_ring(down, ring - 1), up_the_ring(up, 1)
-    half_above, half_below = up_the_ring(down_half, ring - 2), up_the_ring(up_half, 2)
+    opposite = up_the_ring(across, ring // 2)
     near = last(
         near_terms, 3 * height, (shape((3 * height, width), F32), shape((3 * height, LANES), F32))
     )
     up, down = in_vmem(pass_on, "pass_on", (shape((height, width + LANES), jnp.int16),) * 2)(
-        *near, from_below, from_above, half_below, half_above
+        *near, from_below, from_above
     )
     far_above, far_below = up_the_ring(down, ring - 2), up_the_ring(up, 2)
     proof, gradient = in_vmem(
         add_up, "add_up", (shape((1, height), F32), shape((height, width), F32))
-    )(*near, from_below, from_above, far_below, far_above)
+    )(*near, from_below, from_above, opposite, far_below, far_above)
     return proof.reshape(height), gradient
 
 

time: 92 us -> 94 us (1.022)
  the two profiles are of different devices: /device:TPU:8 before, /device:TPU:40 now
where the time goes in v12:
time: 94 us; the launch traced here: 93.8 us
  starting transfers between devices  30.3 us (32%)
  blocking collectives  28.1 us (30%)
  waiting for transfers between devices  18 us (19%)
  Pallas kernels  15.7 us (17%)
  local copies, waits for them, and re-layouts  0.97 us (1%)
    all_to_all x1, blocking collectives, on_device(): lax.all_to_all(chosen, CHIPS, split_axis=0, concat_axis=0, tiled=True)  28.1 us
    ppermute x9, starting transfers between devices, up_the_ring(): lax.ppermute(x, RING, [(place(i), place((i + step) % ring)) for i in rang...  19.4 us
    ppermute x9, waiting for transfers between devices, up_the_ring(): lax.ppermute(x, RING, [(place(i), place((i + step) % ring)) for i in rang...  17.1 us
    pallas_call x8, Pallas kernels, call(): pl.pallas_call(body, out_shape=out_shape, in_specs=[spec] * len(args), ou...  15.7 us
    ppermute x6, starting transfers between devices, along_line(): return lax.ppermute(x, PLANE, pairs)  9.45 us
  transfers between devices with their start and end apart: 20, of which 7 were waited for; matrix products, arithmetic and copies ran while one was open for 0% of the time, Pallas kernels for 9%

profile of v12, /device:TPU:40, one launch (start us, length us, event | category | flops | bytes accessed | tf_op | source)
XLA Modules:
  0.0 93.8 jit_solution(5278616373818987527)
XLA Ops:
  0.6 2.0 %pack_block.1 = (bf16[144,1024]{1,0:T(8,128)(2,1)}, f32[128,1,128]{2,1,0:T(1,128)}) custom-call(bf16[64,1024]{1,0:T(8,128)(2,1)} %pool.1, bf16[64,1024]{1,0:T(8,128)(2,1)} %targets.1, s32[1,64]{1,0:T(1,128)} %bitcast.2), custom_call_target="tpu_custom_call" | custom-call | bytes 1048576 | tf_op jit(solution)/shard_map/pack_block/pallas_call | solution.py:30
  2.6 1.5 %collective-permute-start.2 = (bf16[144,1024]{1,0:T(8,128)(2,1)}, bf16[144,1024]{1,0:T(8,128)(2,1)S(1)}, u32[]{:S(2)}, u32[]{:S(2)}) collective-permute-start(bf16[144,1024]{1,0:T(8,128)(2,1)} %get-tuple-element.26.refs_0_.block), channel_id=1, source_target_pairs={{0,32},{16,20},{4,36},{20,24},{8,40},{24,28},{12,44},{28,16},{32,6... | collective-permute-start | bytes 884744 | tf_op jit(solution)/shard_map/ppermute | solution.py:277
  4.1 1.7 %collective-permute-start.3 = (bf16[144,1024]{1,0:T(8,128)(2,1)}, bf16[144,1024]{1,0:T(8,128)(2,1)S(1)}, u32[]{:S(2)}, u32[]{:S(2)}) collective-permute-start(bf16[144,1024]{1,0:T(8,128)(2,1)} %get-tuple-element.26.refs_0_.block), channel_id=1, source_target_pairs={{0,96},{16,28},{4,100},{20,16},{8,104},{24,20},{12,108},{28,24},{3... | collective-permute-start | bytes 884744 | tf_op jit(solution)/shard_map/ppermute | solution.py:277
  5.8 1.8 %collective-permute-start.4 = (bf16[144,1024]{1,0:T(8,128)(2,1)}, bf16[144,1024]{1,0:T(8,128)(2,1)S(1)}, u32[]{:S(2)}, u32[]{:S(2)}) collective-permute-start(bf16[144,1024]{1,0:T(8,128)(2,1)} %get-tuple-element.26.refs_0_.block), channel_id=1, source_target_pairs={{0,64},{16,24},{4,68},{20,28},{8,72},{24,16},{12,76},{28,20},{32,9... | collective-permute-start | bytes 884744 | tf_op jit(solution)/shard_map/ppermute | solution.py:277
  7.7 1.9 %collective-permute-start = (bf16[64,1024]{1,0:T(8,128)(2,1)}, bf16[64,1024]{1,0:T(8,128)(2,1)S(1)}, u32[]{:S(2)}, u32[]{:S(2)}) collective-permute-start(bf16[64,1024]{1,0:T(8,128)(2,1)} %pool.1), channel_id=1, source_target_pairs={{0,128},{128,1},{1,129},{129,2},{2,130},{130,3},{3,131},{131,0},{4... | collective-permute-start | bytes 393224 | tf_op jit(solution)/shard_map/ppermute | solution.py:267
  9.7 3.2 %collective-permute-done.refs_4_.below = bf16[64,1024]{1,0:T(8,128)(2,1)S(1)} collective-permute-done((bf16[64,1024]{1,0:T(8,128)(2,1)}, bf16[64,1024]{1,0:T(8,128)(2,1)S(1)}, u32[]{:S(2)}, u32[]{:S(2)}) %collective-permute-start) | collective-permute-done | bytes 131104 | tf_op jit(solution)/shard_map/ppermute | solution.py:267
  12.8 1.9 %collective-permute-done.1.refs_5_.above = bf16[64,1024]{1,0:T(8,128)(2,1)S(1)} collective-permute-done((bf16[64,1024]{1,0:T(8,128)(2,1)}, bf16[64,1024]{1,0:T(8,128)(2,1)S(1)}, u32[]{:S(2)}, u32[]{:S(2)}) %collective-permute-start.1) | collective-permute-done | bytes 131104 | tf_op jit(solution)/shard_map/ppermute | solution.py:267
  14.8 0.1 collective-permute-done.4.refs_3_
  14.9 1.0 %copy-done = bf16[144,1024]{1,0:T(8,128)(2,1)S(1)} copy-done((bf16[144,1024]{1,0:T(8,128)(2,1)S(1)}, bf16[144,1024]{1,0:T(8,128)(2,1)}, u32[]{:S(2)}) %copy-start) | copy-done | bytes 294936
  15.9 0.1 pack_line.1
  16.0 1.7 %collective-permute-start.7 = (bf16[528,1024]{1,0:T(8,128)(2,1)S(1)}, bf16[528,1024]{1,0:T(8,128)(2,1)S(1)}, u32[]{:S(2)}, u32[]{:S(2)}) collective-permute-start(bf16[528,1024]{1,0:T(8,128)(2,1)S(1)} %get-tuple-element.29.refs_0_), channel_id=1, source_target_pairs={{0,4},{16,48},{4,8},{20,52},{8,12},{24,56},{12,0},{28,60},{32,36},... | collective-permute-start | bytes 3244040 | tf_op jit(solution)/shard_map/ppermute | solution.py:277
  17.6 0.5 collective-permute-start.8
  18.1 2.3 %collective-permute-start.9 = (bf16[528,1024]{1,0:T(8,128)(2,1)S(1)}, bf16[528,1024]{1,0:T(8,128)(2,1)S(1)}, u32[]{:S(2)}, u32[]{:S(2)}) collective-permute-start(bf16[528,1024]{1,0:T(8,128)(2,1)S(1)} %get-tuple-element.29.refs_0_), channel_id=1, source_target_pairs={{0,8},{16,80},{4,12},{20,84},{8,0},{24,88},{12,4},{28,92},{32,40},... | collective-permute-start | bytes 3244040 | tf_op jit(solution)/shard_map/ppermute | solution.py:277
  20.4 5.8 %collective-permute-start.5 = (bf16[160,1024]{1,0:T(8,128)(2,1)S(1)}, bf16[160,1024]{1,0:T(8,128)(2,1)S(1)}, u32[]{:S(2)}, u32[]{:S(2)}) collective-permute-start(bf16[160,1024]{1,0:T(8,128)(2,1)S(1)} %get-tuple-element.27), channel_id=1, source_target_pairs={{0,129},{128,2},{1,130},{129,3},{2,131},{130,0},{3,128},{131,1},{4... | collective-permute-start | bytes 983048 | tf_op jit(solution)/shard_map/ppermute | solution.py:267
  26.2 28.1 %all_to_all.5.refs_4_.chosen = f32[128,1,128]{2,1,0:T(1,128)S(1)} all-to-all(f32[128,1,128]{2,1,0:T(1,128)S(1)} %copy-done.2), channel_id=1, replica_groups=mesh['zl'=2,'x'=4,'c'=2,'y'=4,'zh'=4] {'zl','x','y','zh'}, dimensions={0} | all-to-all | bytes 131072 | tf_op jit(solution)/shard_map/all_to_all | solution.py:300
  54.5 0.5 collective-permute-start.11
  55.1 0.4 collective-permute-start.13
  55.5 0.1 add_counts.1.refs_10_
  55.6 0.4 collective-permute-start.14
  56.0 5.1 %first_columns.1 = (bf16[512,1024]{1,0:T(8,128)(2,1)S(1)}, f32[512,128]{1,0:T(8,128)S(1)}, f32[512,1024]{1,0:T(8,128)S(1)}, f32[512,1024]{1,0:T(8,128)S(1)}, f32...) custom-call(bf16[144,1024]{1,0:T(8,128)(2,1)S(1)} %copy-done.1, bf16[64,1024]{1,0:T(8,128)(2,1)S(1)} %collective-permute-done.refs_4_.below, ...), custom_call_target="tpu_custom_call" | custom-call | flops 4294967296 | bytes 1048576 | tf_op jit(solution)/shard_map/first_columns/pallas_call | solution.py:30
  61.2 0.7 collective-permute-done.14.refs_11_
  61.9 4.0 %far_terms.1 = (s16[128,1152]{1,0:T(8,128)(2,1)S(1)}, s16[128,1152]{1,0:T(8,128)(2,1)S(1)}, s16[64,1152]{1,0:T(8,128)(2,1)S(1)}) custom-call(bf16[512,1024]{1,0:T(8,128)(2,1)S(1)} %get-tuple-element.35.refs_0_, f32[512,128]{1,0:T(8,128)S(1)} %get-tuple-element.36.refs_1_, bf16[528,1024]{1,0:T(8,128)(2,1)S(1)} %collective-permute-done.10.refs_2_, ...), custom_call_target="tpu_custom_call" | custom-call | flops 2684354560 | bytes 1048576 | tf_op jit(solution)/shard_map/far_terms/pallas_call | solution.py:30
  65.9 0.9 collective-permute-start.15
  66.7 1.2 %collective-permute-start.16 = (s16[128,1152]{1,0:T(8,128)(2,1)S(1)}, s16[128,1152]{1,0:T(8,128)(2,1)S(1)}, u32[]{:S(2)}, u32[]{:S(2)}) collective-permute-start(s16[128,1152]{1,0:T(8,128)(2,1)S(1)} %get-tuple-element.44), channel_id=1, source_target_pairs={{0,131},{128,0},{1,128},{129,1},{2,129},{130,2},{3,130},{131,3},{4... | collective-permute-start | bytes 884744 | tf_op jit(solution)/shard_map/ppermute | solution.py:267
  68.0 1.6 %collective-permute-start.17 = (s16[64,1152]{1,0:T(8,128)(2,1)S(1)}, s16[64,1152]{1,0:T(8,128)(2,1)S(1)}, u32[]{:S(2)}, u32[]{:S(2)}) collective-permute-start(s16[64,1152]{1,0:T(8,128)(2,1)S(1)} %get-tuple-element.45), channel_id=1, source_target_pairs={{0,2},{128,130},{1,3},{129,131},{2,0},{130,128},{3,1},{131,129},{4... | collective-permute-start | bytes 442376 | tf_op jit(solution)/shard_map/ppermute | solution.py:267
  69.6 2.7 %near_terms.1 = (f32[192,1024]{1,0:T(8,128)S(1)}, f32[192,128]{1,0:T(8,128)S(1)}) custom-call(bf16[512,1024]{1,0:T(8,128)(2,1)S(1)} %get-tuple-element.35.refs_0_, f32[512,128]{1,0:T(8,128)S(1)} %get-tuple-element.36.refs_1_, bf16[528,1024]{1,0:T(8,128)(2,1)S(1)} %collective-permute-done.10.refs_2_, bf16[528,1024]{1,0:T(8,128)(2,1)S(1)} %collective-permute-done.11.refs_3_, ...), custom_call_target="tpu_custom_call" | custom-call | flops 1610612736 | bytes 1048576 | tf_op jit(solution)/shard_map/near_terms/pallas_call | solution.py:30
  72.3 5.2 %collective-permute-done.15.from_below = s16[128,1152]{1,0:T(8,128)(2,1)S(1)} collective-permute-done((s16[128,1152]{1,0:T(8,128)(2,1)S(1)}, s16[128,1152]{1,0:T(8,128)(2,1)S(1)}, u32[]{:S(2)}, u32[]{:S(2)}) %collective-permute-start.15) | collective-permute-done | bytes 294944 | tf_op jit(solution)/shard_map/ppermute | solution.py:267
  77.5 0.5 pass_on.1
  78.0 7.8 %collective-permute-start.18 = (s16[64,1152]{1,0:T(8,128)(2,1)S(1)}, s16[64,1152]{1,0:T(8,128)(2,1)S(1)}, u32[]{:S(2)}, u32[]{:S(2)}) collective-permute-start(s16[64,1152]{1,0:T(8,128)(2,1)S(1)} %get-tuple-element.46), channel_id=1, source_target_pairs={{0,1},{128,129},{1,2},{129,130},{2,3},{130,131},{3,0},{131,128},{4... | collective-permute-start | bytes 442376 | tf_op jit(solution)/shard_map/ppermute | solution.py:267
  85.8 2.7 %collective-permute-done.18.far_below = s16[64,1152]{1,0:T(8,128)(2,1)S(1)} collective-permute-done((s16[64,1152]{1,0:T(8,128)(2,1)S(1)}, s16[64,1152]{1,0:T(8,128)(2,1)S(1)}, u32[]{:S(2)}, u32[]{:S(2)}) %collective-permute-start.18) | collective-permute-done | bytes 147488 | tf_op jit(solution)/shard_map/ppermute | solution.py:267
  88.5 4.2 %collective-permute-done.19.far_above = s16[64,1152]{1,0:T(8,128)(2,1)S(1)} collective-permute-done((s16[64,1152]{1,0:T(8,128)(2,1)S(1)}, s16[64,1152]{1,0:T(8,128)(2,1)S(1)}, u32[]{:S(2)}, u32[]{:S(2)}) %collective-permute-start.19) | collective-permute-done | bytes 147488 | tf_op jit(solution)/shard_map/ppermute | solution.py:267
  92.7 1.1 %add_up.1 = (f32[1,64]{1,0:T(1,128)}, f32[64,1024]{1,0:T(8,128)}) custom-call(f32[192,1024]{1,0:T(8,128)S(1)} %get-tuple-element.41.gradient, f32[192,128]{1,0:T(8,128)S(1)} %get-tuple-element.42.proof, s16[128,1152]{1,0:T(8,128)(2,1)S(1)} %collective-permute-done.15.from_below, s16[128,1152]{1,0:T(8,128)(2,1)S(1)} %collective-permute-done.16.from_above, ...), custom_call_target="tpu_custom_call" | custom-call | bytes 1048576 | tf_op jit(solution)/shard_map/add_up/pallas_call | solution.py:30
  (24 shorter events, 0.4 us)
Async XLA Ops:
  2.6 12.2 %collective-permute-start.2 = (bf16[144,1024]{1,0:T(8,128)(2,1)}, bf16[144,1024]{1,0:T(8,128)(2,1)S(1)}, u32[]{:S(2)}, u32[]{:S(2)}) collective-permute-start(bf16[144,1024]{1,0:T(8,128)(2,1)} %get-tuple-element.26.refs_0_.block), channel_id=1, source_target_pairs={{0,32},{16,20},{4,36},{20,24},{8,40},{24,28},{12,44},{28,16},{32,6... | collective-permute-start | bytes 884744 | tf_op jit(solution)/shard_map/ppermute | solution.py:277
  4.1 10.7 %collective-permute-start.3 = (bf16[144,1024]{1,0:T(8,128)(2,1)}, bf16[144,1024]{1,0:T(8,128)(2,1)S(1)}, u32[]{:S(2)}, u32[]{:S(2)}) collective-permute-start(bf16[144,1024]{1,0:T(8,128)(2,1)} %get-tuple-element.26.refs_0_.block), channel_id=1, source_target_pairs={{0,96},{16,28},{4,100},{20,16},{8,104},{24,20},{12,108},{28,24},{3... | collective-permute-start | bytes 884744 | tf_op jit(solution)/shard_map/ppermute | solution.py:277
  5.8 9.1 %collective-permute-start.4 = (bf16[144,1024]{1,0:T(8,128)(2,1)}, bf16[144,1024]{1,0:T(8,128)(2,1)S(1)}, u32[]{:S(2)}, u32[]{:S(2)}) collective-permute-start(bf16[144,1024]{1,0:T(8,128)(2,1)} %get-tuple-element.26.refs_0_.block), channel_id=1, source_target_pairs={{0,64},{16,24},{4,68},{20,28},{8,72},{24,16},{12,76},{28,20},{32,9... | collective-permute-start | bytes 884744 | tf_op jit(solution)/shard_map/ppermute | solution.py:277
  7.7 5.2 %collective-permute-start = (bf16[64,1024]{1,0:T(8,128)(2,1)}, bf16[64,1024]{1,0:T(8,128)(2,1)S(1)}, u32[]{:S(2)}, u32[]{:S(2)}) collective-permute-start(bf16[64,1024]{1,0:T(8,128)(2,1)} %pool.1), channel_id=1, source_target_pairs={{0,128},{128,1},{1,129},{129,2},{2,130},{130,3},{3,131},{131,0},{4... | collective-permute-start | bytes 393224 | tf_op jit(solution)/shard_map/ppermute | solution.py:267
  9.6 5.2 %collective-permute-start.1 = (bf16[64,1024]{1,0:T(8,128)(2,1)}, bf16[64,1024]{1,0:T(8,128)(2,1)S(1)}, u32[]{:S(2)}, u32[]{:S(2)}) collective-permute-start(bf16[64,1024]{1,0:T(8,128)(2,1)} %pool.1), channel_id=1, source_target_pairs={{0,131},{128,0},{1,128},{129,1},{2,129},{130,2},{3,130},{131,3},{4... | collective-permute-start | bytes 393224 | tf_op jit(solution)/shard_map/ppermute | solution.py:267
  14.9 1.0 %copy-start = (bf16[144,1024]{1,0:T(8,128)(2,1)S(1)}, bf16[144,1024]{1,0:T(8,128)(2,1)}, u32[]{:S(2)}) copy-start(bf16[144,1024]{1,0:T(8,128)(2,1)} %get-tuple-element.26.refs_0_.block) | copy-start | bytes 884740
  15.9 10.4 %copy-start.2 = (f32[128,1,128]{2,1,0:T(1,128)S(1)}, f32[128,1,128]{2,1,0:T(1,128)}, u32[]{:S(2)}) copy-start(f32[128,1,128]{2,1,0:T(1,128)} %get-tuple-element.30) | copy-start | bytes 196612
  16.0 38.4 %collective-permute-start.7 = (bf16[528,1024]{1,0:T(8,128)(2,1)S(1)}, bf16[528,1024]{1,0:T(8,128)(2,1)S(1)}, u32[]{:S(2)}, u32[]{:S(2)}) collective-permute-start(bf16[528,1024]{1,0:T(8,128)(2,1)S(1)} %get-tuple-element.29.refs_0_), channel_id=1, source_target_pairs={{0,4},{16,48},{4,8},{20,52},{8,12},{24,56},{12,0},{28,60},{32,36},... | collective-permute-start | bytes 3244040 | tf_op jit(solution)/shard_map/ppermute | solution.py:277
  17.6 36.7 %collective-permute-start.8 = (bf16[528,1024]{1,0:T(8,128)(2,1)S(1)}, bf16[528,1024]{1,0:T(8,128)(2,1)S(1)}, u32[]{:S(2)}, u32[]{:S(2)}) collective-permute-start(bf16[528,1024]{1,0:T(8,128)(2,1)S(1)} %get-tuple-element.29.refs_0_), channel_id=1, source_target_pairs={{0,12},{16,112},{4,0},{20,116},{8,4},{24,120},{12,8},{28,124},{32,... | collective-permute-start | bytes 3244040 | tf_op jit(solution)/shard_map/ppermute | solution.py:277
  18.1 36.3 %collective-permute-start.9 = (bf16[528,1024]{1,0:T(8,128)(2,1)S(1)}, bf16[528,1024]{1,0:T(8,128)(2,1)S(1)}, u32[]{:S(2)}, u32[]{:S(2)}) collective-permute-start(bf16[528,1024]{1,0:T(8,128)(2,1)S(1)} %get-tuple-element.29.refs_0_), channel_id=1, source_target_pairs={{0,8},{16,80},{4,12},{20,84},{8,0},{24,88},{12,4},{28,92},{32,40},... | collective-permute-start | bytes 3244040 | tf_op jit(solution)/shard_map/ppermute | solution.py:277
  20.4 34.0 %collective-permute-start.5 = (bf16[160,1024]{1,0:T(8,128)(2,1)S(1)}, bf16[160,1024]{1,0:T(8,128)(2,1)S(1)}, u32[]{:S(2)}, u32[]{:S(2)}) collective-permute-start(bf16[160,1024]{1,0:T(8,128)(2,1)S(1)} %get-tuple-element.27), channel_id=1, source_target_pairs={{0,129},{128,2},{1,130},{129,3},{2,131},{130,0},{3,128},{131,1},{4... | collective-permute-start | bytes 983048 | tf_op jit(solution)/shard_map/ppermute | solution.py:267
  26.2 28.1 %collective-permute-start.6 = (bf16[160,1024]{1,0:T(8,128)(2,1)S(1)}, bf16[160,1024]{1,0:T(8,128)(2,1)S(1)}, u32[]{:S(2)}, u32[]{:S(2)}) collective-permute-start(bf16[160,1024]{1,0:T(8,128)(2,1)S(1)} %get-tuple-element.28), channel_id=1, source_target_pairs={{0,130},{128,3},{1,131},{129,0},{2,128},{130,1},{3,129},{131,2},{4... | collective-permute-start | bytes 983048 | tf_op jit(solution)/shard_map/ppermute | solution.py:267
  54.3 1.7 %copy-start.1 = (bf16[144,1024]{1,0:T(8,128)(2,1)S(1)}, bf16[144,1024]{1,0:T(8,128)(2,1)}, u32[]{:S(2)}) copy-start(bf16[144,1024]{1,0:T(8,128)(2,1)} %get-tuple-element.26.refs_0_.block) | copy-start | bytes 884740
  54.4 7.4 %collective-permute-start.10 = (bf16[528,1024]{1,0:T(8,128)(2,1)S(1)}, bf16[528,1024]{1,0:T(8,128)(2,1)S(1)}, u32[]{:S(2)}, u32[]{:S(2)}) collective-permute-start(bf16[528,1024]{1,0:T(8,128)(2,1)S(1)} %get-tuple-element.31.refs_0_), channel_id=1, source_target_pairs={{0,16},{16,0},{1,17},{17,1},{2,18},{18,2},{3,19},{19,3},{4,20},{20... | collective-permute-start | bytes 3244040 | tf_op jit(solution)/shard_map/ppermute | solution.py:285
  54.5 7.3 %collective-permute-start.11 = (bf16[528,1024]{1,0:T(8,128)(2,1)S(1)}, bf16[528,1024]{1,0:T(8,128)(2,1)S(1)}, u32[]{:S(2)}, u32[]{:S(2)}) collective-permute-start(bf16[528,1024]{1,0:T(8,128)(2,1)S(1)} %get-tuple-element.32.refs_1_), channel_id=1, source_target_pairs={{0,16},{16,0},{1,17},{17,1},{2,18},{18,2},{3,19},{19,3},{4,20},{20... | collective-permute-start | bytes 3244040 | tf_op jit(solution)/shard_map/ppermute | solution.py:285
  55.0 6.9 %collective-permute-start.12 = (bf16[528,1024]{1,0:T(8,128)(2,1)S(1)}, bf16[528,1024]{1,0:T(8,128)(2,1)S(1)}, u32[]{:S(2)}, u32[]{:S(2)}) collective-permute-start(bf16[528,1024]{1,0:T(8,128)(2,1)S(1)} %get-tuple-element.33.refs_2_), channel_id=1, source_target_pairs={{0,16},{16,0},{1,17},{17,1},{2,18},{18,2},{3,19},{19,3},{4,20},{20... | collective-permute-start | bytes 3244040 | tf_op jit(solution)/shard_map/ppermute | solution.py:285
  55.1 6.8 %collective-permute-start.13 = (bf16[528,1024]{1,0:T(8,128)(2,1)S(1)}, bf16[528,1024]{1,0:T(8,128)(2,1)S(1)}, u32[]{:S(2)}, u32[]{:S(2)}) collective-permute-start(bf16[528,1024]{1,0:T(8,128)(2,1)S(1)} %get-tuple-element.34.refs_3_), channel_id=1, source_target_pairs={{0,16},{16,0},{1,17},{17,1},{2,18},{18,2},{3,19},{19,3},{4,20},{20... | collective-permute-start | bytes 3244040 | tf_op jit(solution)/shard_map/ppermute | solution.py:285
  55.6 6.2 %collective-permute-start.14 = (f32[8,128]{1,0:T(8,128)S(1)}, f32[8,128]{1,0:T(8,128)S(1)}, u32[]{:S(2)}, u32[]{:S(2)}) collective-permute-start(f32[8,128]{1,0:T(8,128)S(1)} %add_counts.1.refs_10_), channel_id=1, source_target_pairs={{0,16},{16,0},{1,17},{17,1},{2,18},{18,2},{3,19},{19,3},{4,20},{20... | collective-permute-start | bytes 12296 | tf_op jit(solution)/shard_map/ppermute | solution.py:285
  65.9 11.7 %collective-permute-start.15 = (s16[128,1152]{1,0:T(8,128)(2,1)S(1)}, s16[128,1152]{1,0:T(8,128)(2,1)S(1)}, u32[]{:S(2)}, u32[]{:S(2)}) collective-permute-start(s16[128,1152]{1,0:T(8,128)(2,1)S(1)} %get-tuple-element.43), channel_id=1, source_target_pairs={{0,128},{128,1},{1,129},{129,2},{2,130},{130,3},{3,131},{131,0},{4... | collective-permute-start | bytes 884744 | tf_op jit(solution)/shard_map/ppermute | solution.py:267
  66.7 10.8 %collective-permute-start.16 = (s16[128,1152]{1,0:T(8,128)(2,1)S(1)}, s16[128,1152]{1,0:T(8,128)(2,1)S(1)}, u32[]{:S(2)}, u32[]{:S(2)}) collective-permute-start(s16[128,1152]{1,0:T(8,128)(2,1)S(1)} %get-tuple-element.44), channel_id=1, source_target_pairs={{0,131},{128,0},{1,128},{129,1},{2,129},{130,2},{3,130},{131,3},{4... | collective-permute-start | bytes 884744 | tf_op jit(solution)/shard_map/ppermute | solution.py:267
  68.0 17.9 %collective-permute-start.17 = (s16[64,1152]{1,0:T(8,128)(2,1)S(1)}, s16[64,1152]{1,0:T(8,128)(2,1)S(1)}, u32[]{:S(2)}, u32[]{:S(2)}) collective-permute-start(s16[64,1152]{1,0:T(8,128)(2,1)S(1)} %get-tuple-element.45), channel_id=1, source_target_pairs={{0,2},{128,130},{1,3},{129,131},{2,0},{130,128},{3,1},{131,129},{4... | collective-permute-start | bytes 442376 | tf_op jit(solution)/shard_map/ppermute | solution.py:267
  78.0 10.5 %collective-permute-start.18 = (s16[64,1152]{1,0:T(8,128)(2,1)S(1)}, s16[64,1152]{1,0:T(8,128)(2,1)S(1)}, u32[]{:S(2)}, u32[]{:S(2)}) collective-permute-start(s16[64,1152]{1,0:T(8,128)(2,1)S(1)} %get-tuple-element.46), channel_id=1, source_target_pairs={{0,1},{128,129},{1,2},{129,130},{2,3},{130,131},{3,0},{131,128},{4... | collective-permute-start | bytes 442376 | tf_op jit(solution)/shard_map/ppermute | solution.py:267
  85.8 6.8 %collective-permute-start.19 = (s16[64,1152]{1,0:T(8,128)(2,1)S(1)}, s16[64,1152]{1,0:T(8,128)(2,1)S(1)}, u32[]{:S(2)}, u32[]{:S(2)}) collective-permute-start(s16[64,1152]{1,0:T(8,128)(2,1)S(1)} %get-tuple-element.47), channel_id=1, source_target_pairs={{0,3},{128,131},{1,0},{129,128},{2,1},{130,129},{3,2},{131,130},{4... | collective-permute-start | bytes 442376 | tf_op jit(solution)/shard_map/ppermute | solution.py:267
